TPU v7x, 32 devices: a whole 2x2x4 slice. The times are simulated.
32 devices in a mesh: grp: 4 (over z), sub: 8 (over y, x, core).
Axes of the slice: x: 2, y: 2, z: 4, core: 2. Of those that a mesh axis runs over, the one named last changes fastest.
Arguments:
- residual: float32 [8, 24576], P(None, 'sub'), may hold values from -6 to 6
- margin: int32 [8, 8], replicated, may hold values from 0 to 191, as said below
- aggregate: int32 [192], P('sub'), may hold values from 0 to 63
- local_factor: bfloat16 [8, 4096, 4096], P('sub', 'grp'), may hold values from -0.09375 to 0.09375
- coarse_factor: bfloat16 [8192, 8192], P('sub'), may hold values from -0.0625 to 0.0625
Outputs:
- preconditioned: float32 [8, 24576], P('grp', 'sub')
Inputs may be any that keep to these rules, and one draw needn't show every extreme that they name: `margin`: for subdomain s, every entry names a block owned by another subdomain (block b is owned by subdomain b // 24); the entries of one row are distinct. Up to 8 entries of one row may name blocks of the same owner, and in every draw some row takes all of its entries from a single owner. `aggregate`: the counts of global blocks for each coarse block are whole numbers and may cross devices as int32.
All inputs are finite; a program needn't handle non-finite values.
Results may differ from a plain program's by a relative error of at most 0.0033.
Values sent between devices are 32-bit elements; how exact they have to be, the bound alone decides.
No kernel may reach another device: no remote copies, remote signals or barrier semaphores. Data moves between devices by JAX's collectives and lax.ppermute only.
A program may use at most 64 MiB of HBM per device.

v0:
```python
import jax
import jax.numpy as jnp
from jax import lax
from jax.sharding import PartitionSpec as P

BLK = 128
NCB = 64


def row_of(table, index):
    return lax.dynamic_index_in_dim(table, index, 0, keepdims=False)


def pick_table(row_owners, row_slots, target, owned):
    hits = (row_owners == target).astype(jnp.float32)
    places = (row_slots[..., None] == jnp.arange(owned, dtype=jnp.int32)).astype(jnp.float32)
    return hits[..., None] * places


def on_device(residual, margin, aggregate, local_factor, coarse_factor):
    sub_count = lax.axis_size("sub")
    grp_count = lax.axis_size("grp")
    my_index = lax.axis_index("sub")
    grp_index = lax.axis_index("grp")
    rhs_count, own_width = residual.shape
    owned = own_width // BLK
    group_rows = rhs_count // grp_count
    blocks = residual.reshape(rhs_count, owned, BLK)
    owners = margin // owned
    in_slot = margin % owned
    exact = lax.Precision.HIGHEST
    picker_all = pick_table(owners, in_slot, my_index, owned)
    outgoing = jnp.einsum("skb,rbc->srkc", picker_all, blocks, precision=exact)
    arrived = lax.all_to_all(outgoing, "sub", split_axis=0, concat_axis=0, tiled=True)
    halo_rows = jnp.sum(arrived, axis=0)
    local_rhs = (
        jnp.concatenate([blocks, halo_rows], axis=1).reshape(rhs_count, -1).astype(jnp.bfloat16)
    )
    factor = local_factor[0]
    inner_term = jnp.dot(local_rhs, factor.T, preferred_element_type=jnp.float32).astype(
        jnp.bfloat16
    )
    local_sol = lax.psum_scatter(
        jnp.dot(inner_term, factor, preferred_element_type=jnp.float32),
        "grp",
        scatter_dimension=0,
        tiled=True,
    )
    local_sol = local_sol.reshape(group_rows, -1, BLK)
    own_part = local_sol[:, :owned]
    back_rows = local_sol[:, owned:]
    my_owners = row_of(owners, my_index)
    targets = jnp.arange(sub_count, dtype=jnp.int32)
    sending = (my_owners[None, :] == targets[:, None]).astype(jnp.float32)
    outgoing_back = sending[:, None, :, None] * back_rows[None]
    arrived_back = lax.all_to_all(outgoing_back, "sub", split_axis=0, concat_axis=0, tiled=True)
    returned = jnp.einsum("skb,srkc->rbc", picker_all, arrived_back, precision=exact)
    catalog = jnp.arange(NCB, dtype=jnp.int32)
    member = (aggregate[:, None] == catalog[None, :]).astype(jnp.float32)
    mine = lax.dynamic_slice_in_dim(blocks, grp_index * group_rows, group_rows, 0)
    sums_part = jnp.einsum("rbk,bj->rjk", mine, member, precision=exact)
    sums, counts = lax.psum((sums_part, jnp.sum(member, axis=0)), "sub")
    coarse_rhs = (
        (sums / jnp.maximum(counts, 1.0)[None, :, None])
        .reshape(group_rows, -1)
        .astype(jnp.bfloat16)
    )
    inner_coarse = jnp.dot(coarse_rhs, coarse_factor.T, preferred_element_type=jnp.float32).astype(
        jnp.bfloat16
    )
    coarse_part = jnp.dot(inner_coarse, coarse_factor, preferred_element_type=jnp.float32)
    coarse_sol = lax.psum(coarse_part, "sub")
    prolonged = jnp.einsum(
        "rjk,bj->rbk", coarse_sol.reshape(group_rows, NCB, BLK), member, precision=exact
    )
    result = own_part + returned + prolonged
    return result.reshape(group_rows, -1)


def solution(mesh):
    placed = (P(None, "sub"), P(), P("sub"), P("sub", "grp", None), P("sub", None))
    return jax.shard_map(
        on_device, mesh=mesh, in_specs=placed, out_specs=P("grp", "sub"), check_vma=False
    )
```

profile of v0, /device:TPU:0, one launch (start us, length us, event | category | flops | bytes accessed | tf_op | source)
XLA Modules:
  0.0 183.1 jit_solution(9201780765833317884)
XLA Ops:
  7.4 0.7 add_select_fusion
  8.1 0.7 compare_convert_fusion
  8.8 0.1 copy.10
  8.8 0.1 copy.9
  8.9 0.1 select_bitcast_fusion
  9.0 2.0 %convolution_bitcast_fusion = f32[8,8,8,128]{3,2,1,0:T(8,128)} fusion(f32[1,8,24,128]{3,1,2,0:T(8,128)} %bitcast.79, f32[8,8,24,1]{2,0,1,3:T(8,128)S(1)} %select_bitcast_fusion), kind=kOutput, calls=%fused_computation.4 | convolution fusion | flops 18874368 | bytes 366592 | tf_op jit(solution)/shard_map/skb,rbc->srkc/dot_general | solution.py:33
  11.0 5.2 %all-to-all-start = ((f32[8,8,8,128]{3,2,1,0:T(8,128)}), f32[8,8,8,128]{3,2,1,0:T(8,128)S(1)}, u32[]{:S(2)}, u32[]{:S(2)}) async-start(f32[8,8,8,128]{3,2,1,0:T(8,128)} %convolution_bitcast_fusion), calls=%async_computation | async-start | bytes 524288 | tf_op jit(solution)/shard_map/all_to_all | solution.py:34
  16.1 0.0 all-reduce.5.cloned.1.call-start
  16.2 0.9 copy.49
  17.1 1.6 convolution_bitcast_fusion.2
  18.7 0.0 all-reduce.5.cloned.1.call-update
  18.7 0.0 all-reduce.9.cloned.1.call-start
  18.7 0.7 convert_reduce_fusion
  19.5 14.4 %psum.22 = f32[64]{0:T(128)S(1)} all-reduce(f32[64]{0:T(128)S(1)} %convert_reduce_fusion), channel_id=1, replica_groups=mesh['grp'=4,'sub'=8] {'sub'}, use_global_device_ids=true, to_apply=%region_4.5 | all-reduce | flops 64 | bytes 512 | tf_op jit(solution)/shard_map/psum | solution.py:62
  34.0 0.9 copy.53
  34.9 1.2 dynamic-slice
  36.8 37.7 %all-reduce.5.cloned.1.call-done = f32[2,64,128]{2,1,0:T(8,128)} async-done(((f32[2,64,128]{2,1,0:T(8,128)}), f32[2,64,128]{2,1,0:T(8,128)}) %all-reduce.5.cloned.1.call-update) | async-done | bytes 65552 | tf_op jit(solution)/shard_map/psum | solution.py:62
  74.5 0.9 fusion.22
  75.4 0.0 all-to-all-done
  75.5 9.8 %fusion = f32[8,4096]{1,0:T(8,128)} fusion(bf16[1,1024,4096]{2,1,0:T(8,128)(2,1)} %param.8, bf16[1,8,32,128]{3,2,1,0:T(8,128)(2,1)S(1)} %maximum_bitcast_fusion), kind=kOutput, calls=%fused_computation | convolution fusion | flops 134225920 | bytes 8585216 | tf_op jit(solution)/shard_map/dot_general | solution.py:44
  85.3 0.0 all-reduce.9.cloned.1.call-update
  85.3 0.0 copy-start
  85.3 0.0 all-reduce.7.cloned.1.call-start
  85.4 16.9 %convolution_bitcast_fusion.1 = f32[1,2,64,128]{3,1,2,0:T(2,128)S(1)} fusion(bf16[1024,8192]{1,0:T(8,128)(2,1)} %param.9, bf16[1,2,64,128]{3,2,1,0:T(8,128)(2,1)S(1)} %fusion.22), kind=kOutput, calls=%fused_computation.5 | convolution fusion | flops 67110912 | bytes 16875520 | tf_op jit(solution)/shard_map/dot_general | solution.py:71
  102.3 0.6 copy.50
  102.9 0.0 all-reduce.7.cloned.1.call-update
  103.0 16.2 %all-reduce.9.cloned.1.call-done = f32[8,4096]{1,0:T(8,128)} async-done(((f32[8,4096]{1,0:T(8,128)}), f32[8,4096]{1,0:T(8,128)}) %all-reduce.9.cloned.1.call-update) | async-done | bytes 131088
  119.2 0.9 dynamic-slice_bitcast_fusion
  120.1 0.7 broadcast_multiply_fusion
  120.8 3.7 %all-to-all-start.1 = ((f32[8,2,8,128]{3,2,1,0:T(8,128)}), f32[8,2,8,128]{3,2,1,0:T(8,128)S(1)}, u32[]{:S(2)}, u32[]{:S(2)}) async-start(f32[8,2,8,128]{3,2,1,0:T(8,128)} %broadcast_multiply_fusion), calls=%async_computation.1 | async-start | bytes 131072 | tf_op jit(solution)/shard_map/all_to_all | solution.py:56
  124.5 49.3 %all-reduce.7.cloned.1.call-done = f32[2,64,128]{2,1,0:T(8,128)} async-done(((f32[2,64,128]{2,1,0:T(8,128)}), f32[2,64,128]{2,1,0:T(8,128)}) %all-reduce.7.cloned.1.call-update) | async-done | bytes 65552 | tf_op jit(solution)/shard_map/psum | solution.py:72
  173.8 0.0 copy-done
  173.8 1.0 convolution_bitcast_fusion.4
  174.8 0.0 all-to-all-done.1
  174.9 0.2 fusion.11
  175.1 0.6 copy.52
  (7 shorter events, 0.1 us)
Async XLA Ops:
  11.0 64.5 %all-to-all-start = ((f32[8,8,8,128]{3,2,1,0:T(8,128)}), f32[8,8,8,128]{3,2,1,0:T(8,128)S(1)}, u32[]{:S(2)}, u32[]{:S(2)}) async-start(f32[8,8,8,128]{3,2,1,0:T(8,128)} %convolution_bitcast_fusion), calls=%async_computation | async-start | bytes 524288 | tf_op jit(solution)/shard_map/all_to_all | solution.py:34
  16.1 58.4 %all-reduce.5.cloned.1.call-start = ((), (), s32[]{:S(2)}) async-start(), calls=%async_computation.2 | async-start | bytes 131072 | tf_op jit(solution)/shard_map/psum | solution.py:62
  18.7 100.5 %all-reduce.9.cloned.1.call-start = ((), (), s32[]{:S(2)}) async-start(), calls=%async_computation.4 | async-start | bytes 262144
  85.3 88.5 %copy-start = (s32[24]{0:T(128)S(1)}, s32[24]{0:T(128)}, u32[]{:S(2)}) copy-start(s32[24]{0:T(128)} %param.7) | copy-start | bytes 292
  85.3 88.5 %all-reduce.7.cloned.1.call-start = ((), (), s32[]{:S(2)}) async-start(), calls=%async_computation.3 | async-start | bytes 131072 | tf_op jit(solution)/shard_map/psum | solution.py:72
  120.8 54.0 %all-to-all-start.1 = ((f32[8,2,8,128]{3,2,1,0:T(8,128)}), f32[8,2,8,128]{3,2,1,0:T(8,128)S(1)}, u32[]{:S(2)}, u32[]{:S(2)}) async-start(f32[8,2,8,128]{3,2,1,0:T(8,128)} %broadcast_multiply_fusion), calls=%async_computation.1 | async-start | bytes 131072 | tf_op jit(solution)/shard_map/all_to_all | solution.py:56
Sparse Core Ops, SparseCore 0:
  20.3 54.1 all-reduce.4
Sparse Core Ops, SparseCore 1:
  85.4 33.8 all-reduce.8
  122.1 51.6 all-reduce.6
where the time goes:
time: 184 us; the launch traced here: 183 us
  waiting for transfers between devices  103 us (56%)
  matrix products  31.5 us (17%)
  between operations  15.6 us (8%)
  blocking collectives  14.4 us (8%)
  starting transfers between devices  8.95 us (5%)
  local copies, waits for them, and re-layouts  5.41 us (3%)
  other arithmetic  3.88 us (2%)
    psum x1, waiting for transfers between devices, on_device(): coarse_sol = lax.psum(coarse_part, 'sub')  49.3 us
    psum x1, waiting for transfers between devices, on_device(): sums, counts = lax.psum((sums_part, jnp.sum(member, axis=0)), 'sub')  37.7 us
    dot_general x1, matrix products, on_device(): jnp.dot(inner_coarse, coarse_factor, preferred_element_type=jnp.float32)  16.9 us
    unnamed x4, waiting for transfers between devices  16.3 us
    psum x1, blocking collectives, on_device(): sums, counts = lax.psum((sums_part, jnp.sum(member, axis=0)), 'sub')  14.4 us
    dot_general x1, matrix products, on_device(): jnp.dot(inner_term, factor, preferred_element_type=jnp.float32)  9.79 us
    unnamed x9, local copies, waits for them, and re-layouts  5.26 us
    all_to_all x1, starting transfers between devices, on_device(): lax.all_to_all(outgoing, 'sub', split_axis=0, concat_axis=0, tiled=True)  5.17 us
  transfers between devices with their start and end apart: 5, of which 3 were waited for; matrix products, arithmetic and copies ran while one was open for 15% of the time, Pallas kernels for 0%

commit v1 on v0

v1 whole, which is shorter than its diff:
```python
import functools

import jax
import jax.numpy as jnp
from jax import lax
from jax.experimental import pallas as pl
from jax.experimental.pallas import tpu as pltpu
from jax.sharding import PartitionSpec as P

BLK = 128
MIB = 1024 * 1024
VMEM = pl.BlockSpec(memory_space=pltpu.VMEM)
SMEM = pl.BlockSpec(memory_space=pltpu.SMEM)
NT = (((1,), (1,)), ((), ()))
TN = (((0,), (0,)), ((), ()))


def call(kernel, out, specs, scratch=(), limit=12 * MIB, flops=0, moved=0, **options):
    return pl.pallas_call(
        kernel,
        out_shape=out,
        in_specs=specs,
        out_specs=VMEM,
        scratch_shapes=scratch,
        compiler_params=pltpu.CompilerParams(vmem_limit_bytes=limit),
        cost_estimate=pl.CostEstimate(flops=flops, bytes_accessed=moved, transcendentals=0),
        **options,
    )


def mm(left, right, dims=(((1,), (0,)), ((), ()))):
    return lax.dot_general(left, right, dims, preferred_element_type=jnp.float32)


def split3(value):
    high = value.astype(jnp.bfloat16)
    rest = value - high.astype(jnp.float32)
    middle = rest.astype(jnp.bfloat16)
    low = (rest - middle.astype(jnp.float32)).astype(jnp.bfloat16)
    return [high, middle, low]


def pack_kernel(own, rows, pad, margin, aggregate, residual, out, block_rows):
    targets, halo = margin.shape
    rhs = residual.shape[0]
    me = lax.axis_index("sub")
    first = lax.axis_index("grp") * rows
    for b in range(own):
        block_rows[pl.ds(b, rhs, stride=own), :] = residual[:, b * BLK : (b + 1) * BLK]
    mine = block_rows[pl.ds(pl.multiple_of(first * own, 8), rows * own), :]
    names = aggregate[...].astype(jnp.float32)
    at = own * rows
    for t in range(targets):
        out[t, :at, :] = mine
        out[t, at : at + pad, :] = jnp.zeros((pad, BLK), jnp.float32)
        out[t, at : at + 1, :own] = names
        for k in range(halo):
            slot = jnp.clip(margin[t, k] - me * own, 0, own - 1)
            out[t, at + pad + k * rhs : at + pad + (k + 1) * rhs, :] = residual[
                :, pl.ds(pl.multiple_of(slot * BLK, BLK), BLK)
            ]


def fine_kernel(own, start, chunk, margin, residual, arrived, factor, out, inner):
    rhs = residual.shape[0]
    halo = margin.shape[1]
    depth, width = factor.shape[1:]
    blocks = width // BLK
    me = lax.axis_index("sub")
    tiles = [residual[...].astype(jnp.bfloat16)]
    for k in range(halo):
        owner = margin[me, k] // own
        tiles.append(arrived[owner, start + k * rhs : start + (k + 1) * rhs, :].astype(jnp.bfloat16))
    local = jnp.concatenate(tiles, axis=1)
    for n in range(depth // chunk):
        span = slice(n * chunk, (n + 1) * chunk)
        inner[:, span] = mm(local, factor[0, span, :], NT)
    mid = inner[...].astype(jnp.bfloat16)
    for n in range(width // chunk):
        part = mm(mid, factor[0, :, n * chunk : (n + 1) * chunk])
        for i in range(chunk // BLK):
            b = n * (chunk // BLK) + i
            out[pl.ds(b, rhs, stride=blocks), :] = part[:, i * BLK : (i + 1) * BLK]


def coarse_kernel(own, rows, chunk, arrived, factor, out, table, inner):
    sources = arrived.shape[0]
    depth, width = factor.shape
    coarse = width // BLK
    names = arrived[:, own * rows, :].T
    catalog = lax.broadcasted_iota(jnp.int32, (own, coarse), 1).astype(jnp.float32)
    member = jnp.concatenate(
        [(names[:own, s : s + 1] == catalog).astype(jnp.float32) for s in range(sources)], axis=0
    ).astype(jnp.bfloat16)
    whole = jnp.concatenate(
        [
            jnp.concatenate([arrived[s, r * own : (r + 1) * own, :] for s in range(sources)], axis=0)
            for r in range(rows)
        ],
        axis=1,
    )
    ones = jnp.ones((own * sources, BLK), jnp.bfloat16)
    span = rows * BLK
    found = mm(member, jnp.concatenate(split3(whole) + [ones], axis=1), TN)
    sums = found[:, :span] + found[:, span : 2 * span] + found[:, 2 * span : 3 * span]
    counts = jnp.maximum(found[:, 3 * span :], 1.0)
    for r in range(rows):
        table[r * coarse : (r + 1) * coarse, :] = sums[:, r * BLK : (r + 1) * BLK] / counts
    right = jnp.concatenate(
        [table[pl.ds(j, rows, stride=coarse), :] for j in range(coarse)], axis=1
    ).astype(jnp.bfloat16)
    for n in range(depth // chunk):
        inner[:, n * chunk : (n + 1) * chunk] = mm(right, factor[n * chunk : (n + 1) * chunk, :], NT)
    mid = inner[...].astype(jnp.bfloat16)
    for n in range(width // chunk):
        part = mm(mid, factor[:, n * chunk : (n + 1) * chunk])
        for i in range(chunk // BLK):
            j = n * (chunk // BLK) + i
            table[pl.ds(j, rows, stride=coarse), :] = part[:, i * BLK : (i + 1) * BLK]
    solved = jnp.concatenate([table[r * coarse : (r + 1) * coarse, :] for r in range(rows)], axis=1)
    spread = mm(member, jnp.concatenate(split3(solved), axis=1))
    spread = spread[:, :span] + spread[:, span : 2 * span] + spread[:, 2 * span :]
    for s in range(sources):
        for r in range(rows):
            out[s, r * own : (r + 1) * own, :] = spread[
                s * own : (s + 1) * own, r * BLK : (r + 1) * BLK
            ]


def merge_kernel(own, rows, margin, arrived, spread, out, total):
    halo = margin.shape[1]
    blocks = own + halo
    me = lax.axis_index("sub")
    summed = arrived[0]
    for g in range(1, arrived.shape[0]):
        summed = summed + arrived[g]
    total[...] = summed
    out[...] = spread[...]
    for r in range(rows):
        here = out[me, r * own : (r + 1) * own, :]
        out[me, r * own : (r + 1) * own, :] = here + total[r * blocks : r * blocks + own, :]
    for k in range(halo):
        block = margin[me, k]
        owner = block // own
        slot = block - owner * own
        where = pl.ds(slot, rows, stride=own)
        out[owner, where, :] = out[owner, where, :] + total[pl.ds(own + k, rows, stride=blocks), :]


def last_kernel(own, rows, arrived, out, total):
    summed = arrived[0]
    for s in range(1, arrived.shape[0]):
        summed = summed + arrived[s]
    total[...] = summed
    for b in range(own):
        out[:, b * BLK : (b + 1) * BLK] = total[pl.ds(b, rows, stride=own), :]


def on_device(residual, margin, aggregate, local_factor, coarse_factor):
    sub_count = lax.axis_size("sub")
    grp_count = lax.axis_size("grp")
    rhs, own_width = residual.shape
    own = own_width // BLK
    rows = rhs // grp_count
    halo = margin.shape[1]
    pad = 8
    start = own * rows + pad
    f32 = jnp.float32
    sds = jax.ShapeDtypeStruct
    _, depth, width = local_factor.shape
    coarse_depth, coarse_width = coarse_factor.shape
    blocks = width // BLK

    local_factor = pltpu.with_memory_space_constraint(local_factor, pltpu.VMEM)
    coarse_factor = pltpu.with_memory_space_constraint(coarse_factor, pltpu.VMEM)

    outgoing = call(
        functools.partial(pack_kernel, own, rows, pad),
        sds((sub_count, start + halo * rhs, BLK), f32),
        [SMEM, VMEM, VMEM],
        [pltpu.VMEM((own * rhs, BLK), f32)],
    )(margin, aggregate.reshape(1, own), residual)
    arrived = lax.all_to_all(outgoing, "sub", split_axis=0, concat_axis=0, tiled=True)
    fine = call(
        functools.partial(fine_kernel, own, start, 256),
        sds((rhs * blocks, BLK), f32),
        [SMEM, VMEM, VMEM, VMEM],
        [pltpu.VMEM((rhs, depth), f32)],
        flops=4 * rhs * depth * width,
        moved=2 * depth * width,
    )(margin, residual, arrived, local_factor)
    panels = lax.all_to_all(
        fine.reshape(grp_count, rows * blocks, BLK), "grp", split_axis=0, concat_axis=0, tiled=True
    )
    spread = call(
        functools.partial(coarse_kernel, own, rows, 256),
        sds((sub_count, own * rows, BLK), f32),
        [VMEM, VMEM],
        [pltpu.VMEM((rows * (coarse_width // BLK), BLK), f32), pltpu.VMEM((rows, coarse_depth), f32)],
        flops=4 * rows * coarse_depth * coarse_width,
        moved=2 * coarse_depth * coarse_width,
    )(arrived, coarse_factor)
    merged = call(
        functools.partial(merge_kernel, own, rows),
        sds((sub_count, own * rows, BLK), f32),
        [SMEM, VMEM, VMEM],
        [pltpu.VMEM((rows * blocks, BLK), f32)],
    )(margin, panels, spread)
    back = lax.all_to_all(merged, "sub", split_axis=0, concat_axis=0, tiled=True)
    return call(
        functools.partial(last_kernel, own, rows),
        sds((rows, own_width), f32),
        [VMEM],
        [pltpu.VMEM((own * rows, BLK), f32)],
    )(back)


def solution(mesh):
    placed = (P(None, "sub"), P(), P("sub"), P("sub", "grp", None), P("sub", None))
    return jax.shard_map(
        on_device, mesh=mesh, in_specs=placed, out_specs=P("grp", "sub"), check_vma=False
    )
```

time: 184 us -> 53.7 us (0.29)
  waiting for transfers between devices: 103 us -> 0.01 us
  matrix products: 31.5 us -> 0 us
  between operations: 15.6 us -> 0.05 us
  Pallas kernels: 0 us -> 13.9 us
  blocking collectives: 14.4 us -> 23 us
  local copies, waits for them, and re-layouts: 5.41 us -> 11.4 us
  starting transfers between devices: 8.95 us -> 4.87 us
  other arithmetic: 3.88 us -> 0 us
    psum x2 -> x0, waiting for transfers between devices: 87 us -> none  [the longest x1 49.3 us: on_device(): coarse_sol = lax.psum(coarse_part, 'sub')]
    dot_general x6 -> x0, matrix products: 31.5 us -> none  [the longest x1 16.9 us: on_device(): jnp.dot(inner_coarse, coarse_factor, preferred_element_type=jnp.float32)]
    all_to_all x0 -> x2, blocking collectives: none -> 23 us  [the longest x1 14.4 us: on_device(): lax.all_to_all(outgoing, 'sub', split_axis=0, concat_axis=0, tiled=True)]
    unnamed x4 -> x0, waiting for transfers between devices: 16.3 us -> none
    psum x1 -> x0, blocking collectives: 14.4 us -> none  [on_device(): sums, counts = lax.psum((sums_part, jnp.sum(member, axis=0)), 'sub')]
    pallas_call x0 -> x5, Pallas kernels: none -> 13.9 us  [the longest x1 7.21 us: on_device(): call(functools.partial(coarse_kernel, own, rows, 256), sds((sub_count, ow...]
    unnamed x9 -> x12, local copies, waits for them, and re-layouts: 5.26 us -> 11.4 us
    all_to_all x2 -> x1, starting transfers between devices: 8.83 us -> 4.87 us  [on_device(): lax.all_to_all(fine.reshape(grp_count, rows * blocks, BLK), 'grp', split_...]
  transfers between devices with their start and end apart: 5 -> 1, of which waited for: 3 -> 0; matrix products, arithmetic and copies ran while one was open for 15% -> 0% of each run, Pallas kernels for 0% -> 14%
where the time goes in v1:
time: 53.7 us; the launch traced here: 53.2 us
  blocking collectives  23 us (43%)
  Pallas kernels  13.9 us (26%)
  local copies, waits for them, and re-layouts  11.4 us (21%)
  starting transfers between devices  4.87 us (9%)
    all_to_all x1, blocking collectives, on_device(): lax.all_to_all(outgoing, 'sub', split_axis=0, concat_axis=0, tiled=True)  14.4 us
    unnamed x12, local copies, waits for them, and re-layouts  11.4 us
    all_to_all x1, blocking collectives, on_device(): lax.all_to_all(merged, 'sub', split_axis=0, concat_axis=0, tiled=True)  8.63 us
    pallas_call x1, Pallas kernels, on_device(): call(functools.partial(coarse_kernel, own, rows, 256), sds((sub_count, ow...  7.21 us
    all_to_all x1, starting transfers between devices, on_device(): lax.all_to_all(fine.reshape(grp_count, rows * blocks, BLK), 'grp', split_...  4.87 us
    pallas_call x1, Pallas kernels, on_device(): call(functools.partial(fine_kernel, own, start, 256), sds((rhs * blocks,...  4.62 us
  transfers between devices with their start and end apart: 1, of which 0 were waited for; matrix products, arithmetic and copies ran while one was open for 0% of the time, Pallas kernels for 14%

profile of v1, /device:TPU:0, one launch (start us, length us, event | category | flops | bytes accessed | tf_op | source)
XLA Modules:
  0.0 53.2 jit_solution(3055441400208496332)
XLA Ops:
  0.0 0.0 copy-start.2
  0.0 0.9 %copy-done.2 = f32[8,3072]{1,0:T(8,128)S(1)} copy-done((f32[8,3072]{1,0:T(8,128)S(1)}, f32[8,3072]{1,0:T(8,128)}, u32[]{:S(2)}) %copy-start.2) | copy-done | bytes 98328
  0.9 0.0 copy-start.3
  0.9 0.7 %copy-done.3 = s32[8,8]{1,0:T(8,128)S(1)} copy-done((s32[8,8]{1,0:T(8,128)S(1)}, s32[8,8]{1,0:T(8,128)}, u32[]{:S(2)}) %copy-start.3) | copy-done | bytes 280
  1.6 0.0 copy-start.5
  1.6 0.7 %copy-done.5 = s32[24]{0:T(128)S(1)} copy-done((s32[24]{0:T(128)S(1)}, s32[24]{0:T(128)}, u32[]{:S(2)}) %copy-start.5) | copy-done | bytes 120
  2.2 0.0 copy-start.4
  2.2 0.8 %shard_map.55 = f32[8,120,128]{2,1,0:T(8,128)S(1)} custom-call(s32[8,8]{1,0:T(8,128)S(1)} %copy-done.3, s32[1,24]{1,0:T(1,128)S(1)} %bitcast.2, f32[8,3072]{1,0:T(8,128)S(1)} %copy-done.2), custom_call_target="tpu_custom_call" | custom-call | tf_op jit(solution)/shard_map/pallas_call | solution.py:177
  3.1 14.4 %all_to_all.15.arrived = f32[8,120,128]{2,1,0:T(8,128)S(1)} all-to-all(f32[8,120,128]{2,1,0:T(8,128)S(1)} %shard_map.55), channel_id=1, replica_groups=mesh['grp'=4,'sub'=8] {'sub'}, dimensions={0} | all-to-all | bytes 983040 | tf_op jit(solution)/shard_map/all_to_all | solution.py:183
  17.4 0.0 copy-start.1
  17.4 3.4 %copy-done.1 = bf16[1,1024,4096]{2,1,0:T(8,128)(2,1)S(1)} copy-done((bf16[1,1024,4096]{2,1,0:T(8,128)(2,1)S(1)}, bf16[1,1024,4096]{2,1,0:T(8,128)(2,1)}, u32[]{:S(2)}) %copy-start.1) | copy-done | bytes 8388632
  20.8 4.6 %shard_map.56 = f32[256,128]{1,0:T(8,128)} custom-call(s32[8,8]{1,0:T(8,128)S(1)} %copy-done.3, f32[8,3072]{1,0:T(8,128)S(1)} %copy-done.2, f32[8,120,128]{2,1,0:T(8,128)S(1)} %all_to_all.15.arrived, bf16[1,1024,4096]{2,1,0:T(8,128)(2,1)S(1)} %copy-done.1), custom_call_target="tpu_custom_call" | custom-call | flops 134217728 | bytes 8388608 | tf_op jit(solution)/shard_map/pallas_call | solution.py:184
  25.4 4.9 %all-to-all-start.1 = ((f32[4,64,128]{2,1,0:T(8,128)}), f32[4,64,128]{2,1,0:T(8,128)S(1)}, u32[]{:S(2)}, u32[]{:S(2)}) async-start(f32[4,64,128]{2,1,0:T(8,128)} %bitcast.1), calls=%async_computation.1 | async-start | bytes 262144 | tf_op jit(solution)/shard_map/all_to_all | solution.py:192
  30.3 0.0 copy-start
  30.3 5.8 %copy-done = bf16[1024,8192]{1,0:T(8,128)(2,1)S(1)} copy-done((bf16[1024,8192]{1,0:T(8,128)(2,1)S(1)}, bf16[1024,8192]{1,0:T(8,128)(2,1)}, u32[]{:S(2)}) %copy-start) | copy-done | bytes 16777240
  36.1 7.2 %shard_map.57.spread = f32[8,48,128]{2,1,0:T(8,128)S(1)} custom-call(f32[8,120,128]{2,1,0:T(8,128)S(1)} %all_to_all.15.arrived, bf16[1024,8192]{1,0:T(8,128)(2,1)S(1)} %copy-done), custom_call_target="tpu_custom_call" | custom-call | flops 67108864 | bytes 16777216 | tf_op jit(solution)/shard_map/pallas_call | solution.py:195
  43.3 0.0 all-to-all-done.1.arrived
  43.3 0.0 copy-done.4
  43.3 0.7 %shard_map.58 = f32[8,48,128]{2,1,0:T(8,128)S(1)} custom-call(s32[8,8]{1,0:T(8,128)S(1)} %copy-done.4, f32[4,64,128]{2,1,0:T(8,128)S(1)} %all-to-all-done.1.arrived, f32[8,48,128]{2,1,0:T(8,128)S(1)} %shard_map.57.spread), custom_call_target="tpu_custom_call" | custom-call | tf_op jit(solution)/shard_map/pallas_call | solution.py:203
  44.0 8.6 %all_to_all.16.arrived = f32[8,48,128]{2,1,0:T(8,128)S(1)} all-to-all(f32[8,48,128]{2,1,0:T(8,128)S(1)} %shard_map.58), channel_id=1, replica_groups=mesh['grp'=4,'sub'=8] {'sub'}, dimensions={0} | all-to-all | bytes 393216 | tf_op jit(solution)/shard_map/all_to_all | solution.py:209
  52.6 0.6 %shard_map.59 = f32[2,3072]{1,0:T(2,128)} custom-call(f32[8,48,128]{2,1,0:T(8,128)S(1)} %all_to_all.16.arrived), custom_call_target="tpu_custom_call" | custom-call | tf_op jit(solution)/shard_map/pallas_call | solution.py:210
Async XLA Ops:
  0.0 0.9 %copy-start.2 = (f32[8,3072]{1,0:T(8,128)S(1)}, f32[8,3072]{1,0:T(8,128)}, u32[]{:S(2)}) copy-start(f32[8,3072]{1,0:T(8,128)} %residual.3) | copy-start | bytes 294916
  0.9 0.7 %copy-start.3 = (s32[8,8]{1,0:T(8,128)S(1)}, s32[8,8]{1,0:T(8,128)}, u32[]{:S(2)}) copy-start(s32[8,8]{1,0:T(8,128)} %margin.5) | copy-start | bytes 772
  1.6 0.7 %copy-start.5 = (s32[24]{0:T(128)S(1)}, s32[24]{0:T(128)}, u32[]{:S(2)}) copy-start(s32[24]{0:T(128)} %param.7) | copy-start | bytes 292
  2.2 41.0 %copy-start.4 = (s32[8,8]{1,0:T(8,128)S(1)}, s32[8,8]{1,0:T(8,128)}, u32[]{:S(2)}) copy-start(s32[8,8]{1,0:T(8,128)} %margin.5) | copy-start | bytes 772
  17.4 3.4 %copy-start.1 = (bf16[1,1024,4096]{2,1,0:T(8,128)(2,1)S(1)}, bf16[1,1024,4096]{2,1,0:T(8,128)(2,1)}, u32[]{:S(2)}) copy-start(bf16[1,1024,4096]{2,1,0:T(8,128)(2,1)} %factor.2) | copy-start | bytes 25165828
  25.4 17.9 %all-to-all-start.1 = ((f32[4,64,128]{2,1,0:T(8,128)}), f32[4,64,128]{2,1,0:T(8,128)S(1)}, u32[]{:S(2)}, u32[]{:S(2)}) async-start(f32[4,64,128]{2,1,0:T(8,128)} %bitcast.1), calls=%async_computation.1 | async-start | bytes 262144 | tf_op jit(solution)/shard_map/all_to_all | solution.py:192
  30.3 5.8 %copy-start = (bf16[1024,8192]{1,0:T(8,128)(2,1)S(1)}, bf16[1024,8192]{1,0:T(8,128)(2,1)}, u32[]{:S(2)}) copy-start(bf16[1024,8192]{1,0:T(8,128)(2,1)} %factor.3) | copy-start | bytes 50331652

commit v2 on v1

--- a/solution.py
+++ b/solution.py
@@ -11,6 +11,7 @@
 MIB = 1024 * 1024
 VMEM = pl.BlockSpec(memory_space=pltpu.VMEM)
 SMEM = pl.BlockSpec(memory_space=pltpu.SMEM)
+HBM = pl.BlockSpec(memory_space=pltpu.HBM)
 NT = (((1,), (1,)), ((), ()))
 TN = (((0,), (0,)), ((), ()))
 
@@ -20,7 +21,7 @@
         kernel,
         out_shape=out,
         in_specs=specs,
-        out_specs=VMEM,
+        out_specs=jax.tree.map(lambda _: VMEM, out),
         scratch_shapes=scratch,
         compiler_params=pltpu.CompilerParams(vmem_limit_bytes=limit),
         cost_estimate=pl.CostEstimate(flops=flops, bytes_accessed=moved, transcendentals=0),
@@ -40,7 +41,15 @@
     return [high, middle, low]
 
 
-def pack_kernel(own, rows, pad, margin, aggregate, residual, out, block_rows):
+def pack_kernel(
+    own, rows, pad, margin_hbm, aggregate_hbm, residual_hbm, out, block_rows, margin, aggregate, residual, sems
+):
+    pairs = ((residual_hbm, residual), (margin_hbm, margin), (aggregate_hbm, aggregate))
+    copies = [pltpu.make_async_copy(a, b, sems.at[i]) for i, (a, b) in enumerate(pairs)]
+    for copy in copies:
+        copy.start()
+    for copy in copies:
+        copy.wait()
     targets, halo = margin.shape
     rhs = residual.shape[0]
     me = lax.axis_index("sub")
@@ -61,20 +70,51 @@
             ]
 
 
-def fine_kernel(own, start, chunk, margin, residual, arrived, factor, out, inner):
-    rhs = residual.shape[0]
+def load_kernel(chunk, residual_hbm, fine_hbm, coarse_hbm, inner, fine, coarse, residual, sems):
+    depth = fine.shape[1]
+    own_width = residual.shape[1]
+    first = pltpu.make_async_copy(residual_hbm, residual, sems.at[0])
+    first.start()
+    copies = []
+    for n in range(depth // chunk):
+        span = pl.ds(n * chunk, chunk)
+        copies.append(
+            pltpu.make_async_copy(fine_hbm.at[0, span], fine.at[0, span], sems.at[1 + n])
+        )
+    last = []
+    for n in range(coarse.shape[0] // chunk):
+        span = pl.ds(n * chunk, chunk)
+        last.append(
+            pltpu.make_async_copy(
+                coarse_hbm.at[span], coarse.at[span], sems.at[1 + len(copies) + n]
+            )
+        )
+    for copy in copies + last:
+        copy.start()
+    first.wait()
+    local = residual[...].astype(jnp.bfloat16)
+    for n, copy in enumerate(copies):
+        copy.wait()
+        span = slice(n * chunk, (n + 1) * chunk)
+        inner[:, span] = mm(local, fine[0, span, :own_width], NT)
+    for copy in last:
+        copy.wait()
+
+
+def fine_kernel(own, start, chunk, margin, begun, arrived, factor, out, inner):
+    rhs = begun.shape[0]
     halo = margin.shape[1]
     depth, width = factor.shape[1:]
     blocks = width // BLK
     me = lax.axis_index("sub")
-    tiles = [residual[...].astype(jnp.bfloat16)]
+    tiles = []
     for k in range(halo):
         owner = margin[me, k] // own
         tiles.append(arrived[owner, start + k * rhs : start + (k + 1) * rhs, :].astype(jnp.bfloat16))
     local = jnp.concatenate(tiles, axis=1)
     for n in range(depth // chunk):
         span = slice(n * chunk, (n + 1) * chunk)
-        inner[:, span] = mm(local, factor[0, span, :], NT)
+        inner[:, span] = begun[:, span] + mm(local, factor[0, span, own * BLK :], NT)
     mid = inner[...].astype(jnp.bfloat16)
     for n in range(width // chunk):
         part = mm(mid, factor[0, :, n * chunk : (n + 1) * chunk])
@@ -171,24 +211,44 @@
     coarse_depth, coarse_width = coarse_factor.shape
     blocks = width // BLK
 
-    local_factor = pltpu.with_memory_space_constraint(local_factor, pltpu.VMEM)
-    coarse_factor = pltpu.with_memory_space_constraint(coarse_factor, pltpu.VMEM)
-
+    in_hbm = functools.partial(pltpu.with_memory_space_constraint, memory_space=pltpu.HBM)
     outgoing = call(
         functools.partial(pack_kernel, own, rows, pad),
         sds((sub_count, start + halo * rhs, BLK), f32),
-        [SMEM, VMEM, VMEM],
-        [pltpu.VMEM((own * rhs, BLK), f32)],
-    )(margin, aggregate.reshape(1, own), residual)
+        [HBM, HBM, HBM],
+        [
+            pltpu.VMEM((own * rhs, BLK), f32),
+            pltpu.SMEM(margin.shape, jnp.int32),
+            pltpu.VMEM((1, own), jnp.int32),
+            pltpu.VMEM(residual.shape, f32),
+            pltpu.SemaphoreType.DMA((3,)),
+        ],
+    )(in_hbm(margin), in_hbm(aggregate.reshape(1, own)), in_hbm(residual))
     arrived = lax.all_to_all(outgoing, "sub", split_axis=0, concat_axis=0, tiled=True)
+    chunk = 256
+    begun, local_factor, coarse_factor = call(
+        functools.partial(load_kernel, chunk),
+        (
+            sds((rhs, depth), f32),
+            sds(local_factor.shape, local_factor.dtype),
+            sds(coarse_factor.shape, coarse_factor.dtype),
+        ),
+        [HBM, HBM, HBM],
+        [
+            pltpu.VMEM(residual.shape, f32),
+            pltpu.SemaphoreType.DMA((1 + depth // chunk + coarse_depth // chunk,)),
+        ],
+        flops=2 * rhs * depth * own_width,
+        moved=2 * depth * width + 2 * coarse_depth * coarse_width,
+    )(in_hbm(residual), in_hbm(local_factor), in_hbm(coarse_factor))
     fine = call(
-        functools.partial(fine_kernel, own, start, 256),
+        functools.partial(fine_kernel, own, start, chunk),
         sds((rhs * blocks, BLK), f32),
         [SMEM, VMEM, VMEM, VMEM],
         [pltpu.VMEM((rhs, depth), f32)],
         flops=4 * rhs * depth * width,
         moved=2 * depth * width,
-    )(margin, residual, arrived, local_factor)
+    )(margin, begun, arrived, local_factor)
     panels = lax.all_to_all(
         fine.reshape(grp_count, rows * blocks, BLK), "grp", split_axis=0, concat_axis=0, tiled=True
     )

time: 53.7 us -> 60.7 us (1.13)
  blocking collectives: 23 us -> 10.2 us
  Pallas kernels: 13.9 us -> 21.8 us
  local copies, waits for them, and re-layouts: 11.4 us -> 18.1 us
  starting transfers between devices: 4.87 us -> 10.1 us
    all_to_all x1 -> x0, blocking collectives: 14.4 us -> none  [on_device(): lax.all_to_all(outgoing, 'sub', split_axis=0, concat_axis=0, tiled=True)]
    pallas_call x1 -> x2, Pallas kernels: 4.62 us -> 11.4 us  [the longest x1 8.37 us: on_device(): call(functools.partial(load_kernel, chunk), (sds((rhs, depth), f32), sds(...]
    unnamed x12 -> x10, local copies, waits for them, and re-layouts: 11.4 us -> 18.1 us
    all_to_all x0 -> x1, starting transfers between devices: none -> 5.18 us  [on_device(): lax.all_to_all(outgoing, 'sub', split_axis=0, concat_axis=0, tiled=True)]
    all_to_all x1, blocking collectives: 8.63 us -> 10.2 us  [on_device(): lax.all_to_all(merged, 'sub', split_axis=0, concat_axis=0, tiled=True)]
    pallas_call x1, Pallas kernels: 0.8 us -> 1.96 us  [on_device(): call(functools.partial(pack_kernel, own, rows, pad), sds((sub_count, star...]
  transfers between devices with their start and end apart: 1 -> 2, of which waited for: 0 -> 0; matrix products, arithmetic and copies ran while one was open for 0% -> 0% of each run, Pallas kernels for 14% -> 26%
where the time goes in v2:
time: 60.7 us; the launch traced here: 60.3 us
  Pallas kernels  21.8 us (36%)
  local copies, waits for them, and re-layouts  18.1 us (30%)
  blocking collectives  10.2 us (17%)
  starting transfers between devices  10.1 us (17%)
    unnamed x10, local copies, waits for them, and re-layouts  18.1 us
    all_to_all x1, blocking collectives, on_device(): lax.all_to_all(merged, 'sub', split_axis=0, concat_axis=0, tiled=True)  10.2 us
    pallas_call x1, Pallas kernels, on_device(): call(functools.partial(load_kernel, chunk), (sds((rhs, depth), f32), sds(...  8.37 us
    pallas_call x1, Pallas kernels, on_device(): call(functools.partial(coarse_kernel, own, rows, 256), sds((sub_count, ow...  7.21 us
    all_to_all x1, starting transfers between devices, on_device(): lax.all_to_all(outgoing, 'sub', split_axis=0, concat_axis=0, tiled=True)  5.18 us
    all_to_all x1, starting transfers between devices, on_device(): lax.all_to_all(fine.reshape(grp_count, rows * blocks, BLK), 'grp', split_...  4.87 us
    pallas_call x1, Pallas kernels, on_device(): call(functools.partial(fine_kernel, own, start, chunk), sds((rhs * blocks...  2.99 us
    pallas_call x1, Pallas kernels, on_device(): call(functools.partial(pack_kernel, own, rows, pad), sds((sub_count, star...  1.96 us
  transfers between devices with their start and end apart: 2, of which 0 were waited for; matrix products, arithmetic and copies ran while one was open for 0% of the time, Pallas kernels for 26%

profile of v2, /device:TPU:0, one launch (start us, length us, event | category | flops | bytes accessed | tf_op | source)
XLA Modules:
  0.0 60.3 jit_solution(1172875600174528044)
XLA Ops:
  0.0 0.0 copy-start.4
  0.0 2.0 %shard_map.56 = f32[8,120,128]{2,1,0:T(8,128)} custom-call(s32[8,8]{1,0:T(8,128)} %margin.3, s32[1,24]{1,0:T(1,128)} %bitcast.2, f32[8,3072]{1,0:T(8,128)} %residual_hbm.3), custom_call_target="tpu_custom_call" | custom-call | tf_op jit(solution)/shard_map/pallas_call | solution.py:215
  2.0 5.2 %all-to-all-start = ((f32[8,120,128]{2,1,0:T(8,128)}), f32[8,120,128]{2,1,0:T(8,128)S(1)}, u32[]{:S(2)}, u32[]{:S(2)}) async-start(f32[8,120,128]{2,1,0:T(8,128)} %shard_map.56), calls=%async_computation | async-start | bytes 983040 | tf_op jit(solution)/shard_map/all_to_all | solution.py:227
  7.2 8.4 %shard_map.55 = (f32[8,1024]{1,0:T(8,128)S(1)}, bf16[1,1024,4096]{2,1,0:T(8,128)(2,1)S(1)}, bf16[1024,8192]{1,0:T(8,128)(2,1)S(1)}) custom-call(f32[8,3072]{1,0:T(8,128)} %residual_hbm.3, bf16[1,1024,4096]{2,1,0:T(8,128)(2,1)} %fine_hbm.1, bf16[1024,8192]{1,0:T(8,128)(2,1)} %coarse_hbm.1), custom_call_target="tpu_custom_call" | custom-call | flops 50331648 | bytes 25165824 | tf_op jit(solution)/shard_map/pallas_call | solution.py:229
  15.5 0.0 copy-start
  15.5 5.7 %copy-done = bf16[1024,8192]{1,0:T(8,128)(2,1)} copy-done((bf16[1024,8192]{1,0:T(8,128)(2,1)}, bf16[1024,8192]{1,0:T(8,128)(2,1)S(1)}, u32[]{:S(2)}) %copy-start) | copy-done | bytes 16777240
  21.3 0.0 copy-start.2
  21.3 3.2 %copy-done.2 = bf16[1,1024,4096]{2,1,0:T(8,128)(2,1)} copy-done((bf16[1,1024,4096]{2,1,0:T(8,128)(2,1)}, bf16[1,1024,4096]{2,1,0:T(8,128)(2,1)S(1)}, u32[]{:S(2)}) %copy-start.2) | copy-done | bytes 8388632
  24.5 0.0 all-to-all-done.arrived
  24.5 0.0 copy-done.4
  24.5 0.0 copy-start.3
  24.5 3.4 %copy-done.3 = bf16[1,1024,4096]{2,1,0:T(8,128)(2,1)S(1)} copy-done((bf16[1,1024,4096]{2,1,0:T(8,128)(2,1)S(1)}, bf16[1,1024,4096]{2,1,0:T(8,128)(2,1)}, u32[]{:S(2)}) %copy-start.3) | copy-done | bytes 8388632
  27.9 3.0 %shard_map.57 = f32[256,128]{1,0:T(8,128)} custom-call(s32[8,8]{1,0:T(8,128)S(1)} %copy-done.4, f32[8,1024]{1,0:T(8,128)S(1)} %get-tuple-element.8.begun, f32[8,120,128]{2,1,0:T(8,128)S(1)} %all-to-all-done.arrived, bf16[1,1024,4096]{2,1,0:T(8,128)(2,1)S(1)} %copy-done.3), custom_call_target="tpu_custom_call" | custom-call | flops 134217728 | bytes 8388608 | tf_op jit(solution)/shard_map/pallas_call | solution.py:244
  30.9 4.9 %all-to-all-start.1 = ((f32[4,64,128]{2,1,0:T(8,128)}), f32[4,64,128]{2,1,0:T(8,128)S(1)}, u32[]{:S(2)}, u32[]{:S(2)}) async-start(f32[4,64,128]{2,1,0:T(8,128)} %bitcast.1), calls=%async_computation.1 | async-start | bytes 262144 | tf_op jit(solution)/shard_map/all_to_all | solution.py:252
  35.7 0.0 copy-start.1
  35.7 5.8 %copy-done.1 = bf16[1024,8192]{1,0:T(8,128)(2,1)S(1)} copy-done((bf16[1024,8192]{1,0:T(8,128)(2,1)S(1)}, bf16[1024,8192]{1,0:T(8,128)(2,1)}, u32[]{:S(2)}) %copy-start.1) | copy-done | bytes 16777240
  41.5 7.2 %shard_map.58.spread = f32[8,48,128]{2,1,0:T(8,128)S(1)} custom-call(f32[8,120,128]{2,1,0:T(8,128)S(1)} %all-to-all-done.arrived, bf16[1024,8192]{1,0:T(8,128)(2,1)S(1)} %copy-done.1), custom_call_target="tpu_custom_call" | custom-call | flops 67108864 | bytes 16777216 | tf_op jit(solution)/shard_map/pallas_call | solution.py:255
  48.7 0.0 all-to-all-done.1.arrived
  48.7 0.7 %shard_map.59 = f32[8,48,128]{2,1,0:T(8,128)S(1)} custom-call(s32[8,8]{1,0:T(8,128)S(1)} %copy-done.4, f32[4,64,128]{2,1,0:T(8,128)S(1)} %all-to-all-done.1.arrived, f32[8,48,128]{2,1,0:T(8,128)S(1)} %shard_map.58.spread), custom_call_target="tpu_custom_call" | custom-call | tf_op jit(solution)/shard_map/pallas_call | solution.py:263
  49.4 10.2 %all_to_all.15.arrived = f32[8,48,128]{2,1,0:T(8,128)S(1)} all-to-all(f32[8,48,128]{2,1,0:T(8,128)S(1)} %shard_map.59), channel_id=1, replica_groups=mesh['grp'=4,'sub'=8] {'sub'}, dimensions={0} | all-to-all | bytes 393216 | tf_op jit(solution)/shard_map/all_to_all | solution.py:269
  59.6 0.6 %shard_map.60 = f32[2,3072]{1,0:T(2,128)} custom-call(f32[8,48,128]{2,1,0:T(8,128)S(1)} %all_to_all.15.arrived), custom_call_target="tpu_custom_call" | custom-call | tf_op jit(solution)/shard_map/pallas_call | solution.py:270
Async XLA Ops:
  0.0 24.5 %copy-start.4 = (s32[8,8]{1,0:T(8,128)S(1)}, s32[8,8]{1,0:T(8,128)}, u32[]{:S(2)}) copy-start(s32[8,8]{1,0:T(8,128)} %margin.3) | copy-start | bytes 772
  2.0 22.5 %all-to-all-start = ((f32[8,120,128]{2,1,0:T(8,128)}), f32[8,120,128]{2,1,0:T(8,128)S(1)}, u32[]{:S(2)}, u32[]{:S(2)}) async-start(f32[8,120,128]{2,1,0:T(8,128)} %shard_map.56), calls=%async_computation | async-start | bytes 983040 | tf_op jit(solution)/shard_map/all_to_all | solution.py:227
  15.5 5.7 %copy-start = (bf16[1024,8192]{1,0:T(8,128)(2,1)}, bf16[1024,8192]{1,0:T(8,128)(2,1)S(1)}, u32[]{:S(2)}) copy-start(bf16[1024,8192]{1,0:T(8,128)(2,1)S(1)} %get-tuple-element.10.factor) | copy-start | bytes 50331652
  21.3 3.2 %copy-start.2 = (bf16[1,1024,4096]{2,1,0:T(8,128)(2,1)}, bf16[1,1024,4096]{2,1,0:T(8,128)(2,1)S(1)}, u32[]{:S(2)}) copy-start(bf16[1,1024,4096]{2,1,0:T(8,128)(2,1)S(1)} %get-tuple-element.9.factor) | copy-start | bytes 25165828
  24.5 3.4 %copy-start.3 = (bf16[1,1024,4096]{2,1,0:T(8,128)(2,1)S(1)}, bf16[1,1024,4096]{2,1,0:T(8,128)(2,1)}, u32[]{:S(2)}) copy-start(bf16[1,1024,4096]{2,1,0:T(8,128)(2,1)} %copy-done.2) | copy-start | bytes 25165828
  30.9 17.9 %all-to-all-start.1 = ((f32[4,64,128]{2,1,0:T(8,128)}), f32[4,64,128]{2,1,0:T(8,128)S(1)}, u32[]{:S(2)}, u32[]{:S(2)}) async-start(f32[4,64,128]{2,1,0:T(8,128)} %bitcast.1), calls=%async_computation.1 | async-start | bytes 262144 | tf_op jit(solution)/shard_map/all_to_all | solution.py:252
  35.7 5.8 %copy-start.1 = (bf16[1024,8192]{1,0:T(8,128)(2,1)S(1)}, bf16[1024,8192]{1,0:T(8,128)(2,1)}, u32[]{:S(2)}) copy-start(bf16[1024,8192]{1,0:T(8,128)(2,1)} %copy-done) | copy-start | bytes 50331652

commit v3 on v2

--- a/solution.py
+++ b/solution.py
@@ -41,16 +41,15 @@
     return [high, middle, low]
 
 
-def pack_kernel(
-    own, rows, pad, margin_hbm, aggregate_hbm, residual_hbm, out, block_rows, margin, aggregate, residual, sems
-):
+def pack_kernel(own, rows, pad, margin_hbm, aggregate_hbm, residual_hbm, *refs):
+    *outs, block_rows, margin, aggregate, residual, sems = refs
     pairs = ((residual_hbm, residual), (margin_hbm, margin), (aggregate_hbm, aggregate))
     copies = [pltpu.make_async_copy(a, b, sems.at[i]) for i, (a, b) in enumerate(pairs)]
     for copy in copies:
         copy.start()
     for copy in copies:
         copy.wait()
-    targets, halo = margin.shape
+    halo = margin.shape[1]
     rhs = residual.shape[0]
     me = lax.axis_index("sub")
     first = lax.axis_index("grp") * rows
@@ -59,13 +58,16 @@
     mine = block_rows[pl.ds(pl.multiple_of(first * own, 8), rows * own), :]
     names = aggregate[...].astype(jnp.float32)
     at = own * rows
-    for t in range(targets):
-        out[t, :at, :] = mine
-        out[t, at : at + pad, :] = jnp.zeros((pad, BLK), jnp.float32)
-        out[t, at : at + 1, :own] = names
+    for d, out in enumerate(outs):
+        out[:at, :] = mine
+        out[at : at + pad, :] = jnp.zeros((pad, BLK), jnp.float32)
+        out[at : at + 1, :own] = names
+        if d == 0:
+            continue
+        target = me ^ d
         for k in range(halo):
-            slot = jnp.clip(margin[t, k] - me * own, 0, own - 1)
-            out[t, at + pad + k * rhs : at + pad + (k + 1) * rhs, :] = residual[
+            slot = jnp.clip(margin[target, k] - me * own, 0, own - 1)
+            out[at + pad + k * rhs : at + pad + (k + 1) * rhs, :] = residual[
                 :, pl.ds(pl.multiple_of(slot * BLK, BLK), BLK)
             ]
 
@@ -101,16 +103,23 @@
         copy.wait()
 
 
-def fine_kernel(own, start, chunk, margin, begun, arrived, factor, out, inner):
+def fine_kernel(own, rows, start, chunk, sources, margin, begun, factor, *refs):
+    arrived = (None, *refs[: sources - 1])
+    *outs, inner, table = refs[sources - 1 :]
     rhs = begun.shape[0]
     halo = margin.shape[1]
     depth, width = factor.shape[1:]
     blocks = width // BLK
     me = lax.axis_index("sub")
+    group = lax.axis_index("grp")
     tiles = []
     for k in range(halo):
-        owner = margin[me, k] // own
-        tiles.append(arrived[owner, start + k * rhs : start + (k + 1) * rhs, :].astype(jnp.bfloat16))
+        away = me ^ (margin[me, k] // own)
+        span = slice(start + k * rhs, start + (k + 1) * rhs)
+        tile = arrived[1][span, :]
+        for d in range(2, sources):
+            tile = jnp.where(away == d, arrived[d][span, :], tile)
+        tiles.append(tile.astype(jnp.bfloat16))
     local = jnp.concatenate(tiles, axis=1)
     for n in range(depth // chunk):
         span = slice(n * chunk, (n + 1) * chunk)
@@ -120,21 +129,26 @@
         part = mm(mid, factor[0, :, n * chunk : (n + 1) * chunk])
         for i in range(chunk // BLK):
             b = n * (chunk // BLK) + i
-            out[pl.ds(b, rhs, stride=blocks), :] = part[:, i * BLK : (i + 1) * BLK]
-
-
-def coarse_kernel(own, rows, chunk, arrived, factor, out, table, inner):
-    sources = arrived.shape[0]
+            table[pl.ds(b, rhs, stride=blocks), :] = part[:, i * BLK : (i + 1) * BLK]
+    size = rows * blocks
+    for d, out in enumerate(outs):
+        out[...] = table[pl.ds(pl.multiple_of((group ^ d) * size, 8), size), :]
+
+
+def coarse_kernel(own, rows, chunk, sources, factor, *refs):
+    arrived = refs[:sources]
+    out, table, inner = refs[sources:]
     depth, width = factor.shape
     coarse = width // BLK
-    names = arrived[:, own * rows, :].T
+    names = [part[own * rows : own * rows + 1, :] for part in arrived]
+    names = jnp.concatenate(names, axis=0).T
     catalog = lax.broadcasted_iota(jnp.int32, (own, coarse), 1).astype(jnp.float32)
     member = jnp.concatenate(
         [(names[:own, s : s + 1] == catalog).astype(jnp.float32) for s in range(sources)], axis=0
     ).astype(jnp.bfloat16)
     whole = jnp.concatenate(
         [
-            jnp.concatenate([arrived[s, r * own : (r + 1) * own, :] for s in range(sources)], axis=0)
+            jnp.concatenate([part[r * own : (r + 1) * own, :] for part in arrived], axis=0)
             for r in range(rows)
         ],
         axis=1,
@@ -167,33 +181,45 @@
             ]
 
 
-def merge_kernel(own, rows, margin, arrived, spread, out, total):
+def merge_kernel(own, rows, groups, margin, spread, *refs):
+    arrived = refs[:groups]
+    *outs, total, field = refs[groups:]
     halo = margin.shape[1]
     blocks = own + halo
     me = lax.axis_index("sub")
-    summed = arrived[0]
-    for g in range(1, arrived.shape[0]):
-        summed = summed + arrived[g]
+    summed = arrived[0][...]
+    for part in arrived[1:]:
+        summed = summed + part[...]
     total[...] = summed
-    out[...] = spread[...]
+    field[...] = spread[...]
     for r in range(rows):
-        here = out[me, r * own : (r + 1) * own, :]
-        out[me, r * own : (r + 1) * own, :] = here + total[r * blocks : r * blocks + own, :]
+        span = slice(r * own, (r + 1) * own)
+        field[0, span, :] = field[0, span, :] + total[r * blocks : r * blocks + own, :]
     for k in range(halo):
         block = margin[me, k]
         owner = block // own
-        slot = block - owner * own
-        where = pl.ds(slot, rows, stride=own)
-        out[owner, where, :] = out[owner, where, :] + total[pl.ds(own + k, rows, stride=blocks), :]
-
-
-def last_kernel(own, rows, arrived, out, total):
-    summed = arrived[0]
-    for s in range(1, arrived.shape[0]):
-        summed = summed + arrived[s]
+        where = pl.ds(block - owner * own, rows, stride=own)
+        away = me ^ owner
+        field[away, where, :] = field[away, where, :] + total[pl.ds(own + k, rows, stride=blocks), :]
+    for d, out in enumerate(outs):
+        out[...] = field[d]
+
+
+def last_kernel(own, rows, *refs):
+    *arrived, out, total = refs
+    summed = arrived[0][...]
+    for part in arrived[1:]:
+        summed = summed + part[...]
     total[...] = summed
     for b in range(own):
         out[:, b * BLK : (b + 1) * BLK] = total[pl.ds(b, rows, stride=own), :]
+
+
+def exchange(parts, axis):
+    count = lax.axis_size(axis)
+    return [parts[0]] + [
+        lax.ppermute(parts[d], axis, [(i, i ^ d) for i in range(count)]) for d in range(1, count)
+    ]
 
 
 def on_device(residual, margin, aggregate, local_factor, coarse_factor):
@@ -214,7 +240,7 @@
     in_hbm = functools.partial(pltpu.with_memory_space_constraint, memory_space=pltpu.HBM)
     outgoing = call(
         functools.partial(pack_kernel, own, rows, pad),
-        sds((sub_count, start + halo * rhs, BLK), f32),
+        [sds((start, BLK), f32)] + [sds((start + halo * rhs, BLK), f32)] * (sub_count - 1),
         [HBM, HBM, HBM],
         [
             pltpu.VMEM((own * rhs, BLK), f32),
@@ -224,7 +250,7 @@
             pltpu.SemaphoreType.DMA((3,)),
         ],
     )(in_hbm(margin), in_hbm(aggregate.reshape(1, own)), in_hbm(residual))
-    arrived = lax.all_to_all(outgoing, "sub", split_axis=0, concat_axis=0, tiled=True)
+    arrived = exchange(outgoing, "sub")
     chunk = 256
     begun, local_factor, coarse_factor = call(
         functools.partial(load_kernel, chunk),
@@ -242,37 +268,35 @@
         moved=2 * depth * width + 2 * coarse_depth * coarse_width,
     )(in_hbm(residual), in_hbm(local_factor), in_hbm(coarse_factor))
     fine = call(
-        functools.partial(fine_kernel, own, start, chunk),
-        sds((rhs * blocks, BLK), f32),
-        [SMEM, VMEM, VMEM, VMEM],
-        [pltpu.VMEM((rhs, depth), f32)],
+        functools.partial(fine_kernel, own, rows, start, chunk, sub_count),
+        [sds((rows * blocks, BLK), f32)] * grp_count,
+        [SMEM] + [VMEM] * (sub_count + 1),
+        [pltpu.VMEM((rhs, depth), f32), pltpu.VMEM((rhs * blocks, BLK), f32)],
         flops=4 * rhs * depth * width,
         moved=2 * depth * width,
-    )(margin, begun, arrived, local_factor)
-    panels = lax.all_to_all(
-        fine.reshape(grp_count, rows * blocks, BLK), "grp", split_axis=0, concat_axis=0, tiled=True
-    )
+    )(margin, begun, local_factor, *arrived[1:])
+    panels = exchange(fine, "grp")
     spread = call(
-        functools.partial(coarse_kernel, own, rows, 256),
+        functools.partial(coarse_kernel, own, rows, chunk, sub_count),
         sds((sub_count, own * rows, BLK), f32),
-        [VMEM, VMEM],
+        [VMEM] * (1 + sub_count),
         [pltpu.VMEM((rows * (coarse_width // BLK), BLK), f32), pltpu.VMEM((rows, coarse_depth), f32)],
         flops=4 * rows * coarse_depth * coarse_width,
         moved=2 * coarse_depth * coarse_width,
-    )(arrived, coarse_factor)
+    )(coarse_factor, *arrived)
     merged = call(
-        functools.partial(merge_kernel, own, rows),
-        sds((sub_count, own * rows, BLK), f32),
-        [SMEM, VMEM, VMEM],
-        [pltpu.VMEM((rows * blocks, BLK), f32)],
-    )(margin, panels, spread)
-    back = lax.all_to_all(merged, "sub", split_axis=0, concat_axis=0, tiled=True)
+        functools.partial(merge_kernel, own, rows, grp_count),
+        [sds((own * rows, BLK), f32)] * sub_count,
+        [SMEM] + [VMEM] * (1 + grp_count),
+        [pltpu.VMEM((rows * blocks, BLK), f32), pltpu.VMEM((sub_count, own * rows, BLK), f32)],
+    )(margin, spread, *panels)
+    back = exchange(merged, "sub")
     return call(
         functools.partial(last_kernel, own, rows),
         sds((rows, own_width), f32),
-        [VMEM],
+        [VMEM] * sub_count,
         [pltpu.VMEM((own * rows, BLK), f32)],
-    )(back)
+    )(*back)
 
 
 def solution(mesh):

time: 60.7 us -> 43.1 us (0.71)
  local copies, waits for them, and re-layouts: 18.1 us -> 0.01 us
  blocking collectives: 10.2 us -> 0 us
  starting transfers between devices: 10.1 us -> 18.5 us
  waiting for transfers between devices: 0.01 us -> 3.97 us
  Pallas kernels: 21.8 us -> 20.4 us
    ppermute x0 -> x17, starting transfers between devices: none -> 18.5 us  [exchange(): lax.ppermute(parts[d], axis, [(i, i ^ d) for i in range(count)])]
    unnamed x10 -> x2, local copies, waits for them, and re-layouts: 18.1 us -> 0.01 us
    all_to_all x1 -> x0, blocking collectives: 10.2 us -> none  [on_device(): lax.all_to_all(merged, 'sub', split_axis=0, concat_axis=0, tiled=True)]
    all_to_all x2 -> x0, starting transfers between devices: 10.1 us -> none  [the longest x1 5.18 us: on_device(): lax.all_to_all(outgoing, 'sub', split_axis=0, concat_axis=0, tiled=True)]
    ppermute x0 -> x17, waiting for transfers between devices: none -> 3.97 us  [exchange(): lax.ppermute(parts[d], axis, [(i, i ^ d) for i in range(count)])]
    pallas_call x4, Pallas kernels: 12.8 us -> 11.4 us  [the longest x1 7.21 us: on_device(): call(functools.partial(coarse_kernel, own, rows, chunk, sub_count), sds((...]
  transfers between devices with their start and end apart: 2 -> 17, of which waited for: 0 -> 3; matrix products, arithmetic and copies ran while one was open for 0% -> 0% of each run, Pallas kernels for 26% -> 36%
where the time goes in v3:
time: 43.1 us; the launch traced here: 43 us
  Pallas kernels  20.4 us (47%)
  starting transfers between devices  18.5 us (43%)
  waiting for transfers between devices  3.97 us (9%)
    ppermute x17, starting transfers between devices, exchange(): lax.ppermute(parts[d], axis, [(i, i ^ d) for i in range(count)])  18.5 us
    pallas_call x1, Pallas kernels, on_device(): call(functools.partial(load_kernel, chunk), (sds((rhs, depth), f32), sds(...  8.37 us
    pallas_call x1, Pallas kernels, on_device(): call(functools.partial(coarse_kernel, own, rows, chunk, sub_count), sds((...  7.21 us
    ppermute x17, waiting for transfers between devices, exchange(): lax.ppermute(parts[d], axis, [(i, i ^ d) for i in range(count)])  3.97 us
    pallas_call x1, Pallas kernels, on_device(): call(functools.partial(fine_kernel, own, rows, start, chunk, sub_count),...  2.36 us
    pallas_call x1, Pallas kernels, on_device(): call(functools.partial(pack_kernel, own, rows, pad), [sds((start, BLK), f...  1.13 us
  transfers between devices with their start and end apart: 17, of which 3 were waited for; matrix products, arithmetic and copies ran while one was open for 0% of the time, Pallas kernels for 36%

profile of v3, /device:TPU:0, one launch (start us, length us, event | category | flops | bytes accessed | tf_op | source)
XLA Modules:
  0.0 43.0 jit_solution(8778538839322950231)
XLA Ops:
  0.0 0.0 copy-start
  0.0 1.1 %shard_map.56 = (f32[56,128]{1,0:T(8,128)S(1)}, f32[120,128]{1,0:T(8,128)S(1)}, f32[120,128]{1,0:T(8,128)S(1)}, f32[120,128]{1,0:T(8,128)S(1)}, f32[120,128]{1,0...) custom-call(s32[8,8]{1,0:T(8,128)} %margin.3, s32[1,24]{1,0:T(1,128)} %bitcast.1, ...), custom_call_target="tpu_custom_call" | custom-call | tf_op jit(solution)/shard_map/pallas_call | solution.py:241
  1.1 0.5 %collective-permute-start = (f32[120,128]{1,0:T(8,128)S(1)}, f32[120,128]{1,0:T(8,128)S(1)}, u32[]{:S(2)}, u32[]{:S(2)}) collective-permute-start(f32[120,128]{1,0:T(8,128)S(1)} %get-tuple-element.30), channel_id=1, source_target_pairs={{0,1},{1,0},{2,3},{3,2},{4,5},{5,4},{6,7},{7,6},{8,9},{9,8},{10,11... | collective-permute-start | bytes 184328 | tf_op jit(solution)/shard_map/ppermute | solution.py:221
  1.7 2.6 %collective-permute-start.1 = (f32[120,128]{1,0:T(8,128)S(1)}, f32[120,128]{1,0:T(8,128)S(1)}, u32[]{:S(2)}, u32[]{:S(2)}) collective-permute-start(f32[120,128]{1,0:T(8,128)S(1)} %get-tuple-element.31), channel_id=1, source_target_pairs={{0,2},{1,3},{2,0},{3,1},{4,6},{5,7},{6,4},{7,5},{8,10},{9,11},{10,... | collective-permute-start | bytes 184328 | tf_op jit(solution)/shard_map/ppermute | solution.py:221
  4.2 0.1 collective-permute-start.2
  4.3 1.8 %collective-permute-start.3 = (f32[120,128]{1,0:T(8,128)S(1)}, f32[120,128]{1,0:T(8,128)S(1)}, u32[]{:S(2)}, u32[]{:S(2)}) collective-permute-start(f32[120,128]{1,0:T(8,128)S(1)} %get-tuple-element.33), channel_id=1, source_target_pairs={{0,4},{1,5},{2,6},{3,7},{4,0},{5,1},{6,2},{7,3},{8,12},{9,13},{10,... | collective-permute-start | bytes 184328 | tf_op jit(solution)/shard_map/ppermute | solution.py:221
  6.1 0.0 collective-permute-start.4
  6.1 0.0 collective-permute-done.refs_1_.refs_0_
  6.1 2.6 %collective-permute-start.5 = (f32[120,128]{1,0:T(8,128)S(1)}, f32[120,128]{1,0:T(8,128)S(1)}, u32[]{:S(2)}, u32[]{:S(2)}) collective-permute-start(f32[120,128]{1,0:T(8,128)S(1)} %get-tuple-element.35), channel_id=1, source_target_pairs={{0,6},{1,7},{2,4},{3,5},{4,2},{5,3},{6,0},{7,1},{8,14},{9,15},{10,... | collective-permute-start | bytes 184328 | tf_op jit(solution)/shard_map/ppermute | solution.py:221
  8.7 0.0 collective-permute-done.1.refs_2_.refs_1_
  8.7 0.1 collective-permute-start.6
  8.8 8.4 %shard_map.55 = (f32[8,1024]{1,0:T(8,128)S(1)}, bf16[1,1024,4096]{2,1,0:T(8,128)(2,1)S(1)}, bf16[1024,8192]{1,0:T(8,128)(2,1)S(1)}) custom-call(f32[8,3072]{1,0:T(8,128)} %residual_hbm.3, bf16[1,1024,4096]{2,1,0:T(8,128)(2,1)} %fine_hbm.1, bf16[1024,8192]{1,0:T(8,128)(2,1)} %coarse_hbm.1), custom_call_target="tpu_custom_call" | custom-call | flops 50331648 | bytes 25165824 | tf_op jit(solution)/shard_map/pallas_call | solution.py:255
  17.2 0.0 collective-permute-done.2.refs_3_.refs_2_
  17.2 0.0 collective-permute-done.3.refs_4_.refs_3_
  17.2 0.0 collective-permute-done.4.refs_5_.refs_4_
  17.2 0.0 collective-permute-done.5.refs_6_.refs_5_
  17.2 0.0 collective-permute-done.6.refs_7_.refs_6_
  17.2 0.0 copy-done
  17.2 2.4 %shard_map.58 = (f32[64,128]{1,0:T(8,128)S(1)}, f32[64,128]{1,0:T(8,128)S(1)}, f32[64,128]{1,0:T(8,128)S(1)}, f32[64,128]{1,0:T(8,128)S(1)}) custom-call(s32[8,8]{1,0:T(8,128)S(1)} %copy-done, f32[8,1024]{1,0:T(8,128)S(1)} %get-tuple-element.37.begun, bf16[1,1024,4096]{2,1,0:T(8,128)(2,1)S(1)} %get-tuple-element.38.factor, ...), custom_call_target="tpu_custom_call" | custom-call | flops 134217728 | bytes 8388608 | tf_op jit(solution)/shard_map/pallas_call | solution.py:270
  19.6 1.8 %collective-permute-start.7 = (f32[64,128]{1,0:T(8,128)S(1)}, f32[64,128]{1,0:T(8,128)S(1)}, u32[]{:S(2)}, u32[]{:S(2)}) collective-permute-start(f32[64,128]{1,0:T(8,128)S(1)} %get-tuple-element.40), channel_id=1, source_target_pairs={{0,8},{8,0},{16,24},{24,16},{1,9},{9,1},{17,25},{25,17},{2,10},{10... | collective-permute-start | bytes 98312 | tf_op jit(solution)/shard_map/ppermute | solution.py:221
  21.4 2.6 %collective-permute-start.8 = (f32[64,128]{1,0:T(8,128)S(1)}, f32[64,128]{1,0:T(8,128)S(1)}, u32[]{:S(2)}, u32[]{:S(2)}) collective-permute-start(f32[64,128]{1,0:T(8,128)S(1)} %get-tuple-element.41), channel_id=1, source_target_pairs={{0,16},{8,24},{16,0},{24,8},{1,17},{9,25},{17,1},{25,9},{2,18},{10... | collective-permute-start | bytes 98312 | tf_op jit(solution)/shard_map/ppermute | solution.py:221
  24.0 0.1 collective-permute-start.9
  24.1 7.2 %shard_map.57.spread = f32[8,48,128]{2,1,0:T(8,128)S(1)} custom-call(bf16[1024,8192]{1,0:T(8,128)(2,1)S(1)} %get-tuple-element.28.factor, f32[56,128]{1,0:T(8,128)S(1)} %get-tuple-element.29.refs_0_, f32[120,128]{1,0:T(8,128)S(1)} %collective-permute-done.refs_1_.refs_0_, f32[120,128]{1,0:T(8,128)S(1)} %collective-permute-done.1.refs_2_.refs_1_, ...), custom_call_target="tpu_custom_call" | custom-call | flops 67108864 | bytes 16777216 | tf_op jit(solution)/shard_map/pallas_call | solution.py:279
  31.3 0.0 collective-permute-done.7.refs_1_
  31.3 0.0 collective-permute-done.8.refs_2_
  31.3 0.0 collective-permute-done.9.refs_3_
  31.3 0.7 %shard_map.59 = (f32[48,128]{1,0:T(8,128)S(1)}, f32[48,128]{1,0:T(8,128)S(1)}, f32[48,128]{1,0:T(8,128)S(1)}, f32[48,128]{1,0:T(8,128)S(1)}, f32[48,128]{1,0:T(8...) custom-call(s32[8,8]{1,0:T(8,128)S(1)} %copy-done, ...), custom_call_target="tpu_custom_call" | custom-call | tf_op jit(solution)/shard_map/pallas_call | solution.py:287
  32.0 0.6 %collective-permute-start.10 = (f32[48,128]{1,0:T(8,128)S(1)}, f32[48,128]{1,0:T(8,128)S(1)}, u32[]{:S(2)}, u32[]{:S(2)}) collective-permute-start(f32[48,128]{1,0:T(8,128)S(1)} %get-tuple-element.44), channel_id=1, source_target_pairs={{0,1},{1,0},{2,3},{3,2},{4,5},{5,4},{6,7},{7,6},{8,9},{9,8},{10,11... | collective-permute-start | bytes 73736 | tf_op jit(solution)/shard_map/ppermute | solution.py:221
  32.6 1.2 %collective-permute-start.11 = (f32[48,128]{1,0:T(8,128)S(1)}, f32[48,128]{1,0:T(8,128)S(1)}, u32[]{:S(2)}, u32[]{:S(2)}) collective-permute-start(f32[48,128]{1,0:T(8,128)S(1)} %get-tuple-element.45), channel_id=1, source_target_pairs={{0,2},{1,3},{2,0},{3,1},{4,6},{5,7},{6,4},{7,5},{8,10},{9,11},{10,... | collective-permute-start | bytes 73736 | tf_op jit(solution)/shard_map/ppermute | solution.py:221
  33.8 0.3 collective-permute-start.12
  34.0 1.6 %collective-permute-start.13 = (f32[48,128]{1,0:T(8,128)S(1)}, f32[48,128]{1,0:T(8,128)S(1)}, u32[]{:S(2)}, u32[]{:S(2)}) collective-permute-start(f32[48,128]{1,0:T(8,128)S(1)} %get-tuple-element.47), channel_id=1, source_target_pairs={{0,4},{1,5},{2,6},{3,7},{4,0},{5,1},{6,2},{7,3},{8,12},{9,13},{10,... | collective-permute-start | bytes 73736 | tf_op jit(solution)/shard_map/ppermute | solution.py:221
  35.6 0.5 %collective-permute-start.14 = (f32[48,128]{1,0:T(8,128)S(1)}, f32[48,128]{1,0:T(8,128)S(1)}, u32[]{:S(2)}, u32[]{:S(2)}) collective-permute-start(f32[48,128]{1,0:T(8,128)S(1)} %get-tuple-element.48), channel_id=1, source_target_pairs={{0,5},{1,4},{2,7},{3,6},{4,1},{5,0},{6,3},{7,2},{8,13},{9,12},{10,... | collective-permute-start | bytes 73736 | tf_op jit(solution)/shard_map/ppermute | solution.py:221
  36.1 0.0 collective-permute-done.10.refs_1_
  36.1 2.1 %collective-permute-start.15 = (f32[48,128]{1,0:T(8,128)S(1)}, f32[48,128]{1,0:T(8,128)S(1)}, u32[]{:S(2)}, u32[]{:S(2)}) collective-permute-start(f32[48,128]{1,0:T(8,128)S(1)} %get-tuple-element.49), channel_id=1, source_target_pairs={{0,6},{1,7},{2,4},{3,5},{4,2},{5,3},{6,0},{7,1},{8,14},{9,15},{10,... | collective-permute-start | bytes 73736 | tf_op jit(solution)/shard_map/ppermute | solution.py:221
  38.2 0.0 collective-permute-done.11.refs_2_
  38.2 0.2 collective-permute-start.16
  38.4 0.0 collective-permute-done.12.refs_3_
  38.4 0.0 collective-permute-done.13.refs_4_
  38.4 0.4 %collective-permute-done.14.refs_5_ = f32[48,128]{1,0:T(8,128)S(1)} collective-permute-done((f32[48,128]{1,0:T(8,128)S(1)}, f32[48,128]{1,0:T(8,128)S(1)}, u32[]{:S(2)}, u32[]{:S(2)}) %collective-permute-start.14) | collective-permute-done | bytes 24608 | tf_op jit(solution)/shard_map/ppermute | solution.py:221
  38.9 2.0 %collective-permute-done.15.refs_6_ = f32[48,128]{1,0:T(8,128)S(1)} collective-permute-done((f32[48,128]{1,0:T(8,128)S(1)}, f32[48,128]{1,0:T(8,128)S(1)}, u32[]{:S(2)}, u32[]{:S(2)}) %collective-permute-start.15) | collective-permute-done | bytes 24608 | tf_op jit(solution)/shard_map/ppermute | solution.py:221
  40.8 1.5 %collective-permute-done.16.refs_7_ = f32[48,128]{1,0:T(8,128)S(1)} collective-permute-done((f32[48,128]{1,0:T(8,128)S(1)}, f32[48,128]{1,0:T(8,128)S(1)}, u32[]{:S(2)}, u32[]{:S(2)}) %collective-permute-start.16) | collective-permute-done | bytes 24608 | tf_op jit(solution)/shard_map/ppermute | solution.py:221
  42.4 0.6 %shard_map.60 = f32[2,3072]{1,0:T(2,128)} custom-call(f32[48,128]{1,0:T(8,128)S(1)} %get-tuple-element.43.refs_0_, f32[48,128]{1,0:T(8,128)S(1)} %collective-permute-done.10.refs_1_, f32[48,128]{1,0:T(8,128)S(1)} %collective-permute-done.11.refs_2_, f32[48,128]{1,0:T(8,128)S(1)} %collective-permute-done.12.refs_3_, ...), custom_call_target="tpu_custom_call" | custom-call | tf_op jit(solution)/shard_map/pallas_call | solution.py:294
Async XLA Ops:
  0.0 17.2 %copy-start = (s32[8,8]{1,0:T(8,128)S(1)}, s32[8,8]{1,0:T(8,128)}, u32[]{:S(2)}) copy-start(s32[8,8]{1,0:T(8,128)} %margin.3) | copy-start | bytes 772
  1.1 4.9 %collective-permute-start = (f32[120,128]{1,0:T(8,128)S(1)}, f32[120,128]{1,0:T(8,128)S(1)}, u32[]{:S(2)}, u32[]{:S(2)}) collective-permute-start(f32[120,128]{1,0:T(8,128)S(1)} %get-tuple-element.30), channel_id=1, source_target_pairs={{0,1},{1,0},{2,3},{3,2},{4,5},{5,4},{6,7},{7,6},{8,9},{9,8},{10,11... | collective-permute-start | bytes 184328 | tf_op jit(solution)/shard_map/ppermute | solution.py:221
  1.7 7.0 %collective-permute-start.1 = (f32[120,128]{1,0:T(8,128)S(1)}, f32[120,128]{1,0:T(8,128)S(1)}, u32[]{:S(2)}, u32[]{:S(2)}) collective-permute-start(f32[120,128]{1,0:T(8,128)S(1)} %get-tuple-element.31), channel_id=1, source_target_pairs={{0,2},{1,3},{2,0},{3,1},{4,6},{5,7},{6,4},{7,5},{8,10},{9,11},{10,... | collective-permute-start | bytes 184328 | tf_op jit(solution)/shard_map/ppermute | solution.py:221
  4.2 13.0 %collective-permute-start.2 = (f32[120,128]{1,0:T(8,128)S(1)}, f32[120,128]{1,0:T(8,128)S(1)}, u32[]{:S(2)}, u32[]{:S(2)}) collective-permute-start(f32[120,128]{1,0:T(8,128)S(1)} %get-tuple-element.32), channel_id=1, source_target_pairs={{0,3},{1,2},{2,1},{3,0},{4,7},{5,6},{6,5},{7,4},{8,11},{9,10},{10,... | collective-permute-start | bytes 184328 | tf_op jit(solution)/shard_map/ppermute | solution.py:221
  4.3 12.9 %collective-permute-start.3 = (f32[120,128]{1,0:T(8,128)S(1)}, f32[120,128]{1,0:T(8,128)S(1)}, u32[]{:S(2)}, u32[]{:S(2)}) collective-permute-start(f32[120,128]{1,0:T(8,128)S(1)} %get-tuple-element.33), channel_id=1, source_target_pairs={{0,4},{1,5},{2,6},{3,7},{4,0},{5,1},{6,2},{7,3},{8,12},{9,13},{10,... | collective-permute-start | bytes 184328 | tf_op jit(solution)/shard_map/ppermute | solution.py:221
  6.1 11.1 %collective-permute-start.4 = (f32[120,128]{1,0:T(8,128)S(1)}, f32[120,128]{1,0:T(8,128)S(1)}, u32[]{:S(2)}, u32[]{:S(2)}) collective-permute-start(f32[120,128]{1,0:T(8,128)S(1)} %get-tuple-element.34), channel_id=1, source_target_pairs={{0,5},{1,4},{2,7},{3,6},{4,1},{5,0},{6,3},{7,2},{8,13},{9,12},{10,... | collective-permute-start | bytes 184328 | tf_op jit(solution)/shard_map/ppermute | solution.py:221
  6.1 11.1 %collective-permute-start.5 = (f32[120,128]{1,0:T(8,128)S(1)}, f32[120,128]{1,0:T(8,128)S(1)}, u32[]{:S(2)}, u32[]{:S(2)}) collective-permute-start(f32[120,128]{1,0:T(8,128)S(1)} %get-tuple-element.35), channel_id=1, source_target_pairs={{0,6},{1,7},{2,4},{3,5},{4,2},{5,3},{6,0},{7,1},{8,14},{9,15},{10,... | collective-permute-start | bytes 184328 | tf_op jit(solution)/shard_map/ppermute | solution.py:221
  8.7 8.5 %collective-permute-start.6 = (f32[120,128]{1,0:T(8,128)S(1)}, f32[120,128]{1,0:T(8,128)S(1)}, u32[]{:S(2)}, u32[]{:S(2)}) collective-permute-start(f32[120,128]{1,0:T(8,128)S(1)} %get-tuple-element.36), channel_id=1, source_target_pairs={{0,7},{1,6},{2,5},{3,4},{4,3},{5,2},{6,1},{7,0},{8,15},{9,14},{10,... | collective-permute-start | bytes 184328 | tf_op jit(solution)/shard_map/ppermute | solution.py:221
  19.6 11.7 %collective-permute-start.7 = (f32[64,128]{1,0:T(8,128)S(1)}, f32[64,128]{1,0:T(8,128)S(1)}, u32[]{:S(2)}, u32[]{:S(2)}) collective-permute-start(f32[64,128]{1,0:T(8,128)S(1)} %get-tuple-element.40), channel_id=1, source_target_pairs={{0,8},{8,0},{16,24},{24,16},{1,9},{9,1},{17,25},{25,17},{2,10},{10... | collective-permute-start | bytes 98312 | tf_op jit(solution)/shard_map/ppermute | solution.py:221
  21.4 9.9 %collective-permute-start.8 = (f32[64,128]{1,0:T(8,128)S(1)}, f32[64,128]{1,0:T(8,128)S(1)}, u32[]{:S(2)}, u32[]{:S(2)}) collective-permute-start(f32[64,128]{1,0:T(8,128)S(1)} %get-tuple-element.41), channel_id=1, source_target_pairs={{0,16},{8,24},{16,0},{24,8},{1,17},{9,25},{17,1},{25,9},{2,18},{10... | collective-permute-start | bytes 98312 | tf_op jit(solution)/shard_map/ppermute | solution.py:221
  24.0 7.3 %collective-permute-start.9 = (f32[64,128]{1,0:T(8,128)S(1)}, f32[64,128]{1,0:T(8,128)S(1)}, u32[]{:S(2)}, u32[]{:S(2)}) collective-permute-start(f32[64,128]{1,0:T(8,128)S(1)} %get-tuple-element.42), channel_id=1, source_target_pairs={{0,24},{8,16},{16,8},{24,0},{1,25},{9,17},{17,9},{25,1},{2,26},{10... | collective-permute-start | bytes 98312 | tf_op jit(solution)/shard_map/ppermute | solution.py:221
  32.0 4.1 %collective-permute-start.10 = (f32[48,128]{1,0:T(8,128)S(1)}, f32[48,128]{1,0:T(8,128)S(1)}, u32[]{:S(2)}, u32[]{:S(2)}) collective-permute-start(f32[48,128]{1,0:T(8,128)S(1)} %get-tuple-element.44), channel_id=1, source_target_pairs={{0,1},{1,0},{2,3},{3,2},{4,5},{5,4},{6,7},{7,6},{8,9},{9,8},{10,11... | collective-permute-start | bytes 73736 | tf_op jit(solution)/shard_map/ppermute | solution.py:221
  32.6 5.6 %collective-permute-start.11 = (f32[48,128]{1,0:T(8,128)S(1)}, f32[48,128]{1,0:T(8,128)S(1)}, u32[]{:S(2)}, u32[]{:S(2)}) collective-permute-start(f32[48,128]{1,0:T(8,128)S(1)} %get-tuple-element.45), channel_id=1, source_target_pairs={{0,2},{1,3},{2,0},{3,1},{4,6},{5,7},{6,4},{7,5},{8,10},{9,11},{10,... | collective-permute-start | bytes 73736 | tf_op jit(solution)/shard_map/ppermute | solution.py:221
  33.8 4.7 %collective-permute-start.12 = (f32[48,128]{1,0:T(8,128)S(1)}, f32[48,128]{1,0:T(8,128)S(1)}, u32[]{:S(2)}, u32[]{:S(2)}) collective-permute-start(f32[48,128]{1,0:T(8,128)S(1)} %get-tuple-element.46), channel_id=1, source_target_pairs={{0,3},{1,2},{2,1},{3,0},{4,7},{5,6},{6,5},{7,4},{8,11},{9,10},{10,... | collective-permute-start | bytes 73736 | tf_op jit(solution)/shard_map/ppermute | solution.py:221
  34.0 4.4 %collective-permute-start.13 = (f32[48,128]{1,0:T(8,128)S(1)}, f32[48,128]{1,0:T(8,128)S(1)}, u32[]{:S(2)}, u32[]{:S(2)}) collective-permute-start(f32[48,128]{1,0:T(8,128)S(1)} %get-tuple-element.47), channel_id=1, source_target_pairs={{0,4},{1,5},{2,6},{3,7},{4,0},{5,1},{6,2},{7,3},{8,12},{9,13},{10,... | collective-permute-start | bytes 73736 | tf_op jit(solution)/shard_map/ppermute | solution.py:221
  35.6 3.3 %collective-permute-start.14 = (f32[48,128]{1,0:T(8,128)S(1)}, f32[48,128]{1,0:T(8,128)S(1)}, u32[]{:S(2)}, u32[]{:S(2)}) collective-permute-start(f32[48,128]{1,0:T(8,128)S(1)} %get-tuple-element.48), channel_id=1, source_target_pairs={{0,5},{1,4},{2,7},{3,6},{4,1},{5,0},{6,3},{7,2},{8,13},{9,12},{10,... | collective-permute-start | bytes 73736 | tf_op jit(solution)/shard_map/ppermute | solution.py:221
  36.1 4.7 %collective-permute-start.15 = (f32[48,128]{1,0:T(8,128)S(1)}, f32[48,128]{1,0:T(8,128)S(1)}, u32[]{:S(2)}, u32[]{:S(2)}) collective-permute-start(f32[48,128]{1,0:T(8,128)S(1)} %get-tuple-element.49), channel_id=1, source_target_pairs={{0,6},{1,7},{2,4},{3,5},{4,2},{5,3},{6,0},{7,1},{8,14},{9,15},{10,... | collective-permute-start | bytes 73736 | tf_op jit(solution)/shard_map/ppermute | solution.py:221
  38.2 4.2 %collective-permute-start.16 = (f32[48,128]{1,0:T(8,128)S(1)}, f32[48,128]{1,0:T(8,128)S(1)}, u32[]{:S(2)}, u32[]{:S(2)}) collective-permute-start(f32[48,128]{1,0:T(8,128)S(1)} %get-tuple-element.50), channel_id=1, source_target_pairs={{0,7},{1,6},{2,5},{3,4},{4,3},{5,2},{6,1},{7,0},{8,15},{9,14},{10,... | collective-permute-start | bytes 73736 | tf_op jit(solution)/shard_map/ppermute | solution.py:221

commit v4 on v3

--- a/solution.py
+++ b/solution.py
@@ -72,26 +72,22 @@
             ]
 
 
-def load_kernel(chunk, residual_hbm, fine_hbm, coarse_hbm, inner, fine, coarse, residual, sems):
-    depth = fine.shape[1]
+def panel_copies(source, target, chunk, sems, first=0):
+    copies = []
+    for n in range(target.shape[0] // chunk):
+        span = pl.ds(first + n * chunk, chunk)
+        copies.append(
+            pltpu.make_async_copy(source.at[span], target.at[pl.ds(n * chunk, chunk)], sems.at[n])
+        )
+    return copies
+
+
+def load_kernel(chunk, residual_hbm, fine_hbm, inner, fine, residual, sem, sems):
     own_width = residual.shape[1]
-    first = pltpu.make_async_copy(residual_hbm, residual, sems.at[0])
+    first = pltpu.make_async_copy(residual_hbm, residual, sem)
     first.start()
-    copies = []
-    for n in range(depth // chunk):
-        span = pl.ds(n * chunk, chunk)
-        copies.append(
-            pltpu.make_async_copy(fine_hbm.at[0, span], fine.at[0, span], sems.at[1 + n])
-        )
-    last = []
-    for n in range(coarse.shape[0] // chunk):
-        span = pl.ds(n * chunk, chunk)
-        last.append(
-            pltpu.make_async_copy(
-                coarse_hbm.at[span], coarse.at[span], sems.at[1 + len(copies) + n]
-            )
-        )
-    for copy in copies + last:
+    copies = panel_copies(fine_hbm.at[0], fine.at[0], chunk, sems)
+    for copy in copies:
         copy.start()
     first.wait()
     local = residual[...].astype(jnp.bfloat16)
@@ -99,13 +95,14 @@
         copy.wait()
         span = slice(n * chunk, (n + 1) * chunk)
         inner[:, span] = mm(local, fine[0, span, :own_width], NT)
-    for copy in last:
-        copy.wait()
-
-
-def fine_kernel(own, rows, start, chunk, sources, margin, begun, factor, *refs):
+
+
+def fine_kernel(own, rows, start, chunk, sources, margin, begun, factor, coarse_hbm, *refs):
     arrived = (None, *refs[: sources - 1])
-    *outs, inner, table = refs[sources - 1 :]
+    *outs, coarse, inner, table, sems = refs[sources - 1 :]
+    copies = panel_copies(coarse_hbm, coarse, chunk, sems)
+    for copy in copies:
+        copy.start()
     rhs = begun.shape[0]
     halo = margin.shape[1]
     depth, width = factor.shape[1:]
@@ -133,12 +130,18 @@
     size = rows * blocks
     for d, out in enumerate(outs):
         out[...] = table[pl.ds(pl.multiple_of((group ^ d) * size, 8), size), :]
-
-
-def coarse_kernel(own, rows, chunk, sources, factor, *refs):
+    for copy in copies:
+        copy.wait()
+
+
+def coarse_kernel(own, rows, chunk, sources, upper, factor_hbm, *refs):
     arrived = refs[:sources]
-    out, table, inner = refs[sources:]
-    depth, width = factor.shape
+    out, table, total, lower, sems = refs[sources:]
+    done = upper.shape[0]
+    depth, width = factor_hbm.shape
+    copies = panel_copies(factor_hbm, lower, chunk, sems, done)
+    for copy in copies:
+        copy.start()
     coarse = width // BLK
     names = [part[own * rows : own * rows + 1, :] for part in arrived]
     names = jnp.concatenate(names, axis=0).T
@@ -163,14 +166,20 @@
     right = jnp.concatenate(
         [table[pl.ds(j, rows, stride=coarse), :] for j in range(coarse)], axis=1
     ).astype(jnp.bfloat16)
-    for n in range(depth // chunk):
-        inner[:, n * chunk : (n + 1) * chunk] = mm(right, factor[n * chunk : (n + 1) * chunk, :], NT)
-    mid = inner[...].astype(jnp.bfloat16)
-    for n in range(width // chunk):
-        part = mm(mid, factor[:, n * chunk : (n + 1) * chunk])
-        for i in range(chunk // BLK):
-            j = n * (chunk // BLK) + i
-            table[pl.ds(j, rows, stride=coarse), :] = part[:, i * BLK : (i + 1) * BLK]
+    panels = [upper.at[pl.ds(n * chunk, chunk)] for n in range(done // chunk)]
+    panels += [lower.at[pl.ds(n * chunk, chunk)] for n in range((depth - done) // chunk)]
+    waits = [None] * (done // chunk) + copies
+    step = 4 * chunk
+    for p, (panel, copy) in enumerate(zip(panels, waits)):
+        if copy is not None:
+            copy.wait()
+        mid = mm(right, panel[...], NT).astype(jnp.bfloat16)
+        for n in range(width // step):
+            where = slice(n * step, (n + 1) * step)
+            part = mm(mid, panel[:, where])
+            total[:, where] = part if p == 0 else total[:, where] + part
+    for j in range(coarse):
+        table[pl.ds(j, rows, stride=coarse), :] = total[:, j * BLK : (j + 1) * BLK]
     solved = jnp.concatenate([table[r * coarse : (r + 1) * coarse, :] for r in range(rows)], axis=1)
     spread = mm(member, jnp.concatenate(split3(solved), axis=1))
     spread = spread[:, :span] + spread[:, span : 2 * span] + spread[:, 2 * span :]
@@ -183,7 +192,7 @@
 
 def merge_kernel(own, rows, groups, margin, spread, *refs):
     arrived = refs[:groups]
-    *outs, total, field = refs[groups:]
+    out, total, field = refs[groups:]
     halo = margin.shape[1]
     blocks = own + halo
     me = lax.axis_index("sub")
@@ -201,15 +210,14 @@
         where = pl.ds(block - owner * own, rows, stride=own)
         away = me ^ owner
         field[away, where, :] = field[away, where, :] + total[pl.ds(own + k, rows, stride=blocks), :]
-    for d, out in enumerate(outs):
-        out[...] = field[d]
-
-
-def last_kernel(own, rows, *refs):
-    *arrived, out, total = refs
-    summed = arrived[0][...]
-    for part in arrived[1:]:
-        summed = summed + part[...]
+    for d in range(out.shape[0]):
+        out[me ^ d] = field[d]
+
+
+def last_kernel(own, rows, arrived, out, total):
+    summed = arrived[0]
+    for s in range(1, arrived.shape[0]):
+        summed = summed + arrived[s]
     total[...] = summed
     for b in range(own):
         out[:, b * BLK : (b + 1) * BLK] = total[pl.ds(b, rows, stride=own), :]
@@ -252,51 +260,63 @@
     )(in_hbm(margin), in_hbm(aggregate.reshape(1, own)), in_hbm(residual))
     arrived = exchange(outgoing, "sub")
     chunk = 256
-    begun, local_factor, coarse_factor = call(
+    begun, local_factor = call(
         functools.partial(load_kernel, chunk),
-        (
-            sds((rhs, depth), f32),
-            sds(local_factor.shape, local_factor.dtype),
-            sds(coarse_factor.shape, coarse_factor.dtype),
-        ),
-        [HBM, HBM, HBM],
+        (sds((rhs, depth), f32), sds(local_factor.shape, local_factor.dtype)),
+        [HBM, HBM],
         [
             pltpu.VMEM(residual.shape, f32),
-            pltpu.SemaphoreType.DMA((1 + depth // chunk + coarse_depth // chunk,)),
+            pltpu.SemaphoreType.DMA,
+            pltpu.SemaphoreType.DMA((depth // chunk,)),
         ],
         flops=2 * rhs * depth * own_width,
-        moved=2 * depth * width + 2 * coarse_depth * coarse_width,
-    )(in_hbm(residual), in_hbm(local_factor), in_hbm(coarse_factor))
-    fine = call(
-        functools.partial(fine_kernel, own, rows, start, chunk, sub_count),
-        [sds((rows * blocks, BLK), f32)] * grp_count,
-        [SMEM] + [VMEM] * (sub_count + 1),
-        [pltpu.VMEM((rhs, depth), f32), pltpu.VMEM((rhs * blocks, BLK), f32)],
+        moved=2 * depth * width,
+    )(in_hbm(residual), in_hbm(local_factor))
+    coarse_factor = in_hbm(coarse_factor)
+    panel = min(chunk, coarse_depth // 2)
+    upper = coarse_depth // 2
+    *fine, coarse_upper = call(
+        functools.partial(fine_kernel, own, rows, start, panel, sub_count),
+        [sds((rows * blocks, BLK), f32)] * grp_count
+        + [sds((upper, coarse_width), coarse_factor.dtype)],
+        [SMEM, VMEM, VMEM, HBM] + [VMEM] * (sub_count - 1),
+        [
+            pltpu.VMEM((rhs, depth), f32),
+            pltpu.VMEM((rhs * blocks, BLK), f32),
+            pltpu.SemaphoreType.DMA((upper // panel,)),
+        ],
         flops=4 * rhs * depth * width,
-        moved=2 * depth * width,
-    )(margin, begun, local_factor, *arrived[1:])
+        moved=2 * depth * width + 2 * upper * coarse_width,
+    )(margin, begun, local_factor, coarse_factor, *arrived[1:])
     panels = exchange(fine, "grp")
+    lower = coarse_depth - upper
     spread = call(
-        functools.partial(coarse_kernel, own, rows, chunk, sub_count),
+        functools.partial(coarse_kernel, own, rows, panel, sub_count),
         sds((sub_count, own * rows, BLK), f32),
-        [VMEM] * (1 + sub_count),
-        [pltpu.VMEM((rows * (coarse_width // BLK), BLK), f32), pltpu.VMEM((rows, coarse_depth), f32)],
+        [VMEM, HBM] + [VMEM] * sub_count,
+        [
+            pltpu.VMEM((rows * (coarse_width // BLK), BLK), f32),
+            pltpu.VMEM((rows, coarse_width), f32),
+            pltpu.VMEM((lower, coarse_width), coarse_factor.dtype),
+            pltpu.SemaphoreType.DMA((lower // panel,)),
+        ],
         flops=4 * rows * coarse_depth * coarse_width,
         moved=2 * coarse_depth * coarse_width,
-    )(coarse_factor, *arrived)
+        limit=24 * MIB,
+    )(coarse_upper, coarse_factor, *arrived)
     merged = call(
         functools.partial(merge_kernel, own, rows, grp_count),
-        [sds((own * rows, BLK), f32)] * sub_count,
+        sds((sub_count, own * rows, BLK), f32),
         [SMEM] + [VMEM] * (1 + grp_count),
         [pltpu.VMEM((rows * blocks, BLK), f32), pltpu.VMEM((sub_count, own * rows, BLK), f32)],
     )(margin, spread, *panels)
-    back = exchange(merged, "sub")
+    back = lax.all_to_all(merged, "sub", split_axis=0, concat_axis=0, tiled=True)
     return call(
         functools.partial(last_kernel, own, rows),
         sds((rows, own_width), f32),
-        [VMEM] * sub_count,
+        [VMEM],
         [pltpu.VMEM((own * rows, BLK), f32)],
-    )(*back)
+    )(back)
 
 
 def solution(mesh):

time: 43.1 us -> 50.4 us (1.17)
  blocking collectives: 0 us -> 9.88 us
  Pallas kernels: 20.4 us -> 28 us
  starting transfers between devices: 18.5 us -> 12.1 us
  waiting for transfers between devices: 3.97 us -> 0.03 us
    all_to_all x0 -> x1, blocking collectives: none -> 9.88 us  [on_device(): lax.all_to_all(merged, 'sub', split_axis=0, concat_axis=0, tiled=True)]
    pallas_call x3, Pallas kernels: 10.3 us -> 19.8 us  [the longest x1 14.3 us: on_device(): call(functools.partial(coarse_kernel, own, rows, panel, sub_count), sds((...]
    ppermute x17 -> x10, starting transfers between devices: 18.5 us -> 12.1 us  [exchange(): lax.ppermute(parts[d], axis, [(i, i ^ d) for i in range(count)])]
    ppermute x17 -> x10, waiting for transfers between devices: 3.97 us -> 0.03 us  [exchange(): lax.ppermute(parts[d], axis, [(i, i ^ d) for i in range(count)])]
    pallas_call x1, Pallas kernels: 8.37 us -> 6.51 us  [on_device(): call(functools.partial(load_kernel, chunk), (sds((rhs, depth), f32), sds(...]
  transfers between devices with their start and end apart: 17 -> 10, of which waited for: 3 -> 0; matrix products, arithmetic and copies ran while one was open for 0% -> 0% of each run, Pallas kernels for 36% -> 41%
where the time goes in v4:
time: 50.4 us; the launch traced here: 50.2 us
  Pallas kernels  28 us (56%)
  starting transfers between devices  12.1 us (24%)
  blocking collectives  9.88 us (20%)
    pallas_call x1, Pallas kernels, on_device(): call(functools.partial(coarse_kernel, own, rows, panel, sub_count), sds((...  14.3 us
    ppermute x10, starting transfers between devices, exchange(): lax.ppermute(parts[d], axis, [(i, i ^ d) for i in range(count)])  12.1 us
    all_to_all x1, blocking collectives, on_device(): lax.all_to_all(merged, 'sub', split_axis=0, concat_axis=0, tiled=True)  9.88 us
    pallas_call x1, Pallas kernels, on_device(): call(functools.partial(load_kernel, chunk), (sds((rhs, depth), f32), sds(...  6.51 us
    pallas_call x1, Pallas kernels, on_device(): call(functools.partial(fine_kernel, own, rows, start, panel, sub_count),...  4.76 us
    pallas_call x1, Pallas kernels, on_device(): call(functools.partial(pack_kernel, own, rows, pad), [sds((start, BLK), f...  1.13 us
  transfers between devices with their start and end apart: 10, of which 0 were waited for; matrix products, arithmetic and copies ran while one was open for 0% of the time, Pallas kernels for 41%

profile of v4, /device:TPU:0, one launch (start us, length us, event | category | flops | bytes accessed | tf_op | source)
XLA Modules:
  0.0 50.2 jit_solution(1779421574366152667)
XLA Ops:
  0.0 0.0 copy-start
  0.0 1.1 %shard_map.56 = (f32[56,128]{1,0:T(8,128)S(1)}, f32[120,128]{1,0:T(8,128)S(1)}, f32[120,128]{1,0:T(8,128)S(1)}, f32[120,128]{1,0:T(8,128)S(1)}, f32[120,128]{1,0...) custom-call(s32[8,8]{1,0:T(8,128)} %margin.3, s32[1,24]{1,0:T(1,128)} %bitcast.1, ...), custom_call_target="tpu_custom_call" | custom-call | tf_op jit(solution)/shard_map/pallas_call | solution.py:249
  1.1 0.5 %collective-permute-start = (f32[120,128]{1,0:T(8,128)S(1)}, f32[120,128]{1,0:T(8,128)S(1)}, u32[]{:S(2)}, u32[]{:S(2)}) collective-permute-start(f32[120,128]{1,0:T(8,128)S(1)} %get-tuple-element.22), channel_id=1, source_target_pairs={{0,1},{1,0},{2,3},{3,2},{4,5},{5,4},{6,7},{7,6},{8,9},{9,8},{10,11... | collective-permute-start | bytes 184328 | tf_op jit(solution)/shard_map/ppermute | solution.py:229
  1.7 2.6 %collective-permute-start.1 = (f32[120,128]{1,0:T(8,128)S(1)}, f32[120,128]{1,0:T(8,128)S(1)}, u32[]{:S(2)}, u32[]{:S(2)}) collective-permute-start(f32[120,128]{1,0:T(8,128)S(1)} %get-tuple-element.23), channel_id=1, source_target_pairs={{0,2},{1,3},{2,0},{3,1},{4,6},{5,7},{6,4},{7,5},{8,10},{9,11},{10,... | collective-permute-start | bytes 184328 | tf_op jit(solution)/shard_map/ppermute | solution.py:229
  4.2 0.1 collective-permute-start.2
  4.3 1.8 %collective-permute-start.3 = (f32[120,128]{1,0:T(8,128)S(1)}, f32[120,128]{1,0:T(8,128)S(1)}, u32[]{:S(2)}, u32[]{:S(2)}) collective-permute-start(f32[120,128]{1,0:T(8,128)S(1)} %get-tuple-element.25), channel_id=1, source_target_pairs={{0,4},{1,5},{2,6},{3,7},{4,0},{5,1},{6,2},{7,3},{8,12},{9,13},{10,... | collective-permute-start | bytes 184328 | tf_op jit(solution)/shard_map/ppermute | solution.py:229
  6.1 0.0 collective-permute-start.4
  6.1 0.0 collective-permute-done.refs_0_.refs_1_
  6.1 2.6 %collective-permute-start.5 = (f32[120,128]{1,0:T(8,128)S(1)}, f32[120,128]{1,0:T(8,128)S(1)}, u32[]{:S(2)}, u32[]{:S(2)}) collective-permute-start(f32[120,128]{1,0:T(8,128)S(1)} %get-tuple-element.27), channel_id=1, source_target_pairs={{0,6},{1,7},{2,4},{3,5},{4,2},{5,3},{6,0},{7,1},{8,14},{9,15},{10,... | collective-permute-start | bytes 184328 | tf_op jit(solution)/shard_map/ppermute | solution.py:229
  8.7 0.0 collective-permute-done.1.refs_1_.refs_2_
  8.7 0.1 collective-permute-start.6
  8.8 6.5 %shard_map.55 = (f32[8,1024]{1,0:T(8,128)S(1)}, bf16[1,1024,4096]{2,1,0:T(8,128)(2,1)S(1)}) custom-call(f32[8,3072]{1,0:T(8,128)} %residual_hbm.3, bf16[1,1024,4096]{2,1,0:T(8,128)(2,1)} %fine_hbm.1), custom_call_target="tpu_custom_call" | custom-call | flops 50331648 | bytes 8388608 | tf_op jit(solution)/shard_map/pallas_call | solution.py:263
  15.3 0.0 collective-permute-done.2.refs_2_.refs_3_
  15.3 0.0 collective-permute-done.3.refs_3_.refs_4_
  15.3 0.0 collective-permute-done.4.refs_4_.refs_5_
  15.4 0.0 collective-permute-done.5.refs_5_.refs_6_
  15.4 0.0 collective-permute-done.6.refs_6_.refs_7_
  15.4 0.0 copy-done
  15.4 4.8 %shard_map.57 = (f32[64,128]{1,0:T(8,128)S(1)}, f32[64,128]{1,0:T(8,128)S(1)}, f32[64,128]{1,0:T(8,128)S(1)}, f32[64,128]{1,0:T(8,128)S(1)}, bf16[512,8192]{1,0:T(8,128)(2,1)S(1)}) custom-call(s32[8,8]{1,0:T(8,128)S(1)} %copy-done, f32[8,1024]{1,0:T(8,128)S(1)} %get-tuple-element.20.begun, bf16[1,1024,4096]{2,1,0:T(8,128)(2,1)S(1)} %get-tuple-element.21.factor, ...), custom_call_target="tpu_custom_call" | custom-call | flops 134217728 | bytes 16777216 | tf_op jit(solution)/shard_map/pallas_call | solution.py:278
  20.2 1.8 %collective-permute-start.7 = (f32[64,128]{1,0:T(8,128)S(1)}, f32[64,128]{1,0:T(8,128)S(1)}, u32[]{:S(2)}, u32[]{:S(2)}) collective-permute-start(f32[64,128]{1,0:T(8,128)S(1)} %get-tuple-element.32), channel_id=1, source_target_pairs={{0,8},{8,0},{16,24},{24,16},{1,9},{9,1},{17,25},{25,17},{2,10},{10... | collective-permute-start | bytes 98312 | tf_op jit(solution)/shard_map/ppermute | solution.py:229
  21.9 2.6 %collective-permute-start.8 = (f32[64,128]{1,0:T(8,128)S(1)}, f32[64,128]{1,0:T(8,128)S(1)}, u32[]{:S(2)}, u32[]{:S(2)}) collective-permute-start(f32[64,128]{1,0:T(8,128)S(1)} %get-tuple-element.33), channel_id=1, source_target_pairs={{0,16},{8,24},{16,0},{24,8},{1,17},{9,25},{17,1},{25,9},{2,18},{10... | collective-permute-start | bytes 98312 | tf_op jit(solution)/shard_map/ppermute | solution.py:229
  24.5 0.1 collective-permute-start.9
  24.6 14.3 %shard_map.58.spread = f32[8,48,128]{2,1,0:T(8,128)S(1)} custom-call(bf16[512,8192]{1,0:T(8,128)(2,1)S(1)} %get-tuple-element.29.upper, bf16[1024,8192]{1,0:T(8,128)(2,1)} %factor_hbm.1, f32[56,128]{1,0:T(8,128)S(1)} %get-tuple-element.30.refs_0_, f32[120,128]{1,0:T(8,128)S(1)} %collective-permute-done.refs_0_.refs_1_, ...), custom_call_target="tpu_custom_call" | custom-call | flops 67108864 | bytes 16777216 | tf_op jit(solution)/shard_map/pallas_call | solution.py:293
  38.9 0.0 collective-permute-done.7.refs_1_
  38.9 0.0 collective-permute-done.8.refs_2_
  39.0 0.0 collective-permute-done.9.refs_3_
  39.0 0.7 %shard_map.59 = f32[8,48,128]{2,1,0:T(8,128)S(1)} custom-call(s32[8,8]{1,0:T(8,128)S(1)} %copy-done, f32[8,48,128]{2,1,0:T(8,128)S(1)} %shard_map.58.spread, f32[64,128]{1,0:T(8,128)S(1)} %get-tuple-element.31.refs_0_, f32[64,128]{1,0:T(8,128)S(1)} %collective-permute-done.7.refs_1_, f32[64,128]{1,0:T(8,128)S(1)} %collective-permute-done.8.refs_2_, ...), custom_call_target="tpu_custom_call" | custom-call | tf_op jit(solution)/shard_map/pallas_call | solution.py:307
  39.7 9.9 %all_to_all.5.arrived = f32[8,48,128]{2,1,0:T(8,128)S(1)} all-to-all(f32[8,48,128]{2,1,0:T(8,128)S(1)} %shard_map.59), channel_id=1, replica_groups=mesh['grp'=4,'sub'=8] {'sub'}, dimensions={0} | all-to-all | bytes 393216 | tf_op jit(solution)/shard_map/all_to_all | solution.py:313
  49.5 0.6 %shard_map.60 = f32[2,3072]{1,0:T(2,128)} custom-call(f32[8,48,128]{2,1,0:T(8,128)S(1)} %all_to_all.5.arrived), custom_call_target="tpu_custom_call" | custom-call | tf_op jit(solution)/shard_map/pallas_call | solution.py:314
Async XLA Ops:
  0.0 15.4 %copy-start = (s32[8,8]{1,0:T(8,128)S(1)}, s32[8,8]{1,0:T(8,128)}, u32[]{:S(2)}) copy-start(s32[8,8]{1,0:T(8,128)} %margin.3) | copy-start | bytes 772
  1.1 4.9 %collective-permute-start = (f32[120,128]{1,0:T(8,128)S(1)}, f32[120,128]{1,0:T(8,128)S(1)}, u32[]{:S(2)}, u32[]{:S(2)}) collective-permute-start(f32[120,128]{1,0:T(8,128)S(1)} %get-tuple-element.22), channel_id=1, source_target_pairs={{0,1},{1,0},{2,3},{3,2},{4,5},{5,4},{6,7},{7,6},{8,9},{9,8},{10,11... | collective-permute-start | bytes 184328 | tf_op jit(solution)/shard_map/ppermute | solution.py:229
  1.7 7.0 %collective-permute-start.1 = (f32[120,128]{1,0:T(8,128)S(1)}, f32[120,128]{1,0:T(8,128)S(1)}, u32[]{:S(2)}, u32[]{:S(2)}) collective-permute-start(f32[120,128]{1,0:T(8,128)S(1)} %get-tuple-element.23), channel_id=1, source_target_pairs={{0,2},{1,3},{2,0},{3,1},{4,6},{5,7},{6,4},{7,5},{8,10},{9,11},{10,... | collective-permute-start | bytes 184328 | tf_op jit(solution)/shard_map/ppermute | solution.py:229
  4.2 11.1 %collective-permute-start.2 = (f32[120,128]{1,0:T(8,128)S(1)}, f32[120,128]{1,0:T(8,128)S(1)}, u32[]{:S(2)}, u32[]{:S(2)}) collective-permute-start(f32[120,128]{1,0:T(8,128)S(1)} %get-tuple-element.24), channel_id=1, source_target_pairs={{0,3},{1,2},{2,1},{3,0},{4,7},{5,6},{6,5},{7,4},{8,11},{9,10},{10,... | collective-permute-start | bytes 184328 | tf_op jit(solution)/shard_map/ppermute | solution.py:229
  4.3 11.0 %collective-permute-start.3 = (f32[120,128]{1,0:T(8,128)S(1)}, f32[120,128]{1,0:T(8,128)S(1)}, u32[]{:S(2)}, u32[]{:S(2)}) collective-permute-start(f32[120,128]{1,0:T(8,128)S(1)} %get-tuple-element.25), channel_id=1, source_target_pairs={{0,4},{1,5},{2,6},{3,7},{4,0},{5,1},{6,2},{7,3},{8,12},{9,13},{10,... | collective-permute-start | bytes 184328 | tf_op jit(solution)/shard_map/ppermute | solution.py:229
  6.1 9.3 %collective-permute-start.4 = (f32[120,128]{1,0:T(8,128)S(1)}, f32[120,128]{1,0:T(8,128)S(1)}, u32[]{:S(2)}, u32[]{:S(2)}) collective-permute-start(f32[120,128]{1,0:T(8,128)S(1)} %get-tuple-element.26), channel_id=1, source_target_pairs={{0,5},{1,4},{2,7},{3,6},{4,1},{5,0},{6,3},{7,2},{8,13},{9,12},{10,... | collective-permute-start | bytes 184328 | tf_op jit(solution)/shard_map/ppermute | solution.py:229
  6.1 9.3 %collective-permute-start.5 = (f32[120,128]{1,0:T(8,128)S(1)}, f32[120,128]{1,0:T(8,128)S(1)}, u32[]{:S(2)}, u32[]{:S(2)}) collective-permute-start(f32[120,128]{1,0:T(8,128)S(1)} %get-tuple-element.27), channel_id=1, source_target_pairs={{0,6},{1,7},{2,4},{3,5},{4,2},{5,3},{6,0},{7,1},{8,14},{9,15},{10,... | collective-permute-start | bytes 184328 | tf_op jit(solution)/shard_map/ppermute | solution.py:229
  8.7 6.7 %collective-permute-start.6 = (f32[120,128]{1,0:T(8,128)S(1)}, f32[120,128]{1,0:T(8,128)S(1)}, u32[]{:S(2)}, u32[]{:S(2)}) collective-permute-start(f32[120,128]{1,0:T(8,128)S(1)} %get-tuple-element.28), channel_id=1, source_target_pairs={{0,7},{1,6},{2,5},{3,4},{4,3},{5,2},{6,1},{7,0},{8,15},{9,14},{10,... | collective-permute-start | bytes 184328 | tf_op jit(solution)/shard_map/ppermute | solution.py:229
  20.2 18.8 %collective-permute-start.7 = (f32[64,128]{1,0:T(8,128)S(1)}, f32[64,128]{1,0:T(8,128)S(1)}, u32[]{:S(2)}, u32[]{:S(2)}) collective-permute-start(f32[64,128]{1,0:T(8,128)S(1)} %get-tuple-element.32), channel_id=1, source_target_pairs={{0,8},{8,0},{16,24},{24,16},{1,9},{9,1},{17,25},{25,17},{2,10},{10... | collective-permute-start | bytes 98312 | tf_op jit(solution)/shard_map/ppermute | solution.py:229
  21.9 17.0 %collective-permute-start.8 = (f32[64,128]{1,0:T(8,128)S(1)}, f32[64,128]{1,0:T(8,128)S(1)}, u32[]{:S(2)}, u32[]{:S(2)}) collective-permute-start(f32[64,128]{1,0:T(8,128)S(1)} %get-tuple-element.33), channel_id=1, source_target_pairs={{0,16},{8,24},{16,0},{24,8},{1,17},{9,25},{17,1},{25,9},{2,18},{10... | collective-permute-start | bytes 98312 | tf_op jit(solution)/shard_map/ppermute | solution.py:229
  24.5 14.4 %collective-permute-start.9 = (f32[64,128]{1,0:T(8,128)S(1)}, f32[64,128]{1,0:T(8,128)S(1)}, u32[]{:S(2)}, u32[]{:S(2)}) collective-permute-start(f32[64,128]{1,0:T(8,128)S(1)} %get-tuple-element.34), channel_id=1, source_target_pairs={{0,24},{8,16},{16,8},{24,0},{1,25},{9,17},{17,9},{25,1},{2,26},{10... | collective-permute-start | bytes 98312 | tf_op jit(solution)/shard_map/ppermute | solution.py:229

commit v5 on v4

--- a/solution.py
+++ b/solution.py
@@ -79,30 +79,36 @@
         copies.append(
             pltpu.make_async_copy(source.at[span], target.at[pl.ds(n * chunk, chunk)], sems.at[n])
         )
+    for copy in copies:
+        copy.start()
     return copies
 
 
-def load_kernel(chunk, residual_hbm, fine_hbm, inner, fine, residual, sem, sems):
+def first_product(factor, right, tile, copies=()):
+    depth = factor.shape[0]
+    each = len(copies) * tile // depth
+    parts = []
+    for n in range(depth // tile):
+        for copy in copies[n * each : (n + 1) * each]:
+            copy.wait()
+        parts.append(mm(factor[n * tile : (n + 1) * tile, :], right, NT).T)
+    return jnp.concatenate(parts, axis=1)
+
+
+def load_kernel(chunk, tile, residual_hbm, fine_hbm, inner, fine, residual, sem, sems):
     own_width = residual.shape[1]
     first = pltpu.make_async_copy(residual_hbm, residual, sem)
     first.start()
     copies = panel_copies(fine_hbm.at[0], fine.at[0], chunk, sems)
-    for copy in copies:
-        copy.start()
     first.wait()
     local = residual[...].astype(jnp.bfloat16)
-    for n, copy in enumerate(copies):
-        copy.wait()
-        span = slice(n * chunk, (n + 1) * chunk)
-        inner[:, span] = mm(local, fine[0, span, :own_width], NT)
-
-
-def fine_kernel(own, rows, start, chunk, sources, margin, begun, factor, coarse_hbm, *refs):
+    inner[...] = first_product(fine.at[0, :, pl.ds(0, own_width)], local, tile, copies)
+
+
+def fine_kernel(own, rows, start, chunk, tile, sources, margin, begun, factor, coarse_hbm, *refs):
     arrived = (None, *refs[: sources - 1])
-    *outs, coarse, inner, table, sems = refs[sources - 1 :]
+    *outs, coarse, table, sems = refs[sources - 1 :]
     copies = panel_copies(coarse_hbm, coarse, chunk, sems)
-    for copy in copies:
-        copy.start()
     rhs = begun.shape[0]
     halo = margin.shape[1]
     depth, width = factor.shape[1:]
@@ -113,19 +119,17 @@
     for k in range(halo):
         away = me ^ (margin[me, k] // own)
         span = slice(start + k * rhs, start + (k + 1) * rhs)
-        tile = arrived[1][span, :]
+        part = arrived[1][span, :]
         for d in range(2, sources):
-            tile = jnp.where(away == d, arrived[d][span, :], tile)
-        tiles.append(tile.astype(jnp.bfloat16))
+            part = jnp.where(away == d, arrived[d][span, :], part)
+        tiles.append(part.astype(jnp.bfloat16))
     local = jnp.concatenate(tiles, axis=1)
-    for n in range(depth // chunk):
-        span = slice(n * chunk, (n + 1) * chunk)
-        inner[:, span] = begun[:, span] + mm(local, factor[0, span, own * BLK :], NT)
-    mid = inner[...].astype(jnp.bfloat16)
-    for n in range(width // chunk):
-        part = mm(mid, factor[0, :, n * chunk : (n + 1) * chunk])
-        for i in range(chunk // BLK):
-            b = n * (chunk // BLK) + i
+    far = factor.at[0, :, pl.ds(own * BLK, halo * BLK)]
+    mid = (begun[...] + first_product(far, local, tile)).astype(jnp.bfloat16)
+    for n in range(width // 256):
+        part = mm(mid, factor[0, :, n * 256 : (n + 1) * 256])
+        for i in range(256 // BLK):
+            b = n * (256 // BLK) + i
             table[pl.ds(b, rhs, stride=blocks), :] = part[:, i * BLK : (i + 1) * BLK]
     size = rows * blocks
     for d, out in enumerate(outs):
@@ -134,14 +138,12 @@
         copy.wait()
 
 
-def coarse_kernel(own, rows, chunk, sources, upper, factor_hbm, *refs):
+def coarse_kernel(own, rows, chunk, tile, sources, upper, factor_hbm, *refs):
     arrived = refs[:sources]
-    out, table, total, lower, sems = refs[sources:]
+    out, table, lower, sems = refs[sources:]
     done = upper.shape[0]
-    depth, width = factor_hbm.shape
+    width = upper.shape[1]
     copies = panel_copies(factor_hbm, lower, chunk, sems, done)
-    for copy in copies:
-        copy.start()
     coarse = width // BLK
     names = [part[own * rows : own * rows + 1, :] for part in arrived]
     names = jnp.concatenate(names, axis=0).T
@@ -166,20 +168,14 @@
     right = jnp.concatenate(
         [table[pl.ds(j, rows, stride=coarse), :] for j in range(coarse)], axis=1
     ).astype(jnp.bfloat16)
-    panels = [upper.at[pl.ds(n * chunk, chunk)] for n in range(done // chunk)]
-    panels += [lower.at[pl.ds(n * chunk, chunk)] for n in range((depth - done) // chunk)]
-    waits = [None] * (done // chunk) + copies
-    step = 4 * chunk
-    for p, (panel, copy) in enumerate(zip(panels, waits)):
-        if copy is not None:
-            copy.wait()
-        mid = mm(right, panel[...], NT).astype(jnp.bfloat16)
-        for n in range(width // step):
-            where = slice(n * step, (n + 1) * step)
-            part = mm(mid, panel[:, where])
-            total[:, where] = part if p == 0 else total[:, where] + part
-    for j in range(coarse):
-        table[pl.ds(j, rows, stride=coarse), :] = total[:, j * BLK : (j + 1) * BLK]
+    high = first_product(upper, right, min(tile, done)).astype(jnp.bfloat16)
+    low = first_product(lower, right, min(tile, done), copies).astype(jnp.bfloat16)
+    for n in range(width // 256):
+        where = slice(n * 256, (n + 1) * 256)
+        part = mm(high, upper[:, where]) + mm(low, lower[:, where])
+        for i in range(256 // BLK):
+            j = n * (256 // BLK) + i
+            table[pl.ds(j, rows, stride=coarse), :] = part[:, i * BLK : (i + 1) * BLK]
     solved = jnp.concatenate([table[r * coarse : (r + 1) * coarse, :] for r in range(rows)], axis=1)
     spread = mm(member, jnp.concatenate(split3(solved), axis=1))
     spread = spread[:, :span] + spread[:, span : 2 * span] + spread[:, 2 * span :]
@@ -259,9 +255,9 @@
         ],
     )(in_hbm(margin), in_hbm(aggregate.reshape(1, own)), in_hbm(residual))
     arrived = exchange(outgoing, "sub")
-    chunk = 256
+    chunk, tile = 64, 256
     begun, local_factor = call(
-        functools.partial(load_kernel, chunk),
+        functools.partial(load_kernel, chunk, tile),
         (sds((rhs, depth), f32), sds(local_factor.shape, local_factor.dtype)),
         [HBM, HBM],
         [
@@ -273,32 +269,26 @@
         moved=2 * depth * width,
     )(in_hbm(residual), in_hbm(local_factor))
     coarse_factor = in_hbm(coarse_factor)
-    panel = min(chunk, coarse_depth // 2)
-    upper = coarse_depth // 2
+    upper = coarse_depth // 4
     *fine, coarse_upper = call(
-        functools.partial(fine_kernel, own, rows, start, panel, sub_count),
+        functools.partial(fine_kernel, own, rows, start, chunk, tile, sub_count),
         [sds((rows * blocks, BLK), f32)] * grp_count
         + [sds((upper, coarse_width), coarse_factor.dtype)],
         [SMEM, VMEM, VMEM, HBM] + [VMEM] * (sub_count - 1),
-        [
-            pltpu.VMEM((rhs, depth), f32),
-            pltpu.VMEM((rhs * blocks, BLK), f32),
-            pltpu.SemaphoreType.DMA((upper // panel,)),
-        ],
+        [pltpu.VMEM((rhs * blocks, BLK), f32), pltpu.SemaphoreType.DMA((upper // chunk,))],
         flops=4 * rhs * depth * width,
         moved=2 * depth * width + 2 * upper * coarse_width,
     )(margin, begun, local_factor, coarse_factor, *arrived[1:])
     panels = exchange(fine, "grp")
     lower = coarse_depth - upper
     spread = call(
-        functools.partial(coarse_kernel, own, rows, panel, sub_count),
+        functools.partial(coarse_kernel, own, rows, chunk, tile, sub_count),
         sds((sub_count, own * rows, BLK), f32),
         [VMEM, HBM] + [VMEM] * sub_count,
         [
             pltpu.VMEM((rows * (coarse_width // BLK), BLK), f32),
-            pltpu.VMEM((rows, coarse_width), f32),
             pltpu.VMEM((lower, coarse_width), coarse_factor.dtype),
-            pltpu.SemaphoreType.DMA((lower // panel,)),
+            pltpu.SemaphoreType.DMA((lower // chunk,)),
         ],
         flops=4 * rows * coarse_depth * coarse_width,
         moved=2 * coarse_depth * coarse_width,

time: 50.4 us -> 47.8 us (0.948)
  Pallas kernels: 28 us -> 25.5 us
    pallas_call x3, Pallas kernels: 25.6 us -> 23 us  [the longest x1 12.2 us: on_device(): call(functools.partial(coarse_kernel, own, rows, chunk, tile, sub_count),...]
where the time goes in v5:
time: 47.8 us; the launch traced here: 47.6 us
  Pallas kernels  25.5 us (53%)
  starting transfers between devices  12.1 us (25%)
  blocking collectives  9.88 us (21%)
    pallas_call x1, Pallas kernels, on_device(): call(functools.partial(coarse_kernel, own, rows, chunk, tile, sub_count),...  12.2 us
    ppermute x10, starting transfers between devices, exchange(): lax.ppermute(parts[d], axis, [(i, i ^ d) for i in range(count)])  12.1 us
    all_to_all x1, blocking collectives, on_device(): lax.all_to_all(merged, 'sub', split_axis=0, concat_axis=0, tiled=True)  9.88 us
    pallas_call x1, Pallas kernels, on_device(): call(functools.partial(load_kernel, chunk, tile), (sds((rhs, depth), f32)...  7.24 us
    pallas_call x1, Pallas kernels, on_device(): call(functools.partial(fine_kernel, own, rows, start, chunk, tile, sub_co...  3.59 us
    pallas_call x1, Pallas kernels, on_device(): call(functools.partial(pack_kernel, own, rows, pad), [sds((start, BLK), f...  1.13 us
  transfers between devices with their start and end apart: 10, of which 0 were waited for; matrix products, arithmetic and copies ran while one was open for 0% of the time, Pallas kernels for 41%

profile of v5, /device:TPU:0, one launch (start us, length us, event | category | flops | bytes accessed | tf_op | source)
XLA Modules:
  0.0 47.6 jit_solution(7203870035145522361)
XLA Ops:
  0.0 0.0 copy-start
  0.0 1.1 %shard_map.56 = (f32[56,128]{1,0:T(8,128)S(1)}, f32[120,128]{1,0:T(8,128)S(1)}, f32[120,128]{1,0:T(8,128)S(1)}, f32[120,128]{1,0:T(8,128)S(1)}, f32[120,128]{1,0...) custom-call(s32[8,8]{1,0:T(8,128)} %margin.3, s32[1,24]{1,0:T(1,128)} %bitcast.1, ...), custom_call_target="tpu_custom_call" | custom-call | tf_op jit(solution)/shard_map/pallas_call | solution.py:245
  1.1 0.5 %collective-permute-start = (f32[120,128]{1,0:T(8,128)S(1)}, f32[120,128]{1,0:T(8,128)S(1)}, u32[]{:S(2)}, u32[]{:S(2)}) collective-permute-start(f32[120,128]{1,0:T(8,128)S(1)} %get-tuple-element.22), channel_id=1, source_target_pairs={{0,1},{1,0},{2,3},{3,2},{4,5},{5,4},{6,7},{7,6},{8,9},{9,8},{10,11... | collective-permute-start | bytes 184328 | tf_op jit(solution)/shard_map/ppermute | solution.py:225
  1.7 2.6 %collective-permute-start.1 = (f32[120,128]{1,0:T(8,128)S(1)}, f32[120,128]{1,0:T(8,128)S(1)}, u32[]{:S(2)}, u32[]{:S(2)}) collective-permute-start(f32[120,128]{1,0:T(8,128)S(1)} %get-tuple-element.23), channel_id=1, source_target_pairs={{0,2},{1,3},{2,0},{3,1},{4,6},{5,7},{6,4},{7,5},{8,10},{9,11},{10,... | collective-permute-start | bytes 184328 | tf_op jit(solution)/shard_map/ppermute | solution.py:225
  4.2 0.1 collective-permute-start.2
  4.3 1.8 %collective-permute-start.3 = (f32[120,128]{1,0:T(8,128)S(1)}, f32[120,128]{1,0:T(8,128)S(1)}, u32[]{:S(2)}, u32[]{:S(2)}) collective-permute-start(f32[120,128]{1,0:T(8,128)S(1)} %get-tuple-element.25), channel_id=1, source_target_pairs={{0,4},{1,5},{2,6},{3,7},{4,0},{5,1},{6,2},{7,3},{8,12},{9,13},{10,... | collective-permute-start | bytes 184328 | tf_op jit(solution)/shard_map/ppermute | solution.py:225
  6.1 0.0 collective-permute-start.4
  6.1 0.0 collective-permute-done.refs_0_.refs_1_
  6.1 2.6 %collective-permute-start.5 = (f32[120,128]{1,0:T(8,128)S(1)}, f32[120,128]{1,0:T(8,128)S(1)}, u32[]{:S(2)}, u32[]{:S(2)}) collective-permute-start(f32[120,128]{1,0:T(8,128)S(1)} %get-tuple-element.27), channel_id=1, source_target_pairs={{0,6},{1,7},{2,4},{3,5},{4,2},{5,3},{6,0},{7,1},{8,14},{9,15},{10,... | collective-permute-start | bytes 184328 | tf_op jit(solution)/shard_map/ppermute | solution.py:225
  8.7 0.0 collective-permute-done.1.refs_1_.refs_2_
  8.7 0.1 collective-permute-start.6
  8.8 7.2 %shard_map.55 = (f32[8,1024]{1,0:T(8,128)S(1)}, bf16[1,1024,4096]{2,1,0:T(8,128)(2,1)S(1)}) custom-call(f32[8,3072]{1,0:T(8,128)} %residual_hbm.3, bf16[1,1024,4096]{2,1,0:T(8,128)(2,1)} %fine_hbm.1), custom_call_target="tpu_custom_call" | custom-call | flops 50331648 | bytes 8388608 | tf_op jit(solution)/shard_map/pallas_call | solution.py:259
  16.0 0.0 collective-permute-done.2.refs_2_.refs_3_
  16.1 0.0 collective-permute-done.3.refs_3_.refs_4_
  16.1 0.0 collective-permute-done.4.refs_4_.refs_5_
  16.1 0.0 collective-permute-done.5.refs_5_.refs_6_
  16.1 0.0 collective-permute-done.6.refs_6_.refs_7_
  16.1 0.0 copy-done
  16.1 3.6 %shard_map.57 = (f32[64,128]{1,0:T(8,128)S(1)}, f32[64,128]{1,0:T(8,128)S(1)}, f32[64,128]{1,0:T(8,128)S(1)}, f32[64,128]{1,0:T(8,128)S(1)}, bf16[256,8192]{1,0:T(8,128)(2,1)S(1)}) custom-call(s32[8,8]{1,0:T(8,128)S(1)} %copy-done, f32[8,1024]{1,0:T(8,128)S(1)} %get-tuple-element.20.begun, bf16[1,1024,4096]{2,1,0:T(8,128)(2,1)S(1)} %get-tuple-element.21.factor, ...), custom_call_target="tpu_custom_call" | custom-call | flops 134217728 | bytes 12582912 | tf_op jit(solution)/shard_map/pallas_call | solution.py:273
  19.7 1.8 %collective-permute-start.7 = (f32[64,128]{1,0:T(8,128)S(1)}, f32[64,128]{1,0:T(8,128)S(1)}, u32[]{:S(2)}, u32[]{:S(2)}) collective-permute-start(f32[64,128]{1,0:T(8,128)S(1)} %get-tuple-element.32), channel_id=1, source_target_pairs={{0,8},{8,0},{16,24},{24,16},{1,9},{9,1},{17,25},{25,17},{2,10},{10... | collective-permute-start | bytes 98312 | tf_op jit(solution)/shard_map/ppermute | solution.py:225
  21.5 2.6 %collective-permute-start.8 = (f32[64,128]{1,0:T(8,128)S(1)}, f32[64,128]{1,0:T(8,128)S(1)}, u32[]{:S(2)}, u32[]{:S(2)}) collective-permute-start(f32[64,128]{1,0:T(8,128)S(1)} %get-tuple-element.33), channel_id=1, source_target_pairs={{0,16},{8,24},{16,0},{24,8},{1,17},{9,25},{17,1},{25,9},{2,18},{10... | collective-permute-start | bytes 98312 | tf_op jit(solution)/shard_map/ppermute | solution.py:225
  24.1 0.1 collective-permute-start.9
  24.2 12.2 %shard_map.58.spread = f32[8,48,128]{2,1,0:T(8,128)S(1)} custom-call(bf16[256,8192]{1,0:T(8,128)(2,1)S(1)} %get-tuple-element.29.upper, bf16[1024,8192]{1,0:T(8,128)(2,1)} %factor_hbm.1, f32[56,128]{1,0:T(8,128)S(1)} %get-tuple-element.30.refs_0_, f32[120,128]{1,0:T(8,128)S(1)} %collective-permute-done.refs_0_.refs_1_, ...), custom_call_target="tpu_custom_call" | custom-call | flops 67108864 | bytes 16777216 | tf_op jit(solution)/shard_map/pallas_call | solution.py:284
  36.4 0.0 collective-permute-done.7.refs_1_
  36.4 0.0 collective-permute-done.8.refs_2_
  36.4 0.0 collective-permute-done.9.refs_3_
  36.4 0.7 %shard_map.59 = f32[8,48,128]{2,1,0:T(8,128)S(1)} custom-call(s32[8,8]{1,0:T(8,128)S(1)} %copy-done, f32[8,48,128]{2,1,0:T(8,128)S(1)} %shard_map.58.spread, f32[64,128]{1,0:T(8,128)S(1)} %get-tuple-element.31.refs_0_, f32[64,128]{1,0:T(8,128)S(1)} %collective-permute-done.7.refs_1_, f32[64,128]{1,0:T(8,128)S(1)} %collective-permute-done.8.refs_2_, ...), custom_call_target="tpu_custom_call" | custom-call | tf_op jit(solution)/shard_map/pallas_call | solution.py:297
  37.1 9.9 %all_to_all.5.arrived = f32[8,48,128]{2,1,0:T(8,128)S(1)} all-to-all(f32[8,48,128]{2,1,0:T(8,128)S(1)} %shard_map.59), channel_id=1, replica_groups=mesh['grp'=4,'sub'=8] {'sub'}, dimensions={0} | all-to-all | bytes 393216 | tf_op jit(solution)/shard_map/all_to_all | solution.py:303
  47.0 0.6 %shard_map.60 = f32[2,3072]{1,0:T(2,128)} custom-call(f32[8,48,128]{2,1,0:T(8,128)S(1)} %all_to_all.5.arrived), custom_call_target="tpu_custom_call" | custom-call | tf_op jit(solution)/shard_map/pallas_call | solution.py:304
Async XLA Ops:
  0.0 16.1 %copy-start = (s32[8,8]{1,0:T(8,128)S(1)}, s32[8,8]{1,0:T(8,128)}, u32[]{:S(2)}) copy-start(s32[8,8]{1,0:T(8,128)} %margin.3) | copy-start | bytes 772
  1.1 4.9 %collective-permute-start = (f32[120,128]{1,0:T(8,128)S(1)}, f32[120,128]{1,0:T(8,128)S(1)}, u32[]{:S(2)}, u32[]{:S(2)}) collective-permute-start(f32[120,128]{1,0:T(8,128)S(1)} %get-tuple-element.22), channel_id=1, source_target_pairs={{0,1},{1,0},{2,3},{3,2},{4,5},{5,4},{6,7},{7,6},{8,9},{9,8},{10,11... | collective-permute-start | bytes 184328 | tf_op jit(solution)/shard_map/ppermute | solution.py:225
  1.7 7.0 %collective-permute-start.1 = (f32[120,128]{1,0:T(8,128)S(1)}, f32[120,128]{1,0:T(8,128)S(1)}, u32[]{:S(2)}, u32[]{:S(2)}) collective-permute-start(f32[120,128]{1,0:T(8,128)S(1)} %get-tuple-element.23), channel_id=1, source_target_pairs={{0,2},{1,3},{2,0},{3,1},{4,6},{5,7},{6,4},{7,5},{8,10},{9,11},{10,... | collective-permute-start | bytes 184328 | tf_op jit(solution)/shard_map/ppermute | solution.py:225
  4.2 11.8 %collective-permute-start.2 = (f32[120,128]{1,0:T(8,128)S(1)}, f32[120,128]{1,0:T(8,128)S(1)}, u32[]{:S(2)}, u32[]{:S(2)}) collective-permute-start(f32[120,128]{1,0:T(8,128)S(1)} %get-tuple-element.24), channel_id=1, source_target_pairs={{0,3},{1,2},{2,1},{3,0},{4,7},{5,6},{6,5},{7,4},{8,11},{9,10},{10,... | collective-permute-start | bytes 184328 | tf_op jit(solution)/shard_map/ppermute | solution.py:225
  4.3 11.8 %collective-permute-start.3 = (f32[120,128]{1,0:T(8,128)S(1)}, f32[120,128]{1,0:T(8,128)S(1)}, u32[]{:S(2)}, u32[]{:S(2)}) collective-permute-start(f32[120,128]{1,0:T(8,128)S(1)} %get-tuple-element.25), channel_id=1, source_target_pairs={{0,4},{1,5},{2,6},{3,7},{4,0},{5,1},{6,2},{7,3},{8,12},{9,13},{10,... | collective-permute-start | bytes 184328 | tf_op jit(solution)/shard_map/ppermute | solution.py:225
  6.1 10.0 %collective-permute-start.4 = (f32[120,128]{1,0:T(8,128)S(1)}, f32[120,128]{1,0:T(8,128)S(1)}, u32[]{:S(2)}, u32[]{:S(2)}) collective-permute-start(f32[120,128]{1,0:T(8,128)S(1)} %get-tuple-element.26), channel_id=1, source_target_pairs={{0,5},{1,4},{2,7},{3,6},{4,1},{5,0},{6,3},{7,2},{8,13},{9,12},{10,... | collective-permute-start | bytes 184328 | tf_op jit(solution)/shard_map/ppermute | solution.py:225
  6.1 10.0 %collective-permute-start.5 = (f32[120,128]{1,0:T(8,128)S(1)}, f32[120,128]{1,0:T(8,128)S(1)}, u32[]{:S(2)}, u32[]{:S(2)}) collective-permute-start(f32[120,128]{1,0:T(8,128)S(1)} %get-tuple-element.27), channel_id=1, source_target_pairs={{0,6},{1,7},{2,4},{3,5},{4,2},{5,3},{6,0},{7,1},{8,14},{9,15},{10,... | collective-permute-start | bytes 184328 | tf_op jit(solution)/shard_map/ppermute | solution.py:225
  8.7 7.4 %collective-permute-start.6 = (f32[120,128]{1,0:T(8,128)S(1)}, f32[120,128]{1,0:T(8,128)S(1)}, u32[]{:S(2)}, u32[]{:S(2)}) collective-permute-start(f32[120,128]{1,0:T(8,128)S(1)} %get-tuple-element.28), channel_id=1, source_target_pairs={{0,7},{1,6},{2,5},{3,4},{4,3},{5,2},{6,1},{7,0},{8,15},{9,14},{10,... | collective-permute-start | bytes 184328 | tf_op jit(solution)/shard_map/ppermute | solution.py:225
  19.7 16.7 %collective-permute-start.7 = (f32[64,128]{1,0:T(8,128)S(1)}, f32[64,128]{1,0:T(8,128)S(1)}, u32[]{:S(2)}, u32[]{:S(2)}) collective-permute-start(f32[64,128]{1,0:T(8,128)S(1)} %get-tuple-element.32), channel_id=1, source_target_pairs={{0,8},{8,0},{16,24},{24,16},{1,9},{9,1},{17,25},{25,17},{2,10},{10... | collective-permute-start | bytes 98312 | tf_op jit(solution)/shard_map/ppermute | solution.py:225
  21.5 14.9 %collective-permute-start.8 = (f32[64,128]{1,0:T(8,128)S(1)}, f32[64,128]{1,0:T(8,128)S(1)}, u32[]{:S(2)}, u32[]{:S(2)}) collective-permute-start(f32[64,128]{1,0:T(8,128)S(1)} %get-tuple-element.33), channel_id=1, source_target_pairs={{0,16},{8,24},{16,0},{24,8},{1,17},{9,25},{17,1},{25,9},{2,18},{10... | collective-permute-start | bytes 98312 | tf_op jit(solution)/shard_map/ppermute | solution.py:225
  24.1 12.3 %collective-permute-start.9 = (f32[64,128]{1,0:T(8,128)S(1)}, f32[64,128]{1,0:T(8,128)S(1)}, u32[]{:S(2)}, u32[]{:S(2)}) collective-permute-start(f32[64,128]{1,0:T(8,128)S(1)} %get-tuple-element.34), channel_id=1, source_target_pairs={{0,24},{8,16},{16,8},{24,0},{1,25},{9,17},{17,9},{25,1},{2,26},{10... | collective-permute-start | bytes 98312 | tf_op jit(solution)/shard_map/ppermute | solution.py:225

commit v6 on v5

v6 whole, which is shorter than its diff:
```python
import functools

import jax
import jax.numpy as jnp
from jax import lax
from jax.experimental import pallas as pl
from jax.experimental.pallas import tpu as pltpu
from jax.sharding import PartitionSpec as P

BLK = 128
MIB = 1024 * 1024
VMEM = pl.BlockSpec(memory_space=pltpu.VMEM)
SMEM = pl.BlockSpec(memory_space=pltpu.SMEM)
HBM = pl.BlockSpec(memory_space=pltpu.HBM)
NT = (((1,), (1,)), ((), ()))
TN = (((0,), (0,)), ((), ()))


def call(kernel, out, specs, scratch=(), limit=12 * MIB, flops=0, moved=0, **options):
    return pl.pallas_call(
        kernel,
        out_shape=out,
        in_specs=specs,
        out_specs=jax.tree.map(lambda _: VMEM, out),
        scratch_shapes=scratch,
        compiler_params=pltpu.CompilerParams(vmem_limit_bytes=limit),
        cost_estimate=pl.CostEstimate(flops=flops, bytes_accessed=moved, transcendentals=0),
        **options,
    )


def mm(left, right, dims=(((1,), (0,)), ((), ()))):
    return lax.dot_general(left, right, dims, preferred_element_type=jnp.float32)


def split3(value):
    high = value.astype(jnp.bfloat16)
    rest = value - high.astype(jnp.float32)
    middle = rest.astype(jnp.bfloat16)
    low = (rest - middle.astype(jnp.float32)).astype(jnp.bfloat16)
    return [high, middle, low]


def pack_kernel(own, rows, pad, margin_hbm, aggregate_hbm, residual_hbm, near_names, near, *refs):
    *outs, block_rows, margin, aggregate, residual, sems = refs
    pairs = ((residual_hbm, residual), (margin_hbm, margin), (aggregate_hbm, aggregate))
    copies = [pltpu.make_async_copy(a, b, sems.at[i]) for i, (a, b) in enumerate(pairs)]
    for copy in copies:
        copy.start()
    for copy in copies:
        copy.wait()
    halo = margin.shape[1]
    rhs = residual.shape[0]
    me = lax.axis_index("sub")
    first = lax.axis_index("grp") * rows
    size = own * rows
    mine = []
    for i, part in enumerate((residual, near)):
        for b in range(own):
            block_rows[i, pl.ds(b, rhs, stride=own), :] = part[:, b * BLK : (b + 1) * BLK]
        mine.append(block_rows[i, pl.ds(pl.multiple_of(first * own, 8), size), :])
    names = [aggregate[...].astype(jnp.float32), near_names[...].astype(jnp.float32)]
    at = 2 * size
    for e, out in enumerate(outs):
        out[at : at + pad, :] = jnp.zeros((pad, BLK), jnp.float32)
        for i in range(2):
            out[i * size : (i + 1) * size, :] = mine[i]
            out[at + i : at + i + 1, :own] = names[i]
        if e == 0:
            continue
        target = me ^ (2 * e)
        for k in range(halo):
            block = margin[target, k]
            owner = block // own
            where = pl.ds(pl.multiple_of((block - owner * own) * BLK, BLK), BLK)
            out[at + pad + k * rhs : at + pad + (k + 1) * rhs, :] = jnp.where(
                owner == me, residual[:, where], near[:, where]
            )


def panel_copies(source, target, chunk, sems, first=0):
    copies = []
    for n in range(target.shape[0] // chunk):
        span = pl.ds(first + n * chunk, chunk)
        copies.append(
            pltpu.make_async_copy(source.at[span], target.at[pl.ds(n * chunk, chunk)], sems.at[n])
        )
    return copies


def start(copies):
    for copy in copies:
        copy.start()


def first_product(factor, right, tile, copies=(), ahead=0):
    depth = factor.shape[0]
    each = len(copies) * tile // depth
    parts = []
    for n in range(depth // tile):
        for i in range(n * each, (n + 1) * each):
            copies[i].wait()
            if i + ahead < len(copies):
                copies[i + ahead].start()
        parts.append(mm(right, factor[n * tile : (n + 1) * tile, :], NT))
    return jnp.concatenate(parts, axis=1)


def load_kernel(chunk, tile, ahead, residual_hbm, fine_hbm, after, inner, fine, residual, sem, sems):
    own_width = residual.shape[1]
    first = pltpu.make_async_copy(residual_hbm, residual, sem)
    first.start()
    copies = panel_copies(fine_hbm.at[0], fine.at[0], chunk, sems)
    start(copies[:ahead])
    first.wait()
    local = residual[...].astype(jnp.bfloat16)
    inner[...] = first_product(fine.at[0, :, pl.ds(0, own_width)], local, tile, copies, ahead)


def fine_kernel(own, rows, begin, chunk, tile, pairs, margin, begun, factor, coarse_hbm, near, *refs):
    arrived = (None, *refs[: pairs - 1])
    *outs, coarse, table, sems = refs[pairs - 1 :]
    copies = panel_copies(coarse_hbm, coarse, chunk, sems)
    start(copies)
    rhs = begun.shape[0]
    halo = margin.shape[1]
    depth, width = factor.shape[1:]
    blocks = width // BLK
    me = lax.axis_index("sub")
    group = lax.axis_index("grp")
    tiles = []
    for k in range(halo):
        block = margin[me, k]
        owner = block // own
        away = (me ^ owner) // 2
        span = slice(begin + k * rhs, begin + (k + 1) * rhs)
        part = near[:, pl.ds(pl.multiple_of((block - owner * own) * BLK, BLK), BLK)]
        for e in range(1, pairs):
            part = jnp.where(away == e, arrived[e][span, :], part)
        tiles.append(part.astype(jnp.bfloat16))
    local = jnp.concatenate(tiles, axis=1)
    far = factor.at[0, :, pl.ds(own * BLK, halo * BLK)]
    mid = (begun[...] + first_product(far, local, tile)).astype(jnp.bfloat16)
    for n in range(width // 256):
        part = mm(mid, factor[0, :, n * 256 : (n + 1) * 256])
        for i in range(256 // BLK):
            b = n * (256 // BLK) + i
            table[pl.ds(b, rhs, stride=blocks), :] = part[:, i * BLK : (i + 1) * BLK]
    size = rows * blocks
    for d, out in enumerate(outs):
        out[...] = table[pl.ds(pl.multiple_of((group ^ d) * size, 8), size), :]
    for copy in copies:
        copy.wait()


def coarse_kernel(own, rows, chunk, tile, ahead, pairs, upper, factor_hbm, *refs):
    arrived = refs[:pairs]
    out, table, lower, sems = refs[pairs:]
    done = upper.shape[0]
    width = upper.shape[1]
    copies = panel_copies(factor_hbm, lower, chunk, sems, done)
    start(copies[:ahead])
    coarse = width // BLK
    size = own * rows
    sources = 2 * pairs
    parts = [(part, i) for part in arrived for i in range(2)]
    names = jnp.concatenate(
        [part[2 * size + i : 2 * size + i + 1, :] for part, i in parts], axis=0
    ).T
    catalog = lax.broadcasted_iota(jnp.int32, (own, coarse), 1).astype(jnp.float32)
    member = jnp.concatenate(
        [(names[:own, s : s + 1] == catalog).astype(jnp.float32) for s in range(sources)], axis=0
    ).astype(jnp.bfloat16)
    whole = jnp.concatenate(
        [
            jnp.concatenate(
                [part[i * size + r * own : i * size + (r + 1) * own, :] for part, i in parts],
                axis=0,
            )
            for r in range(rows)
        ],
        axis=1,
    )
    ones = jnp.ones((own * sources, BLK), jnp.bfloat16)
    span = rows * BLK
    found = mm(member, jnp.concatenate(split3(whole) + [ones], axis=1), TN)
    sums = found[:, :span] + found[:, span : 2 * span] + found[:, 2 * span : 3 * span]
    counts = jnp.maximum(found[:, 3 * span :], 1.0)
    for r in range(rows):
        table[r * coarse : (r + 1) * coarse, :] = sums[:, r * BLK : (r + 1) * BLK] / counts
    right = jnp.concatenate(
        [table[pl.ds(j, rows, stride=coarse), :] for j in range(coarse)], axis=1
    ).astype(jnp.bfloat16)
    high = first_product(upper, right, tile).astype(jnp.bfloat16)
    low = first_product(lower, right, tile, copies, ahead).astype(jnp.bfloat16)
    for n in range(width // 256):
        where = slice(n * 256, (n + 1) * 256)
        part = mm(high, upper[:, where]) + mm(low, lower[:, where])
        for i in range(256 // BLK):
            j = n * (256 // BLK) + i
            table[pl.ds(j, rows, stride=coarse), :] = part[:, i * BLK : (i + 1) * BLK]
    solved = jnp.concatenate([table[r * coarse : (r + 1) * coarse, :] for r in range(rows)], axis=1)
    spread = mm(member, jnp.concatenate(split3(solved), axis=1))
    spread = spread[:, :span] + spread[:, span : 2 * span] + spread[:, 2 * span :]
    for s in range(sources):
        for r in range(rows):
            out[s, r * own : (r + 1) * own, :] = spread[
                s * own : (s + 1) * own, r * BLK : (r + 1) * BLK
            ]


def merge_kernel(own, rows, groups, margin, spread, *refs):
    arrived = refs[:groups]
    kept, near, total, field = refs[groups:]
    halo = margin.shape[1]
    blocks = own + halo
    me = lax.axis_index("sub")
    summed = arrived[0][...]
    for part in arrived[1:]:
        summed = summed + part[...]
    total[...] = summed
    field[...] = spread[...]
    for r in range(rows):
        span = slice(r * own, (r + 1) * own)
        field[0, span, :] = field[0, span, :] + total[r * blocks : r * blocks + own, :]
    for k in range(halo):
        block = margin[me, k]
        owner = block // own
        where = pl.ds(block - owner * own, rows, stride=own)
        away = me ^ owner
        field[away, where, :] = field[away, where, :] + total[pl.ds(own + k, rows, stride=blocks), :]
    for e in range(kept.shape[0]):
        kept[e] = field[2 * e]
        near[e] = field[2 * e + 1]


def add_kernel(kept, arrived, *outs):
    for e, out in enumerate(outs):
        out[...] = kept[e] + arrived[e]


def last_kernel(own, rows, *refs):
    *arrived, out, total = refs
    summed = arrived[0][...]
    for part in arrived[1:]:
        summed = summed + part[...]
    total[...] = summed
    for b in range(own):
        out[:, b * BLK : (b + 1) * BLK] = total[pl.ds(b, rows, stride=own), :]


def swap(value, axis, distance):
    count = lax.axis_size(axis)
    return lax.ppermute(value, axis, [(i, i ^ distance) for i in range(count)])


def exchange(parts, axis, unit=1):
    return [parts[0]] + [swap(part, axis, d * unit) for d, part in enumerate(parts) if d > 0]


def on_device(residual, margin, aggregate, local_factor, coarse_factor):
    pairs = lax.axis_size("sub") // 2
    grp_count = lax.axis_size("grp")
    rhs, own_width = residual.shape
    own = own_width // BLK
    rows = rhs // grp_count
    halo = margin.shape[1]
    pad = 8
    begin = 2 * own * rows + pad
    f32 = jnp.float32
    sds = jax.ShapeDtypeStruct
    _, depth, width = local_factor.shape
    coarse_depth, coarse_width = coarse_factor.shape
    blocks = width // BLK
    in_hbm = functools.partial(pltpu.with_memory_space_constraint, memory_space=pltpu.HBM)
    aggregate = aggregate.reshape(1, own)
    local_factor = in_hbm(local_factor)
    coarse_factor = in_hbm(coarse_factor)

    near = swap(residual, "sub", 1)
    near_names = swap(aggregate, "sub", 1)
    outgoing = call(
        functools.partial(pack_kernel, own, rows, pad),
        [sds((begin, BLK), f32)] + [sds((begin + halo * rhs, BLK), f32)] * (pairs - 1),
        [HBM, HBM, HBM, VMEM, VMEM],
        [
            pltpu.VMEM((2, own * rhs, BLK), f32),
            pltpu.SMEM(margin.shape, jnp.int32),
            pltpu.VMEM((1, own), jnp.int32),
            pltpu.VMEM(residual.shape, f32),
            pltpu.SemaphoreType.DMA((3,)),
        ],
    )(in_hbm(margin), in_hbm(aggregate), in_hbm(residual), near_names, near)
    arrived = exchange(outgoing, "sub", 2)
    tile = min(256, coarse_depth // 2, depth // 2)
    chunk = tile // 4
    ahead = 2 * tile // chunk
    begun, local_factor = call(
        functools.partial(load_kernel, chunk, tile, ahead),
        (sds((rhs, depth), f32), sds(local_factor.shape, local_factor.dtype)),
        [HBM, HBM, pl.BlockSpec(memory_space=pl.ANY)],
        [
            pltpu.VMEM(residual.shape, f32),
            pltpu.SemaphoreType.DMA,
            pltpu.SemaphoreType.DMA((depth // chunk,)),
        ],
        flops=2 * rhs * depth * own_width,
        moved=2 * depth * width,
    )(in_hbm(residual), local_factor, arrived[0])
    chunk = tile // 8
    ahead = tile // chunk
    upper, lower = tile, coarse_depth - tile
    *fine, coarse_upper = call(
        functools.partial(fine_kernel, own, rows, begin, chunk, tile, pairs),
        [sds((rows * blocks, BLK), f32)] * grp_count
        + [sds((upper, coarse_width), coarse_factor.dtype)],
        [SMEM, VMEM, VMEM, HBM, VMEM] + [VMEM] * (pairs - 1),
        [pltpu.VMEM((rhs * blocks, BLK), f32), pltpu.SemaphoreType.DMA((upper // chunk,))],
        flops=4 * rhs * depth * width,
        moved=2 * depth * width + 2 * upper * coarse_width,
    )(margin, begun, local_factor, coarse_factor, near, *arrived[1:])
    panels = exchange(fine, "grp")
    spread = call(
        functools.partial(coarse_kernel, own, rows, chunk, tile, ahead, pairs),
        sds((2 * pairs, own * rows, BLK), f32),
        [VMEM, HBM] + [VMEM] * pairs,
        [
            pltpu.VMEM((rows * (coarse_width // BLK), BLK), f32),
            pltpu.VMEM((lower, coarse_width), coarse_factor.dtype),
            pltpu.SemaphoreType.DMA((lower // chunk,)),
        ],
        flops=4 * rows * coarse_depth * coarse_width,
        moved=2 * coarse_depth * coarse_width,
        limit=24 * MIB,
    )(coarse_upper, coarse_factor, *arrived)
    field = sds((pairs, own * rows, BLK), f32)
    kept, crossing = call(
        functools.partial(merge_kernel, own, rows, grp_count),
        [field, field],
        [SMEM] + [VMEM] * (1 + grp_count),
        [
            pltpu.VMEM((rows * blocks, BLK), f32),
            pltpu.VMEM((2 * pairs, own * rows, BLK), f32),
        ],
    )(margin, spread, *panels)
    back = call(add_kernel, [sds((own * rows, BLK), f32)] * pairs, [VMEM, VMEM])(
        kept, swap(crossing, "sub", 1)
    )
    return call(
        functools.partial(last_kernel, own, rows),
        sds((rows, own_width), f32),
        [VMEM] * pairs,
        [pltpu.VMEM((own * rows, BLK), f32)],
    )(*exchange(back, "sub", 2))


def solution(mesh):
    placed = (P(None, "sub"), P(), P("sub"), P("sub", "grp", None), P("sub", None))
    return jax.shard_map(
        on_device, mesh=mesh, in_specs=placed, out_specs=P("grp", "sub"), check_vma=False
    )
```

time: 47.8 us -> 45.2 us (0.946)
  blocking collectives: 9.88 us -> 0 us
  waiting for transfers between devices: 0.03 us -> 6.96 us
  starting transfers between devices: 12.1 us -> 13.2 us
  Pallas kernels: 25.5 us -> 24.8 us
    all_to_all x1 -> x0, blocking collectives: 9.88 us -> none  [on_device(): lax.all_to_all(merged, 'sub', split_axis=0, concat_axis=0, tiled=True)]
    ppermute x10 -> x12, waiting for transfers between devices: 0.03 us -> 6.96 us  [swap(): return lax.ppermute(value, axis, [(i, i ^ distance) for i in range(count)])]
    ppermute x10 -> x12, starting transfers between devices: 12.1 us -> 13.2 us  [swap(): return lax.ppermute(value, axis, [(i, i ^ distance) for i in range(count)])]
    pallas_call x5 -> x6, Pallas kernels: 24.8 us -> 24.2 us  [the longest x1 12.1 us: on_device(): call(functools.partial(coarse_kernel, own, rows, chunk, tile, ahead, pair...]
  transfers between devices with their start and end apart: 10 -> 12, of which waited for: 0 -> 5; matrix products, arithmetic and copies ran while one was open for 0% -> 0% of each run, Pallas kernels for 41% -> 40%
where the time goes in v6:
time: 45.2 us; the launch traced here: 45 us
  Pallas kernels  24.8 us (55%)
  starting transfers between devices  13.2 us (29%)
  waiting for transfers between devices  6.96 us (15%)
    ppermute x12, starting transfers between devices, swap(): return lax.ppermute(value, axis, [(i, i ^ distance) for i in range(count)])  13.2 us
    pallas_call x1, Pallas kernels, on_device(): call(functools.partial(coarse_kernel, own, rows, chunk, tile, ahead, pair...  12.1 us
    ppermute x12, waiting for transfers between devices, swap(): return lax.ppermute(value, axis, [(i, i ^ distance) for i in range(count)])  6.96 us
    pallas_call x1, Pallas kernels, on_device(): call(functools.partial(load_kernel, chunk, tile, ahead), (sds((rhs, depth...  5.88 us
    pallas_call x1, Pallas kernels, on_device(): call(functools.partial(fine_kernel, own, rows, begin, chunk, tile, pairs)...  4.3 us
    pallas_call x1, Pallas kernels, on_device(): call(functools.partial(pack_kernel, own, rows, pad), [sds((begin, BLK), f...  1.15 us
  transfers between devices with their start and end apart: 12, of which 5 were waited for; matrix products, arithmetic and copies ran while one was open for 0% of the time, Pallas kernels for 40%

profile of v6, /device:TPU:0, one launch (start us, length us, event | category | flops | bytes accessed | tf_op | source)
XLA Modules:
  0.0 45.0 jit_solution(5202258348477611294)
XLA Ops:
  0.0 0.0 copy-start
  0.0 0.5 %collective-permute-start.1 = (f32[8,3072]{1,0:T(8,128)}, f32[8,3072]{1,0:T(8,128)S(1)}, u32[]{:S(2)}, u32[]{:S(2)}) collective-permute-start(f32[8,3072]{1,0:T(8,128)} %residual_hbm.3), channel_id=1, source_target_pairs={{0,1},{1,0},{2,3},{3,2},{4,5},{5,4},{6,7},{7,6},{8,9},{9,8},{10,11... | collective-permute-start | bytes 294920 | tf_op jit(solution)/shard_map/ppermute | solution.py:254
  0.5 0.1 collective-permute-start
  0.5 1.2 %collective-permute-done.near_names = s32[1,24]{1,0:T(1,128)S(1)} collective-permute-done((s32[1,24]{1,0:T(1,128)}, s32[1,24]{1,0:T(1,128)S(1)}, u32[]{:S(2)}, u32[]{:S(2)}) %collective-permute-start) | collective-permute-done | bytes 128 | tf_op jit(solution)/shard_map/ppermute | solution.py:254
  1.7 0.0 collective-permute-done.1.near
  1.7 1.2 %shard_map.55 = (f32[104,128]{1,0:T(8,128)S(1)}, f32[168,128]{1,0:T(8,128)S(1)}, f32[168,128]{1,0:T(8,128)S(1)}, f32[168,128]{1,0:T(8,128)S(1)}) custom-call(s32[8,8]{1,0:T(8,128)} %margin.3, s32[1,24]{1,0:T(1,128)} %bitcast.2, f32[8,3072]{1,0:T(8,128)} %residual_hbm.3, s32[1,24]{1,0:T(1,128)S(1)} %collective-permute-done.near_names, ...), custom_call_target="tpu_custom_call" | custom-call | tf_op jit(solution)/shard_map/pallas_call | solution.py:282
  2.9 2.8 %collective-permute-start.2 = (f32[168,128]{1,0:T(8,128)S(1)}, f32[168,128]{1,0:T(8,128)S(1)}, u32[]{:S(2)}, u32[]{:S(2)}) collective-permute-start(f32[168,128]{1,0:T(8,128)S(1)} %get-tuple-element.25), channel_id=1, source_target_pairs={{0,2},{1,3},{2,0},{3,1},{4,6},{5,7},{6,4},{7,5},{8,10},{9,11},{10,... | collective-permute-start | bytes 258056 | tf_op jit(solution)/shard_map/ppermute | solution.py:254
  5.7 1.5 %collective-permute-start.3 = (f32[168,128]{1,0:T(8,128)S(1)}, f32[168,128]{1,0:T(8,128)S(1)}, u32[]{:S(2)}, u32[]{:S(2)}) collective-permute-start(f32[168,128]{1,0:T(8,128)S(1)} %get-tuple-element.26), channel_id=1, source_target_pairs={{0,4},{1,5},{2,6},{3,7},{4,0},{5,1},{6,2},{7,3},{8,12},{9,13},{10,... | collective-permute-start | bytes 258056 | tf_op jit(solution)/shard_map/ppermute | solution.py:254
  7.2 0.0 collective-permute-start.4
  7.2 5.9 %shard_map.56 = (f32[8,1024]{1,0:T(8,128)S(1)}, bf16[1,1024,4096]{2,1,0:T(8,128)(2,1)S(1)}) custom-call(f32[8,3072]{1,0:T(8,128)} %residual_hbm.3, bf16[1,1024,4096]{2,1,0:T(8,128)(2,1)} %fine_hbm.1, f32[104,128]{1,0:T(8,128)S(1)} %get-tuple-element.22.after.refs_0_), custom_call_target="tpu_custom_call" | custom-call | flops 50331648 | bytes 8388608 | tf_op jit(solution)/shard_map/pallas_call | solution.py:298
  13.1 0.0 collective-permute-done.2.refs_0_.refs_1_
  13.1 0.0 collective-permute-done.3.refs_1_.refs_2_
  13.1 0.0 collective-permute-done.4.refs_2_.refs_3_
  13.1 0.0 copy-done
  13.2 4.3 %shard_map.57 = (f32[64,128]{1,0:T(8,128)S(1)}, f32[64,128]{1,0:T(8,128)S(1)}, f32[64,128]{1,0:T(8,128)S(1)}, f32[64,128]{1,0:T(8,128)S(1)}, bf16[256,8192]{1,0:T(8,128)(2,1)S(1)}) custom-call(s32[8,8]{1,0:T(8,128)S(1)} %copy-done, f32[8,1024]{1,0:T(8,128)S(1)} %get-tuple-element.23.begun, bf16[1,1024,4096]{2,1,0:T(8,128)(2,1)S(1)} %get-tuple-element.24.factor, ...), custom_call_target="tpu_custom_call" | custom-call | flops 134217728 | bytes 12582912 | tf_op jit(solution)/shard_map/pallas_call | solution.py:313
  17.5 2.1 %collective-permute-start.5 = (f32[64,128]{1,0:T(8,128)S(1)}, f32[64,128]{1,0:T(8,128)S(1)}, u32[]{:S(2)}, u32[]{:S(2)}) collective-permute-start(f32[64,128]{1,0:T(8,128)S(1)} %get-tuple-element.30), channel_id=1, source_target_pairs={{0,8},{8,0},{16,24},{24,16},{1,9},{9,1},{17,25},{25,17},{2,10},{10... | collective-permute-start | bytes 98312 | tf_op jit(solution)/shard_map/ppermute | solution.py:254
  19.6 2.6 %collective-permute-start.6 = (f32[64,128]{1,0:T(8,128)S(1)}, f32[64,128]{1,0:T(8,128)S(1)}, u32[]{:S(2)}, u32[]{:S(2)}) collective-permute-start(f32[64,128]{1,0:T(8,128)S(1)} %get-tuple-element.31), channel_id=1, source_target_pairs={{0,16},{8,24},{16,0},{24,8},{1,17},{9,25},{17,1},{25,9},{2,18},{10... | collective-permute-start | bytes 98312 | tf_op jit(solution)/shard_map/ppermute | solution.py:254
  22.2 0.0 collective-permute-start.7
  22.2 12.1 %shard_map.58.spread = f32[8,48,128]{2,1,0:T(8,128)S(1)} custom-call(bf16[256,8192]{1,0:T(8,128)(2,1)S(1)} %get-tuple-element.28.upper, bf16[1024,8192]{1,0:T(8,128)(2,1)} %factor_hbm.1, f32[104,128]{1,0:T(8,128)S(1)} %get-tuple-element.22.after.refs_0_, f32[168,128]{1,0:T(8,128)S(1)} %collective-permute-done.2.refs_0_.refs_1_, ...), custom_call_target="tpu_custom_call" | custom-call | flops 67108864 | bytes 16777216 | tf_op jit(solution)/shard_map/pallas_call | solution.py:323
  34.3 0.0 collective-permute-done.5.refs_1_
  34.3 0.0 collective-permute-done.6.refs_2_
  34.3 0.0 collective-permute-done.7.refs_3_
  34.3 0.7 %shard_map.59 = (f32[4,48,128]{2,1,0:T(8,128)S(1)}, f32[4,48,128]{2,1,0:T(8,128)S(1)}) custom-call(s32[8,8]{1,0:T(8,128)S(1)} %copy-done, f32[8,48,128]{2,1,0:T(8,128)S(1)} %shard_map.58.spread, f32[64,128]{1,0:T(8,128)S(1)} %get-tuple-element.29.refs_0_, f32[64,128]{1,0:T(8,128)S(1)} %collective-permute-done.5.refs_1_, ...), custom_call_target="tpu_custom_call" | custom-call | tf_op jit(solution)/shard_map/pallas_call | solution.py:337
  35.0 0.1 collective-permute-start.8
  35.1 1.3 %collective-permute-done.8.arrived = f32[4,48,128]{2,1,0:T(8,128)S(1)} collective-permute-done((f32[4,48,128]{2,1,0:T(8,128)S(1)}, f32[4,48,128]{2,1,0:T(8,128)S(1)}, u32[]{:S(2)}, u32[]{:S(2)}) %collective-permute-start.8) | collective-permute-done | bytes 98336 | tf_op jit(solution)/shard_map/ppermute | solution.py:254
  36.4 1.8 %collective-permute-start.9 = (f32[48,128]{1,0:T(8,128)S(1)}, f32[48,128]{1,0:T(8,128)S(1)}, u32[]{:S(2)}, u32[]{:S(2)}) collective-permute-start(f32[48,128]{1,0:T(8,128)S(1)} %get-tuple-element.36), channel_id=1, source_target_pairs={{0,2},{1,3},{2,0},{3,1},{4,6},{5,7},{6,4},{7,5},{8,10},{9,11},{10,... | collective-permute-start | bytes 73736 | tf_op jit(solution)/shard_map/ppermute | solution.py:254
  38.2 1.5 %collective-permute-start.10 = (f32[48,128]{1,0:T(8,128)S(1)}, f32[48,128]{1,0:T(8,128)S(1)}, u32[]{:S(2)}, u32[]{:S(2)}) collective-permute-start(f32[48,128]{1,0:T(8,128)S(1)} %get-tuple-element.37), channel_id=1, source_target_pairs={{0,4},{1,5},{2,6},{3,7},{4,0},{5,1},{6,2},{7,3},{8,12},{9,13},{10,... | collective-permute-start | bytes 73736 | tf_op jit(solution)/shard_map/ppermute | solution.py:254
  39.7 0.3 collective-permute-start.11
  40.0 0.3 collective-permute-done.9.refs_1_
  40.3 1.7 %collective-permute-done.10.refs_2_ = f32[48,128]{1,0:T(8,128)S(1)} collective-permute-done((f32[48,128]{1,0:T(8,128)S(1)}, f32[48,128]{1,0:T(8,128)S(1)}, u32[]{:S(2)}, u32[]{:S(2)}) %collective-permute-start.10) | collective-permute-done | bytes 24608 | tf_op jit(solution)/shard_map/ppermute | solution.py:254
  42.0 2.4 %collective-permute-done.11.refs_3_ = f32[48,128]{1,0:T(8,128)S(1)} collective-permute-done((f32[48,128]{1,0:T(8,128)S(1)}, f32[48,128]{1,0:T(8,128)S(1)}, u32[]{:S(2)}, u32[]{:S(2)}) %collective-permute-start.11) | collective-permute-done | bytes 24608 | tf_op jit(solution)/shard_map/ppermute | solution.py:254
  44.4 0.6 %shard_map.61 = f32[2,3072]{1,0:T(2,128)} custom-call(f32[48,128]{1,0:T(8,128)S(1)} %get-tuple-element.35.refs_0_, f32[48,128]{1,0:T(8,128)S(1)} %collective-permute-done.9.refs_1_, f32[48,128]{1,0:T(8,128)S(1)} %collective-permute-done.10.refs_2_, f32[48,128]{1,0:T(8,128)S(1)} %collective-permute-done.11.refs_3_), custom_call_target="tpu_custom_call" | custom-call | tf_op jit(solution)/shard_map/pallas_call | solution.py:349
  (1 shorter events, 0.0 us)
Async XLA Ops:
  0.0 13.1 %copy-start = (s32[8,8]{1,0:T(8,128)S(1)}, s32[8,8]{1,0:T(8,128)}, u32[]{:S(2)}) copy-start(s32[8,8]{1,0:T(8,128)} %margin.3) | copy-start | bytes 772
  0.0 1.7 %collective-permute-start.1 = (f32[8,3072]{1,0:T(8,128)}, f32[8,3072]{1,0:T(8,128)S(1)}, u32[]{:S(2)}, u32[]{:S(2)}) collective-permute-start(f32[8,3072]{1,0:T(8,128)} %residual_hbm.3), channel_id=1, source_target_pairs={{0,1},{1,0},{2,3},{3,2},{4,5},{5,4},{6,7},{7,6},{8,9},{9,8},{10,11... | collective-permute-start | bytes 294920 | tf_op jit(solution)/shard_map/ppermute | solution.py:254
  0.5 1.3 %collective-permute-start = (s32[1,24]{1,0:T(1,128)}, s32[1,24]{1,0:T(1,128)S(1)}, u32[]{:S(2)}, u32[]{:S(2)}) collective-permute-start(s32[1,24]{1,0:T(1,128)} %bitcast.1), channel_id=1, source_target_pairs={{0,1},{1,0},{2,3},{3,2},{4,5},{5,4},{6,7},{7,6},{8,9},{9,8},{10,11... | collective-permute-start | bytes 296 | tf_op jit(solution)/shard_map/ppermute | solution.py:254
  2.9 10.2 %collective-permute-start.2 = (f32[168,128]{1,0:T(8,128)S(1)}, f32[168,128]{1,0:T(8,128)S(1)}, u32[]{:S(2)}, u32[]{:S(2)}) collective-permute-start(f32[168,128]{1,0:T(8,128)S(1)} %get-tuple-element.25), channel_id=1, source_target_pairs={{0,2},{1,3},{2,0},{3,1},{4,6},{5,7},{6,4},{7,5},{8,10},{9,11},{10,... | collective-permute-start | bytes 258056 | tf_op jit(solution)/shard_map/ppermute | solution.py:254
  5.7 7.4 %collective-permute-start.3 = (f32[168,128]{1,0:T(8,128)S(1)}, f32[168,128]{1,0:T(8,128)S(1)}, u32[]{:S(2)}, u32[]{:S(2)}) collective-permute-start(f32[168,128]{1,0:T(8,128)S(1)} %get-tuple-element.26), channel_id=1, source_target_pairs={{0,4},{1,5},{2,6},{3,7},{4,0},{5,1},{6,2},{7,3},{8,12},{9,13},{10,... | collective-permute-start | bytes 258056 | tf_op jit(solution)/shard_map/ppermute | solution.py:254
  7.2 5.9 %collective-permute-start.4 = (f32[168,128]{1,0:T(8,128)S(1)}, f32[168,128]{1,0:T(8,128)S(1)}, u32[]{:S(2)}, u32[]{:S(2)}) collective-permute-start(f32[168,128]{1,0:T(8,128)S(1)} %get-tuple-element.27), channel_id=1, source_target_pairs={{0,6},{1,7},{2,4},{3,5},{4,2},{5,3},{6,0},{7,1},{8,14},{9,15},{10,... | collective-permute-start | bytes 258056 | tf_op jit(solution)/shard_map/ppermute | solution.py:254
  17.5 16.8 %collective-permute-start.5 = (f32[64,128]{1,0:T(8,128)S(1)}, f32[64,128]{1,0:T(8,128)S(1)}, u32[]{:S(2)}, u32[]{:S(2)}) collective-permute-start(f32[64,128]{1,0:T(8,128)S(1)} %get-tuple-element.30), channel_id=1, source_target_pairs={{0,8},{8,0},{16,24},{24,16},{1,9},{9,1},{17,25},{25,17},{2,10},{10... | collective-permute-start | bytes 98312 | tf_op jit(solution)/shard_map/ppermute | solution.py:254
  19.6 14.7 %collective-permute-start.6 = (f32[64,128]{1,0:T(8,128)S(1)}, f32[64,128]{1,0:T(8,128)S(1)}, u32[]{:S(2)}, u32[]{:S(2)}) collective-permute-start(f32[64,128]{1,0:T(8,128)S(1)} %get-tuple-element.31), channel_id=1, source_target_pairs={{0,16},{8,24},{16,0},{24,8},{1,17},{9,25},{17,1},{25,9},{2,18},{10... | collective-permute-start | bytes 98312 | tf_op jit(solution)/shard_map/ppermute | solution.py:254
  22.2 12.2 %collective-permute-start.7 = (f32[64,128]{1,0:T(8,128)S(1)}, f32[64,128]{1,0:T(8,128)S(1)}, u32[]{:S(2)}, u32[]{:S(2)}) collective-permute-start(f32[64,128]{1,0:T(8,128)S(1)} %get-tuple-element.32), channel_id=1, source_target_pairs={{0,24},{8,16},{16,8},{24,0},{1,25},{9,17},{17,9},{25,1},{2,26},{10... | collective-permute-start | bytes 98312 | tf_op jit(solution)/shard_map/ppermute | solution.py:254
  35.0 1.4 %collective-permute-start.8 = (f32[4,48,128]{2,1,0:T(8,128)S(1)}, f32[4,48,128]{2,1,0:T(8,128)S(1)}, u32[]{:S(2)}, u32[]{:S(2)}) collective-permute-start(f32[4,48,128]{2,1,0:T(8,128)S(1)} %get-tuple-element.34), channel_id=1, source_target_pairs={{0,1},{1,0},{2,3},{3,2},{4,5},{5,4},{6,7},{7,6},{8,9},{9,8},{10,11... | collective-permute-start | bytes 294920 | tf_op jit(solution)/shard_map/ppermute | solution.py:254
  36.4 3.9 %collective-permute-start.9 = (f32[48,128]{1,0:T(8,128)S(1)}, f32[48,128]{1,0:T(8,128)S(1)}, u32[]{:S(2)}, u32[]{:S(2)}) collective-permute-start(f32[48,128]{1,0:T(8,128)S(1)} %get-tuple-element.36), channel_id=1, source_target_pairs={{0,2},{1,3},{2,0},{3,1},{4,6},{5,7},{6,4},{7,5},{8,10},{9,11},{10,... | collective-permute-start | bytes 73736 | tf_op jit(solution)/shard_map/ppermute | solution.py:254
  38.2 3.8 %collective-permute-start.10 = (f32[48,128]{1,0:T(8,128)S(1)}, f32[48,128]{1,0:T(8,128)S(1)}, u32[]{:S(2)}, u32[]{:S(2)}) collective-permute-start(f32[48,128]{1,0:T(8,128)S(1)} %get-tuple-element.37), channel_id=1, source_target_pairs={{0,4},{1,5},{2,6},{3,7},{4,0},{5,1},{6,2},{7,3},{8,12},{9,13},{10,... | collective-permute-start | bytes 73736 | tf_op jit(solution)/shard_map/ppermute | solution.py:254
  39.7 4.7 %collective-permute-start.11 = (f32[48,128]{1,0:T(8,128)S(1)}, f32[48,128]{1,0:T(8,128)S(1)}, u32[]{:S(2)}, u32[]{:S(2)}) collective-permute-start(f32[48,128]{1,0:T(8,128)S(1)} %get-tuple-element.38), channel_id=1, source_target_pairs={{0,6},{1,7},{2,4},{3,5},{4,2},{5,3},{6,0},{7,1},{8,14},{9,15},{10,... | collective-permute-start | bytes 73736 | tf_op jit(solution)/shard_map/ppermute | solution.py:254

commit v7 on v6

--- a/solution.py
+++ b/solution.py
@@ -93,34 +93,52 @@
         copy.start()
 
 
-def first_product(factor, right, tile, copies=(), ahead=0):
-    depth = factor.shape[0]
-    each = len(copies) * tile // depth
-    parts = []
-    for n in range(depth // tile):
-        for i in range(n * each, (n + 1) * each):
-            copies[i].wait()
-            if i + ahead < len(copies):
-                copies[i + ahead].start()
-        parts.append(mm(right, factor[n * tile : (n + 1) * tile, :], NT))
+def first_product(factor, right, tile):
+    parts = [
+        mm(right, factor[n * tile : (n + 1) * tile, :], NT) for n in range(factor.shape[0] // tile)
+    ]
     return jnp.concatenate(parts, axis=1)
 
 
-def load_kernel(chunk, tile, ahead, residual_hbm, fine_hbm, after, inner, fine, residual, sem, sems):
+def in_own_block(body):
+    pl.when(lax.axis_index("sub") >= 0)(body)
+
+
+def load_kernel(
+    chunk, tile, residual_hbm, fine_hbm, coarse_hbm, after, inner, fine, coarse, residual, sem, sems, more
+):
+    depth = fine.shape[1]
     own_width = residual.shape[1]
+    half = depth // 2
+    each = half // chunk
     first = pltpu.make_async_copy(residual_hbm, residual, sem)
     first.start()
-    copies = panel_copies(fine_hbm.at[0], fine.at[0], chunk, sems)
-    start(copies[:ahead])
+    start(panel_copies(fine_hbm.at[0], fine.at[0], chunk, sems))
+    late = panel_copies(coarse_hbm, coarse, coarse.shape[0] // 4, more)
     first.wait()
-    local = residual[...].astype(jnp.bfloat16)
-    inner[...] = first_product(fine.at[0, :, pl.ds(0, own_width)], local, tile, copies, ahead)
+
+    def step(n, carry):
+        for i in range(each):
+            span = pl.ds(pl.multiple_of(n * half + i * chunk, chunk), chunk)
+            pltpu.make_async_copy(fine_hbm.at[0, span], fine.at[0, span], sems.at[n * each + i]).wait()
+        pl.when(n == 0)(lambda: start(late))
+        local = residual[...].astype(jnp.bfloat16)
+        for i in range(half // tile):
+            at = pl.multiple_of(n * half + i * tile, tile)
+            rows = fine[0, pl.ds(at, tile), pl.ds(0, own_width)]
+            inner[:, pl.ds(at, tile)] = mm(local, rows, NT)
+        return carry
+
+    lax.fori_loop(0, 2, step, 0)
+    for copy in late:
+        copy.wait()
 
 
 def fine_kernel(own, rows, begin, chunk, tile, pairs, margin, begun, factor, coarse_hbm, near, *refs):
     arrived = (None, *refs[: pairs - 1])
     *outs, coarse, table, sems = refs[pairs - 1 :]
-    copies = panel_copies(coarse_hbm, coarse, chunk, sems)
+    done = coarse_hbm.shape[0] // 4
+    copies = panel_copies(coarse_hbm, coarse, chunk, sems, done)
     start(copies)
     rhs = begun.shape[0]
     halo = margin.shape[1]
@@ -149,17 +167,20 @@
     size = rows * blocks
     for d, out in enumerate(outs):
         out[...] = table[pl.ds(pl.multiple_of((group ^ d) * size, 8), size), :]
-    for copy in copies:
-        copy.wait()
-
-
-def coarse_kernel(own, rows, chunk, tile, ahead, pairs, upper, factor_hbm, *refs):
+
+    @in_own_block
+    def _():
+        for copy in copies:
+            copy.wait()
+
+
+def coarse_kernel(own, rows, chunk, tile, pairs, upper, middle, factor_hbm, *refs):
     arrived = refs[:pairs]
-    out, table, lower, sems = refs[pairs:]
-    done = upper.shape[0]
+    out, table, lower, begun, field, sems = refs[pairs:]
+    done = upper.shape[0] + middle.shape[0]
     width = upper.shape[1]
     copies = panel_copies(factor_hbm, lower, chunk, sems, done)
-    start(copies[:ahead])
+    start(copies)
     coarse = width // BLK
     size = own * rows
     sources = 2 * pairs
@@ -191,22 +212,36 @@
     right = jnp.concatenate(
         [table[pl.ds(j, rows, stride=coarse), :] for j in range(coarse)], axis=1
     ).astype(jnp.bfloat16)
-    high = first_product(upper, right, tile).astype(jnp.bfloat16)
-    low = first_product(lower, right, tile, copies, ahead).astype(jnp.bfloat16)
-    for n in range(width // 256):
-        where = slice(n * 256, (n + 1) * 256)
-        part = mm(high, upper[:, where]) + mm(low, lower[:, where])
-        for i in range(256 // BLK):
-            j = n * (256 // BLK) + i
-            table[pl.ds(j, rows, stride=coarse), :] = part[:, i * BLK : (i + 1) * BLK]
-    solved = jnp.concatenate([table[r * coarse : (r + 1) * coarse, :] for r in range(rows)], axis=1)
-    spread = mm(member, jnp.concatenate(split3(solved), axis=1))
-    spread = spread[:, :span] + spread[:, span : 2 * span] + spread[:, 2 * span :]
-    for s in range(sources):
-        for r in range(rows):
-            out[s, r * own : (r + 1) * own, :] = spread[
-                s * own : (s + 1) * own, r * BLK : (r + 1) * BLK
-            ]
+    field[...] = member.astype(jnp.float32)
+    begun[:, : upper.shape[0]] = first_product(upper, right, tile)
+    begun[:, upper.shape[0] : done] = first_product(middle, right, tile)
+
+    @in_own_block
+    def _():
+        for copy in copies:
+            copy.wait()
+        right = jnp.concatenate(
+            [table[pl.ds(j, rows, stride=coarse), :] for j in range(coarse)], axis=1
+        ).astype(jnp.bfloat16)
+        low = first_product(lower, right, tile).astype(jnp.bfloat16)
+        mid = begun[...].astype(jnp.bfloat16)
+        high = mid[:, : upper.shape[0]]
+        mid = mid[:, upper.shape[0] :]
+        for n in range(width // 256):
+            where = slice(n * 256, (n + 1) * 256)
+            part = mm(high, upper[:, where]) + mm(mid, middle[:, where]) + mm(low, lower[:, where])
+            for i in range(256 // BLK):
+                j = n * (256 // BLK) + i
+                table[pl.ds(j, rows, stride=coarse), :] = part[:, i * BLK : (i + 1) * BLK]
+        member = field[...].astype(jnp.bfloat16)
+        solved = jnp.concatenate([table[r * coarse : (r + 1) * coarse, :] for r in range(rows)], axis=1)
+        spread = mm(member, jnp.concatenate(split3(solved), axis=1))
+        spread = spread[:, :span] + spread[:, span : 2 * span] + spread[:, 2 * span :]
+        for s in range(sources):
+            for r in range(rows):
+                out[s, r * own : (r + 1) * own, :] = spread[
+                    s * own : (s + 1) * own, r * BLK : (r + 1) * BLK
+                ]
 
 
 def merge_kernel(own, rows, groups, margin, spread, *refs):
@@ -234,17 +269,14 @@
         near[e] = field[2 * e + 1]
 
 
-def add_kernel(kept, arrived, *outs):
-    for e, out in enumerate(outs):
-        out[...] = kept[e] + arrived[e]
-
-
-def last_kernel(own, rows, *refs):
-    *arrived, out, total = refs
-    summed = arrived[0][...]
-    for part in arrived[1:]:
-        summed = summed + part[...]
-    total[...] = summed
+def add_kernel(kept_in, arrived, kept, near):
+    for e in range(kept.shape[0]):
+        kept[e] = kept_in[2 * e] + arrived[2 * e]
+        near[e] = kept_in[2 * e + 1] + arrived[2 * e + 1]
+
+
+def last_kernel(own, rows, kept, arrived, out, total):
+    total[...] = kept[0] + arrived[0]
     for b in range(own):
         out[:, b * BLK : (b + 1) * BLK] = total[pl.ds(b, rows, stride=own), :]
 
@@ -292,66 +324,74 @@
         ],
     )(in_hbm(margin), in_hbm(aggregate), in_hbm(residual), near_names, near)
     arrived = exchange(outgoing, "sub", 2)
-    tile = min(256, coarse_depth // 2, depth // 2)
-    chunk = tile // 4
-    ahead = 2 * tile // chunk
-    begun, local_factor = call(
-        functools.partial(load_kernel, chunk, tile, ahead),
-        (sds((rhs, depth), f32), sds(local_factor.shape, local_factor.dtype)),
-        [HBM, HBM, pl.BlockSpec(memory_space=pl.ANY)],
+    quarter = coarse_depth // 4
+    tile, coarse_tile = min(256, depth // 2), min(256, quarter)
+    chunk = depth // 8
+    begun, local_factor, coarse_upper = call(
+        functools.partial(load_kernel, chunk, tile),
+        (
+            sds((rhs, depth), f32),
+            sds(local_factor.shape, local_factor.dtype),
+            sds((quarter, coarse_width), coarse_factor.dtype),
+        ),
+        [HBM, HBM, HBM, pl.BlockSpec(memory_space=pl.ANY)],
         [
             pltpu.VMEM(residual.shape, f32),
             pltpu.SemaphoreType.DMA,
             pltpu.SemaphoreType.DMA((depth // chunk,)),
+            pltpu.SemaphoreType.DMA((4,)),
         ],
         flops=2 * rhs * depth * own_width,
-        moved=2 * depth * width,
-    )(in_hbm(residual), local_factor, arrived[0])
-    chunk = tile // 8
-    ahead = tile // chunk
-    upper, lower = tile, coarse_depth - tile
-    *fine, coarse_upper = call(
+        moved=2 * depth * width + 2 * quarter * coarse_width,
+    )(in_hbm(residual), local_factor, coarse_factor, arrived[0])
+    chunk = quarter // 4
+    *fine, coarse_middle = call(
         functools.partial(fine_kernel, own, rows, begin, chunk, tile, pairs),
         [sds((rows * blocks, BLK), f32)] * grp_count
-        + [sds((upper, coarse_width), coarse_factor.dtype)],
+        + [sds((quarter, coarse_width), coarse_factor.dtype)],
         [SMEM, VMEM, VMEM, HBM, VMEM] + [VMEM] * (pairs - 1),
-        [pltpu.VMEM((rhs * blocks, BLK), f32), pltpu.SemaphoreType.DMA((upper // chunk,))],
+        [pltpu.VMEM((rhs * blocks, BLK), f32), pltpu.SemaphoreType.DMA((quarter // chunk,))],
         flops=4 * rhs * depth * width,
-        moved=2 * depth * width + 2 * upper * coarse_width,
+        moved=2 * depth * width + 2 * quarter * coarse_width,
     )(margin, begun, local_factor, coarse_factor, near, *arrived[1:])
     panels = exchange(fine, "grp")
+    lower = coarse_depth - 2 * quarter
+    size = own * rows
     spread = call(
-        functools.partial(coarse_kernel, own, rows, chunk, tile, ahead, pairs),
-        sds((2 * pairs, own * rows, BLK), f32),
-        [VMEM, HBM] + [VMEM] * pairs,
+        functools.partial(coarse_kernel, own, rows, chunk, coarse_tile, pairs),
+        sds((2 * pairs, size, BLK), f32),
+        [VMEM, VMEM, HBM] + [VMEM] * pairs,
         [
             pltpu.VMEM((rows * (coarse_width // BLK), BLK), f32),
             pltpu.VMEM((lower, coarse_width), coarse_factor.dtype),
+            pltpu.VMEM((rows, 2 * quarter), f32),
+            pltpu.VMEM((2 * pairs * own, coarse_width // BLK), f32),
             pltpu.SemaphoreType.DMA((lower // chunk,)),
         ],
         flops=4 * rows * coarse_depth * coarse_width,
         moved=2 * coarse_depth * coarse_width,
         limit=24 * MIB,
-    )(coarse_upper, coarse_factor, *arrived)
-    field = sds((pairs, own * rows, BLK), f32)
+    )(coarse_upper, coarse_middle, coarse_factor, *arrived)
+    field = sds((pairs, size, BLK), f32)
     kept, crossing = call(
         functools.partial(merge_kernel, own, rows, grp_count),
         [field, field],
         [SMEM] + [VMEM] * (1 + grp_count),
-        [
-            pltpu.VMEM((rows * blocks, BLK), f32),
-            pltpu.VMEM((2 * pairs, own * rows, BLK), f32),
-        ],
+        [pltpu.VMEM((rows * blocks, BLK), f32), pltpu.VMEM((2 * pairs, size, BLK), f32)],
     )(margin, spread, *panels)
-    back = call(add_kernel, [sds((own * rows, BLK), f32)] * pairs, [VMEM, VMEM])(
-        kept, swap(crossing, "sub", 1)
-    )
+    distance = 1
+    while kept.shape[0] > 1:
+        half = sds((kept.shape[0] // 2, size, BLK), f32)
+        kept, crossing = call(add_kernel, [half, half], [VMEM, VMEM])(
+            kept, swap(crossing, "sub", distance)
+        )
+        distance *= 2
     return call(
         functools.partial(last_kernel, own, rows),
         sds((rows, own_width), f32),
-        [VMEM] * pairs,
-        [pltpu.VMEM((own * rows, BLK), f32)],
-    )(*exchange(back, "sub", 2))
+        [VMEM, VMEM],
+        [pltpu.VMEM((size, BLK), f32)],
+    )(kept, swap(crossing, "sub", distance))
 
 
 def solution(mesh):

time: 45.2 us -> 40.1 us (0.89)
  Pallas kernels: 24.8 us -> 19.7 us
    pallas_call x3 -> x4, Pallas kernels: 18 us -> 13.8 us  [the longest x1 8.29 us: on_device(): call(functools.partial(coarse_kernel, own, rows, chunk, coarse_tile, pair...]
    pallas_call x1, Pallas kernels: 4.3 us -> 3.47 us  [on_device(): call(functools.partial(fine_kernel, own, rows, begin, chunk, tile, pairs)...]
    ppermute x12 -> x11, waiting for transfers between devices: 6.96 us -> 6.97 us  [swap(): return lax.ppermute(value, axis, [(i, i ^ distance) for i in range(count)])]
    ppermute x12 -> x11, starting transfers between devices: 13.2 us -> 13.2 us  [swap(): return lax.ppermute(value, axis, [(i, i ^ distance) for i in range(count)])]
  transfers between devices with their start and end apart: 12 -> 11, of which waited for: 5 -> 4; matrix products, arithmetic and copies ran while one was open for 0% -> 0% of each run, Pallas kernels for 40% -> 34%
where the time goes in v7:
time: 40.1 us; the launch traced here: 40 us
  Pallas kernels  19.7 us (49%)
  starting transfers between devices  13.2 us (33%)
  waiting for transfers between devices  6.97 us (17%)
    ppermute x11, starting transfers between devices, swap(): return lax.ppermute(value, axis, [(i, i ^ distance) for i in range(count)])  13.2 us
    pallas_call x1, Pallas kernels, on_device(): call(functools.partial(coarse_kernel, own, rows, chunk, coarse_tile, pair...  8.29 us
    ppermute x11, waiting for transfers between devices, swap(): return lax.ppermute(value, axis, [(i, i ^ distance) for i in range(count)])  6.97 us
    pallas_call x1, Pallas kernels, on_device(): call(functools.partial(load_kernel, chunk, tile), (sds((rhs, depth), f32)...  5.45 us
    pallas_call x1, Pallas kernels, on_device(): call(functools.partial(fine_kernel, own, rows, begin, chunk, tile, pairs)...  3.47 us
    pallas_call x1, Pallas kernels, on_device(): call(functools.partial(pack_kernel, own, rows, pad), [sds((begin, BLK), f...  1.15 us
  transfers between devices with their start and end apart: 11, of which 4 were waited for; matrix products, arithmetic and copies ran while one was open for 0% of the time, Pallas kernels for 34%

profile of v7, /device:TPU:0, one launch (start us, length us, event | category | flops | bytes accessed | tf_op | source)
XLA Modules:
  0.0 40.0 jit_solution(16394575756800696650)
XLA Ops:
  0.0 0.5 %collective-permute-start.1 = (f32[8,3072]{1,0:T(8,128)}, f32[8,3072]{1,0:T(8,128)S(1)}, u32[]{:S(2)}, u32[]{:S(2)}) collective-permute-start(f32[8,3072]{1,0:T(8,128)} %residual_hbm.3), channel_id=1, source_target_pairs={{0,1},{1,0},{2,3},{3,2},{4,5},{5,4},{6,7},{7,6},{8,9},{9,8},{10,11... | collective-permute-start | bytes 294920 | tf_op jit(solution)/shard_map/ppermute | solution.py:286
  0.5 0.1 collective-permute-start
  0.5 1.2 %collective-permute-done.near_names = s32[1,24]{1,0:T(1,128)S(1)} collective-permute-done((s32[1,24]{1,0:T(1,128)}, s32[1,24]{1,0:T(1,128)S(1)}, u32[]{:S(2)}, u32[]{:S(2)}) %collective-permute-start) | collective-permute-done | bytes 128 | tf_op jit(solution)/shard_map/ppermute | solution.py:286
  1.7 0.0 collective-permute-done.1.near
  1.7 1.2 %shard_map.55 = (f32[104,128]{1,0:T(8,128)S(1)}, f32[168,128]{1,0:T(8,128)S(1)}, f32[168,128]{1,0:T(8,128)S(1)}, f32[168,128]{1,0:T(8,128)S(1)}) custom-call(s32[8,8]{1,0:T(8,128)} %margin.3, s32[1,24]{1,0:T(1,128)} %bitcast.2, f32[8,3072]{1,0:T(8,128)} %residual_hbm.3, s32[1,24]{1,0:T(1,128)S(1)} %collective-permute-done.near_names, ...), custom_call_target="tpu_custom_call" | custom-call | tf_op jit(solution)/shard_map/pallas_call | solution.py:314
  2.9 2.8 %collective-permute-start.2 = (f32[168,128]{1,0:T(8,128)S(1)}, f32[168,128]{1,0:T(8,128)S(1)}, u32[]{:S(2)}, u32[]{:S(2)}) collective-permute-start(f32[168,128]{1,0:T(8,128)S(1)} %get-tuple-element.27), channel_id=1, source_target_pairs={{0,2},{1,3},{2,0},{3,1},{4,6},{5,7},{6,4},{7,5},{8,10},{9,11},{10,... | collective-permute-start | bytes 258056 | tf_op jit(solution)/shard_map/ppermute | solution.py:286
  5.7 1.5 %collective-permute-start.3 = (f32[168,128]{1,0:T(8,128)S(1)}, f32[168,128]{1,0:T(8,128)S(1)}, u32[]{:S(2)}, u32[]{:S(2)}) collective-permute-start(f32[168,128]{1,0:T(8,128)S(1)} %get-tuple-element.28), channel_id=1, source_target_pairs={{0,4},{1,5},{2,6},{3,7},{4,0},{5,1},{6,2},{7,3},{8,12},{9,13},{10,... | collective-permute-start | bytes 258056 | tf_op jit(solution)/shard_map/ppermute | solution.py:286
  7.2 0.0 collective-permute-start.4
  7.2 0.0 copy-start
  7.2 5.4 %shard_map.56 = (f32[8,1024]{1,0:T(8,128)S(1)}, bf16[1,1024,4096]{2,1,0:T(8,128)(2,1)S(1)}, bf16[256,8192]{1,0:T(8,128)(2,1)S(1)}) custom-call(f32[8,3072]{1,0:T(8,128)} %residual_hbm.3, bf16[1,1024,4096]{2,1,0:T(8,128)(2,1)} %fine_hbm.1, bf16[1024,8192]{1,0:T(8,128)(2,1)} %factor_hbm.1, f32[104,128]{1,0:T(8,128)S(1)} %get-tuple-element.23.after.refs_0_), custom_call_target="tpu_custom_call" | custom-call | flops 50331648 | bytes 12582912 | tf_op jit(solution)/shard_map/pallas_call | solution.py:330
  12.7 0.0 collective-permute-done.2.refs_0_.refs_1_
  12.7 0.0 collective-permute-done.3.refs_1_.refs_2_
  12.7 0.0 collective-permute-done.4.refs_2_.refs_3_
  12.7 0.0 copy-done
  12.7 3.5 %shard_map.57 = (f32[64,128]{1,0:T(8,128)S(1)}, f32[64,128]{1,0:T(8,128)S(1)}, f32[64,128]{1,0:T(8,128)S(1)}, f32[64,128]{1,0:T(8,128)S(1)}, bf16[256,8192]{1,0:T(8,128)(2,1)S(1)}) custom-call(s32[8,8]{1,0:T(8,128)S(1)} %copy-done, f32[8,1024]{1,0:T(8,128)S(1)} %get-tuple-element.25.begun, bf16[1,1024,4096]{2,1,0:T(8,128)(2,1)S(1)} %get-tuple-element.26.factor, ...), custom_call_target="tpu_custom_call" | custom-call | flops 134217728 | bytes 12582912 | tf_op jit(solution)/shard_map/pallas_call | solution.py:348
  16.2 2.1 %collective-permute-start.5 = (f32[64,128]{1,0:T(8,128)S(1)}, f32[64,128]{1,0:T(8,128)S(1)}, u32[]{:S(2)}, u32[]{:S(2)}) collective-permute-start(f32[64,128]{1,0:T(8,128)S(1)} %get-tuple-element.32), channel_id=1, source_target_pairs={{0,8},{8,0},{16,24},{24,16},{1,9},{9,1},{17,25},{25,17},{2,10},{10... | collective-permute-start | bytes 98312 | tf_op jit(solution)/shard_map/ppermute | solution.py:286
  18.3 2.6 %collective-permute-start.6 = (f32[64,128]{1,0:T(8,128)S(1)}, f32[64,128]{1,0:T(8,128)S(1)}, u32[]{:S(2)}, u32[]{:S(2)}) collective-permute-start(f32[64,128]{1,0:T(8,128)S(1)} %get-tuple-element.33), channel_id=1, source_target_pairs={{0,16},{8,24},{16,0},{24,8},{1,17},{9,25},{17,1},{25,9},{2,18},{10... | collective-permute-start | bytes 98312 | tf_op jit(solution)/shard_map/ppermute | solution.py:286
  20.9 0.0 collective-permute-start.7
  20.9 8.3 %shard_map.58.spread = f32[8,48,128]{2,1,0:T(8,128)S(1)} custom-call(bf16[256,8192]{1,0:T(8,128)(2,1)S(1)} %get-tuple-element.24.upper, bf16[256,8192]{1,0:T(8,128)(2,1)S(1)} %get-tuple-element.30.middle, bf16[1024,8192]{1,0:T(8,128)(2,1)} %factor_hbm.1, f32[104,128]{1,0:T(8,128)S(1)} %get-tuple-element.23.after.refs_0_, ...), custom_call_target="tpu_custom_call" | custom-call | flops 67108864 | bytes 16777216 | tf_op jit(solution)/shard_map/pallas_call | solution.py:360
  29.2 0.0 collective-permute-done.5.refs_1_
  29.2 0.0 collective-permute-done.6.refs_2_
  29.2 0.0 collective-permute-done.7.refs_3_
  29.2 0.7 %shard_map.59 = (f32[4,48,128]{2,1,0:T(8,128)S(1)}, f32[4,48,128]{2,1,0:T(8,128)S(1)}) custom-call(s32[8,8]{1,0:T(8,128)S(1)} %copy-done, f32[8,48,128]{2,1,0:T(8,128)S(1)} %shard_map.58.spread, f32[64,128]{1,0:T(8,128)S(1)} %get-tuple-element.31.refs_0_, f32[64,128]{1,0:T(8,128)S(1)} %collective-permute-done.5.refs_1_, ...), custom_call_target="tpu_custom_call" | custom-call | tf_op jit(solution)/shard_map/pallas_call | solution.py:376
  29.9 0.1 collective-permute-start.8
  30.0 1.3 %collective-permute-done.8.arrived = f32[4,48,128]{2,1,0:T(8,128)S(1)} collective-permute-done((f32[4,48,128]{2,1,0:T(8,128)S(1)}, f32[4,48,128]{2,1,0:T(8,128)S(1)}, u32[]{:S(2)}, u32[]{:S(2)}) %collective-permute-start.8) | collective-permute-done | bytes 98336 | tf_op jit(solution)/shard_map/ppermute | solution.py:286
  31.3 1.8 %collective-permute-start.9 = (f32[2,48,128]{2,1,0:T(8,128)S(1)}, f32[2,48,128]{2,1,0:T(8,128)S(1)}, u32[]{:S(2)}, u32[]{:S(2)}) collective-permute-start(f32[2,48,128]{2,1,0:T(8,128)S(1)} %get-tuple-element.38), channel_id=1, source_target_pairs={{0,2},{1,3},{2,0},{3,1},{4,6},{5,7},{6,4},{7,5},{8,10},{9,11},{10,... | collective-permute-start | bytes 147464 | tf_op jit(solution)/shard_map/ppermute | solution.py:286
  33.1 2.4 %collective-permute-done.9.arrived = f32[2,48,128]{2,1,0:T(8,128)S(1)} collective-permute-done((f32[2,48,128]{2,1,0:T(8,128)S(1)}, f32[2,48,128]{2,1,0:T(8,128)S(1)}, u32[]{:S(2)}, u32[]{:S(2)}) %collective-permute-start.9) | collective-permute-done | bytes 49184 | tf_op jit(solution)/shard_map/ppermute | solution.py:286
  35.5 1.8 %collective-permute-start.10 = (f32[1,48,128]{2,1,0:T(8,128)S(1)}, f32[1,48,128]{2,1,0:T(8,128)S(1)}, u32[]{:S(2)}, u32[]{:S(2)}) collective-permute-start(f32[1,48,128]{2,1,0:T(8,128)S(1)} %get-tuple-element.40), channel_id=1, source_target_pairs={{0,4},{1,5},{2,6},{3,7},{4,0},{5,1},{6,2},{7,3},{8,12},{9,13},{10,... | collective-permute-start | bytes 73736 | tf_op jit(solution)/shard_map/ppermute | solution.py:286
  37.3 2.1 %collective-permute-done.10.arrived = f32[1,48,128]{2,1,0:T(8,128)S(1)} collective-permute-done((f32[1,48,128]{2,1,0:T(8,128)S(1)}, f32[1,48,128]{2,1,0:T(8,128)S(1)}, u32[]{:S(2)}, u32[]{:S(2)}) %collective-permute-start.10) | collective-permute-done | bytes 24608 | tf_op jit(solution)/shard_map/ppermute | solution.py:286
  39.3 0.6 %shard_map.62 = f32[2,3072]{1,0:T(2,128)} custom-call(f32[1,48,128]{2,1,0:T(8,128)S(1)} %get-tuple-element.39.kept, f32[1,48,128]{2,1,0:T(8,128)S(1)} %collective-permute-done.10.arrived), custom_call_target="tpu_custom_call" | custom-call | tf_op jit(solution)/shard_map/pallas_call | solution.py:389
  (2 shorter events, 0.0 us)
Async XLA Ops:
  0.0 1.7 %collective-permute-start.1 = (f32[8,3072]{1,0:T(8,128)}, f32[8,3072]{1,0:T(8,128)S(1)}, u32[]{:S(2)}, u32[]{:S(2)}) collective-permute-start(f32[8,3072]{1,0:T(8,128)} %residual_hbm.3), channel_id=1, source_target_pairs={{0,1},{1,0},{2,3},{3,2},{4,5},{5,4},{6,7},{7,6},{8,9},{9,8},{10,11... | collective-permute-start | bytes 294920 | tf_op jit(solution)/shard_map/ppermute | solution.py:286
  0.5 1.3 %collective-permute-start = (s32[1,24]{1,0:T(1,128)}, s32[1,24]{1,0:T(1,128)S(1)}, u32[]{:S(2)}, u32[]{:S(2)}) collective-permute-start(s32[1,24]{1,0:T(1,128)} %bitcast.1), channel_id=1, source_target_pairs={{0,1},{1,0},{2,3},{3,2},{4,5},{5,4},{6,7},{7,6},{8,9},{9,8},{10,11... | collective-permute-start | bytes 296 | tf_op jit(solution)/shard_map/ppermute | solution.py:286
  2.9 9.8 %collective-permute-start.2 = (f32[168,128]{1,0:T(8,128)S(1)}, f32[168,128]{1,0:T(8,128)S(1)}, u32[]{:S(2)}, u32[]{:S(2)}) collective-permute-start(f32[168,128]{1,0:T(8,128)S(1)} %get-tuple-element.27), channel_id=1, source_target_pairs={{0,2},{1,3},{2,0},{3,1},{4,6},{5,7},{6,4},{7,5},{8,10},{9,11},{10,... | collective-permute-start | bytes 258056 | tf_op jit(solution)/shard_map/ppermute | solution.py:286
  5.7 7.0 %collective-permute-start.3 = (f32[168,128]{1,0:T(8,128)S(1)}, f32[168,128]{1,0:T(8,128)S(1)}, u32[]{:S(2)}, u32[]{:S(2)}) collective-permute-start(f32[168,128]{1,0:T(8,128)S(1)} %get-tuple-element.28), channel_id=1, source_target_pairs={{0,4},{1,5},{2,6},{3,7},{4,0},{5,1},{6,2},{7,3},{8,12},{9,13},{10,... | collective-permute-start | bytes 258056 | tf_op jit(solution)/shard_map/ppermute | solution.py:286
  7.2 5.5 %collective-permute-start.4 = (f32[168,128]{1,0:T(8,128)S(1)}, f32[168,128]{1,0:T(8,128)S(1)}, u32[]{:S(2)}, u32[]{:S(2)}) collective-permute-start(f32[168,128]{1,0:T(8,128)S(1)} %get-tuple-element.29), channel_id=1, source_target_pairs={{0,6},{1,7},{2,4},{3,5},{4,2},{5,3},{6,0},{7,1},{8,14},{9,15},{10,... | collective-permute-start | bytes 258056 | tf_op jit(solution)/shard_map/ppermute | solution.py:286
  7.2 5.5 %copy-start = (s32[8,8]{1,0:T(8,128)S(1)}, s32[8,8]{1,0:T(8,128)}, u32[]{:S(2)}) copy-start(s32[8,8]{1,0:T(8,128)} %margin.3) | copy-start | bytes 772
  16.2 13.0 %collective-permute-start.5 = (f32[64,128]{1,0:T(8,128)S(1)}, f32[64,128]{1,0:T(8,128)S(1)}, u32[]{:S(2)}, u32[]{:S(2)}) collective-permute-start(f32[64,128]{1,0:T(8,128)S(1)} %get-tuple-element.32), channel_id=1, source_target_pairs={{0,8},{8,0},{16,24},{24,16},{1,9},{9,1},{17,25},{25,17},{2,10},{10... | collective-permute-start | bytes 98312 | tf_op jit(solution)/shard_map/ppermute | solution.py:286
  18.3 10.9 %collective-permute-start.6 = (f32[64,128]{1,0:T(8,128)S(1)}, f32[64,128]{1,0:T(8,128)S(1)}, u32[]{:S(2)}, u32[]{:S(2)}) collective-permute-start(f32[64,128]{1,0:T(8,128)S(1)} %get-tuple-element.33), channel_id=1, source_target_pairs={{0,16},{8,24},{16,0},{24,8},{1,17},{9,25},{17,1},{25,9},{2,18},{10... | collective-permute-start | bytes 98312 | tf_op jit(solution)/shard_map/ppermute | solution.py:286
  20.9 8.3 %collective-permute-start.7 = (f32[64,128]{1,0:T(8,128)S(1)}, f32[64,128]{1,0:T(8,128)S(1)}, u32[]{:S(2)}, u32[]{:S(2)}) collective-permute-start(f32[64,128]{1,0:T(8,128)S(1)} %get-tuple-element.34), channel_id=1, source_target_pairs={{0,24},{8,16},{16,8},{24,0},{1,25},{9,17},{17,9},{25,1},{2,26},{10... | collective-permute-start | bytes 98312 | tf_op jit(solution)/shard_map/ppermute | solution.py:286
  29.9 1.4 %collective-permute-start.8 = (f32[4,48,128]{2,1,0:T(8,128)S(1)}, f32[4,48,128]{2,1,0:T(8,128)S(1)}, u32[]{:S(2)}, u32[]{:S(2)}) collective-permute-start(f32[4,48,128]{2,1,0:T(8,128)S(1)} %get-tuple-element.36), channel_id=1, source_target_pairs={{0,1},{1,0},{2,3},{3,2},{4,5},{5,4},{6,7},{7,6},{8,9},{9,8},{10,11... | collective-permute-start | bytes 294920 | tf_op jit(solution)/shard_map/ppermute | solution.py:286
  31.3 4.2 %collective-permute-start.9 = (f32[2,48,128]{2,1,0:T(8,128)S(1)}, f32[2,48,128]{2,1,0:T(8,128)S(1)}, u32[]{:S(2)}, u32[]{:S(2)}) collective-permute-start(f32[2,48,128]{2,1,0:T(8,128)S(1)} %get-tuple-element.38), channel_id=1, source_target_pairs={{0,2},{1,3},{2,0},{3,1},{4,6},{5,7},{6,4},{7,5},{8,10},{9,11},{10,... | collective-permute-start | bytes 147464 | tf_op jit(solution)/shard_map/ppermute | solution.py:286
  35.5 3.9 %collective-permute-start.10 = (f32[1,48,128]{2,1,0:T(8,128)S(1)}, f32[1,48,128]{2,1,0:T(8,128)S(1)}, u32[]{:S(2)}, u32[]{:S(2)}) collective-permute-start(f32[1,48,128]{2,1,0:T(8,128)S(1)} %get-tuple-element.40), channel_id=1, source_target_pairs={{0,4},{1,5},{2,6},{3,7},{4,0},{5,1},{6,2},{7,3},{8,12},{9,13},{10,... | collective-permute-start | bytes 73736 | tf_op jit(solution)/shard_map/ppermute | solution.py:286

commit v8 on v7

--- a/solution.py
+++ b/solution.py
@@ -41,33 +41,45 @@
     return [high, middle, low]
 
 
-def pack_kernel(own, rows, pad, margin_hbm, aggregate_hbm, residual_hbm, near_names, near, *refs):
-    *outs, block_rows, margin, aggregate, residual, sems = refs
-    pairs = ((residual_hbm, residual), (margin_hbm, margin), (aggregate_hbm, aggregate))
+def stage_kernel(own, rows, residual_hbm, aggregate_hbm, residual, mine, names, block_rows, aggregate, sems):
+    pairs = ((residual_hbm, residual), (aggregate_hbm, aggregate))
     copies = [pltpu.make_async_copy(a, b, sems.at[i]) for i, (a, b) in enumerate(pairs)]
-    for copy in copies:
-        copy.start()
+    start(copies)
     for copy in copies:
         copy.wait()
+    names[...] = aggregate[...].astype(jnp.float32)
+    mine[...] = rows_of(residual, own, rows, block_rows)
+
+
+def rows_of(residual, own, rows, block_rows):
+    rhs = residual.shape[0]
+    for b in range(own):
+        block_rows[pl.ds(b, rhs, stride=own), :] = residual[:, b * BLK : (b + 1) * BLK]
+    first = lax.axis_index("grp") * rows * own
+    return block_rows[pl.ds(pl.multiple_of(first, 8), rows * own), :]
+
+
+def pack_kernel(own, rows, pad, margin_hbm, residual, mine, names, near_names, near, *refs):
+    *outs, away, block_rows, margin, sem = refs
+    copy = pltpu.make_async_copy(margin_hbm, margin, sem)
+    copy.start()
     halo = margin.shape[1]
     rhs = residual.shape[0]
     me = lax.axis_index("sub")
-    first = lax.axis_index("grp") * rows
     size = own * rows
-    mine = []
-    for i, part in enumerate((residual, near)):
-        for b in range(own):
-            block_rows[i, pl.ds(b, rhs, stride=own), :] = part[:, b * BLK : (b + 1) * BLK]
-        mine.append(block_rows[i, pl.ds(pl.multiple_of(first * own, 8), size), :])
-    names = [aggregate[...].astype(jnp.float32), near_names[...].astype(jnp.float32)]
+    both = [mine[...], rows_of(near, own, rows, block_rows)]
+    labels = [names[...], near_names[...].astype(jnp.float32)]
     at = 2 * size
-    for e, out in enumerate(outs):
+    for out in outs:
         out[at : at + pad, :] = jnp.zeros((pad, BLK), jnp.float32)
         for i in range(2):
-            out[i * size : (i + 1) * size, :] = mine[i]
-            out[at + i : at + i + 1, :own] = names[i]
-        if e == 0:
-            continue
+            out[i * size : (i + 1) * size, :] = both[i]
+            out[at + i : at + i + 1, :own] = labels[i]
+    copy.wait()
+    for k in range(halo):
+        distance = (me ^ (margin[me, k] // own)) // 2
+        away[k : k + 1, :] = jnp.full((1, BLK), distance, jnp.int32)
+    for e, out in enumerate(outs):
         target = me ^ (2 * e)
         for k in range(halo):
             block = margin[target, k]
@@ -93,10 +105,11 @@
         copy.start()
 
 
-def first_product(factor, right, tile):
-    parts = [
-        mm(right, factor[n * tile : (n + 1) * tile, :], NT) for n in range(factor.shape[0] // tile)
-    ]
+def first_product(factor, right, tile, turned=False):
+    parts = []
+    for n in range(factor.shape[0] // tile):
+        rows = factor[n * tile : (n + 1) * tile, :]
+        parts.append(mm(rows, right, NT).T if turned else mm(right, rows, NT))
     return jnp.concatenate(parts, axis=1)
 
 
@@ -105,17 +118,14 @@
 
 
 def load_kernel(
-    chunk, tile, residual_hbm, fine_hbm, coarse_hbm, after, inner, fine, coarse, residual, sem, sems, more
+    chunk, tile, residual, fine_hbm, coarse_hbm, after, inner, fine, coarse, sems, more
 ):
     depth = fine.shape[1]
     own_width = residual.shape[1]
     half = depth // 2
     each = half // chunk
-    first = pltpu.make_async_copy(residual_hbm, residual, sem)
-    first.start()
     start(panel_copies(fine_hbm.at[0], fine.at[0], chunk, sems))
     late = panel_copies(coarse_hbm, coarse, coarse.shape[0] // 4, more)
-    first.wait()
 
     def step(n, carry):
         for i in range(each):
@@ -134,27 +144,24 @@
         copy.wait()
 
 
-def fine_kernel(own, rows, begin, chunk, tile, pairs, margin, begun, factor, coarse_hbm, near, *refs):
-    arrived = (None, *refs[: pairs - 1])
-    *outs, coarse, table, sems = refs[pairs - 1 :]
+def fine_kernel(own, rows, begin, chunk, tile, pairs, away, begun, factor, coarse_hbm, *refs):
+    arrived = refs[:pairs]
+    *outs, coarse, table, sems = refs[pairs:]
     done = coarse_hbm.shape[0] // 4
     copies = panel_copies(coarse_hbm, coarse, chunk, sems, done)
     start(copies)
     rhs = begun.shape[0]
-    halo = margin.shape[1]
+    halo = away.shape[0]
     depth, width = factor.shape[1:]
     blocks = width // BLK
-    me = lax.axis_index("sub")
     group = lax.axis_index("grp")
     tiles = []
     for k in range(halo):
-        block = margin[me, k]
-        owner = block // own
-        away = (me ^ owner) // 2
         span = slice(begin + k * rhs, begin + (k + 1) * rhs)
-        part = near[:, pl.ds(pl.multiple_of((block - owner * own) * BLK, BLK), BLK)]
+        distance = away[k : k + 1, :]
+        part = arrived[0][span, :]
         for e in range(1, pairs):
-            part = jnp.where(away == e, arrived[e][span, :], part)
+            part = jnp.where(distance == e, arrived[e][span, :], part)
         tiles.append(part.astype(jnp.bfloat16))
     local = jnp.concatenate(tiles, axis=1)
     far = factor.at[0, :, pl.ds(own * BLK, halo * BLK)]
@@ -174,9 +181,11 @@
             copy.wait()
 
 
-def coarse_kernel(own, rows, chunk, tile, pairs, upper, middle, factor_hbm, *refs):
+def coarse_kernel(own, rows, chunk, tile, pairs, margin_hbm, upper, middle, factor_hbm, *refs):
     arrived = refs[:pairs]
-    out, table, lower, begun, field, sems = refs[pairs:]
+    out, place, table, lower, begun, field, margin, sem, sems = refs[pairs:]
+    small = pltpu.make_async_copy(margin_hbm, margin, sem)
+    small.start()
     done = upper.shape[0] + middle.shape[0]
     width = upper.shape[1]
     copies = panel_copies(factor_hbm, lower, chunk, sems, done)
@@ -214,16 +223,27 @@
     ).astype(jnp.bfloat16)
     field[...] = member.astype(jnp.float32)
     begun[:, : upper.shape[0]] = first_product(upper, right, tile)
-    begun[:, upper.shape[0] : done] = first_product(middle, right, tile)
+    begun[:, upper.shape[0] : done] = first_product(middle, right, tile, True)
+    place[...] = jnp.zeros(place.shape, jnp.int32)
 
     @in_own_block
     def _():
-        for copy in copies:
+        for copy in copies + [small]:
             copy.wait()
+        me = lax.axis_index("sub")
+        for k in range(margin.shape[1]):
+            block = margin[me, k]
+            owner = block // own
+            row = (me ^ owner) * own + block - owner * own
+            place[pl.ds(row, 1), :] = jnp.full((1, BLK), k + 1, jnp.int32)
         right = jnp.concatenate(
             [table[pl.ds(j, rows, stride=coarse), :] for j in range(coarse)], axis=1
         ).astype(jnp.bfloat16)
-        low = first_product(lower, right, tile).astype(jnp.bfloat16)
+        half = lower.shape[0] // 2
+        low = [
+            first_product(lower.at[pl.ds(i * half, half)], right, tile, i == 1) for i in range(2)
+        ]
+        low = jnp.concatenate(low, axis=1).astype(jnp.bfloat16)
         mid = begun[...].astype(jnp.bfloat16)
         high = mid[:, : upper.shape[0]]
         mid = mid[:, upper.shape[0] :]
@@ -244,39 +264,39 @@
                 ]
 
 
-def merge_kernel(own, rows, groups, margin, spread, *refs):
+def merge_kernel(own, rows, groups, halo, place, spread, *refs):
     arrived = refs[:groups]
-    kept, near, total, field = refs[groups:]
-    halo = margin.shape[1]
+    kept, near = refs[groups:]
     blocks = own + halo
-    me = lax.axis_index("sub")
+    total = arrived[0][...]
+    for part in arrived[1:]:
+        total = total + part[...]
+    for d in range(spread.shape[0]):
+        where = place[d * own : (d + 1) * own, :]
+        hits = [where == k + 1 for k in range(halo)] if d else []
+        out = near if d % 2 else kept
+        for r in range(rows):
+            span = slice(r * own, (r + 1) * own)
+            field = spread[d, span, :]
+            if d == 0:
+                field = field + total[r * blocks : r * blocks + own, :]
+            for k, hit in enumerate(hits):
+                row = r * blocks + own + k
+                field = field + jnp.where(hit, total[row : row + 1, :], 0.0)
+            out[d // 2, span, :] = field
+
+
+def add_kernel(kept, arrived, *outs):
+    for e, out in enumerate(outs):
+        out[...] = kept[e] + arrived[e]
+
+
+def last_kernel(own, rows, *refs):
+    *arrived, out, total = refs
     summed = arrived[0][...]
     for part in arrived[1:]:
         summed = summed + part[...]
     total[...] = summed
-    field[...] = spread[...]
-    for r in range(rows):
-        span = slice(r * own, (r + 1) * own)
-        field[0, span, :] = field[0, span, :] + total[r * blocks : r * blocks + own, :]
-    for k in range(halo):
-        block = margin[me, k]
-        owner = block // own
-        where = pl.ds(block - owner * own, rows, stride=own)
-        away = me ^ owner
-        field[away, where, :] = field[away, where, :] + total[pl.ds(own + k, rows, stride=blocks), :]
-    for e in range(kept.shape[0]):
-        kept[e] = field[2 * e]
-        near[e] = field[2 * e + 1]
-
-
-def add_kernel(kept_in, arrived, kept, near):
-    for e in range(kept.shape[0]):
-        kept[e] = kept_in[2 * e] + arrived[2 * e]
-        near[e] = kept_in[2 * e + 1] + arrived[2 * e + 1]
-
-
-def last_kernel(own, rows, kept, arrived, out, total):
-    total[...] = kept[0] + arrived[0]
     for b in range(own):
         out[:, b * BLK : (b + 1) * BLK] = total[pl.ds(b, rows, stride=own), :]
 
@@ -287,7 +307,8 @@
 
 
 def exchange(parts, axis, unit=1):
-    return [parts[0]] + [swap(part, axis, d * unit) for d, part in enumerate(parts) if d > 0]
+    there = [swap(parts[d], axis, d * unit) for d in range(len(parts) - 1, 0, -1)]
+    return [parts[0]] + there[::-1]
 
 
 def on_device(residual, margin, aggregate, local_factor, coarse_factor):
@@ -311,18 +332,28 @@
 
     near = swap(residual, "sub", 1)
     near_names = swap(aggregate, "sub", 1)
-    outgoing = call(
+    held, mine, names = call(
+        functools.partial(stage_kernel, own, rows),
+        (sds(residual.shape, f32), sds((own * rows, BLK), f32), sds((1, own), f32)),
+        [HBM, HBM],
+        [
+            pltpu.VMEM((own * rhs, BLK), f32),
+            pltpu.VMEM((1, own), jnp.int32),
+            pltpu.SemaphoreType.DMA((2,)),
+        ],
+        moved=8 * rhs * own_width,
+    )(in_hbm(residual), in_hbm(aggregate))
+    margin = in_hbm(margin)
+    *outgoing, away = call(
         functools.partial(pack_kernel, own, rows, pad),
-        [sds((begin, BLK), f32)] + [sds((begin + halo * rhs, BLK), f32)] * (pairs - 1),
-        [HBM, HBM, HBM, VMEM, VMEM],
+        [sds((begin + halo * rhs, BLK), f32)] * pairs + [sds((halo, BLK), jnp.int32)],
+        [HBM] + [VMEM] * 5,
         [
-            pltpu.VMEM((2, own * rhs, BLK), f32),
+            pltpu.VMEM((own * rhs, BLK), f32),
             pltpu.SMEM(margin.shape, jnp.int32),
-            pltpu.VMEM((1, own), jnp.int32),
-            pltpu.VMEM(residual.shape, f32),
-            pltpu.SemaphoreType.DMA((3,)),
+            pltpu.SemaphoreType.DMA,
         ],
-    )(in_hbm(margin), in_hbm(aggregate), in_hbm(residual), near_names, near)
+    )(margin, held, mine, names, near_names, near)
     arrived = exchange(outgoing, "sub", 2)
     quarter = coarse_depth // 4
     tile, coarse_tile = min(256, depth // 2), min(256, quarter)
@@ -334,64 +365,59 @@
             sds(local_factor.shape, local_factor.dtype),
             sds((quarter, coarse_width), coarse_factor.dtype),
         ),
-        [HBM, HBM, HBM, pl.BlockSpec(memory_space=pl.ANY)],
+        [VMEM, HBM, HBM, pl.BlockSpec(memory_space=pl.ANY)],
         [
-            pltpu.VMEM(residual.shape, f32),
-            pltpu.SemaphoreType.DMA,
             pltpu.SemaphoreType.DMA((depth // chunk,)),
             pltpu.SemaphoreType.DMA((4,)),
         ],
         flops=2 * rhs * depth * own_width,
         moved=2 * depth * width + 2 * quarter * coarse_width,
-    )(in_hbm(residual), local_factor, coarse_factor, arrived[0])
+    )(held, local_factor, coarse_factor, arrived[0])
     chunk = quarter // 4
     *fine, coarse_middle = call(
         functools.partial(fine_kernel, own, rows, begin, chunk, tile, pairs),
         [sds((rows * blocks, BLK), f32)] * grp_count
         + [sds((quarter, coarse_width), coarse_factor.dtype)],
-        [SMEM, VMEM, VMEM, HBM, VMEM] + [VMEM] * (pairs - 1),
+        [VMEM, VMEM, VMEM, HBM] + [VMEM] * pairs,
         [pltpu.VMEM((rhs * blocks, BLK), f32), pltpu.SemaphoreType.DMA((quarter // chunk,))],
         flops=4 * rhs * depth * width,
         moved=2 * depth * width + 2 * quarter * coarse_width,
-    )(margin, begun, local_factor, coarse_factor, near, *arrived[1:])
+    )(away, begun, local_factor, coarse_factor, *arrived)
     panels = exchange(fine, "grp")
     lower = coarse_depth - 2 * quarter
     size = own * rows
-    spread = call(
+    spread, place = call(
         functools.partial(coarse_kernel, own, rows, chunk, coarse_tile, pairs),
-        sds((2 * pairs, size, BLK), f32),
-        [VMEM, VMEM, HBM] + [VMEM] * pairs,
+        (sds((2 * pairs, size, BLK), f32), sds((2 * pairs * own, BLK), jnp.int32)),
+        [HBM, VMEM, VMEM, HBM] + [VMEM] * pairs,
         [
             pltpu.VMEM((rows * (coarse_width // BLK), BLK), f32),
             pltpu.VMEM((lower, coarse_width), coarse_factor.dtype),
             pltpu.VMEM((rows, 2 * quarter), f32),
             pltpu.VMEM((2 * pairs * own, coarse_width // BLK), f32),
+            pltpu.SMEM(margin.shape, jnp.int32),
+            pltpu.SemaphoreType.DMA,
             pltpu.SemaphoreType.DMA((lower // chunk,)),
         ],
         flops=4 * rows * coarse_depth * coarse_width,
         moved=2 * coarse_depth * coarse_width,
         limit=24 * MIB,
-    )(coarse_upper, coarse_middle, coarse_factor, *arrived)
+    )(margin, coarse_upper, coarse_middle, coarse_factor, *arrived)
     field = sds((pairs, size, BLK), f32)
     kept, crossing = call(
-        functools.partial(merge_kernel, own, rows, grp_count),
+        functools.partial(merge_kernel, own, rows, grp_count, halo),
         [field, field],
-        [SMEM] + [VMEM] * (1 + grp_count),
-        [pltpu.VMEM((rows * blocks, BLK), f32), pltpu.VMEM((2 * pairs, size, BLK), f32)],
-    )(margin, spread, *panels)
-    distance = 1
-    while kept.shape[0] > 1:
-        half = sds((kept.shape[0] // 2, size, BLK), f32)
-        kept, crossing = call(add_kernel, [half, half], [VMEM, VMEM])(
-            kept, swap(crossing, "sub", distance)
-        )
-        distance *= 2
+        [VMEM] * (2 + grp_count),
+    )(place, spread, *panels)
+    back = call(add_kernel, [sds((size, BLK), f32)] * pairs, [VMEM, VMEM])(
+        kept, swap(crossing, "sub", 1)
+    )
     return call(
         functools.partial(last_kernel, own, rows),
         sds((rows, own_width), f32),
-        [VMEM, VMEM],
+        [VMEM] * pairs,
         [pltpu.VMEM((size, BLK), f32)],
-    )(kept, swap(crossing, "sub", distance))
+    )(*exchange(list(back), "sub", 2)[::-1])
 
 
 def solution(mesh):

time: 40.1 us -> 37.6 us (0.938)
  waiting for transfers between devices: 6.97 us -> 5.32 us
  Pallas kernels: 19.7 us -> 19 us
    ppermute x11 -> x12, waiting for transfers between devices: 6.97 us -> 5.32 us  [swap(): return lax.ppermute(value, axis, [(i, i ^ distance) for i in range(count)])]
    pallas_call x1, Pallas kernels: 3.47 us -> 2.88 us  [on_device(): call(functools.partial(fine_kernel, own, rows, begin, chunk, tile, pairs)...]
    pallas_call x1, Pallas kernels: 5.45 us -> 4.94 us  [on_device(): call(functools.partial(load_kernel, chunk, tile), (sds((rhs, depth), f32)...]
    ppermute x11 -> x12, starting transfers between devices: 13.2 us -> 12.9 us  [swap(): return lax.ppermute(value, axis, [(i, i ^ distance) for i in range(count)])]
  transfers between devices with their start and end apart: 11 -> 12, of which waited for: 4 -> 6; matrix products, arithmetic and copies ran while one was open for 0% -> 0% of each run, Pallas kernels for 34% -> 38%
where the time goes in v8:
time: 37.6 us; the launch traced here: 37.4 us
  Pallas kernels  19 us (51%)
  starting transfers between devices  12.9 us (34%)
  waiting for transfers between devices  5.32 us (14%)
    ppermute x12, starting transfers between devices, swap(): return lax.ppermute(value, axis, [(i, i ^ distance) for i in range(count)])  12.9 us
    pallas_call x1, Pallas kernels, on_device(): call(functools.partial(coarse_kernel, own, rows, chunk, coarse_tile, pair...  8.44 us
    ppermute x12, waiting for transfers between devices, swap(): return lax.ppermute(value, axis, [(i, i ^ distance) for i in range(count)])  5.32 us
    pallas_call x1, Pallas kernels, on_device(): call(functools.partial(load_kernel, chunk, tile), (sds((rhs, depth), f32)...  4.94 us
    pallas_call x1, Pallas kernels, on_device(): call(functools.partial(fine_kernel, own, rows, begin, chunk, tile, pairs)...  2.88 us
    pallas_call x1, Pallas kernels, on_device(): call(functools.partial(pack_kernel, own, rows, pad), [sds((begin + halo *...  1.07 us
    pallas_call x1, Pallas kernels, on_device(): call(functools.partial(stage_kernel, own, rows), (sds(residual.shape, f32...  0.93 us
  transfers between devices with their start and end apart: 12, of which 6 were waited for; matrix products, arithmetic and copies ran while one was open for 0% of the time, Pallas kernels for 38%

profile of v8, /device:TPU:0, one launch (start us, length us, event | category | flops | bytes accessed | tf_op | source)
XLA Modules:
  0.0 37.4 jit_solution(8338242040109319528)
XLA Ops:
  0.0 0.5 %collective-permute-start.1 = (f32[8,3072]{1,0:T(8,128)}, f32[8,3072]{1,0:T(8,128)S(1)}, u32[]{:S(2)}, u32[]{:S(2)}) collective-permute-start(f32[8,3072]{1,0:T(8,128)} %residual_hbm.1), channel_id=1, source_target_pairs={{0,1},{1,0},{2,3},{3,2},{4,5},{5,4},{6,7},{7,6},{8,9},{9,8},{10,11... | collective-permute-start | bytes 294920 | tf_op jit(solution)/shard_map/ppermute | solution.py:306
  0.5 0.1 collective-permute-start
  0.5 0.9 %shard_map.55 = (f32[8,3072]{1,0:T(8,128)S(1)}, f32[48,128]{1,0:T(8,128)S(1)}, f32[1,24]{1,0:T(1,128)S(1)}) custom-call(f32[8,3072]{1,0:T(8,128)} %residual_hbm.1, s32[1,24]{1,0:T(1,128)} %bitcast.2), custom_call_target="tpu_custom_call" | custom-call | bytes 196608 | tf_op jit(solution)/shard_map/pallas_call | solution.py:335
  1.5 0.3 collective-permute-done.near_names
  1.7 0.0 collective-permute-done.1.near
  1.7 1.1 %shard_map.56 = (f32[168,128]{1,0:T(8,128)S(1)}, f32[168,128]{1,0:T(8,128)S(1)}, f32[168,128]{1,0:T(8,128)S(1)}, f32[168,128]{1,0:T(8,128)S(1)}, s32[8,128]{1,0:T(8,128)S(1)}) custom-call(s32[8,8]{1,0:T(8,128)} %margin_hbm.3, f32[8,3072]{1,0:T(8,128)S(1)} %get-tuple-element.29.residual, f32[48,128]{1,0:T(8,128)S(1)} %get-tuple-element.30.mine, ...), custom_call_target="tpu_custom_call" | custom-call | tf_op jit(solution)/shard_map/pallas_call | solution.py:347
  2.8 2.8 %collective-permute-start.2 = (f32[168,128]{1,0:T(8,128)S(1)}, f32[168,128]{1,0:T(8,128)S(1)}, u32[]{:S(2)}, u32[]{:S(2)}) collective-permute-start(f32[168,128]{1,0:T(8,128)S(1)} %get-tuple-element.37), channel_id=1, source_target_pairs={{0,2},{1,3},{2,0},{3,1},{4,6},{5,7},{6,4},{7,5},{8,10},{9,11},{10,... | collective-permute-start | bytes 258056 | tf_op jit(solution)/shard_map/ppermute | solution.py:306
  5.6 1.5 %collective-permute-start.3 = (f32[168,128]{1,0:T(8,128)S(1)}, f32[168,128]{1,0:T(8,128)S(1)}, u32[]{:S(2)}, u32[]{:S(2)}) collective-permute-start(f32[168,128]{1,0:T(8,128)S(1)} %get-tuple-element.38), channel_id=1, source_target_pairs={{0,4},{1,5},{2,6},{3,7},{4,0},{5,1},{6,2},{7,3},{8,12},{9,13},{10,... | collective-permute-start | bytes 258056 | tf_op jit(solution)/shard_map/ppermute | solution.py:306
  7.1 0.0 collective-permute-start.4
  7.1 4.9 %shard_map.57 = (f32[8,1024]{1,0:T(8,128)S(1)}, bf16[1,1024,4096]{2,1,0:T(8,128)(2,1)S(1)}, bf16[256,8192]{1,0:T(8,128)(2,1)S(1)}) custom-call(f32[8,3072]{1,0:T(8,128)S(1)} %get-tuple-element.29.residual, bf16[1,1024,4096]{2,1,0:T(8,128)(2,1)} %fine_hbm.1, bf16[1024,8192]{1,0:T(8,128)(2,1)} %factor_hbm.1, f32[168,128]{1,0:T(8,128)S(1)} %get-tuple-element.32.after.refs_0_), custom_call_target="tpu_custom_call" | custom-call | flops 50331648 | bytes 12582912 | tf_op jit(solution)/shard_map/pallas_call | solution.py:361
  12.1 0.0 collective-permute-done.2.refs_1_
  12.1 0.0 collective-permute-done.3.refs_2_
  12.1 0.4 %collective-permute-done.4.refs_3_ = f32[168,128]{1,0:T(8,128)S(1)} collective-permute-done((f32[168,128]{1,0:T(8,128)S(1)}, f32[168,128]{1,0:T(8,128)S(1)}, u32[]{:S(2)}, u32[]{:S(2)}) %collective-permute-start.4) | collective-permute-done | bytes 86048 | tf_op jit(solution)/shard_map/ppermute | solution.py:306
  12.5 2.9 %shard_map.58 = (f32[64,128]{1,0:T(8,128)S(1)}, f32[64,128]{1,0:T(8,128)S(1)}, f32[64,128]{1,0:T(8,128)S(1)}, f32[64,128]{1,0:T(8,128)S(1)}, bf16[256,8192]{1,0:T(8,128)(2,1)S(1)}) custom-call(s32[8,128]{1,0:T(8,128)S(1)} %get-tuple-element.34.away, f32[8,1024]{1,0:T(8,128)S(1)} %get-tuple-element.35.begun, ...), custom_call_target="tpu_custom_call" | custom-call | flops 134217728 | bytes 12582912 | tf_op jit(solution)/shard_map/pallas_call | solution.py:377
  15.4 1.7 %collective-permute-start.5 = (f32[64,128]{1,0:T(8,128)S(1)}, f32[64,128]{1,0:T(8,128)S(1)}, u32[]{:S(2)}, u32[]{:S(2)}) collective-permute-start(f32[64,128]{1,0:T(8,128)S(1)} %get-tuple-element.44), channel_id=1, source_target_pairs={{0,8},{8,0},{16,24},{24,16},{1,9},{9,1},{17,25},{25,17},{2,10},{10... | collective-permute-start | bytes 98312 | tf_op jit(solution)/shard_map/ppermute | solution.py:306
  17.1 2.6 %collective-permute-start.6 = (f32[64,128]{1,0:T(8,128)S(1)}, f32[64,128]{1,0:T(8,128)S(1)}, u32[]{:S(2)}, u32[]{:S(2)}) collective-permute-start(f32[64,128]{1,0:T(8,128)S(1)} %get-tuple-element.45), channel_id=1, source_target_pairs={{0,16},{8,24},{16,0},{24,8},{1,17},{9,25},{17,1},{25,9},{2,18},{10... | collective-permute-start | bytes 98312 | tf_op jit(solution)/shard_map/ppermute | solution.py:306
  19.7 0.1 collective-permute-start.7
  19.8 8.4 %shard_map.59 = (f32[8,48,128]{2,1,0:T(8,128)S(1)}, s32[192,128]{1,0:T(8,128)S(1)}) custom-call(s32[8,8]{1,0:T(8,128)} %margin_hbm.3, bf16[256,8192]{1,0:T(8,128)(2,1)S(1)} %get-tuple-element.33.upper, bf16[256,8192]{1,0:T(8,128)(2,1)S(1)} %get-tuple-element.40.middle, bf16[1024,8192]{1,0:T(8,128)(2,1)} %factor_hbm.1, ...), custom_call_target="tpu_custom_call" | custom-call | flops 67108864 | bytes 16777216 | tf_op jit(solution)/shard_map/pallas_call | solution.py:389
  28.3 0.0 collective-permute-done.5.refs_1_
  28.3 0.0 collective-permute-done.6.refs_2_
  28.3 0.0 collective-permute-done.7.refs_3_
  28.3 0.1 shard_map.60
  28.5 0.1 collective-permute-start.8
  28.5 1.3 %collective-permute-done.8.arrived = f32[4,48,128]{2,1,0:T(8,128)S(1)} collective-permute-done((f32[4,48,128]{2,1,0:T(8,128)S(1)}, f32[4,48,128]{2,1,0:T(8,128)S(1)}, u32[]{:S(2)}, u32[]{:S(2)}) %collective-permute-start.8) | collective-permute-done | bytes 98336 | tf_op jit(solution)/shard_map/ppermute | solution.py:306
  29.8 2.6 %collective-permute-start.9 = (f32[48,128]{1,0:T(8,128)S(1)}, f32[48,128]{1,0:T(8,128)S(1)}, u32[]{:S(2)}, u32[]{:S(2)}) collective-permute-start(f32[48,128]{1,0:T(8,128)S(1)} %get-tuple-element.49), channel_id=1, source_target_pairs={{0,6},{1,7},{2,4},{3,5},{4,2},{5,3},{6,0},{7,1},{8,14},{9,15},{10,... | collective-permute-start | bytes 73736 | tf_op jit(solution)/shard_map/ppermute | solution.py:306
  32.4 0.5 %collective-permute-start.10 = (f32[48,128]{1,0:T(8,128)S(1)}, f32[48,128]{1,0:T(8,128)S(1)}, u32[]{:S(2)}, u32[]{:S(2)}) collective-permute-start(f32[48,128]{1,0:T(8,128)S(1)} %get-tuple-element.50), channel_id=1, source_target_pairs={{0,4},{1,5},{2,6},{3,7},{4,0},{5,1},{6,2},{7,3},{8,12},{9,13},{10,... | collective-permute-start | bytes 73736 | tf_op jit(solution)/shard_map/ppermute | solution.py:306
  32.9 0.5 %collective-permute-start.11 = (f32[48,128]{1,0:T(8,128)S(1)}, f32[48,128]{1,0:T(8,128)S(1)}, u32[]{:S(2)}, u32[]{:S(2)}) collective-permute-start(f32[48,128]{1,0:T(8,128)S(1)} %get-tuple-element.51), channel_id=1, source_target_pairs={{0,2},{1,3},{2,0},{3,1},{4,6},{5,7},{6,4},{7,5},{8,10},{9,11},{10,... | collective-permute-start | bytes 73736 | tf_op jit(solution)/shard_map/ppermute | solution.py:306
  33.4 1.2 %collective-permute-done.9.refs_0_ = f32[48,128]{1,0:T(8,128)S(1)} collective-permute-done((f32[48,128]{1,0:T(8,128)S(1)}, f32[48,128]{1,0:T(8,128)S(1)}, u32[]{:S(2)}, u32[]{:S(2)}) %collective-permute-start.9) | collective-permute-done | bytes 24608 | tf_op jit(solution)/shard_map/ppermute | solution.py:306
  34.6 1.6 %collective-permute-done.10.refs_1_ = f32[48,128]{1,0:T(8,128)S(1)} collective-permute-done((f32[48,128]{1,0:T(8,128)S(1)}, f32[48,128]{1,0:T(8,128)S(1)}, u32[]{:S(2)}, u32[]{:S(2)}) %collective-permute-start.10) | collective-permute-done | bytes 24608 | tf_op jit(solution)/shard_map/ppermute | solution.py:306
  36.3 0.5 %collective-permute-done.11.refs_2_ = f32[48,128]{1,0:T(8,128)S(1)} collective-permute-done((f32[48,128]{1,0:T(8,128)S(1)}, f32[48,128]{1,0:T(8,128)S(1)}, u32[]{:S(2)}, u32[]{:S(2)}) %collective-permute-start.11) | collective-permute-done | bytes 24608 | tf_op jit(solution)/shard_map/ppermute | solution.py:306
  36.8 0.6 %shard_map.62 = f32[2,3072]{1,0:T(2,128)} custom-call(f32[48,128]{1,0:T(8,128)S(1)} %collective-permute-done.9.refs_0_, f32[48,128]{1,0:T(8,128)S(1)} %collective-permute-done.10.refs_1_, f32[48,128]{1,0:T(8,128)S(1)} %collective-permute-done.11.refs_2_, f32[48,128]{1,0:T(8,128)S(1)} %get-tuple-element.52.refs_3_), custom_call_target="tpu_custom_call" | custom-call | tf_op jit(solution)/shard_map/pallas_call | solution.py:415
  (1 shorter events, 0.0 us)
Async XLA Ops:
  0.0 1.7 %collective-permute-start.1 = (f32[8,3072]{1,0:T(8,128)}, f32[8,3072]{1,0:T(8,128)S(1)}, u32[]{:S(2)}, u32[]{:S(2)}) collective-permute-start(f32[8,3072]{1,0:T(8,128)} %residual_hbm.1), channel_id=1, source_target_pairs={{0,1},{1,0},{2,3},{3,2},{4,5},{5,4},{6,7},{7,6},{8,9},{9,8},{10,11... | collective-permute-start | bytes 294920 | tf_op jit(solution)/shard_map/ppermute | solution.py:306
  0.5 1.3 %collective-permute-start = (s32[1,24]{1,0:T(1,128)}, s32[1,24]{1,0:T(1,128)S(1)}, u32[]{:S(2)}, u32[]{:S(2)}) collective-permute-start(s32[1,24]{1,0:T(1,128)} %bitcast.1), channel_id=1, source_target_pairs={{0,1},{1,0},{2,3},{3,2},{4,5},{5,4},{6,7},{7,6},{8,9},{9,8},{10,11... | collective-permute-start | bytes 296 | tf_op jit(solution)/shard_map/ppermute | solution.py:306
  2.8 9.3 %collective-permute-start.2 = (f32[168,128]{1,0:T(8,128)S(1)}, f32[168,128]{1,0:T(8,128)S(1)}, u32[]{:S(2)}, u32[]{:S(2)}) collective-permute-start(f32[168,128]{1,0:T(8,128)S(1)} %get-tuple-element.37), channel_id=1, source_target_pairs={{0,2},{1,3},{2,0},{3,1},{4,6},{5,7},{6,4},{7,5},{8,10},{9,11},{10,... | collective-permute-start | bytes 258056 | tf_op jit(solution)/shard_map/ppermute | solution.py:306
  5.6 6.5 %collective-permute-start.3 = (f32[168,128]{1,0:T(8,128)S(1)}, f32[168,128]{1,0:T(8,128)S(1)}, u32[]{:S(2)}, u32[]{:S(2)}) collective-permute-start(f32[168,128]{1,0:T(8,128)S(1)} %get-tuple-element.38), channel_id=1, source_target_pairs={{0,4},{1,5},{2,6},{3,7},{4,0},{5,1},{6,2},{7,3},{8,12},{9,13},{10,... | collective-permute-start | bytes 258056 | tf_op jit(solution)/shard_map/ppermute | solution.py:306
  7.1 5.4 %collective-permute-start.4 = (f32[168,128]{1,0:T(8,128)S(1)}, f32[168,128]{1,0:T(8,128)S(1)}, u32[]{:S(2)}, u32[]{:S(2)}) collective-permute-start(f32[168,128]{1,0:T(8,128)S(1)} %get-tuple-element.39), channel_id=1, source_target_pairs={{0,6},{1,7},{2,4},{3,5},{4,2},{5,3},{6,0},{7,1},{8,14},{9,15},{10,... | collective-permute-start | bytes 258056 | tf_op jit(solution)/shard_map/ppermute | solution.py:306
  15.4 12.9 %collective-permute-start.5 = (f32[64,128]{1,0:T(8,128)S(1)}, f32[64,128]{1,0:T(8,128)S(1)}, u32[]{:S(2)}, u32[]{:S(2)}) collective-permute-start(f32[64,128]{1,0:T(8,128)S(1)} %get-tuple-element.44), channel_id=1, source_target_pairs={{0,8},{8,0},{16,24},{24,16},{1,9},{9,1},{17,25},{25,17},{2,10},{10... | collective-permute-start | bytes 98312 | tf_op jit(solution)/shard_map/ppermute | solution.py:306
  17.1 11.2 %collective-permute-start.6 = (f32[64,128]{1,0:T(8,128)S(1)}, f32[64,128]{1,0:T(8,128)S(1)}, u32[]{:S(2)}, u32[]{:S(2)}) collective-permute-start(f32[64,128]{1,0:T(8,128)S(1)} %get-tuple-element.45), channel_id=1, source_target_pairs={{0,16},{8,24},{16,0},{24,8},{1,17},{9,25},{17,1},{25,9},{2,18},{10... | collective-permute-start | bytes 98312 | tf_op jit(solution)/shard_map/ppermute | solution.py:306
  19.7 8.6 %collective-permute-start.7 = (f32[64,128]{1,0:T(8,128)S(1)}, f32[64,128]{1,0:T(8,128)S(1)}, u32[]{:S(2)}, u32[]{:S(2)}) collective-permute-start(f32[64,128]{1,0:T(8,128)S(1)} %get-tuple-element.46), channel_id=1, source_target_pairs={{0,24},{8,16},{16,8},{24,0},{1,25},{9,17},{17,9},{25,1},{2,26},{10... | collective-permute-start | bytes 98312 | tf_op jit(solution)/shard_map/ppermute | solution.py:306
  28.5 1.4 %collective-permute-start.8 = (f32[4,48,128]{2,1,0:T(8,128)S(1)}, f32[4,48,128]{2,1,0:T(8,128)S(1)}, u32[]{:S(2)}, u32[]{:S(2)}) collective-permute-start(f32[4,48,128]{2,1,0:T(8,128)S(1)} %get-tuple-element.48), channel_id=1, source_target_pairs={{0,1},{1,0},{2,3},{3,2},{4,5},{5,4},{6,7},{7,6},{8,9},{9,8},{10,11... | collective-permute-start | bytes 294920 | tf_op jit(solution)/shard_map/ppermute | solution.py:306
  29.8 4.8 %collective-permute-start.9 = (f32[48,128]{1,0:T(8,128)S(1)}, f32[48,128]{1,0:T(8,128)S(1)}, u32[]{:S(2)}, u32[]{:S(2)}) collective-permute-start(f32[48,128]{1,0:T(8,128)S(1)} %get-tuple-element.49), channel_id=1, source_target_pairs={{0,6},{1,7},{2,4},{3,5},{4,2},{5,3},{6,0},{7,1},{8,14},{9,15},{10,... | collective-permute-start | bytes 73736 | tf_op jit(solution)/shard_map/ppermute | solution.py:306
  32.4 3.8 %collective-permute-start.10 = (f32[48,128]{1,0:T(8,128)S(1)}, f32[48,128]{1,0:T(8,128)S(1)}, u32[]{:S(2)}, u32[]{:S(2)}) collective-permute-start(f32[48,128]{1,0:T(8,128)S(1)} %get-tuple-element.50), channel_id=1, source_target_pairs={{0,4},{1,5},{2,6},{3,7},{4,0},{5,1},{6,2},{7,3},{8,12},{9,13},{10,... | collective-permute-start | bytes 73736 | tf_op jit(solution)/shard_map/ppermute | solution.py:306
  32.9 3.8 %collective-permute-start.11 = (f32[48,128]{1,0:T(8,128)S(1)}, f32[48,128]{1,0:T(8,128)S(1)}, u32[]{:S(2)}, u32[]{:S(2)}) collective-permute-start(f32[48,128]{1,0:T(8,128)S(1)} %get-tuple-element.51), channel_id=1, source_target_pairs={{0,2},{1,3},{2,0},{3,1},{4,6},{5,7},{6,4},{7,5},{8,10},{9,11},{10,... | collective-permute-start | bytes 73736 | tf_op jit(solution)/shard_map/ppermute | solution.py:306

commit v9 on v8

--- a/solution.py
+++ b/solution.py
@@ -105,11 +105,11 @@
         copy.start()
 
 
-def first_product(factor, right, tile, turned=False):
-    parts = []
-    for n in range(factor.shape[0] // tile):
-        rows = factor[n * tile : (n + 1) * tile, :]
-        parts.append(mm(rows, right, NT).T if turned else mm(right, rows, NT))
+def first_product(factor, right, tile):
+    tile = min(tile, factor.shape[0])
+    parts = [
+        mm(right, factor[n * tile : (n + 1) * tile, :], NT) for n in range(factor.shape[0] // tile)
+    ]
     return jnp.concatenate(parts, axis=1)
 
 
@@ -145,7 +145,7 @@
 
 
 def fine_kernel(own, rows, begin, chunk, tile, pairs, away, begun, factor, coarse_hbm, *refs):
-    arrived = refs[:pairs]
+    arrived = refs[:pairs][::-1]
     *outs, coarse, table, sems = refs[pairs:]
     done = coarse_hbm.shape[0] // 4
     copies = panel_copies(coarse_hbm, coarse, chunk, sems, done)
@@ -223,7 +223,7 @@
     ).astype(jnp.bfloat16)
     field[...] = member.astype(jnp.float32)
     begun[:, : upper.shape[0]] = first_product(upper, right, tile)
-    begun[:, upper.shape[0] : done] = first_product(middle, right, tile, True)
+    begun[:, upper.shape[0] : done] = first_product(middle, right, tile)
     place[...] = jnp.zeros(place.shape, jnp.int32)
 
     @in_own_block
@@ -239,11 +239,7 @@
         right = jnp.concatenate(
             [table[pl.ds(j, rows, stride=coarse), :] for j in range(coarse)], axis=1
         ).astype(jnp.bfloat16)
-        half = lower.shape[0] // 2
-        low = [
-            first_product(lower.at[pl.ds(i * half, half)], right, tile, i == 1) for i in range(2)
-        ]
-        low = jnp.concatenate(low, axis=1).astype(jnp.bfloat16)
+        low = first_product(lower, right, tile).astype(jnp.bfloat16)
         mid = begun[...].astype(jnp.bfloat16)
         high = mid[:, : upper.shape[0]]
         mid = mid[:, upper.shape[0] :]
@@ -356,7 +352,7 @@
     )(margin, held, mine, names, near_names, near)
     arrived = exchange(outgoing, "sub", 2)
     quarter = coarse_depth // 4
-    tile, coarse_tile = min(256, depth // 2), min(256, quarter)
+    tile = min(512, depth // 2)
     chunk = depth // 8
     begun, local_factor, coarse_upper = call(
         functools.partial(load_kernel, chunk, tile),
@@ -382,12 +378,12 @@
         [pltpu.VMEM((rhs * blocks, BLK), f32), pltpu.SemaphoreType.DMA((quarter // chunk,))],
         flops=4 * rhs * depth * width,
         moved=2 * depth * width + 2 * quarter * coarse_width,
-    )(away, begun, local_factor, coarse_factor, *arrived)
+    )(away, begun, local_factor, coarse_factor, *arrived[::-1])
     panels = exchange(fine, "grp")
     lower = coarse_depth - 2 * quarter
     size = own * rows
     spread, place = call(
-        functools.partial(coarse_kernel, own, rows, chunk, coarse_tile, pairs),
+        functools.partial(coarse_kernel, own, rows, chunk, tile, pairs),
         (sds((2 * pairs, size, BLK), f32), sds((2 * pairs * own, BLK), jnp.int32)),
         [HBM, VMEM, VMEM, HBM] + [VMEM] * pairs,
         [

time: 37.6 us -> 37.5 us (level)
  transfers between devices with their start and end apart: 12 -> 12, of which waited for: 6 -> 5; matrix products, arithmetic and copies ran while one was open for 0% -> 0% of each run, Pallas kernels for 38% -> 38%
where the time goes in v9:
time: 37.5 us; the launch traced here: 37.3 us
  Pallas kernels  18.9 us (50%)
  starting transfers between devices  13.2 us (35%)
  waiting for transfers between devices  5.07 us (14%)
    ppermute x12, starting transfers between devices, swap(): return lax.ppermute(value, axis, [(i, i ^ distance) for i in range(count)])  13.2 us
    pallas_call x1, Pallas kernels, on_device(): call(functools.partial(coarse_kernel, own, rows, chunk, tile, pairs), (sd...  8.31 us
    ppermute x12, waiting for transfers between devices, swap(): return lax.ppermute(value, axis, [(i, i ^ distance) for i in range(count)])  5.07 us
    pallas_call x1, Pallas kernels, on_device(): call(functools.partial(load_kernel, chunk, tile), (sds((rhs, depth), f32)...  4.94 us
    pallas_call x1, Pallas kernels, on_device(): call(functools.partial(fine_kernel, own, rows, begin, chunk, tile, pairs)...  2.89 us
    pallas_call x1, Pallas kernels, on_device(): call(functools.partial(pack_kernel, own, rows, pad), [sds((begin + halo *...  1.07 us
    pallas_call x1, Pallas kernels, on_device(): call(functools.partial(stage_kernel, own, rows), (sds(residual.shape, f32...  0.93 us
  transfers between devices with their start and end apart: 12, of which 5 were waited for; matrix products, arithmetic and copies ran while one was open for 0% of the time, Pallas kernels for 38%

profile of v9, /device:TPU:0, one launch (start us, length us, event | category | flops | bytes accessed | tf_op | source)
XLA Modules:
  0.0 37.3 jit_solution(14330866693662566246)
XLA Ops:
  0.0 0.5 %collective-permute-start.1 = (f32[8,3072]{1,0:T(8,128)}, f32[8,3072]{1,0:T(8,128)S(1)}, u32[]{:S(2)}, u32[]{:S(2)}) collective-permute-start(f32[8,3072]{1,0:T(8,128)} %residual_hbm.1), channel_id=1, source_target_pairs={{0,1},{1,0},{2,3},{3,2},{4,5},{5,4},{6,7},{7,6},{8,9},{9,8},{10,11... | collective-permute-start | bytes 294920 | tf_op jit(solution)/shard_map/ppermute | solution.py:302
  0.5 0.1 collective-permute-start
  0.5 0.9 %shard_map.55 = (f32[8,3072]{1,0:T(8,128)S(1)}, f32[48,128]{1,0:T(8,128)S(1)}, f32[1,24]{1,0:T(1,128)S(1)}) custom-call(f32[8,3072]{1,0:T(8,128)} %residual_hbm.1, s32[1,24]{1,0:T(1,128)} %bitcast.2), custom_call_target="tpu_custom_call" | custom-call | bytes 196608 | tf_op jit(solution)/shard_map/pallas_call | solution.py:331
  1.5 0.3 collective-permute-done.near_names
  1.7 0.0 collective-permute-done.1.near
  1.7 1.1 %shard_map.56 = (f32[168,128]{1,0:T(8,128)S(1)}, f32[168,128]{1,0:T(8,128)S(1)}, f32[168,128]{1,0:T(8,128)S(1)}, f32[168,128]{1,0:T(8,128)S(1)}, s32[8,128]{1,0:T(8,128)S(1)}) custom-call(s32[8,8]{1,0:T(8,128)} %margin_hbm.3, f32[8,3072]{1,0:T(8,128)S(1)} %get-tuple-element.29.residual, f32[48,128]{1,0:T(8,128)S(1)} %get-tuple-element.30.mine, ...), custom_call_target="tpu_custom_call" | custom-call | tf_op jit(solution)/shard_map/pallas_call | solution.py:343
  2.8 3.8 %collective-permute-start.2 = (f32[168,128]{1,0:T(8,128)S(1)}, f32[168,128]{1,0:T(8,128)S(1)}, u32[]{:S(2)}, u32[]{:S(2)}) collective-permute-start(f32[168,128]{1,0:T(8,128)S(1)} %get-tuple-element.37), channel_id=1, source_target_pairs={{0,6},{1,7},{2,4},{3,5},{4,2},{5,3},{6,0},{7,1},{8,14},{9,15},{10,... | collective-permute-start | bytes 258056 | tf_op jit(solution)/shard_map/ppermute | solution.py:302
  6.6 0.5 %collective-permute-start.3 = (f32[168,128]{1,0:T(8,128)S(1)}, f32[168,128]{1,0:T(8,128)S(1)}, u32[]{:S(2)}, u32[]{:S(2)}) collective-permute-start(f32[168,128]{1,0:T(8,128)S(1)} %get-tuple-element.38), channel_id=1, source_target_pairs={{0,4},{1,5},{2,6},{3,7},{4,0},{5,1},{6,2},{7,3},{8,12},{9,13},{10,... | collective-permute-start | bytes 258056 | tf_op jit(solution)/shard_map/ppermute | solution.py:302
  7.1 0.1 collective-permute-start.4
  7.2 4.9 %shard_map.57 = (f32[8,1024]{1,0:T(8,128)S(1)}, bf16[1,1024,4096]{2,1,0:T(8,128)(2,1)S(1)}, bf16[256,8192]{1,0:T(8,128)(2,1)S(1)}) custom-call(f32[8,3072]{1,0:T(8,128)S(1)} %get-tuple-element.29.residual, bf16[1,1024,4096]{2,1,0:T(8,128)(2,1)} %fine_hbm.1, bf16[1024,8192]{1,0:T(8,128)(2,1)} %factor_hbm.1, f32[168,128]{1,0:T(8,128)S(1)} %get-tuple-element.32.after.refs_3_.refs_0_), custom_call_target="tpu_custom_call" | custom-call | flops 50331648 | bytes 12582912 | tf_op jit(solution)/shard_map/pallas_call | solution.py:357
  12.1 0.0 collective-permute-done.2.refs_0_.refs_3_
  12.2 0.0 collective-permute-done.3.refs_1_.refs_2_
  12.2 0.0 collective-permute-done.4.refs_2_.refs_1_
  12.2 2.9 %shard_map.58 = (f32[64,128]{1,0:T(8,128)S(1)}, f32[64,128]{1,0:T(8,128)S(1)}, f32[64,128]{1,0:T(8,128)S(1)}, f32[64,128]{1,0:T(8,128)S(1)}, bf16[256,8192]{1,0:T(8,128)(2,1)S(1)}) custom-call(s32[8,128]{1,0:T(8,128)S(1)} %get-tuple-element.34.away, f32[8,1024]{1,0:T(8,128)S(1)} %get-tuple-element.35.begun, ...), custom_call_target="tpu_custom_call" | custom-call | flops 134217728 | bytes 12582912 | tf_op jit(solution)/shard_map/pallas_call | solution.py:373
  15.1 2.0 %collective-permute-start.5 = (f32[64,128]{1,0:T(8,128)S(1)}, f32[64,128]{1,0:T(8,128)S(1)}, u32[]{:S(2)}, u32[]{:S(2)}) collective-permute-start(f32[64,128]{1,0:T(8,128)S(1)} %get-tuple-element.44), channel_id=1, source_target_pairs={{0,8},{8,0},{16,24},{24,16},{1,9},{9,1},{17,25},{25,17},{2,10},{10... | collective-permute-start | bytes 98312 | tf_op jit(solution)/shard_map/ppermute | solution.py:302
  17.1 2.6 %collective-permute-start.6 = (f32[64,128]{1,0:T(8,128)S(1)}, f32[64,128]{1,0:T(8,128)S(1)}, u32[]{:S(2)}, u32[]{:S(2)}) collective-permute-start(f32[64,128]{1,0:T(8,128)S(1)} %get-tuple-element.45), channel_id=1, source_target_pairs={{0,16},{8,24},{16,0},{24,8},{1,17},{9,25},{17,1},{25,9},{2,18},{10... | collective-permute-start | bytes 98312 | tf_op jit(solution)/shard_map/ppermute | solution.py:302
  19.7 0.0 collective-permute-start.7
  19.7 8.3 %shard_map.59 = (f32[8,48,128]{2,1,0:T(8,128)S(1)}, s32[192,128]{1,0:T(8,128)S(1)}) custom-call(s32[8,8]{1,0:T(8,128)} %margin_hbm.3, bf16[256,8192]{1,0:T(8,128)(2,1)S(1)} %get-tuple-element.33.upper, bf16[256,8192]{1,0:T(8,128)(2,1)S(1)} %get-tuple-element.40.middle, bf16[1024,8192]{1,0:T(8,128)(2,1)} %factor_hbm.1, ...), custom_call_target="tpu_custom_call" | custom-call | flops 67108864 | bytes 16777216 | tf_op jit(solution)/shard_map/pallas_call | solution.py:385
  28.0 0.0 collective-permute-done.5.refs_1_
  28.0 0.0 collective-permute-done.6.refs_2_
  28.0 0.0 collective-permute-done.7.refs_3_
  28.1 0.1 shard_map.60
  28.2 0.1 collective-permute-start.8
  28.3 1.3 %collective-permute-done.8.arrived = f32[4,48,128]{2,1,0:T(8,128)S(1)} collective-permute-done((f32[4,48,128]{2,1,0:T(8,128)S(1)}, f32[4,48,128]{2,1,0:T(8,128)S(1)}, u32[]{:S(2)}, u32[]{:S(2)}) %collective-permute-start.8) | collective-permute-done | bytes 98336 | tf_op jit(solution)/shard_map/ppermute | solution.py:302
  29.6 2.7 %collective-permute-start.9 = (f32[48,128]{1,0:T(8,128)S(1)}, f32[48,128]{1,0:T(8,128)S(1)}, u32[]{:S(2)}, u32[]{:S(2)}) collective-permute-start(f32[48,128]{1,0:T(8,128)S(1)} %get-tuple-element.49), channel_id=1, source_target_pairs={{0,6},{1,7},{2,4},{3,5},{4,2},{5,3},{6,0},{7,1},{8,14},{9,15},{10,... | collective-permute-start | bytes 73736 | tf_op jit(solution)/shard_map/ppermute | solution.py:302
  32.3 0.5 %collective-permute-start.10 = (f32[48,128]{1,0:T(8,128)S(1)}, f32[48,128]{1,0:T(8,128)S(1)}, u32[]{:S(2)}, u32[]{:S(2)}) collective-permute-start(f32[48,128]{1,0:T(8,128)S(1)} %get-tuple-element.50), channel_id=1, source_target_pairs={{0,4},{1,5},{2,6},{3,7},{4,0},{5,1},{6,2},{7,3},{8,12},{9,13},{10,... | collective-permute-start | bytes 73736 | tf_op jit(solution)/shard_map/ppermute | solution.py:302
  32.8 0.3 collective-permute-start.11
  33.1 1.2 %collective-permute-done.9.refs_0_ = f32[48,128]{1,0:T(8,128)S(1)} collective-permute-done((f32[48,128]{1,0:T(8,128)S(1)}, f32[48,128]{1,0:T(8,128)S(1)}, u32[]{:S(2)}, u32[]{:S(2)}) %collective-permute-start.9) | collective-permute-done | bytes 24608 | tf_op jit(solution)/shard_map/ppermute | solution.py:302
  34.4 1.8 %collective-permute-done.10.refs_1_ = f32[48,128]{1,0:T(8,128)S(1)} collective-permute-done((f32[48,128]{1,0:T(8,128)S(1)}, f32[48,128]{1,0:T(8,128)S(1)}, u32[]{:S(2)}, u32[]{:S(2)}) %collective-permute-start.10) | collective-permute-done | bytes 24608 | tf_op jit(solution)/shard_map/ppermute | solution.py:302
  36.1 0.5 %collective-permute-done.11.refs_2_ = f32[48,128]{1,0:T(8,128)S(1)} collective-permute-done((f32[48,128]{1,0:T(8,128)S(1)}, f32[48,128]{1,0:T(8,128)S(1)}, u32[]{:S(2)}, u32[]{:S(2)}) %collective-permute-start.11) | collective-permute-done | bytes 24608 | tf_op jit(solution)/shard_map/ppermute | solution.py:302
  36.6 0.6 %shard_map.62 = f32[2,3072]{1,0:T(2,128)} custom-call(f32[48,128]{1,0:T(8,128)S(1)} %collective-permute-done.9.refs_0_, f32[48,128]{1,0:T(8,128)S(1)} %collective-permute-done.10.refs_1_, f32[48,128]{1,0:T(8,128)S(1)} %collective-permute-done.11.refs_2_, f32[48,128]{1,0:T(8,128)S(1)} %get-tuple-element.52.refs_3_), custom_call_target="tpu_custom_call" | custom-call | tf_op jit(solution)/shard_map/pallas_call | solution.py:411
  (1 shorter events, 0.0 us)
Async XLA Ops:
  0.0 1.7 %collective-permute-start.1 = (f32[8,3072]{1,0:T(8,128)}, f32[8,3072]{1,0:T(8,128)S(1)}, u32[]{:S(2)}, u32[]{:S(2)}) collective-permute-start(f32[8,3072]{1,0:T(8,128)} %residual_hbm.1), channel_id=1, source_target_pairs={{0,1},{1,0},{2,3},{3,2},{4,5},{5,4},{6,7},{7,6},{8,9},{9,8},{10,11... | collective-permute-start | bytes 294920 | tf_op jit(solution)/shard_map/ppermute | solution.py:302
  0.5 1.3 %collective-permute-start = (s32[1,24]{1,0:T(1,128)}, s32[1,24]{1,0:T(1,128)S(1)}, u32[]{:S(2)}, u32[]{:S(2)}) collective-permute-start(s32[1,24]{1,0:T(1,128)} %bitcast.1), channel_id=1, source_target_pairs={{0,1},{1,0},{2,3},{3,2},{4,5},{5,4},{6,7},{7,6},{8,9},{9,8},{10,11... | collective-permute-start | bytes 296 | tf_op jit(solution)/shard_map/ppermute | solution.py:302
  2.8 9.4 %collective-permute-start.2 = (f32[168,128]{1,0:T(8,128)S(1)}, f32[168,128]{1,0:T(8,128)S(1)}, u32[]{:S(2)}, u32[]{:S(2)}) collective-permute-start(f32[168,128]{1,0:T(8,128)S(1)} %get-tuple-element.37), channel_id=1, source_target_pairs={{0,6},{1,7},{2,4},{3,5},{4,2},{5,3},{6,0},{7,1},{8,14},{9,15},{10,... | collective-permute-start | bytes 258056 | tf_op jit(solution)/shard_map/ppermute | solution.py:302
  6.6 5.6 %collective-permute-start.3 = (f32[168,128]{1,0:T(8,128)S(1)}, f32[168,128]{1,0:T(8,128)S(1)}, u32[]{:S(2)}, u32[]{:S(2)}) collective-permute-start(f32[168,128]{1,0:T(8,128)S(1)} %get-tuple-element.38), channel_id=1, source_target_pairs={{0,4},{1,5},{2,6},{3,7},{4,0},{5,1},{6,2},{7,3},{8,12},{9,13},{10,... | collective-permute-start | bytes 258056 | tf_op jit(solution)/shard_map/ppermute | solution.py:302
  7.1 5.1 %collective-permute-start.4 = (f32[168,128]{1,0:T(8,128)S(1)}, f32[168,128]{1,0:T(8,128)S(1)}, u32[]{:S(2)}, u32[]{:S(2)}) collective-permute-start(f32[168,128]{1,0:T(8,128)S(1)} %get-tuple-element.39), channel_id=1, source_target_pairs={{0,2},{1,3},{2,0},{3,1},{4,6},{5,7},{6,4},{7,5},{8,10},{9,11},{10,... | collective-permute-start | bytes 258056 | tf_op jit(solution)/shard_map/ppermute | solution.py:302
  15.1 13.0 %collective-permute-start.5 = (f32[64,128]{1,0:T(8,128)S(1)}, f32[64,128]{1,0:T(8,128)S(1)}, u32[]{:S(2)}, u32[]{:S(2)}) collective-permute-start(f32[64,128]{1,0:T(8,128)S(1)} %get-tuple-element.44), channel_id=1, source_target_pairs={{0,8},{8,0},{16,24},{24,16},{1,9},{9,1},{17,25},{25,17},{2,10},{10... | collective-permute-start | bytes 98312 | tf_op jit(solution)/shard_map/ppermute | solution.py:302
  17.1 10.9 %collective-permute-start.6 = (f32[64,128]{1,0:T(8,128)S(1)}, f32[64,128]{1,0:T(8,128)S(1)}, u32[]{:S(2)}, u32[]{:S(2)}) collective-permute-start(f32[64,128]{1,0:T(8,128)S(1)} %get-tuple-element.45), channel_id=1, source_target_pairs={{0,16},{8,24},{16,0},{24,8},{1,17},{9,25},{17,1},{25,9},{2,18},{10... | collective-permute-start | bytes 98312 | tf_op jit(solution)/shard_map/ppermute | solution.py:302
  19.7 8.3 %collective-permute-start.7 = (f32[64,128]{1,0:T(8,128)S(1)}, f32[64,128]{1,0:T(8,128)S(1)}, u32[]{:S(2)}, u32[]{:S(2)}) collective-permute-start(f32[64,128]{1,0:T(8,128)S(1)} %get-tuple-element.46), channel_id=1, source_target_pairs={{0,24},{8,16},{16,8},{24,0},{1,25},{9,17},{17,9},{25,1},{2,26},{10... | collective-permute-start | bytes 98312 | tf_op jit(solution)/shard_map/ppermute | solution.py:302
  28.2 1.4 %collective-permute-start.8 = (f32[4,48,128]{2,1,0:T(8,128)S(1)}, f32[4,48,128]{2,1,0:T(8,128)S(1)}, u32[]{:S(2)}, u32[]{:S(2)}) collective-permute-start(f32[4,48,128]{2,1,0:T(8,128)S(1)} %get-tuple-element.48), channel_id=1, source_target_pairs={{0,1},{1,0},{2,3},{3,2},{4,5},{5,4},{6,7},{7,6},{8,9},{9,8},{10,11... | collective-permute-start | bytes 294920 | tf_op jit(solution)/shard_map/ppermute | solution.py:302
  29.6 4.8 %collective-permute-start.9 = (f32[48,128]{1,0:T(8,128)S(1)}, f32[48,128]{1,0:T(8,128)S(1)}, u32[]{:S(2)}, u32[]{:S(2)}) collective-permute-start(f32[48,128]{1,0:T(8,128)S(1)} %get-tuple-element.49), channel_id=1, source_target_pairs={{0,6},{1,7},{2,4},{3,5},{4,2},{5,3},{6,0},{7,1},{8,14},{9,15},{10,... | collective-permute-start | bytes 73736 | tf_op jit(solution)/shard_map/ppermute | solution.py:302
  32.3 3.8 %collective-permute-start.10 = (f32[48,128]{1,0:T(8,128)S(1)}, f32[48,128]{1,0:T(8,128)S(1)}, u32[]{:S(2)}, u32[]{:S(2)}) collective-permute-start(f32[48,128]{1,0:T(8,128)S(1)} %get-tuple-element.50), channel_id=1, source_target_pairs={{0,4},{1,5},{2,6},{3,7},{4,0},{5,1},{6,2},{7,3},{8,12},{9,13},{10,... | collective-permute-start | bytes 73736 | tf_op jit(solution)/shard_map/ppermute | solution.py:302
  32.8 3.8 %collective-permute-start.11 = (f32[48,128]{1,0:T(8,128)S(1)}, f32[48,128]{1,0:T(8,128)S(1)}, u32[]{:S(2)}, u32[]{:S(2)}) collective-permute-start(f32[48,128]{1,0:T(8,128)S(1)} %get-tuple-element.51), channel_id=1, source_target_pairs={{0,2},{1,3},{2,0},{3,1},{4,6},{5,7},{6,4},{7,5},{8,10},{9,11},{10,... | collective-permute-start | bytes 73736 | tf_op jit(solution)/shard_map/ppermute | solution.py:302

commit v10 on v9

--- a/solution.py
+++ b/solution.py
@@ -60,7 +60,7 @@
 
 
 def pack_kernel(own, rows, pad, margin_hbm, residual, mine, names, near_names, near, *refs):
-    *outs, away, block_rows, margin, sem = refs
+    *outs, away, place, block_rows, margin, sem = refs
     copy = pltpu.make_async_copy(margin_hbm, margin, sem)
     copy.start()
     halo = margin.shape[1]
@@ -75,10 +75,15 @@
         for i in range(2):
             out[i * size : (i + 1) * size, :] = both[i]
             out[at + i : at + i + 1, :own] = labels[i]
+    place[...] = jnp.zeros(place.shape, jnp.int32)
     copy.wait()
     for k in range(halo):
-        distance = (me ^ (margin[me, k] // own)) // 2
-        away[k : k + 1, :] = jnp.full((1, BLK), distance, jnp.int32)
+        block = margin[me, k]
+        owner = block // own
+        distance = me ^ owner
+        away[k : k + 1, :] = jnp.full((1, BLK), distance // 2, jnp.int32)
+        row = distance * own + block - owner * own
+        place[pl.ds(row, 1), :] = jnp.full((1, BLK), k + 1, jnp.int32)
     for e, out in enumerate(outs):
         target = me ^ (2 * e)
         for k in range(halo):
@@ -144,9 +149,40 @@
         copy.wait()
 
 
+def form_sums(own, rows, coarse, arrived, named, table):
+    size = own * rows
+    sources = 2 * len(arrived)
+    parts = [(part, i) for part in arrived for i in range(2)]
+    names = jnp.concatenate(
+        [part[2 * size + i : 2 * size + i + 1, :] for part, i in parts], axis=0
+    ).T
+    catalog = lax.broadcasted_iota(jnp.int32, (own, coarse), 1).astype(jnp.float32)
+    member = jnp.concatenate(
+        [(names[:own, s : s + 1] == catalog).astype(jnp.float32) for s in range(sources)], axis=0
+    ).astype(jnp.bfloat16)
+    whole = jnp.concatenate(
+        [
+            jnp.concatenate(
+                [part[i * size + r * own : i * size + (r + 1) * own, :] for part, i in parts],
+                axis=0,
+            )
+            for r in range(rows)
+        ],
+        axis=1,
+    )
+    ones = jnp.ones((own * sources, BLK), jnp.bfloat16)
+    span = rows * BLK
+    found = mm(member, jnp.concatenate(split3(whole) + [ones], axis=1), TN)
+    sums = found[:, :span] + found[:, span : 2 * span] + found[:, 2 * span : 3 * span]
+    counts = jnp.maximum(found[:, 3 * span :], 1.0)
+    for r in range(rows):
+        table[r * coarse : (r + 1) * coarse, :] = sums[:, r * BLK : (r + 1) * BLK] / counts
+    named[...] = member.astype(jnp.float32)
+
+
 def fine_kernel(own, rows, begin, chunk, tile, pairs, away, begun, factor, coarse_hbm, *refs):
     arrived = refs[:pairs][::-1]
-    *outs, coarse, table, sems = refs[pairs:]
+    *outs, coarse, named, sums, table, sems = refs[pairs:]
     done = coarse_hbm.shape[0] // 4
     copies = panel_copies(coarse_hbm, coarse, chunk, sems, done)
     start(copies)
@@ -163,6 +199,7 @@
         for e in range(1, pairs):
             part = jnp.where(distance == e, arrived[e][span, :], part)
         tiles.append(part.astype(jnp.bfloat16))
+    form_sums(own, rows, coarse.shape[1] // BLK, arrived, named, sums)
     local = jnp.concatenate(tiles, axis=1)
     far = factor.at[0, :, pl.ds(own * BLK, halo * BLK)]
     mid = (begun[...] + first_product(far, local, tile)).astype(jnp.bfloat16)
@@ -181,65 +218,28 @@
             copy.wait()
 
 
-def coarse_kernel(own, rows, chunk, tile, pairs, margin_hbm, upper, middle, factor_hbm, *refs):
-    arrived = refs[:pairs]
-    out, place, table, lower, begun, field, margin, sem, sems = refs[pairs:]
-    small = pltpu.make_async_copy(margin_hbm, margin, sem)
-    small.start()
+def coarse_kernel(own, rows, chunk, tile, upper, middle, factor_hbm, member, sums, *refs):
+    out, table, lower, begun, sems = refs
     done = upper.shape[0] + middle.shape[0]
     width = upper.shape[1]
     copies = panel_copies(factor_hbm, lower, chunk, sems, done)
     start(copies)
     coarse = width // BLK
-    size = own * rows
-    sources = 2 * pairs
-    parts = [(part, i) for part in arrived for i in range(2)]
-    names = jnp.concatenate(
-        [part[2 * size + i : 2 * size + i + 1, :] for part, i in parts], axis=0
-    ).T
-    catalog = lax.broadcasted_iota(jnp.int32, (own, coarse), 1).astype(jnp.float32)
-    member = jnp.concatenate(
-        [(names[:own, s : s + 1] == catalog).astype(jnp.float32) for s in range(sources)], axis=0
-    ).astype(jnp.bfloat16)
-    whole = jnp.concatenate(
-        [
-            jnp.concatenate(
-                [part[i * size + r * own : i * size + (r + 1) * own, :] for part, i in parts],
-                axis=0,
-            )
-            for r in range(rows)
-        ],
-        axis=1,
-    )
-    ones = jnp.ones((own * sources, BLK), jnp.bfloat16)
     span = rows * BLK
-    found = mm(member, jnp.concatenate(split3(whole) + [ones], axis=1), TN)
-    sums = found[:, :span] + found[:, span : 2 * span] + found[:, 2 * span : 3 * span]
-    counts = jnp.maximum(found[:, 3 * span :], 1.0)
-    for r in range(rows):
-        table[r * coarse : (r + 1) * coarse, :] = sums[:, r * BLK : (r + 1) * BLK] / counts
-    right = jnp.concatenate(
-        [table[pl.ds(j, rows, stride=coarse), :] for j in range(coarse)], axis=1
-    ).astype(jnp.bfloat16)
-    field[...] = member.astype(jnp.float32)
-    begun[:, : upper.shape[0]] = first_product(upper, right, tile)
-    begun[:, upper.shape[0] : done] = first_product(middle, right, tile)
-    place[...] = jnp.zeros(place.shape, jnp.int32)
+
+    def right():
+        parts = [sums[pl.ds(j, rows, stride=coarse), :] for j in range(coarse)]
+        return jnp.concatenate(parts, axis=1).astype(jnp.bfloat16)
+
+    first = right()
+    begun[:, : upper.shape[0]] = first_product(upper, first, tile)
+    begun[:, upper.shape[0] : done] = first_product(middle, first, tile)
 
     @in_own_block
     def _():
-        for copy in copies + [small]:
+        for copy in copies:
             copy.wait()
-        me = lax.axis_index("sub")
-        for k in range(margin.shape[1]):
-            block = margin[me, k]
-            owner = block // own
-            row = (me ^ owner) * own + block - owner * own
-            place[pl.ds(row, 1), :] = jnp.full((1, BLK), k + 1, jnp.int32)
-        right = jnp.concatenate(
-            [table[pl.ds(j, rows, stride=coarse), :] for j in range(coarse)], axis=1
-        ).astype(jnp.bfloat16)
-        low = first_product(lower, right, tile).astype(jnp.bfloat16)
+        low = first_product(lower, right(), tile).astype(jnp.bfloat16)
         mid = begun[...].astype(jnp.bfloat16)
         high = mid[:, : upper.shape[0]]
         mid = mid[:, upper.shape[0] :]
@@ -249,11 +249,10 @@
             for i in range(256 // BLK):
                 j = n * (256 // BLK) + i
                 table[pl.ds(j, rows, stride=coarse), :] = part[:, i * BLK : (i + 1) * BLK]
-        member = field[...].astype(jnp.bfloat16)
         solved = jnp.concatenate([table[r * coarse : (r + 1) * coarse, :] for r in range(rows)], axis=1)
-        spread = mm(member, jnp.concatenate(split3(solved), axis=1))
+        spread = mm(member[...].astype(jnp.bfloat16), jnp.concatenate(split3(solved), axis=1))
         spread = spread[:, :span] + spread[:, span : 2 * span] + spread[:, 2 * span :]
-        for s in range(sources):
+        for s in range(out.shape[0]):
             for r in range(rows):
                 out[s, r * own : (r + 1) * own, :] = spread[
                     s * own : (s + 1) * own, r * BLK : (r + 1) * BLK
@@ -340,9 +339,10 @@
         moved=8 * rhs * own_width,
     )(in_hbm(residual), in_hbm(aggregate))
     margin = in_hbm(margin)
-    *outgoing, away = call(
+    *outgoing, away, place = call(
         functools.partial(pack_kernel, own, rows, pad),
-        [sds((begin + halo * rhs, BLK), f32)] * pairs + [sds((halo, BLK), jnp.int32)],
+        [sds((begin + halo * rhs, BLK), f32)] * pairs
+        + [sds((halo, BLK), jnp.int32), sds((2 * pairs * own, BLK), jnp.int32)],
         [HBM] + [VMEM] * 5,
         [
             pltpu.VMEM((own * rhs, BLK), f32),
@@ -370,10 +370,15 @@
         moved=2 * depth * width + 2 * quarter * coarse_width,
     )(held, local_factor, coarse_factor, arrived[0])
     chunk = quarter // 4
-    *fine, coarse_middle = call(
+    count = coarse_width // BLK
+    *fine, coarse_middle, member, sums = call(
         functools.partial(fine_kernel, own, rows, begin, chunk, tile, pairs),
         [sds((rows * blocks, BLK), f32)] * grp_count
-        + [sds((quarter, coarse_width), coarse_factor.dtype)],
+        + [
+            sds((quarter, coarse_width), coarse_factor.dtype),
+            sds((2 * pairs * own, count), f32),
+            sds((rows * count, BLK), f32),
+        ],
         [VMEM, VMEM, VMEM, HBM] + [VMEM] * pairs,
         [pltpu.VMEM((rhs * blocks, BLK), f32), pltpu.SemaphoreType.DMA((quarter // chunk,))],
         flops=4 * rhs * depth * width,
@@ -382,23 +387,20 @@
     panels = exchange(fine, "grp")
     lower = coarse_depth - 2 * quarter
     size = own * rows
-    spread, place = call(
-        functools.partial(coarse_kernel, own, rows, chunk, tile, pairs),
-        (sds((2 * pairs, size, BLK), f32), sds((2 * pairs * own, BLK), jnp.int32)),
-        [HBM, VMEM, VMEM, HBM] + [VMEM] * pairs,
+    spread = call(
+        functools.partial(coarse_kernel, own, rows, chunk, tile),
+        sds((2 * pairs, size, BLK), f32),
+        [VMEM, VMEM, HBM, VMEM, VMEM],
         [
-            pltpu.VMEM((rows * (coarse_width // BLK), BLK), f32),
+            pltpu.VMEM((rows * count, BLK), f32),
             pltpu.VMEM((lower, coarse_width), coarse_factor.dtype),
             pltpu.VMEM((rows, 2 * quarter), f32),
-            pltpu.VMEM((2 * pairs * own, coarse_width // BLK), f32),
-            pltpu.SMEM(margin.shape, jnp.int32),
-            pltpu.SemaphoreType.DMA,
             pltpu.SemaphoreType.DMA((lower // chunk,)),
         ],
         flops=4 * rows * coarse_depth * coarse_width,
         moved=2 * coarse_depth * coarse_width,
         limit=24 * MIB,
-    )(margin, coarse_upper, coarse_middle, coarse_factor, *arrived)
+    )(coarse_upper, coarse_middle, coarse_factor, member, sums)
     field = sds((pairs, size, BLK), f32)
     kept, crossing = call(
         functools.partial(merge_kernel, own, rows, grp_count, halo),

time: 37.5 us -> 37.7 us (level)
  no operation moved by 1% of the time
where the time goes in v10:
time: 37.7 us; the launch traced here: 37.5 us
  Pallas kernels  19.2 us (51%)
  starting transfers between devices  13.2 us (35%)
  waiting for transfers between devices  5.07 us (13%)
    ppermute x12, starting transfers between devices, swap(): return lax.ppermute(value, axis, [(i, i ^ distance) for i in range(count)])  13.2 us
    pallas_call x1, Pallas kernels, on_device(): call(functools.partial(coarse_kernel, own, rows, chunk, tile), sds((2 * p...  8.26 us
    ppermute x12, waiting for transfers between devices, swap(): return lax.ppermute(value, axis, [(i, i ^ distance) for i in range(count)])  5.07 us
    pallas_call x1, Pallas kernels, on_device(): call(functools.partial(load_kernel, chunk, tile), (sds((rhs, depth), f32)...  4.94 us
    pallas_call x1, Pallas kernels, on_device(): call(functools.partial(fine_kernel, own, rows, begin, chunk, tile, pairs)...  3.17 us
    pallas_call x1, Pallas kernels, on_device(): call(functools.partial(pack_kernel, own, rows, pad), [sds((begin + halo *...  1.08 us
    pallas_call x1, Pallas kernels, on_device(): call(functools.partial(stage_kernel, own, rows), (sds(residual.shape, f32...  0.93 us
  transfers between devices with their start and end apart: 12, of which 5 were waited for; matrix products, arithmetic and copies ran while one was open for 0% of the time, Pallas kernels for 38%

profile of v10, /device:TPU:0, one launch (start us, length us, event | category | flops | bytes accessed | tf_op | source)
XLA Modules:
  0.0 37.5 jit_solution(156207426191586998)
XLA Ops:
  0.0 0.5 %collective-permute-start.1 = (f32[8,3072]{1,0:T(8,128)}, f32[8,3072]{1,0:T(8,128)S(1)}, u32[]{:S(2)}, u32[]{:S(2)}) collective-permute-start(f32[8,3072]{1,0:T(8,128)} %residual_hbm.1), channel_id=1, source_target_pairs={{0,1},{1,0},{2,3},{3,2},{4,5},{5,4},{6,7},{7,6},{8,9},{9,8},{10,11... | collective-permute-start | bytes 294920 | tf_op jit(solution)/shard_map/ppermute | solution.py:301
  0.5 0.1 collective-permute-start
  0.5 0.9 %shard_map.55 = (f32[8,3072]{1,0:T(8,128)S(1)}, f32[48,128]{1,0:T(8,128)S(1)}, f32[1,24]{1,0:T(1,128)S(1)}) custom-call(f32[8,3072]{1,0:T(8,128)} %residual_hbm.1, s32[1,24]{1,0:T(1,128)} %bitcast.2), custom_call_target="tpu_custom_call" | custom-call | bytes 196608 | tf_op jit(solution)/shard_map/pallas_call | solution.py:330
  1.5 0.3 collective-permute-done.near_names
  1.7 0.0 collective-permute-done.1.near
  1.7 1.1 %shard_map.56 = (f32[168,128]{1,0:T(8,128)S(1)}, f32[168,128]{1,0:T(8,128)S(1)}, f32[168,128]{1,0:T(8,128)S(1)}, f32[168,128]{1,0:T(8,128)S(1)}, s32[8,128]{1,0:T(8,128)S(1)}, /*index=5*/s32[192,128]{1,0:T(8,128)S(1)}) custom-call(s32[8,8]{1,0:T(8,128)} %margin_hbm.1, f32[8,3072]{1,0:T(8,128)S(1)} %get-tuple-element.30.residual, ...), custom_call_target="tpu_custom_call" | custom-call | tf_op jit(solution)/shard_map/pallas_call | solution.py:342
  2.8 3.8 %collective-permute-start.2 = (f32[168,128]{1,0:T(8,128)S(1)}, f32[168,128]{1,0:T(8,128)S(1)}, u32[]{:S(2)}, u32[]{:S(2)}) collective-permute-start(f32[168,128]{1,0:T(8,128)S(1)} %get-tuple-element.39), channel_id=1, source_target_pairs={{0,6},{1,7},{2,4},{3,5},{4,2},{5,3},{6,0},{7,1},{8,14},{9,15},{10,... | collective-permute-start | bytes 258056 | tf_op jit(solution)/shard_map/ppermute | solution.py:301
  6.6 0.5 %collective-permute-start.3 = (f32[168,128]{1,0:T(8,128)S(1)}, f32[168,128]{1,0:T(8,128)S(1)}, u32[]{:S(2)}, u32[]{:S(2)}) collective-permute-start(f32[168,128]{1,0:T(8,128)S(1)} %get-tuple-element.40), channel_id=1, source_target_pairs={{0,4},{1,5},{2,6},{3,7},{4,0},{5,1},{6,2},{7,3},{8,12},{9,13},{10,... | collective-permute-start | bytes 258056 | tf_op jit(solution)/shard_map/ppermute | solution.py:301
  7.1 0.1 collective-permute-start.4
  7.2 4.9 %shard_map.57 = (f32[8,1024]{1,0:T(8,128)S(1)}, bf16[1,1024,4096]{2,1,0:T(8,128)(2,1)S(1)}, bf16[256,8192]{1,0:T(8,128)(2,1)S(1)}) custom-call(f32[8,3072]{1,0:T(8,128)S(1)} %get-tuple-element.30.residual, bf16[1,1024,4096]{2,1,0:T(8,128)(2,1)} %fine_hbm.1, bf16[1024,8192]{1,0:T(8,128)(2,1)} %factor_hbm.1, f32[168,128]{1,0:T(8,128)S(1)} %get-tuple-element.34.after.refs_3_), custom_call_target="tpu_custom_call" | custom-call | flops 50331648 | bytes 12582912 | tf_op jit(solution)/shard_map/pallas_call | solution.py:357
  12.2 0.0 collective-permute-done.2.refs_0_
  12.2 0.0 collective-permute-done.3.refs_1_
  12.2 0.0 collective-permute-done.4.refs_2_
  12.2 3.2 %shard_map.58 = (f32[64,128]{1,0:T(8,128)S(1)}, f32[64,128]{1,0:T(8,128)S(1)}, f32[64,128]{1,0:T(8,128)S(1)}, f32[64,128]{1,0:T(8,128)S(1)}, bf16[256,8192]{1,0:...) custom-call(s32[8,128]{1,0:T(8,128)S(1)} %get-tuple-element.36.away, ...), custom_call_target="tpu_custom_call" | custom-call | flops 134217728 | bytes 12582912 | tf_op jit(solution)/shard_map/pallas_call | solution.py:374
  15.4 2.0 %collective-permute-start.5 = (f32[64,128]{1,0:T(8,128)S(1)}, f32[64,128]{1,0:T(8,128)S(1)}, u32[]{:S(2)}, u32[]{:S(2)}) collective-permute-start(f32[64,128]{1,0:T(8,128)S(1)} %get-tuple-element.46), channel_id=1, source_target_pairs={{0,8},{8,0},{16,24},{24,16},{1,9},{9,1},{17,25},{25,17},{2,10},{10... | collective-permute-start | bytes 98312 | tf_op jit(solution)/shard_map/ppermute | solution.py:301
  17.4 2.6 %collective-permute-start.6 = (f32[64,128]{1,0:T(8,128)S(1)}, f32[64,128]{1,0:T(8,128)S(1)}, u32[]{:S(2)}, u32[]{:S(2)}) collective-permute-start(f32[64,128]{1,0:T(8,128)S(1)} %get-tuple-element.47), channel_id=1, source_target_pairs={{0,16},{8,24},{16,0},{24,8},{1,17},{9,25},{17,1},{25,9},{2,18},{10... | collective-permute-start | bytes 98312 | tf_op jit(solution)/shard_map/ppermute | solution.py:301
  20.0 0.0 collective-permute-start.7
  20.0 8.3 %shard_map.59.spread = f32[8,48,128]{2,1,0:T(8,128)S(1)} custom-call(bf16[256,8192]{1,0:T(8,128)(2,1)S(1)} %get-tuple-element.35.upper, bf16[256,8192]{1,0:T(8,128)(2,1)S(1)} %get-tuple-element.42.middle, bf16[1024,8192]{1,0:T(8,128)(2,1)} %factor_hbm.1, f32[192,64]{1,0:T(8,128)S(1)} %get-tuple-element.43.member, f32[128,128]{1,0:T(8,128)S(1)} %get-tuple-element.44.sums), custom_call_target="tpu_custom_call" | custom-call | flops 67108864 | bytes 16777216 | tf_op jit(solution)/shard_map/pallas_call | solution.py:390
  28.3 0.0 collective-permute-done.5.refs_1_
  28.3 0.0 collective-permute-done.6.refs_2_
  28.3 0.0 collective-permute-done.7.refs_3_
  28.3 0.1 shard_map.60
  28.4 0.1 collective-permute-start.8
  28.5 1.3 %collective-permute-done.8.arrived = f32[4,48,128]{2,1,0:T(8,128)S(1)} collective-permute-done((f32[4,48,128]{2,1,0:T(8,128)S(1)}, f32[4,48,128]{2,1,0:T(8,128)S(1)}, u32[]{:S(2)}, u32[]{:S(2)}) %collective-permute-start.8) | collective-permute-done | bytes 98336 | tf_op jit(solution)/shard_map/ppermute | solution.py:301
  29.8 2.7 %collective-permute-start.9 = (f32[48,128]{1,0:T(8,128)S(1)}, f32[48,128]{1,0:T(8,128)S(1)}, u32[]{:S(2)}, u32[]{:S(2)}) collective-permute-start(f32[48,128]{1,0:T(8,128)S(1)} %get-tuple-element.51), channel_id=1, source_target_pairs={{0,6},{1,7},{2,4},{3,5},{4,2},{5,3},{6,0},{7,1},{8,14},{9,15},{10,... | collective-permute-start | bytes 73736 | tf_op jit(solution)/shard_map/ppermute | solution.py:301
  32.5 0.5 %collective-permute-start.10 = (f32[48,128]{1,0:T(8,128)S(1)}, f32[48,128]{1,0:T(8,128)S(1)}, u32[]{:S(2)}, u32[]{:S(2)}) collective-permute-start(f32[48,128]{1,0:T(8,128)S(1)} %get-tuple-element.52), channel_id=1, source_target_pairs={{0,4},{1,5},{2,6},{3,7},{4,0},{5,1},{6,2},{7,3},{8,12},{9,13},{10,... | collective-permute-start | bytes 73736 | tf_op jit(solution)/shard_map/ppermute | solution.py:301
  33.1 0.3 collective-permute-start.11
  33.4 1.2 %collective-permute-done.9.refs_0_ = f32[48,128]{1,0:T(8,128)S(1)} collective-permute-done((f32[48,128]{1,0:T(8,128)S(1)}, f32[48,128]{1,0:T(8,128)S(1)}, u32[]{:S(2)}, u32[]{:S(2)}) %collective-permute-start.9) | collective-permute-done | bytes 24608 | tf_op jit(solution)/shard_map/ppermute | solution.py:301
  34.6 1.8 %collective-permute-done.10.refs_1_ = f32[48,128]{1,0:T(8,128)S(1)} collective-permute-done((f32[48,128]{1,0:T(8,128)S(1)}, f32[48,128]{1,0:T(8,128)S(1)}, u32[]{:S(2)}, u32[]{:S(2)}) %collective-permute-start.10) | collective-permute-done | bytes 24608 | tf_op jit(solution)/shard_map/ppermute | solution.py:301
  36.4 0.5 %collective-permute-done.11.refs_2_ = f32[48,128]{1,0:T(8,128)S(1)} collective-permute-done((f32[48,128]{1,0:T(8,128)S(1)}, f32[48,128]{1,0:T(8,128)S(1)}, u32[]{:S(2)}, u32[]{:S(2)}) %collective-permute-start.11) | collective-permute-done | bytes 24608 | tf_op jit(solution)/shard_map/ppermute | solution.py:301
  36.9 0.6 %shard_map.62 = f32[2,3072]{1,0:T(2,128)} custom-call(f32[48,128]{1,0:T(8,128)S(1)} %collective-permute-done.9.refs_0_, f32[48,128]{1,0:T(8,128)S(1)} %collective-permute-done.10.refs_1_, f32[48,128]{1,0:T(8,128)S(1)} %collective-permute-done.11.refs_2_, f32[48,128]{1,0:T(8,128)S(1)} %get-tuple-element.54.refs_3_), custom_call_target="tpu_custom_call" | custom-call | tf_op jit(solution)/shard_map/pallas_call | solution.py:413
  (1 shorter events, 0.0 us)
Async XLA Ops:
  0.0 1.7 %collective-permute-start.1 = (f32[8,3072]{1,0:T(8,128)}, f32[8,3072]{1,0:T(8,128)S(1)}, u32[]{:S(2)}, u32[]{:S(2)}) collective-permute-start(f32[8,3072]{1,0:T(8,128)} %residual_hbm.1), channel_id=1, source_target_pairs={{0,1},{1,0},{2,3},{3,2},{4,5},{5,4},{6,7},{7,6},{8,9},{9,8},{10,11... | collective-permute-start | bytes 294920 | tf_op jit(solution)/shard_map/ppermute | solution.py:301
  0.5 1.3 %collective-permute-start = (s32[1,24]{1,0:T(1,128)}, s32[1,24]{1,0:T(1,128)S(1)}, u32[]{:S(2)}, u32[]{:S(2)}) collective-permute-start(s32[1,24]{1,0:T(1,128)} %bitcast.1), channel_id=1, source_target_pairs={{0,1},{1,0},{2,3},{3,2},{4,5},{5,4},{6,7},{7,6},{8,9},{9,8},{10,11... | collective-permute-start | bytes 296 | tf_op jit(solution)/shard_map/ppermute | solution.py:301
  2.8 9.4 %collective-permute-start.2 = (f32[168,128]{1,0:T(8,128)S(1)}, f32[168,128]{1,0:T(8,128)S(1)}, u32[]{:S(2)}, u32[]{:S(2)}) collective-permute-start(f32[168,128]{1,0:T(8,128)S(1)} %get-tuple-element.39), channel_id=1, source_target_pairs={{0,6},{1,7},{2,4},{3,5},{4,2},{5,3},{6,0},{7,1},{8,14},{9,15},{10,... | collective-permute-start | bytes 258056 | tf_op jit(solution)/shard_map/ppermute | solution.py:301
  6.6 5.6 %collective-permute-start.3 = (f32[168,128]{1,0:T(8,128)S(1)}, f32[168,128]{1,0:T(8,128)S(1)}, u32[]{:S(2)}, u32[]{:S(2)}) collective-permute-start(f32[168,128]{1,0:T(8,128)S(1)} %get-tuple-element.40), channel_id=1, source_target_pairs={{0,4},{1,5},{2,6},{3,7},{4,0},{5,1},{6,2},{7,3},{8,12},{9,13},{10,... | collective-permute-start | bytes 258056 | tf_op jit(solution)/shard_map/ppermute | solution.py:301
  7.1 5.1 %collective-permute-start.4 = (f32[168,128]{1,0:T(8,128)S(1)}, f32[168,128]{1,0:T(8,128)S(1)}, u32[]{:S(2)}, u32[]{:S(2)}) collective-permute-start(f32[168,128]{1,0:T(8,128)S(1)} %get-tuple-element.41), channel_id=1, source_target_pairs={{0,2},{1,3},{2,0},{3,1},{4,6},{5,7},{6,4},{7,5},{8,10},{9,11},{10,... | collective-permute-start | bytes 258056 | tf_op jit(solution)/shard_map/ppermute | solution.py:301
  15.4 12.9 %collective-permute-start.5 = (f32[64,128]{1,0:T(8,128)S(1)}, f32[64,128]{1,0:T(8,128)S(1)}, u32[]{:S(2)}, u32[]{:S(2)}) collective-permute-start(f32[64,128]{1,0:T(8,128)S(1)} %get-tuple-element.46), channel_id=1, source_target_pairs={{0,8},{8,0},{16,24},{24,16},{1,9},{9,1},{17,25},{25,17},{2,10},{10... | collective-permute-start | bytes 98312 | tf_op jit(solution)/shard_map/ppermute | solution.py:301
  17.4 10.9 %collective-permute-start.6 = (f32[64,128]{1,0:T(8,128)S(1)}, f32[64,128]{1,0:T(8,128)S(1)}, u32[]{:S(2)}, u32[]{:S(2)}) collective-permute-start(f32[64,128]{1,0:T(8,128)S(1)} %get-tuple-element.47), channel_id=1, source_target_pairs={{0,16},{8,24},{16,0},{24,8},{1,17},{9,25},{17,1},{25,9},{2,18},{10... | collective-permute-start | bytes 98312 | tf_op jit(solution)/shard_map/ppermute | solution.py:301
  20.0 8.3 %collective-permute-start.7 = (f32[64,128]{1,0:T(8,128)S(1)}, f32[64,128]{1,0:T(8,128)S(1)}, u32[]{:S(2)}, u32[]{:S(2)}) collective-permute-start(f32[64,128]{1,0:T(8,128)S(1)} %get-tuple-element.48), channel_id=1, source_target_pairs={{0,24},{8,16},{16,8},{24,0},{1,25},{9,17},{17,9},{25,1},{2,26},{10... | collective-permute-start | bytes 98312 | tf_op jit(solution)/shard_map/ppermute | solution.py:301
  28.4 1.4 %collective-permute-start.8 = (f32[4,48,128]{2,1,0:T(8,128)S(1)}, f32[4,48,128]{2,1,0:T(8,128)S(1)}, u32[]{:S(2)}, u32[]{:S(2)}) collective-permute-start(f32[4,48,128]{2,1,0:T(8,128)S(1)} %get-tuple-element.50), channel_id=1, source_target_pairs={{0,1},{1,0},{2,3},{3,2},{4,5},{5,4},{6,7},{7,6},{8,9},{9,8},{10,11... | collective-permute-start | bytes 294920 | tf_op jit(solution)/shard_map/ppermute | solution.py:301
  29.8 4.8 %collective-permute-start.9 = (f32[48,128]{1,0:T(8,128)S(1)}, f32[48,128]{1,0:T(8,128)S(1)}, u32[]{:S(2)}, u32[]{:S(2)}) collective-permute-start(f32[48,128]{1,0:T(8,128)S(1)} %get-tuple-element.51), channel_id=1, source_target_pairs={{0,6},{1,7},{2,4},{3,5},{4,2},{5,3},{6,0},{7,1},{8,14},{9,15},{10,... | collective-permute-start | bytes 73736 | tf_op jit(solution)/shard_map/ppermute | solution.py:301
  32.5 3.8 %collective-permute-start.10 = (f32[48,128]{1,0:T(8,128)S(1)}, f32[48,128]{1,0:T(8,128)S(1)}, u32[]{:S(2)}, u32[]{:S(2)}) collective-permute-start(f32[48,128]{1,0:T(8,128)S(1)} %get-tuple-element.52), channel_id=1, source_target_pairs={{0,4},{1,5},{2,6},{3,7},{4,0},{5,1},{6,2},{7,3},{8,12},{9,13},{10,... | collective-permute-start | bytes 73736 | tf_op jit(solution)/shard_map/ppermute | solution.py:301
  33.1 3.8 %collective-permute-start.11 = (f32[48,128]{1,0:T(8,128)S(1)}, f32[48,128]{1,0:T(8,128)S(1)}, u32[]{:S(2)}, u32[]{:S(2)}) collective-permute-start(f32[48,128]{1,0:T(8,128)S(1)} %get-tuple-element.53), channel_id=1, source_target_pairs={{0,2},{1,3},{2,0},{3,1},{4,6},{5,7},{6,4},{7,5},{8,10},{9,11},{10,... | collective-permute-start | bytes 73736 | tf_op jit(solution)/shard_map/ppermute | solution.py:301

commit v11 on v10

--- a/solution.py
+++ b/solution.py
@@ -219,7 +219,7 @@
 
 
 def coarse_kernel(own, rows, chunk, tile, upper, middle, factor_hbm, member, sums, *refs):
-    out, table, lower, begun, sems = refs
+    out, table, lower, sems = refs
     done = upper.shape[0] + middle.shape[0]
     width = upper.shape[1]
     copies = panel_copies(factor_hbm, lower, chunk, sems, done)
@@ -231,24 +231,32 @@
         parts = [sums[pl.ds(j, rows, stride=coarse), :] for j in range(coarse)]
         return jnp.concatenate(parts, axis=1).astype(jnp.bfloat16)
 
+    def second_product(mid, *panels):
+        for n in range(width // 256):
+            where = slice(n * 256, (n + 1) * 256)
+            at = 0
+            part = None
+            for panel in panels:
+                piece = mm(mid[:, at : at + panel.shape[0]], panel[:, where])
+                part = piece if part is None else part + piece
+                at += panel.shape[0]
+            for i in range(256 // BLK):
+                yield n * (256 // BLK) + i, part[:, i * BLK : (i + 1) * BLK]
+
     first = right()
-    begun[:, : upper.shape[0]] = first_product(upper, first, tile)
-    begun[:, upper.shape[0] : done] = first_product(middle, first, tile)
+    mid = [first_product(panel, first, tile) for panel in (upper, middle)]
+    mid = jnp.concatenate(mid, axis=1).astype(jnp.bfloat16)
+    for j, part in second_product(mid, upper, middle):
+        table[pl.ds(j, rows, stride=coarse), :] = part
 
     @in_own_block
     def _():
         for copy in copies:
             copy.wait()
-        low = first_product(lower, right(), tile).astype(jnp.bfloat16)
-        mid = begun[...].astype(jnp.bfloat16)
-        high = mid[:, : upper.shape[0]]
-        mid = mid[:, upper.shape[0] :]
-        for n in range(width // 256):
-            where = slice(n * 256, (n + 1) * 256)
-            part = mm(high, upper[:, where]) + mm(mid, middle[:, where]) + mm(low, lower[:, where])
-            for i in range(256 // BLK):
-                j = n * (256 // BLK) + i
-                table[pl.ds(j, rows, stride=coarse), :] = part[:, i * BLK : (i + 1) * BLK]
+        mid = first_product(lower, right(), tile).astype(jnp.bfloat16)
+        for j, part in second_product(mid, lower):
+            where = pl.ds(j, rows, stride=coarse)
+            table[where, :] = table[where, :] + part
         solved = jnp.concatenate([table[r * coarse : (r + 1) * coarse, :] for r in range(rows)], axis=1)
         spread = mm(member[...].astype(jnp.bfloat16), jnp.concatenate(split3(solved), axis=1))
         spread = spread[:, :span] + spread[:, span : 2 * span] + spread[:, 2 * span :]
@@ -394,7 +402,6 @@
         [
             pltpu.VMEM((rows * count, BLK), f32),
             pltpu.VMEM((lower, coarse_width), coarse_factor.dtype),
-            pltpu.VMEM((rows, 2 * quarter), f32),
             pltpu.SemaphoreType.DMA((lower // chunk,)),
         ],
         flops=4 * rows * coarse_depth * coarse_width,

time: 37.7 us -> 39.7 us (1.053)
  Pallas kernels: 19.2 us -> 21.1 us
    pallas_call x1, Pallas kernels: 8.26 us -> 10.2 us  [on_device(): call(functools.partial(coarse_kernel, own, rows, chunk, tile), sds((2 * p...]
  transfers between devices with their start and end apart: 12 -> 12, of which waited for: 5 -> 5; matrix products, arithmetic and copies ran while one was open for 0% -> 0% of each run, Pallas kernels for 38% -> 41%
where the time goes in v11:
time: 39.7 us; the launch traced here: 39.5 us
  Pallas kernels  21.1 us (53%)
  starting transfers between devices  13.2 us (33%)
  waiting for transfers between devices  5.07 us (13%)
    ppermute x12, starting transfers between devices, swap(): return lax.ppermute(value, axis, [(i, i ^ distance) for i in range(count)])  13.2 us
    pallas_call x1, Pallas kernels, on_device(): call(functools.partial(coarse_kernel, own, rows, chunk, tile), sds((2 * p...  10.2 us
    ppermute x12, waiting for transfers between devices, swap(): return lax.ppermute(value, axis, [(i, i ^ distance) for i in range(count)])  5.07 us
    pallas_call x1, Pallas kernels, on_device(): call(functools.partial(load_kernel, chunk, tile), (sds((rhs, depth), f32)...  4.94 us
    pallas_call x1, Pallas kernels, on_device(): call(functools.partial(fine_kernel, own, rows, begin, chunk, tile, pairs)...  3.17 us
    pallas_call x1, Pallas kernels, on_device(): call(functools.partial(pack_kernel, own, rows, pad), [sds((begin + halo *...  1.08 us
    pallas_call x1, Pallas kernels, on_device(): call(functools.partial(stage_kernel, own, rows), (sds(residual.shape, f32...  0.93 us
  transfers between devices with their start and end apart: 12, of which 5 were waited for; matrix products, arithmetic and copies ran while one was open for 0% of the time, Pallas kernels for 41%

profile of v11, /device:TPU:0, one launch (start us, length us, event | category | flops | bytes accessed | tf_op | source)
XLA Modules:
  0.0 39.5 jit_solution(1970460937818496345)
XLA Ops:
  0.0 0.5 %collective-permute-start.1 = (f32[8,3072]{1,0:T(8,128)}, f32[8,3072]{1,0:T(8,128)S(1)}, u32[]{:S(2)}, u32[]{:S(2)}) collective-permute-start(f32[8,3072]{1,0:T(8,128)} %residual_hbm.1), channel_id=1, source_target_pairs={{0,1},{1,0},{2,3},{3,2},{4,5},{5,4},{6,7},{7,6},{8,9},{9,8},{10,11... | collective-permute-start | bytes 294920 | tf_op jit(solution)/shard_map/ppermute | solution.py:309
  0.5 0.1 collective-permute-start
  0.5 0.9 %shard_map.55 = (f32[8,3072]{1,0:T(8,128)S(1)}, f32[48,128]{1,0:T(8,128)S(1)}, f32[1,24]{1,0:T(1,128)S(1)}) custom-call(f32[8,3072]{1,0:T(8,128)} %residual_hbm.1, s32[1,24]{1,0:T(1,128)} %bitcast.2), custom_call_target="tpu_custom_call" | custom-call | bytes 196608 | tf_op jit(solution)/shard_map/pallas_call | solution.py:338
  1.5 0.3 collective-permute-done.near_names
  1.7 0.0 collective-permute-done.1.near
  1.7 1.1 %shard_map.56 = (f32[168,128]{1,0:T(8,128)S(1)}, f32[168,128]{1,0:T(8,128)S(1)}, f32[168,128]{1,0:T(8,128)S(1)}, f32[168,128]{1,0:T(8,128)S(1)}, s32[8,128]{1,0:T(8,128)S(1)}, /*index=5*/s32[192,128]{1,0:T(8,128)S(1)}) custom-call(s32[8,8]{1,0:T(8,128)} %margin_hbm.1, f32[8,3072]{1,0:T(8,128)S(1)} %get-tuple-element.30.residual, ...), custom_call_target="tpu_custom_call" | custom-call | tf_op jit(solution)/shard_map/pallas_call | solution.py:350
  2.8 3.8 %collective-permute-start.2 = (f32[168,128]{1,0:T(8,128)S(1)}, f32[168,128]{1,0:T(8,128)S(1)}, u32[]{:S(2)}, u32[]{:S(2)}) collective-permute-start(f32[168,128]{1,0:T(8,128)S(1)} %get-tuple-element.39), channel_id=1, source_target_pairs={{0,6},{1,7},{2,4},{3,5},{4,2},{5,3},{6,0},{7,1},{8,14},{9,15},{10,... | collective-permute-start | bytes 258056 | tf_op jit(solution)/shard_map/ppermute | solution.py:309
  6.6 0.5 %collective-permute-start.3 = (f32[168,128]{1,0:T(8,128)S(1)}, f32[168,128]{1,0:T(8,128)S(1)}, u32[]{:S(2)}, u32[]{:S(2)}) collective-permute-start(f32[168,128]{1,0:T(8,128)S(1)} %get-tuple-element.40), channel_id=1, source_target_pairs={{0,4},{1,5},{2,6},{3,7},{4,0},{5,1},{6,2},{7,3},{8,12},{9,13},{10,... | collective-permute-start | bytes 258056 | tf_op jit(solution)/shard_map/ppermute | solution.py:309
  7.1 0.1 collective-permute-start.4
  7.2 4.9 %shard_map.57 = (f32[8,1024]{1,0:T(8,128)S(1)}, bf16[1,1024,4096]{2,1,0:T(8,128)(2,1)S(1)}, bf16[256,8192]{1,0:T(8,128)(2,1)S(1)}) custom-call(f32[8,3072]{1,0:T(8,128)S(1)} %get-tuple-element.30.residual, bf16[1,1024,4096]{2,1,0:T(8,128)(2,1)} %fine_hbm.1, bf16[1024,8192]{1,0:T(8,128)(2,1)} %factor_hbm.1, f32[168,128]{1,0:T(8,128)S(1)} %get-tuple-element.34.after.refs_3_), custom_call_target="tpu_custom_call" | custom-call | flops 50331648 | bytes 12582912 | tf_op jit(solution)/shard_map/pallas_call | solution.py:365
  12.2 0.0 collective-permute-done.2.refs_0_
  12.2 0.0 collective-permute-done.3.refs_1_
  12.2 0.0 collective-permute-done.4.refs_2_
  12.2 3.2 %shard_map.58 = (f32[64,128]{1,0:T(8,128)S(1)}, f32[64,128]{1,0:T(8,128)S(1)}, f32[64,128]{1,0:T(8,128)S(1)}, f32[64,128]{1,0:T(8,128)S(1)}, bf16[256,8192]{1,0:...) custom-call(s32[8,128]{1,0:T(8,128)S(1)} %get-tuple-element.36.away, ...), custom_call_target="tpu_custom_call" | custom-call | flops 134217728 | bytes 12582912 | tf_op jit(solution)/shard_map/pallas_call | solution.py:382
  15.4 2.0 %collective-permute-start.5 = (f32[64,128]{1,0:T(8,128)S(1)}, f32[64,128]{1,0:T(8,128)S(1)}, u32[]{:S(2)}, u32[]{:S(2)}) collective-permute-start(f32[64,128]{1,0:T(8,128)S(1)} %get-tuple-element.46), channel_id=1, source_target_pairs={{0,8},{8,0},{16,24},{24,16},{1,9},{9,1},{17,25},{25,17},{2,10},{10... | collective-permute-start | bytes 98312 | tf_op jit(solution)/shard_map/ppermute | solution.py:309
  17.4 2.6 %collective-permute-start.6 = (f32[64,128]{1,0:T(8,128)S(1)}, f32[64,128]{1,0:T(8,128)S(1)}, u32[]{:S(2)}, u32[]{:S(2)}) collective-permute-start(f32[64,128]{1,0:T(8,128)S(1)} %get-tuple-element.47), channel_id=1, source_target_pairs={{0,16},{8,24},{16,0},{24,8},{1,17},{9,25},{17,1},{25,9},{2,18},{10... | collective-permute-start | bytes 98312 | tf_op jit(solution)/shard_map/ppermute | solution.py:309
  20.0 0.0 collective-permute-start.7
  20.0 10.2 %shard_map.59.spread = f32[8,48,128]{2,1,0:T(8,128)S(1)} custom-call(bf16[256,8192]{1,0:T(8,128)(2,1)S(1)} %get-tuple-element.35.upper, bf16[256,8192]{1,0:T(8,128)(2,1)S(1)} %get-tuple-element.42.middle, bf16[1024,8192]{1,0:T(8,128)(2,1)} %factor_hbm.1, f32[192,64]{1,0:T(8,128)S(1)} %get-tuple-element.43.member, f32[128,128]{1,0:T(8,128)S(1)} %get-tuple-element.44.sums), custom_call_target="tpu_custom_call" | custom-call | flops 67108864 | bytes 16777216 | tf_op jit(solution)/shard_map/pallas_call | solution.py:398
  30.2 0.0 collective-permute-done.5.refs_1_
  30.3 0.0 collective-permute-done.6.refs_2_
  30.3 0.0 collective-permute-done.7.refs_3_
  30.3 0.1 shard_map.60
  30.4 0.1 collective-permute-start.8
  30.5 1.3 %collective-permute-done.8.arrived = f32[4,48,128]{2,1,0:T(8,128)S(1)} collective-permute-done((f32[4,48,128]{2,1,0:T(8,128)S(1)}, f32[4,48,128]{2,1,0:T(8,128)S(1)}, u32[]{:S(2)}, u32[]{:S(2)}) %collective-permute-start.8) | collective-permute-done | bytes 98336 | tf_op jit(solution)/shard_map/ppermute | solution.py:309
  31.8 2.7 %collective-permute-start.9 = (f32[48,128]{1,0:T(8,128)S(1)}, f32[48,128]{1,0:T(8,128)S(1)}, u32[]{:S(2)}, u32[]{:S(2)}) collective-permute-start(f32[48,128]{1,0:T(8,128)S(1)} %get-tuple-element.51), channel_id=1, source_target_pairs={{0,6},{1,7},{2,4},{3,5},{4,2},{5,3},{6,0},{7,1},{8,14},{9,15},{10,... | collective-permute-start | bytes 73736 | tf_op jit(solution)/shard_map/ppermute | solution.py:309
  34.5 0.5 %collective-permute-start.10 = (f32[48,128]{1,0:T(8,128)S(1)}, f32[48,128]{1,0:T(8,128)S(1)}, u32[]{:S(2)}, u32[]{:S(2)}) collective-permute-start(f32[48,128]{1,0:T(8,128)S(1)} %get-tuple-element.52), channel_id=1, source_target_pairs={{0,4},{1,5},{2,6},{3,7},{4,0},{5,1},{6,2},{7,3},{8,12},{9,13},{10,... | collective-permute-start | bytes 73736 | tf_op jit(solution)/shard_map/ppermute | solution.py:309
  35.0 0.3 collective-permute-start.11
  35.4 1.2 %collective-permute-done.9.refs_0_ = f32[48,128]{1,0:T(8,128)S(1)} collective-permute-done((f32[48,128]{1,0:T(8,128)S(1)}, f32[48,128]{1,0:T(8,128)S(1)}, u32[]{:S(2)}, u32[]{:S(2)}) %collective-permute-start.9) | collective-permute-done | bytes 24608 | tf_op jit(solution)/shard_map/ppermute | solution.py:309
  36.6 1.8 %collective-permute-done.10.refs_1_ = f32[48,128]{1,0:T(8,128)S(1)} collective-permute-done((f32[48,128]{1,0:T(8,128)S(1)}, f32[48,128]{1,0:T(8,128)S(1)}, u32[]{:S(2)}, u32[]{:S(2)}) %collective-permute-start.10) | collective-permute-done | bytes 24608 | tf_op jit(solution)/shard_map/ppermute | solution.py:309
  38.4 0.5 %collective-permute-done.11.refs_2_ = f32[48,128]{1,0:T(8,128)S(1)} collective-permute-done((f32[48,128]{1,0:T(8,128)S(1)}, f32[48,128]{1,0:T(8,128)S(1)}, u32[]{:S(2)}, u32[]{:S(2)}) %collective-permute-start.11) | collective-permute-done | bytes 24608 | tf_op jit(solution)/shard_map/ppermute | solution.py:309
  38.9 0.6 %shard_map.62 = f32[2,3072]{1,0:T(2,128)} custom-call(f32[48,128]{1,0:T(8,128)S(1)} %collective-permute-done.9.refs_0_, f32[48,128]{1,0:T(8,128)S(1)} %collective-permute-done.10.refs_1_, f32[48,128]{1,0:T(8,128)S(1)} %collective-permute-done.11.refs_2_, f32[48,128]{1,0:T(8,128)S(1)} %get-tuple-element.54.refs_3_), custom_call_target="tpu_custom_call" | custom-call | tf_op jit(solution)/shard_map/pallas_call | solution.py:420
  (1 shorter events, 0.0 us)
Async XLA Ops:
  0.0 1.7 %collective-permute-start.1 = (f32[8,3072]{1,0:T(8,128)}, f32[8,3072]{1,0:T(8,128)S(1)}, u32[]{:S(2)}, u32[]{:S(2)}) collective-permute-start(f32[8,3072]{1,0:T(8,128)} %residual_hbm.1), channel_id=1, source_target_pairs={{0,1},{1,0},{2,3},{3,2},{4,5},{5,4},{6,7},{7,6},{8,9},{9,8},{10,11... | collective-permute-start | bytes 294920 | tf_op jit(solution)/shard_map/ppermute | solution.py:309
  0.5 1.3 %collective-permute-start = (s32[1,24]{1,0:T(1,128)}, s32[1,24]{1,0:T(1,128)S(1)}, u32[]{:S(2)}, u32[]{:S(2)}) collective-permute-start(s32[1,24]{1,0:T(1,128)} %bitcast.1), channel_id=1, source_target_pairs={{0,1},{1,0},{2,3},{3,2},{4,5},{5,4},{6,7},{7,6},{8,9},{9,8},{10,11... | collective-permute-start | bytes 296 | tf_op jit(solution)/shard_map/ppermute | solution.py:309
  2.8 9.4 %collective-permute-start.2 = (f32[168,128]{1,0:T(8,128)S(1)}, f32[168,128]{1,0:T(8,128)S(1)}, u32[]{:S(2)}, u32[]{:S(2)}) collective-permute-start(f32[168,128]{1,0:T(8,128)S(1)} %get-tuple-element.39), channel_id=1, source_target_pairs={{0,6},{1,7},{2,4},{3,5},{4,2},{5,3},{6,0},{7,1},{8,14},{9,15},{10,... | collective-permute-start | bytes 258056 | tf_op jit(solution)/shard_map/ppermute | solution.py:309
  6.6 5.6 %collective-permute-start.3 = (f32[168,128]{1,0:T(8,128)S(1)}, f32[168,128]{1,0:T(8,128)S(1)}, u32[]{:S(2)}, u32[]{:S(2)}) collective-permute-start(f32[168,128]{1,0:T(8,128)S(1)} %get-tuple-element.40), channel_id=1, source_target_pairs={{0,4},{1,5},{2,6},{3,7},{4,0},{5,1},{6,2},{7,3},{8,12},{9,13},{10,... | collective-permute-start | bytes 258056 | tf_op jit(solution)/shard_map/ppermute | solution.py:309
  7.1 5.1 %collective-permute-start.4 = (f32[168,128]{1,0:T(8,128)S(1)}, f32[168,128]{1,0:T(8,128)S(1)}, u32[]{:S(2)}, u32[]{:S(2)}) collective-permute-start(f32[168,128]{1,0:T(8,128)S(1)} %get-tuple-element.41), channel_id=1, source_target_pairs={{0,2},{1,3},{2,0},{3,1},{4,6},{5,7},{6,4},{7,5},{8,10},{9,11},{10,... | collective-permute-start | bytes 258056 | tf_op jit(solution)/shard_map/ppermute | solution.py:309
  15.4 14.9 %collective-permute-start.5 = (f32[64,128]{1,0:T(8,128)S(1)}, f32[64,128]{1,0:T(8,128)S(1)}, u32[]{:S(2)}, u32[]{:S(2)}) collective-permute-start(f32[64,128]{1,0:T(8,128)S(1)} %get-tuple-element.46), channel_id=1, source_target_pairs={{0,8},{8,0},{16,24},{24,16},{1,9},{9,1},{17,25},{25,17},{2,10},{10... | collective-permute-start | bytes 98312 | tf_op jit(solution)/shard_map/ppermute | solution.py:309
  17.4 12.8 %collective-permute-start.6 = (f32[64,128]{1,0:T(8,128)S(1)}, f32[64,128]{1,0:T(8,128)S(1)}, u32[]{:S(2)}, u32[]{:S(2)}) collective-permute-start(f32[64,128]{1,0:T(8,128)S(1)} %get-tuple-element.47), channel_id=1, source_target_pairs={{0,16},{8,24},{16,0},{24,8},{1,17},{9,25},{17,1},{25,9},{2,18},{10... | collective-permute-start | bytes 98312 | tf_op jit(solution)/shard_map/ppermute | solution.py:309
  20.0 10.3 %collective-permute-start.7 = (f32[64,128]{1,0:T(8,128)S(1)}, f32[64,128]{1,0:T(8,128)S(1)}, u32[]{:S(2)}, u32[]{:S(2)}) collective-permute-start(f32[64,128]{1,0:T(8,128)S(1)} %get-tuple-element.48), channel_id=1, source_target_pairs={{0,24},{8,16},{16,8},{24,0},{1,25},{9,17},{17,9},{25,1},{2,26},{10... | collective-permute-start | bytes 98312 | tf_op jit(solution)/shard_map/ppermute | solution.py:309
  30.4 1.4 %collective-permute-start.8 = (f32[4,48,128]{2,1,0:T(8,128)S(1)}, f32[4,48,128]{2,1,0:T(8,128)S(1)}, u32[]{:S(2)}, u32[]{:S(2)}) collective-permute-start(f32[4,48,128]{2,1,0:T(8,128)S(1)} %get-tuple-element.50), channel_id=1, source_target_pairs={{0,1},{1,0},{2,3},{3,2},{4,5},{5,4},{6,7},{7,6},{8,9},{9,8},{10,11... | collective-permute-start | bytes 294920 | tf_op jit(solution)/shard_map/ppermute | solution.py:309
  31.8 4.8 %collective-permute-start.9 = (f32[48,128]{1,0:T(8,128)S(1)}, f32[48,128]{1,0:T(8,128)S(1)}, u32[]{:S(2)}, u32[]{:S(2)}) collective-permute-start(f32[48,128]{1,0:T(8,128)S(1)} %get-tuple-element.51), channel_id=1, source_target_pairs={{0,6},{1,7},{2,4},{3,5},{4,2},{5,3},{6,0},{7,1},{8,14},{9,15},{10,... | collective-permute-start | bytes 73736 | tf_op jit(solution)/shard_map/ppermute | solution.py:309
  34.5 3.8 %collective-permute-start.10 = (f32[48,128]{1,0:T(8,128)S(1)}, f32[48,128]{1,0:T(8,128)S(1)}, u32[]{:S(2)}, u32[]{:S(2)}) collective-permute-start(f32[48,128]{1,0:T(8,128)S(1)} %get-tuple-element.52), channel_id=1, source_target_pairs={{0,4},{1,5},{2,6},{3,7},{4,0},{5,1},{6,2},{7,3},{8,12},{9,13},{10,... | collective-permute-start | bytes 73736 | tf_op jit(solution)/shard_map/ppermute | solution.py:309
  35.0 3.8 %collective-permute-start.11 = (f32[48,128]{1,0:T(8,128)S(1)}, f32[48,128]{1,0:T(8,128)S(1)}, u32[]{:S(2)}, u32[]{:S(2)}) collective-permute-start(f32[48,128]{1,0:T(8,128)S(1)} %get-tuple-element.53), channel_id=1, source_target_pairs={{0,2},{1,3},{2,0},{3,1},{4,6},{5,7},{6,4},{7,5},{8,10},{9,11},{10,... | collective-permute-start | bytes 73736 | tf_op jit(solution)/shard_map/ppermute | solution.py:309

commit v12 on v10

--- a/solution.py
+++ b/solution.py
@@ -177,6 +177,9 @@
     counts = jnp.maximum(found[:, 3 * span :], 1.0)
     for r in range(rows):
         table[r * coarse : (r + 1) * coarse, :] = sums[:, r * BLK : (r + 1) * BLK] / counts
+    rest = table.shape[0] - rows * coarse
+    if rest > 0:
+        table[rows * coarse :, :] = jnp.zeros((rest, BLK), jnp.float32)
     named[...] = member.astype(jnp.float32)
 
 
@@ -226,9 +229,10 @@
     start(copies)
     coarse = width // BLK
     span = rows * BLK
+    padded = table.shape[0] // coarse
 
     def right():
-        parts = [sums[pl.ds(j, rows, stride=coarse), :] for j in range(coarse)]
+        parts = [sums[pl.ds(j, padded, stride=coarse), :] for j in range(coarse)]
         return jnp.concatenate(parts, axis=1).astype(jnp.bfloat16)
 
     first = right()
@@ -248,7 +252,7 @@
             part = mm(high, upper[:, where]) + mm(mid, middle[:, where]) + mm(low, lower[:, where])
             for i in range(256 // BLK):
                 j = n * (256 // BLK) + i
-                table[pl.ds(j, rows, stride=coarse), :] = part[:, i * BLK : (i + 1) * BLK]
+                table[pl.ds(j, padded, stride=coarse), :] = part[:, i * BLK : (i + 1) * BLK]
         solved = jnp.concatenate([table[r * coarse : (r + 1) * coarse, :] for r in range(rows)], axis=1)
         spread = mm(member[...].astype(jnp.bfloat16), jnp.concatenate(split3(solved), axis=1))
         spread = spread[:, :span] + spread[:, span : 2 * span] + spread[:, 2 * span :]
@@ -371,13 +375,14 @@
     )(held, local_factor, coarse_factor, arrived[0])
     chunk = quarter // 4
     count = coarse_width // BLK
+    padded = -(-rows // 8) * 8
     *fine, coarse_middle, member, sums = call(
         functools.partial(fine_kernel, own, rows, begin, chunk, tile, pairs),
         [sds((rows * blocks, BLK), f32)] * grp_count
         + [
             sds((quarter, coarse_width), coarse_factor.dtype),
             sds((2 * pairs * own, count), f32),
-            sds((rows * count, BLK), f32),
+            sds((padded * count, BLK), f32),
         ],
         [VMEM, VMEM, VMEM, HBM] + [VMEM] * pairs,
         [pltpu.VMEM((rhs * blocks, BLK), f32), pltpu.SemaphoreType.DMA((quarter // chunk,))],
@@ -392,9 +397,9 @@
         sds((2 * pairs, size, BLK), f32),
         [VMEM, VMEM, HBM, VMEM, VMEM],
         [
-            pltpu.VMEM((rows * count, BLK), f32),
+            pltpu.VMEM((padded * count, BLK), f32),
             pltpu.VMEM((lower, coarse_width), coarse_factor.dtype),
-            pltpu.VMEM((rows, 2 * quarter), f32),
+            pltpu.VMEM((padded, 2 * quarter), f32),
             pltpu.SemaphoreType.DMA((lower // chunk,)),
         ],
         flops=4 * rows * coarse_depth * coarse_width,

time: 37.7 us -> 37.7 us (level)
  no operation moved by 1% of the time
where the time goes in v12:
time: 37.7 us; the launch traced here: 37.5 us
  Pallas kernels  19.2 us (51%)
  starting transfers between devices  13.2 us (35%)
  waiting for transfers between devices  5.07 us (13%)
    ppermute x12, starting transfers between devices, swap(): return lax.ppermute(value, axis, [(i, i ^ distance) for i in range(count)])  13.2 us
    pallas_call x1, Pallas kernels, on_device(): call(functools.partial(coarse_kernel, own, rows, chunk, tile), sds((2 * p...  8.26 us
    ppermute x12, waiting for transfers between devices, swap(): return lax.ppermute(value, axis, [(i, i ^ distance) for i in range(count)])  5.07 us
    pallas_call x1, Pallas kernels, on_device(): call(functools.partial(load_kernel, chunk, tile), (sds((rhs, depth), f32)...  4.94 us
    pallas_call x1, Pallas kernels, on_device(): call(functools.partial(fine_kernel, own, rows, begin, chunk, tile, pairs)...  3.17 us
    pallas_call x1, Pallas kernels, on_device(): call(functools.partial(pack_kernel, own, rows, pad), [sds((begin + halo *...  1.08 us
    pallas_call x1, Pallas kernels, on_device(): call(functools.partial(stage_kernel, own, rows), (sds(residual.shape, f32...  0.93 us
  transfers between devices with their start and end apart: 12, of which 5 were waited for; matrix products, arithmetic and copies ran while one was open for 0% of the time, Pallas kernels for 38%

profile of v12, /device:TPU:0, one launch (start us, length us, event | category | flops | bytes accessed | tf_op | source)
XLA Modules:
  0.0 37.5 jit_solution(17235408767046977193)
XLA Ops:
  0.0 0.5 %collective-permute-start.1 = (f32[8,3072]{1,0:T(8,128)}, f32[8,3072]{1,0:T(8,128)S(1)}, u32[]{:S(2)}, u32[]{:S(2)}) collective-permute-start(f32[8,3072]{1,0:T(8,128)} %residual_hbm.1), channel_id=1, source_target_pairs={{0,1},{1,0},{2,3},{3,2},{4,5},{5,4},{6,7},{7,6},{8,9},{9,8},{10,11... | collective-permute-start | bytes 294920 | tf_op jit(solution)/shard_map/ppermute | solution.py:305
  0.5 0.1 collective-permute-start
  0.5 0.9 %shard_map.55 = (f32[8,3072]{1,0:T(8,128)S(1)}, f32[48,128]{1,0:T(8,128)S(1)}, f32[1,24]{1,0:T(1,128)S(1)}) custom-call(f32[8,3072]{1,0:T(8,128)} %residual_hbm.1, s32[1,24]{1,0:T(1,128)} %bitcast.2), custom_call_target="tpu_custom_call" | custom-call | bytes 196608 | tf_op jit(solution)/shard_map/pallas_call | solution.py:334
  1.5 0.3 collective-permute-done.near_names
  1.7 0.0 collective-permute-done.1.near
  1.7 1.1 %shard_map.56 = (f32[168,128]{1,0:T(8,128)S(1)}, f32[168,128]{1,0:T(8,128)S(1)}, f32[168,128]{1,0:T(8,128)S(1)}, f32[168,128]{1,0:T(8,128)S(1)}, s32[8,128]{1,0:T(8,128)S(1)}, /*index=5*/s32[192,128]{1,0:T(8,128)S(1)}) custom-call(s32[8,8]{1,0:T(8,128)} %margin_hbm.1, f32[8,3072]{1,0:T(8,128)S(1)} %get-tuple-element.30.residual, ...), custom_call_target="tpu_custom_call" | custom-call | tf_op jit(solution)/shard_map/pallas_call | solution.py:346
  2.8 3.8 %collective-permute-start.2 = (f32[168,128]{1,0:T(8,128)S(1)}, f32[168,128]{1,0:T(8,128)S(1)}, u32[]{:S(2)}, u32[]{:S(2)}) collective-permute-start(f32[168,128]{1,0:T(8,128)S(1)} %get-tuple-element.39), channel_id=1, source_target_pairs={{0,6},{1,7},{2,4},{3,5},{4,2},{5,3},{6,0},{7,1},{8,14},{9,15},{10,... | collective-permute-start | bytes 258056 | tf_op jit(solution)/shard_map/ppermute | solution.py:305
  6.6 0.5 %collective-permute-start.3 = (f32[168,128]{1,0:T(8,128)S(1)}, f32[168,128]{1,0:T(8,128)S(1)}, u32[]{:S(2)}, u32[]{:S(2)}) collective-permute-start(f32[168,128]{1,0:T(8,128)S(1)} %get-tuple-element.40), channel_id=1, source_target_pairs={{0,4},{1,5},{2,6},{3,7},{4,0},{5,1},{6,2},{7,3},{8,12},{9,13},{10,... | collective-permute-start | bytes 258056 | tf_op jit(solution)/shard_map/ppermute | solution.py:305
  7.1 0.1 collective-permute-start.4
  7.2 4.9 %shard_map.57 = (f32[8,1024]{1,0:T(8,128)S(1)}, bf16[1,1024,4096]{2,1,0:T(8,128)(2,1)S(1)}, bf16[256,8192]{1,0:T(8,128)(2,1)S(1)}) custom-call(f32[8,3072]{1,0:T(8,128)S(1)} %get-tuple-element.30.residual, bf16[1,1024,4096]{2,1,0:T(8,128)(2,1)} %fine_hbm.1, bf16[1024,8192]{1,0:T(8,128)(2,1)} %factor_hbm.1, f32[168,128]{1,0:T(8,128)S(1)} %get-tuple-element.34.after.refs_3_), custom_call_target="tpu_custom_call" | custom-call | flops 50331648 | bytes 12582912 | tf_op jit(solution)/shard_map/pallas_call | solution.py:361
  12.2 0.0 collective-permute-done.2.refs_0_
  12.2 0.0 collective-permute-done.3.refs_1_
  12.2 0.0 collective-permute-done.4.refs_2_
  12.2 3.2 %shard_map.58 = (f32[64,128]{1,0:T(8,128)S(1)}, f32[64,128]{1,0:T(8,128)S(1)}, f32[64,128]{1,0:T(8,128)S(1)}, f32[64,128]{1,0:T(8,128)S(1)}, bf16[256,8192]{1,0:...) custom-call(s32[8,128]{1,0:T(8,128)S(1)} %get-tuple-element.36.away, ...), custom_call_target="tpu_custom_call" | custom-call | flops 134217728 | bytes 12582912 | tf_op jit(solution)/shard_map/pallas_call | solution.py:379
  15.4 2.0 %collective-permute-start.5 = (f32[64,128]{1,0:T(8,128)S(1)}, f32[64,128]{1,0:T(8,128)S(1)}, u32[]{:S(2)}, u32[]{:S(2)}) collective-permute-start(f32[64,128]{1,0:T(8,128)S(1)} %get-tuple-element.46), channel_id=1, source_target_pairs={{0,8},{8,0},{16,24},{24,16},{1,9},{9,1},{17,25},{25,17},{2,10},{10... | collective-permute-start | bytes 98312 | tf_op jit(solution)/shard_map/ppermute | solution.py:305
  17.4 2.6 %collective-permute-start.6 = (f32[64,128]{1,0:T(8,128)S(1)}, f32[64,128]{1,0:T(8,128)S(1)}, u32[]{:S(2)}, u32[]{:S(2)}) collective-permute-start(f32[64,128]{1,0:T(8,128)S(1)} %get-tuple-element.47), channel_id=1, source_target_pairs={{0,16},{8,24},{16,0},{24,8},{1,17},{9,25},{17,1},{25,9},{2,18},{10... | collective-permute-start | bytes 98312 | tf_op jit(solution)/shard_map/ppermute | solution.py:305
  20.0 0.0 collective-permute-start.7
  20.0 8.3 %shard_map.59.spread = f32[8,48,128]{2,1,0:T(8,128)S(1)} custom-call(bf16[256,8192]{1,0:T(8,128)(2,1)S(1)} %get-tuple-element.35.upper, bf16[256,8192]{1,0:T(8,128)(2,1)S(1)} %get-tuple-element.42.middle, bf16[1024,8192]{1,0:T(8,128)(2,1)} %factor_hbm.1, f32[192,64]{1,0:T(8,128)S(1)} %get-tuple-element.43.member, f32[512,128]{1,0:T(8,128)S(1)} %get-tuple-element.44.sums), custom_call_target="tpu_custom_call" | custom-call | flops 67108864 | bytes 16777216 | tf_op jit(solution)/shard_map/pallas_call | solution.py:395
  28.3 0.0 collective-permute-done.5.refs_1_
  28.3 0.0 collective-permute-done.6.refs_2_
  28.3 0.0 collective-permute-done.7.refs_3_
  28.3 0.1 shard_map.60
  28.4 0.1 collective-permute-start.8
  28.5 1.3 %collective-permute-done.8.arrived = f32[4,48,128]{2,1,0:T(8,128)S(1)} collective-permute-done((f32[4,48,128]{2,1,0:T(8,128)S(1)}, f32[4,48,128]{2,1,0:T(8,128)S(1)}, u32[]{:S(2)}, u32[]{:S(2)}) %collective-permute-start.8) | collective-permute-done | bytes 98336 | tf_op jit(solution)/shard_map/ppermute | solution.py:305
  29.8 2.7 %collective-permute-start.9 = (f32[48,128]{1,0:T(8,128)S(1)}, f32[48,128]{1,0:T(8,128)S(1)}, u32[]{:S(2)}, u32[]{:S(2)}) collective-permute-start(f32[48,128]{1,0:T(8,128)S(1)} %get-tuple-element.51), channel_id=1, source_target_pairs={{0,6},{1,7},{2,4},{3,5},{4,2},{5,3},{6,0},{7,1},{8,14},{9,15},{10,... | collective-permute-start | bytes 73736 | tf_op jit(solution)/shard_map/ppermute | solution.py:305
  32.5 0.5 %collective-permute-start.10 = (f32[48,128]{1,0:T(8,128)S(1)}, f32[48,128]{1,0:T(8,128)S(1)}, u32[]{:S(2)}, u32[]{:S(2)}) collective-permute-start(f32[48,128]{1,0:T(8,128)S(1)} %get-tuple-element.52), channel_id=1, source_target_pairs={{0,4},{1,5},{2,6},{3,7},{4,0},{5,1},{6,2},{7,3},{8,12},{9,13},{10,... | collective-permute-start | bytes 73736 | tf_op jit(solution)/shard_map/ppermute | solution.py:305
  33.1 0.3 collective-permute-start.11
  33.4 1.2 %collective-permute-done.9.refs_0_ = f32[48,128]{1,0:T(8,128)S(1)} collective-permute-done((f32[48,128]{1,0:T(8,128)S(1)}, f32[48,128]{1,0:T(8,128)S(1)}, u32[]{:S(2)}, u32[]{:S(2)}) %collective-permute-start.9) | collective-permute-done | bytes 24608 | tf_op jit(solution)/shard_map/ppermute | solution.py:305
  34.6 1.8 %collective-permute-done.10.refs_1_ = f32[48,128]{1,0:T(8,128)S(1)} collective-permute-done((f32[48,128]{1,0:T(8,128)S(1)}, f32[48,128]{1,0:T(8,128)S(1)}, u32[]{:S(2)}, u32[]{:S(2)}) %collective-permute-start.10) | collective-permute-done | bytes 24608 | tf_op jit(solution)/shard_map/ppermute | solution.py:305
  36.4 0.5 %collective-permute-done.11.refs_2_ = f32[48,128]{1,0:T(8,128)S(1)} collective-permute-done((f32[48,128]{1,0:T(8,128)S(1)}, f32[48,128]{1,0:T(8,128)S(1)}, u32[]{:S(2)}, u32[]{:S(2)}) %collective-permute-start.11) | collective-permute-done | bytes 24608 | tf_op jit(solution)/shard_map/ppermute | solution.py:305
  36.9 0.6 %shard_map.62 = f32[2,3072]{1,0:T(2,128)} custom-call(f32[48,128]{1,0:T(8,128)S(1)} %collective-permute-done.9.refs_0_, f32[48,128]{1,0:T(8,128)S(1)} %collective-permute-done.10.refs_1_, f32[48,128]{1,0:T(8,128)S(1)} %collective-permute-done.11.refs_2_, f32[48,128]{1,0:T(8,128)S(1)} %get-tuple-element.54.refs_3_), custom_call_target="tpu_custom_call" | custom-call | tf_op jit(solution)/shard_map/pallas_call | solution.py:418
  (1 shorter events, 0.0 us)
Async XLA Ops:
  0.0 1.7 %collective-permute-start.1 = (f32[8,3072]{1,0:T(8,128)}, f32[8,3072]{1,0:T(8,128)S(1)}, u32[]{:S(2)}, u32[]{:S(2)}) collective-permute-start(f32[8,3072]{1,0:T(8,128)} %residual_hbm.1), channel_id=1, source_target_pairs={{0,1},{1,0},{2,3},{3,2},{4,5},{5,4},{6,7},{7,6},{8,9},{9,8},{10,11... | collective-permute-start | bytes 294920 | tf_op jit(solution)/shard_map/ppermute | solution.py:305
  0.5 1.3 %collective-permute-start = (s32[1,24]{1,0:T(1,128)}, s32[1,24]{1,0:T(1,128)S(1)}, u32[]{:S(2)}, u32[]{:S(2)}) collective-permute-start(s32[1,24]{1,0:T(1,128)} %bitcast.1), channel_id=1, source_target_pairs={{0,1},{1,0},{2,3},{3,2},{4,5},{5,4},{6,7},{7,6},{8,9},{9,8},{10,11... | collective-permute-start | bytes 296 | tf_op jit(solution)/shard_map/ppermute | solution.py:305
  2.8 9.4 %collective-permute-start.2 = (f32[168,128]{1,0:T(8,128)S(1)}, f32[168,128]{1,0:T(8,128)S(1)}, u32[]{:S(2)}, u32[]{:S(2)}) collective-permute-start(f32[168,128]{1,0:T(8,128)S(1)} %get-tuple-element.39), channel_id=1, source_target_pairs={{0,6},{1,7},{2,4},{3,5},{4,2},{5,3},{6,0},{7,1},{8,14},{9,15},{10,... | collective-permute-start | bytes 258056 | tf_op jit(solution)/shard_map/ppermute | solution.py:305
  6.6 5.6 %collective-permute-start.3 = (f32[168,128]{1,0:T(8,128)S(1)}, f32[168,128]{1,0:T(8,128)S(1)}, u32[]{:S(2)}, u32[]{:S(2)}) collective-permute-start(f32[168,128]{1,0:T(8,128)S(1)} %get-tuple-element.40), channel_id=1, source_target_pairs={{0,4},{1,5},{2,6},{3,7},{4,0},{5,1},{6,2},{7,3},{8,12},{9,13},{10,... | collective-permute-start | bytes 258056 | tf_op jit(solution)/shard_map/ppermute | solution.py:305
  7.1 5.1 %collective-permute-start.4 = (f32[168,128]{1,0:T(8,128)S(1)}, f32[168,128]{1,0:T(8,128)S(1)}, u32[]{:S(2)}, u32[]{:S(2)}) collective-permute-start(f32[168,128]{1,0:T(8,128)S(1)} %get-tuple-element.41), channel_id=1, source_target_pairs={{0,2},{1,3},{2,0},{3,1},{4,6},{5,7},{6,4},{7,5},{8,10},{9,11},{10,... | collective-permute-start | bytes 258056 | tf_op jit(solution)/shard_map/ppermute | solution.py:305
  15.4 12.9 %collective-permute-start.5 = (f32[64,128]{1,0:T(8,128)S(1)}, f32[64,128]{1,0:T(8,128)S(1)}, u32[]{:S(2)}, u32[]{:S(2)}) collective-permute-start(f32[64,128]{1,0:T(8,128)S(1)} %get-tuple-element.46), channel_id=1, source_target_pairs={{0,8},{8,0},{16,24},{24,16},{1,9},{9,1},{17,25},{25,17},{2,10},{10... | collective-permute-start | bytes 98312 | tf_op jit(solution)/shard_map/ppermute | solution.py:305
  17.4 10.9 %collective-permute-start.6 = (f32[64,128]{1,0:T(8,128)S(1)}, f32[64,128]{1,0:T(8,128)S(1)}, u32[]{:S(2)}, u32[]{:S(2)}) collective-permute-start(f32[64,128]{1,0:T(8,128)S(1)} %get-tuple-element.47), channel_id=1, source_target_pairs={{0,16},{8,24},{16,0},{24,8},{1,17},{9,25},{17,1},{25,9},{2,18},{10... | collective-permute-start | bytes 98312 | tf_op jit(solution)/shard_map/ppermute | solution.py:305
  20.0 8.3 %collective-permute-start.7 = (f32[64,128]{1,0:T(8,128)S(1)}, f32[64,128]{1,0:T(8,128)S(1)}, u32[]{:S(2)}, u32[]{:S(2)}) collective-permute-start(f32[64,128]{1,0:T(8,128)S(1)} %get-tuple-element.48), channel_id=1, source_target_pairs={{0,24},{8,16},{16,8},{24,0},{1,25},{9,17},{17,9},{25,1},{2,26},{10... | collective-permute-start | bytes 98312 | tf_op jit(solution)/shard_map/ppermute | solution.py:305
  28.4 1.4 %collective-permute-start.8 = (f32[4,48,128]{2,1,0:T(8,128)S(1)}, f32[4,48,128]{2,1,0:T(8,128)S(1)}, u32[]{:S(2)}, u32[]{:S(2)}) collective-permute-start(f32[4,48,128]{2,1,0:T(8,128)S(1)} %get-tuple-element.50), channel_id=1, source_target_pairs={{0,1},{1,0},{2,3},{3,2},{4,5},{5,4},{6,7},{7,6},{8,9},{9,8},{10,11... | collective-permute-start | bytes 294920 | tf_op jit(solution)/shard_map/ppermute | solution.py:305
  29.8 4.8 %collective-permute-start.9 = (f32[48,128]{1,0:T(8,128)S(1)}, f32[48,128]{1,0:T(8,128)S(1)}, u32[]{:S(2)}, u32[]{:S(2)}) collective-permute-start(f32[48,128]{1,0:T(8,128)S(1)} %get-tuple-element.51), channel_id=1, source_target_pairs={{0,6},{1,7},{2,4},{3,5},{4,2},{5,3},{6,0},{7,1},{8,14},{9,15},{10,... | collective-permute-start | bytes 73736 | tf_op jit(solution)/shard_map/ppermute | solution.py:305
  32.5 3.8 %collective-permute-start.10 = (f32[48,128]{1,0:T(8,128)S(1)}, f32[48,128]{1,0:T(8,128)S(1)}, u32[]{:S(2)}, u32[]{:S(2)}) collective-permute-start(f32[48,128]{1,0:T(8,128)S(1)} %get-tuple-element.52), channel_id=1, source_target_pairs={{0,4},{1,5},{2,6},{3,7},{4,0},{5,1},{6,2},{7,3},{8,12},{9,13},{10,... | collective-permute-start | bytes 73736 | tf_op jit(solution)/shard_map/ppermute | solution.py:305
  33.1 3.8 %collective-permute-start.11 = (f32[48,128]{1,0:T(8,128)S(1)}, f32[48,128]{1,0:T(8,128)S(1)}, u32[]{:S(2)}, u32[]{:S(2)}) collective-permute-start(f32[48,128]{1,0:T(8,128)S(1)} %get-tuple-element.53), channel_id=1, source_target_pairs={{0,2},{1,3},{2,0},{3,1},{4,6},{5,7},{6,4},{7,5},{8,10},{9,11},{10,... | collective-permute-start | bytes 73736 | tf_op jit(solution)/shard_map/ppermute | solution.py:305

commit v13 on v10

--- a/solution.py
+++ b/solution.py
@@ -41,14 +41,19 @@
     return [high, middle, low]
 
 
-def stage_kernel(own, rows, residual_hbm, aggregate_hbm, residual, mine, names, block_rows, aggregate, sems):
+def stage_kernel(
+    own, rows, residual_hbm, aggregate_hbm, coarse_hbm, residual, mine, names, panel, block_rows, aggregate, sems
+):
     pairs = ((residual_hbm, residual), (aggregate_hbm, aggregate))
     copies = [pltpu.make_async_copy(a, b, sems.at[i]) for i, (a, b) in enumerate(pairs)]
     start(copies)
+    late = panel_copies(coarse_hbm, panel, panel.shape[0], sems.at[pl.ds(len(copies), 1)])
+    start(late)
     for copy in copies:
         copy.wait()
     names[...] = aggregate[...].astype(jnp.float32)
     mine[...] = rows_of(residual, own, rows, block_rows)
+    in_own_block(late[0].wait)
 
 
 def rows_of(residual, own, rows, block_rows):
@@ -59,10 +64,12 @@
     return block_rows[pl.ds(pl.multiple_of(first, 8), rows * own), :]
 
 
-def pack_kernel(own, rows, pad, margin_hbm, residual, mine, names, near_names, near, *refs):
-    *outs, away, place, block_rows, margin, sem = refs
+def pack_kernel(own, rows, pad, margin_hbm, coarse_hbm, residual, mine, names, near_names, near, *refs):
+    *outs, away, place, panel, block_rows, margin, sem, sems = refs
     copy = pltpu.make_async_copy(margin_hbm, margin, sem)
     copy.start()
+    late = panel_copies(coarse_hbm, panel, panel.shape[0], sems, panel.shape[0])
+    start(late)
     halo = margin.shape[1]
     rhs = residual.shape[0]
     me = lax.axis_index("sub")
@@ -93,6 +100,7 @@
             out[at + pad + k * rhs : at + pad + (k + 1) * rhs, :] = jnp.where(
                 owner == me, residual[:, where], near[:, where]
             )
+    in_own_block(late[0].wait)
 
 
 def panel_copies(source, target, chunk, sems, first=0):
@@ -130,7 +138,7 @@
     half = depth // 2
     each = half // chunk
     start(panel_copies(fine_hbm.at[0], fine.at[0], chunk, sems))
-    late = panel_copies(coarse_hbm, coarse, coarse.shape[0] // 4, more)
+    late = panel_copies(coarse_hbm, coarse, coarse.shape[0] // 4, more, coarse_hbm.shape[0] // 8)
 
     def step(n, carry):
         for i in range(each):
@@ -183,7 +191,7 @@
 def fine_kernel(own, rows, begin, chunk, tile, pairs, away, begun, factor, coarse_hbm, *refs):
     arrived = refs[:pairs][::-1]
     *outs, coarse, named, sums, table, sems = refs[pairs:]
-    done = coarse_hbm.shape[0] // 4
+    done = coarse_hbm.shape[0] // 8 + coarse.shape[0]
     copies = panel_copies(coarse_hbm, coarse, chunk, sems, done)
     start(copies)
     rhs = begun.shape[0]
@@ -218,10 +226,11 @@
             copy.wait()
 
 
-def coarse_kernel(own, rows, chunk, tile, upper, middle, factor_hbm, member, sums, *refs):
-    out, table, lower, begun, sems = refs
-    done = upper.shape[0] + middle.shape[0]
-    width = upper.shape[1]
+def coarse_kernel(own, rows, chunk, tile, held, factor_hbm, member, sums, *refs):
+    panels = refs[:held]
+    out, table, lower, begun, sems = refs[held:]
+    done = sum(panel.shape[0] for panel in panels)
+    width = lower.shape[1]
     copies = panel_copies(factor_hbm, lower, chunk, sems, done)
     start(copies)
     coarse = width // BLK
@@ -232,8 +241,12 @@
         return jnp.concatenate(parts, axis=1).astype(jnp.bfloat16)
 
     first = right()
-    begun[:, : upper.shape[0]] = first_product(upper, first, tile)
-    begun[:, upper.shape[0] : done] = first_product(middle, first, tile)
+    spans = []
+    at = 0
+    for panel in panels:
+        spans.append(slice(at, at + panel.shape[0]))
+        begun[:, spans[-1]] = first_product(panel, first, tile)
+        at += panel.shape[0]
 
     @in_own_block
     def _():
@@ -241,11 +254,12 @@
             copy.wait()
         low = first_product(lower, right(), tile).astype(jnp.bfloat16)
         mid = begun[...].astype(jnp.bfloat16)
-        high = mid[:, : upper.shape[0]]
-        mid = mid[:, upper.shape[0] :]
+        mids = [mid[:, part] for part in spans]
         for n in range(width // 256):
             where = slice(n * 256, (n + 1) * 256)
-            part = mm(high, upper[:, where]) + mm(mid, middle[:, where]) + mm(low, lower[:, where])
+            part = mm(low, lower[:, where])
+            for mid, panel in zip(mids, panels):
+                part = part + mm(mid, panel[:, where])
             for i in range(256 // BLK):
                 j = n * (256 // BLK) + i
                 table[pl.ds(j, rows, stride=coarse), :] = part[:, i * BLK : (i + 1) * BLK]
@@ -327,29 +341,31 @@
 
     near = swap(residual, "sub", 1)
     near_names = swap(aggregate, "sub", 1)
-    held, mine, names = call(
+    piece = sds((coarse_depth // 16, coarse_width), coarse_factor.dtype)
+    held, mine, names, first_piece = call(
         functools.partial(stage_kernel, own, rows),
-        (sds(residual.shape, f32), sds((own * rows, BLK), f32), sds((1, own), f32)),
-        [HBM, HBM],
+        (sds(residual.shape, f32), sds((own * rows, BLK), f32), sds((1, own), f32), piece),
+        [HBM, HBM, HBM],
         [
             pltpu.VMEM((own * rhs, BLK), f32),
             pltpu.VMEM((1, own), jnp.int32),
-            pltpu.SemaphoreType.DMA((2,)),
+            pltpu.SemaphoreType.DMA((3,)),
         ],
         moved=8 * rhs * own_width,
-    )(in_hbm(residual), in_hbm(aggregate))
+    )(in_hbm(residual), in_hbm(aggregate), coarse_factor)
     margin = in_hbm(margin)
-    *outgoing, away, place = call(
+    *outgoing, away, place, second_piece = call(
         functools.partial(pack_kernel, own, rows, pad),
         [sds((begin + halo * rhs, BLK), f32)] * pairs
-        + [sds((halo, BLK), jnp.int32), sds((2 * pairs * own, BLK), jnp.int32)],
-        [HBM] + [VMEM] * 5,
+        + [sds((halo, BLK), jnp.int32), sds((2 * pairs * own, BLK), jnp.int32), piece],
+        [HBM, HBM] + [VMEM] * 5,
         [
             pltpu.VMEM((own * rhs, BLK), f32),
             pltpu.SMEM(margin.shape, jnp.int32),
             pltpu.SemaphoreType.DMA,
-        ],
-    )(margin, held, mine, names, near_names, near)
+            pltpu.SemaphoreType.DMA((1,)),
+        ],
+    )(margin, coarse_factor, held, mine, names, near_names, near)
     arrived = exchange(outgoing, "sub", 2)
     quarter = coarse_depth // 4
     tile = min(512, depth // 2)
@@ -385,22 +401,24 @@
         moved=2 * depth * width + 2 * quarter * coarse_width,
     )(away, begun, local_factor, coarse_factor, *arrived[::-1])
     panels = exchange(fine, "grp")
-    lower = coarse_depth - 2 * quarter
+    panels_held = (first_piece, second_piece, coarse_upper, coarse_middle)
+    done = sum(panel.shape[0] for panel in panels_held)
+    lower = coarse_depth - done
     size = own * rows
     spread = call(
-        functools.partial(coarse_kernel, own, rows, chunk, tile),
+        functools.partial(coarse_kernel, own, rows, chunk, tile, len(panels_held)),
         sds((2 * pairs, size, BLK), f32),
-        [VMEM, VMEM, HBM, VMEM, VMEM],
+        [HBM, VMEM, VMEM] + [VMEM] * len(panels_held),
         [
             pltpu.VMEM((rows * count, BLK), f32),
             pltpu.VMEM((lower, coarse_width), coarse_factor.dtype),
-            pltpu.VMEM((rows, 2 * quarter), f32),
+            pltpu.VMEM((rows, done), f32),
             pltpu.SemaphoreType.DMA((lower // chunk,)),
         ],
         flops=4 * rows * coarse_depth * coarse_width,
         moved=2 * coarse_depth * coarse_width,
         limit=24 * MIB,
-    )(coarse_upper, coarse_middle, coarse_factor, member, sums)
+    )(coarse_factor, member, sums, *panels_held)
     field = sds((pairs, size, BLK), f32)
     kept, crossing = call(
         functools.partial(merge_kernel, own, rows, grp_count, halo),

time: 37.7 us -> 38.3 us (1.016)
  Pallas kernels: 19.2 us -> 19.8 us
    pallas_call x1, Pallas kernels: 0.93 us -> 1.32 us  [on_device(): call(functools.partial(stage_kernel, own, rows), (sds(residual.shape, f32...]
  transfers between devices with their start and end apart: 12 -> 12, of which waited for: 5 -> 4; matrix products, arithmetic and copies ran while one was open for 0% -> 0% of each run, Pallas kernels for 38% -> 38%
where the time goes in v13:
time: 38.3 us; the launch traced here: 38.1 us
  Pallas kernels  19.8 us (52%)
  starting transfers between devices  13.4 us (35%)
  waiting for transfers between devices  4.82 us (13%)
    ppermute x12, starting transfers between devices, swap(): return lax.ppermute(value, axis, [(i, i ^ distance) for i in range(count)])  13.4 us
    pallas_call x1, Pallas kernels, on_device(): call(functools.partial(coarse_kernel, own, rows, chunk, tile, len(panels_...  8.35 us
    pallas_call x1, Pallas kernels, on_device(): call(functools.partial(load_kernel, chunk, tile), (sds((rhs, depth), f32)...  4.94 us
    ppermute x12, waiting for transfers between devices, swap(): return lax.ppermute(value, axis, [(i, i ^ distance) for i in range(count)])  4.82 us
    pallas_call x1, Pallas kernels, on_device(): call(functools.partial(fine_kernel, own, rows, begin, chunk, tile, pairs)...  3.17 us
    pallas_call x1, Pallas kernels, on_device(): call(functools.partial(stage_kernel, own, rows), (sds(residual.shape, f32...  1.32 us
    pallas_call x1, Pallas kernels, on_device(): call(functools.partial(pack_kernel, own, rows, pad), [sds((begin + halo *...  1.25 us
  transfers between devices with their start and end apart: 12, of which 4 were waited for; matrix products, arithmetic and copies ran while one was open for 0% of the time, Pallas kernels for 38%

profile of v13, /device:TPU:0, one launch (start us, length us, event | category | flops | bytes accessed | tf_op | source)
XLA Modules:
  0.0 38.1 jit_solution(7684384417443435626)
XLA Ops:
  0.0 0.5 %collective-permute-start.1 = (f32[8,3072]{1,0:T(8,128)}, f32[8,3072]{1,0:T(8,128)S(1)}, u32[]{:S(2)}, u32[]{:S(2)}) collective-permute-start(f32[8,3072]{1,0:T(8,128)} %residual_hbm.1), channel_id=1, source_target_pairs={{0,1},{1,0},{2,3},{3,2},{4,5},{5,4},{6,7},{7,6},{8,9},{9,8},{10,11... | collective-permute-start | bytes 294920 | tf_op jit(solution)/shard_map/ppermute | solution.py:315
  0.5 0.1 collective-permute-start
  0.5 1.3 %shard_map.55 = (f32[8,3072]{1,0:T(8,128)S(1)}, f32[48,128]{1,0:T(8,128)S(1)}, f32[1,24]{1,0:T(1,128)S(1)}, bf16[64,8192]{1,0:T(8,128)(2,1)S(1)}) custom-call(f32[8,3072]{1,0:T(8,128)} %residual_hbm.1, s32[1,24]{1,0:T(1,128)} %bitcast.2, bf16[1024,8192]{1,0:T(8,128)(2,1)} %factor_hbm.1), custom_call_target="tpu_custom_call" | custom-call | bytes 196608 | tf_op jit(solution)/shard_map/pallas_call | solution.py:345
  1.8 0.0 collective-permute-done.near_names
  1.9 0.0 collective-permute-done.1.near
  1.9 1.2 %shard_map.56 = (f32[168,128]{1,0:T(8,128)S(1)}, f32[168,128]{1,0:T(8,128)S(1)}, f32[168,128]{1,0:T(8,128)S(1)}, f32[168,128]{1,0:T(8,128)S(1)}, s32[8,128]{1,0:...) custom-call(s32[8,8]{1,0:T(8,128)} %margin_hbm.1, bf16[1024,8192]{1,0:T(8,128)(2,1)} %factor_hbm.1, ...), custom_call_target="tpu_custom_call" | custom-call | tf_op jit(solution)/shard_map/pallas_call | solution.py:357
  3.1 4.0 %collective-permute-start.2 = (f32[168,128]{1,0:T(8,128)S(1)}, f32[168,128]{1,0:T(8,128)S(1)}, u32[]{:S(2)}, u32[]{:S(2)}) collective-permute-start(f32[168,128]{1,0:T(8,128)S(1)} %get-tuple-element.40), channel_id=1, source_target_pairs={{0,6},{1,7},{2,4},{3,5},{4,2},{5,3},{6,0},{7,1},{8,14},{9,15},{10,... | collective-permute-start | bytes 258056 | tf_op jit(solution)/shard_map/ppermute | solution.py:315
  7.1 0.5 %collective-permute-start.3 = (f32[168,128]{1,0:T(8,128)S(1)}, f32[168,128]{1,0:T(8,128)S(1)}, u32[]{:S(2)}, u32[]{:S(2)}) collective-permute-start(f32[168,128]{1,0:T(8,128)S(1)} %get-tuple-element.41), channel_id=1, source_target_pairs={{0,4},{1,5},{2,6},{3,7},{4,0},{5,1},{6,2},{7,3},{8,12},{9,13},{10,... | collective-permute-start | bytes 258056 | tf_op jit(solution)/shard_map/ppermute | solution.py:315
  7.6 0.1 collective-permute-start.4
  7.7 4.9 %shard_map.57 = (f32[8,1024]{1,0:T(8,128)S(1)}, bf16[1,1024,4096]{2,1,0:T(8,128)(2,1)S(1)}, bf16[256,8192]{1,0:T(8,128)(2,1)S(1)}) custom-call(f32[8,3072]{1,0:T(8,128)S(1)} %get-tuple-element.32.residual, bf16[1,1024,4096]{2,1,0:T(8,128)(2,1)} %fine_hbm.1, bf16[1024,8192]{1,0:T(8,128)(2,1)} %factor_hbm.1, f32[168,128]{1,0:T(8,128)S(1)} %get-tuple-element.37.after.refs_3_), custom_call_target="tpu_custom_call" | custom-call | flops 50331648 | bytes 12582912 | tf_op jit(solution)/shard_map/pallas_call | solution.py:373
  12.7 0.0 collective-permute-done.2.refs_0_
  12.7 0.0 collective-permute-done.3.refs_1_
  12.7 0.0 collective-permute-done.4.refs_2_
  12.7 3.2 %shard_map.58 = (f32[64,128]{1,0:T(8,128)S(1)}, f32[64,128]{1,0:T(8,128)S(1)}, f32[64,128]{1,0:T(8,128)S(1)}, f32[64,128]{1,0:T(8,128)S(1)}, bf16[256,8192]{1,0:...) custom-call(s32[8,128]{1,0:T(8,128)S(1)} %get-tuple-element.36.away, ...), custom_call_target="tpu_custom_call" | custom-call | flops 134217728 | bytes 12582912 | tf_op jit(solution)/shard_map/pallas_call | solution.py:390
  15.9 2.0 %collective-permute-start.5 = (f32[64,128]{1,0:T(8,128)S(1)}, f32[64,128]{1,0:T(8,128)S(1)}, u32[]{:S(2)}, u32[]{:S(2)}) collective-permute-start(f32[64,128]{1,0:T(8,128)S(1)} %get-tuple-element.50), channel_id=1, source_target_pairs={{0,8},{8,0},{16,24},{24,16},{1,9},{9,1},{17,25},{25,17},{2,10},{10... | collective-permute-start | bytes 98312 | tf_op jit(solution)/shard_map/ppermute | solution.py:315
  17.9 2.6 %collective-permute-start.6 = (f32[64,128]{1,0:T(8,128)S(1)}, f32[64,128]{1,0:T(8,128)S(1)}, u32[]{:S(2)}, u32[]{:S(2)}) collective-permute-start(f32[64,128]{1,0:T(8,128)S(1)} %get-tuple-element.51), channel_id=1, source_target_pairs={{0,16},{8,24},{16,0},{24,8},{1,17},{9,25},{17,1},{25,9},{2,18},{10... | collective-permute-start | bytes 98312 | tf_op jit(solution)/shard_map/ppermute | solution.py:315
  20.5 0.0 collective-permute-start.7
  20.5 8.3 %shard_map.59.spread = f32[8,48,128]{2,1,0:T(8,128)S(1)} custom-call(bf16[1024,8192]{1,0:T(8,128)(2,1)} %factor_hbm.1, f32[192,64]{1,0:T(8,128)S(1)} %get-tuple-element.43.member, f32[128,128]{1,0:T(8,128)S(1)} %get-tuple-element.44.sums, bf16[64,8192]{1,0:T(8,128)(2,1)S(1)} %get-tuple-element.45.refs_0_, bf16[64,8192]{1,0:T(8,128)(2,1)S(1)} %get-tuple-element.46.refs_1_, ...), custom_call_target="tpu_custom_call" | custom-call | flops 67108864 | bytes 16777216 | tf_op jit(solution)/shard_map/pallas_call | solution.py:408
  28.9 0.0 collective-permute-done.5.refs_1_
  28.9 0.0 collective-permute-done.6.refs_2_
  28.9 0.0 collective-permute-done.7.refs_3_
  28.9 0.1 shard_map.60
  29.0 0.1 collective-permute-start.8
  29.1 1.3 %collective-permute-done.8.arrived = f32[4,48,128]{2,1,0:T(8,128)S(1)} collective-permute-done((f32[4,48,128]{2,1,0:T(8,128)S(1)}, f32[4,48,128]{2,1,0:T(8,128)S(1)}, u32[]{:S(2)}, u32[]{:S(2)}) %collective-permute-start.8) | collective-permute-done | bytes 98336 | tf_op jit(solution)/shard_map/ppermute | solution.py:315
  30.4 2.7 %collective-permute-start.9 = (f32[48,128]{1,0:T(8,128)S(1)}, f32[48,128]{1,0:T(8,128)S(1)}, u32[]{:S(2)}, u32[]{:S(2)}) collective-permute-start(f32[48,128]{1,0:T(8,128)S(1)} %get-tuple-element.55), channel_id=1, source_target_pairs={{0,6},{1,7},{2,4},{3,5},{4,2},{5,3},{6,0},{7,1},{8,14},{9,15},{10,... | collective-permute-start | bytes 73736 | tf_op jit(solution)/shard_map/ppermute | solution.py:315
  33.2 0.5 %collective-permute-start.10 = (f32[48,128]{1,0:T(8,128)S(1)}, f32[48,128]{1,0:T(8,128)S(1)}, u32[]{:S(2)}, u32[]{:S(2)}) collective-permute-start(f32[48,128]{1,0:T(8,128)S(1)} %get-tuple-element.56), channel_id=1, source_target_pairs={{0,4},{1,5},{2,6},{3,7},{4,0},{5,1},{6,2},{7,3},{8,12},{9,13},{10,... | collective-permute-start | bytes 73736 | tf_op jit(solution)/shard_map/ppermute | solution.py:315
  33.7 0.3 collective-permute-start.11
  34.0 1.2 %collective-permute-done.9.refs_0_ = f32[48,128]{1,0:T(8,128)S(1)} collective-permute-done((f32[48,128]{1,0:T(8,128)S(1)}, f32[48,128]{1,0:T(8,128)S(1)}, u32[]{:S(2)}, u32[]{:S(2)}) %collective-permute-start.9) | collective-permute-done | bytes 24608 | tf_op jit(solution)/shard_map/ppermute | solution.py:315
  35.2 1.8 %collective-permute-done.10.refs_1_ = f32[48,128]{1,0:T(8,128)S(1)} collective-permute-done((f32[48,128]{1,0:T(8,128)S(1)}, f32[48,128]{1,0:T(8,128)S(1)}, u32[]{:S(2)}, u32[]{:S(2)}) %collective-permute-start.10) | collective-permute-done | bytes 24608 | tf_op jit(solution)/shard_map/ppermute | solution.py:315
  37.0 0.5 %collective-permute-done.11.refs_2_ = f32[48,128]{1,0:T(8,128)S(1)} collective-permute-done((f32[48,128]{1,0:T(8,128)S(1)}, f32[48,128]{1,0:T(8,128)S(1)}, u32[]{:S(2)}, u32[]{:S(2)}) %collective-permute-start.11) | collective-permute-done | bytes 24608 | tf_op jit(solution)/shard_map/ppermute | solution.py:315
  37.5 0.6 %shard_map.62 = f32[2,3072]{1,0:T(2,128)} custom-call(f32[48,128]{1,0:T(8,128)S(1)} %collective-permute-done.9.refs_0_, f32[48,128]{1,0:T(8,128)S(1)} %collective-permute-done.10.refs_1_, f32[48,128]{1,0:T(8,128)S(1)} %collective-permute-done.11.refs_2_, f32[48,128]{1,0:T(8,128)S(1)} %get-tuple-element.58.refs_3_), custom_call_target="tpu_custom_call" | custom-call | tf_op jit(solution)/shard_map/pallas_call | solution.py:431
  (1 shorter events, 0.0 us)
Async XLA Ops:
  0.0 1.9 %collective-permute-start.1 = (f32[8,3072]{1,0:T(8,128)}, f32[8,3072]{1,0:T(8,128)S(1)}, u32[]{:S(2)}, u32[]{:S(2)}) collective-permute-start(f32[8,3072]{1,0:T(8,128)} %residual_hbm.1), channel_id=1, source_target_pairs={{0,1},{1,0},{2,3},{3,2},{4,5},{5,4},{6,7},{7,6},{8,9},{9,8},{10,11... | collective-permute-start | bytes 294920 | tf_op jit(solution)/shard_map/ppermute | solution.py:315
  0.5 1.4 %collective-permute-start = (s32[1,24]{1,0:T(1,128)}, s32[1,24]{1,0:T(1,128)S(1)}, u32[]{:S(2)}, u32[]{:S(2)}) collective-permute-start(s32[1,24]{1,0:T(1,128)} %bitcast.1), channel_id=1, source_target_pairs={{0,1},{1,0},{2,3},{3,2},{4,5},{5,4},{6,7},{7,6},{8,9},{9,8},{10,11... | collective-permute-start | bytes 296 | tf_op jit(solution)/shard_map/ppermute | solution.py:315
  3.1 9.6 %collective-permute-start.2 = (f32[168,128]{1,0:T(8,128)S(1)}, f32[168,128]{1,0:T(8,128)S(1)}, u32[]{:S(2)}, u32[]{:S(2)}) collective-permute-start(f32[168,128]{1,0:T(8,128)S(1)} %get-tuple-element.40), channel_id=1, source_target_pairs={{0,6},{1,7},{2,4},{3,5},{4,2},{5,3},{6,0},{7,1},{8,14},{9,15},{10,... | collective-permute-start | bytes 258056 | tf_op jit(solution)/shard_map/ppermute | solution.py:315
  7.1 5.6 %collective-permute-start.3 = (f32[168,128]{1,0:T(8,128)S(1)}, f32[168,128]{1,0:T(8,128)S(1)}, u32[]{:S(2)}, u32[]{:S(2)}) collective-permute-start(f32[168,128]{1,0:T(8,128)S(1)} %get-tuple-element.41), channel_id=1, source_target_pairs={{0,4},{1,5},{2,6},{3,7},{4,0},{5,1},{6,2},{7,3},{8,12},{9,13},{10,... | collective-permute-start | bytes 258056 | tf_op jit(solution)/shard_map/ppermute | solution.py:315
  7.6 5.1 %collective-permute-start.4 = (f32[168,128]{1,0:T(8,128)S(1)}, f32[168,128]{1,0:T(8,128)S(1)}, u32[]{:S(2)}, u32[]{:S(2)}) collective-permute-start(f32[168,128]{1,0:T(8,128)S(1)} %get-tuple-element.42), channel_id=1, source_target_pairs={{0,2},{1,3},{2,0},{3,1},{4,6},{5,7},{6,4},{7,5},{8,10},{9,11},{10,... | collective-permute-start | bytes 258056 | tf_op jit(solution)/shard_map/ppermute | solution.py:315
  15.9 13.0 %collective-permute-start.5 = (f32[64,128]{1,0:T(8,128)S(1)}, f32[64,128]{1,0:T(8,128)S(1)}, u32[]{:S(2)}, u32[]{:S(2)}) collective-permute-start(f32[64,128]{1,0:T(8,128)S(1)} %get-tuple-element.50), channel_id=1, source_target_pairs={{0,8},{8,0},{16,24},{24,16},{1,9},{9,1},{17,25},{25,17},{2,10},{10... | collective-permute-start | bytes 98312 | tf_op jit(solution)/shard_map/ppermute | solution.py:315
  17.9 11.0 %collective-permute-start.6 = (f32[64,128]{1,0:T(8,128)S(1)}, f32[64,128]{1,0:T(8,128)S(1)}, u32[]{:S(2)}, u32[]{:S(2)}) collective-permute-start(f32[64,128]{1,0:T(8,128)S(1)} %get-tuple-element.51), channel_id=1, source_target_pairs={{0,16},{8,24},{16,0},{24,8},{1,17},{9,25},{17,1},{25,9},{2,18},{10... | collective-permute-start | bytes 98312 | tf_op jit(solution)/shard_map/ppermute | solution.py:315
  20.5 8.4 %collective-permute-start.7 = (f32[64,128]{1,0:T(8,128)S(1)}, f32[64,128]{1,0:T(8,128)S(1)}, u32[]{:S(2)}, u32[]{:S(2)}) collective-permute-start(f32[64,128]{1,0:T(8,128)S(1)} %get-tuple-element.52), channel_id=1, source_target_pairs={{0,24},{8,16},{16,8},{24,0},{1,25},{9,17},{17,9},{25,1},{2,26},{10... | collective-permute-start | bytes 98312 | tf_op jit(solution)/shard_map/ppermute | solution.py:315
  29.0 1.4 %collective-permute-start.8 = (f32[4,48,128]{2,1,0:T(8,128)S(1)}, f32[4,48,128]{2,1,0:T(8,128)S(1)}, u32[]{:S(2)}, u32[]{:S(2)}) collective-permute-start(f32[4,48,128]{2,1,0:T(8,128)S(1)} %get-tuple-element.54), channel_id=1, source_target_pairs={{0,1},{1,0},{2,3},{3,2},{4,5},{5,4},{6,7},{7,6},{8,9},{9,8},{10,11... | collective-permute-start | bytes 294920 | tf_op jit(solution)/shard_map/ppermute | solution.py:315
  30.4 4.8 %collective-permute-start.9 = (f32[48,128]{1,0:T(8,128)S(1)}, f32[48,128]{1,0:T(8,128)S(1)}, u32[]{:S(2)}, u32[]{:S(2)}) collective-permute-start(f32[48,128]{1,0:T(8,128)S(1)} %get-tuple-element.55), channel_id=1, source_target_pairs={{0,6},{1,7},{2,4},{3,5},{4,2},{5,3},{6,0},{7,1},{8,14},{9,15},{10,... | collective-permute-start | bytes 73736 | tf_op jit(solution)/shard_map/ppermute | solution.py:315
  33.2 3.8 %collective-permute-start.10 = (f32[48,128]{1,0:T(8,128)S(1)}, f32[48,128]{1,0:T(8,128)S(1)}, u32[]{:S(2)}, u32[]{:S(2)}) collective-permute-start(f32[48,128]{1,0:T(8,128)S(1)} %get-tuple-element.56), channel_id=1, source_target_pairs={{0,4},{1,5},{2,6},{3,7},{4,0},{5,1},{6,2},{7,3},{8,12},{9,13},{10,... | collective-permute-start | bytes 73736 | tf_op jit(solution)/shard_map/ppermute | solution.py:315
  33.7 3.8 %collective-permute-start.11 = (f32[48,128]{1,0:T(8,128)S(1)}, f32[48,128]{1,0:T(8,128)S(1)}, u32[]{:S(2)}, u32[]{:S(2)}) collective-permute-start(f32[48,128]{1,0:T(8,128)S(1)} %get-tuple-element.57), channel_id=1, source_target_pairs={{0,2},{1,3},{2,0},{3,1},{4,6},{5,7},{6,4},{7,5},{8,10},{9,11},{10,... | collective-permute-start | bytes 73736 | tf_op jit(solution)/shard_map/ppermute | solution.py:315

commit v14 on v10

--- a/solution.py
+++ b/solution.py
@@ -130,7 +130,8 @@
     half = depth // 2
     each = half // chunk
     start(panel_copies(fine_hbm.at[0], fine.at[0], chunk, sems))
-    late = panel_copies(coarse_hbm, coarse, coarse.shape[0] // 4, more)
+    quarter = coarse.shape[0] // 4
+    late = panel_copies(coarse_hbm, coarse.at[pl.ds(0, quarter)], quarter // 4, more)
 
     def step(n, carry):
         for i in range(each):
@@ -180,11 +181,11 @@
     named[...] = member.astype(jnp.float32)
 
 
-def fine_kernel(own, rows, begin, chunk, tile, pairs, away, begun, factor, coarse_hbm, *refs):
+def fine_kernel(own, rows, begin, chunk, tile, pairs, away, begun, factor, coarse_hbm, given, *refs):
     arrived = refs[:pairs][::-1]
     *outs, coarse, named, sums, table, sems = refs[pairs:]
-    done = coarse_hbm.shape[0] // 4
-    copies = panel_copies(coarse_hbm, coarse, chunk, sems, done)
+    quarter = coarse.shape[0] // 4
+    copies = panel_copies(coarse_hbm, coarse.at[pl.ds(quarter, quarter)], chunk, sems, quarter)
     start(copies)
     rhs = begun.shape[0]
     halo = away.shape[0]
@@ -218,10 +219,10 @@
             copy.wait()
 
 
-def coarse_kernel(own, rows, chunk, tile, upper, middle, factor_hbm, member, sums, *refs):
-    out, table, lower, begun, sems = refs
-    done = upper.shape[0] + middle.shape[0]
-    width = upper.shape[1]
+def coarse_kernel(own, rows, chunk, tile, given, factor_hbm, member, sums, out, factor, table, begun, sems):
+    depth, width = factor.shape
+    done = depth // 2
+    held, lower = factor.at[pl.ds(0, done)], factor.at[pl.ds(done, depth - done)]
     copies = panel_copies(factor_hbm, lower, chunk, sems, done)
     start(copies)
     coarse = width // BLK
@@ -232,20 +233,17 @@
         return jnp.concatenate(parts, axis=1).astype(jnp.bfloat16)
 
     first = right()
-    begun[:, : upper.shape[0]] = first_product(upper, first, tile)
-    begun[:, upper.shape[0] : done] = first_product(middle, first, tile)
+    begun[:, :done] = first_product(held, first, tile)
 
     @in_own_block
     def _():
         for copy in copies:
             copy.wait()
-        low = first_product(lower, right(), tile).astype(jnp.bfloat16)
+        begun[:, done:] = first_product(lower, right(), tile)
         mid = begun[...].astype(jnp.bfloat16)
-        high = mid[:, : upper.shape[0]]
-        mid = mid[:, upper.shape[0] :]
         for n in range(width // 256):
             where = slice(n * 256, (n + 1) * 256)
-            part = mm(high, upper[:, where]) + mm(mid, middle[:, where]) + mm(low, lower[:, where])
+            part = mm(mid, factor[:, where])
             for i in range(256 // BLK):
                 j = n * (256 // BLK) + i
                 table[pl.ds(j, rows, stride=coarse), :] = part[:, i * BLK : (i + 1) * BLK]
@@ -354,12 +352,13 @@
     quarter = coarse_depth // 4
     tile = min(512, depth // 2)
     chunk = depth // 8
-    begun, local_factor, coarse_upper = call(
+    coarse_held = sds(coarse_factor.shape, coarse_factor.dtype)
+    begun, local_factor, coarse_part = call(
         functools.partial(load_kernel, chunk, tile),
         (
             sds((rhs, depth), f32),
             sds(local_factor.shape, local_factor.dtype),
-            sds((quarter, coarse_width), coarse_factor.dtype),
+            coarse_held,
         ),
         [VMEM, HBM, HBM, pl.BlockSpec(memory_space=pl.ANY)],
         [
@@ -371,36 +370,36 @@
     )(held, local_factor, coarse_factor, arrived[0])
     chunk = quarter // 4
     count = coarse_width // BLK
-    *fine, coarse_middle, member, sums = call(
+    *fine, coarse_part, member, sums = call(
         functools.partial(fine_kernel, own, rows, begin, chunk, tile, pairs),
         [sds((rows * blocks, BLK), f32)] * grp_count
         + [
-            sds((quarter, coarse_width), coarse_factor.dtype),
+            coarse_held,
             sds((2 * pairs * own, count), f32),
             sds((rows * count, BLK), f32),
         ],
-        [VMEM, VMEM, VMEM, HBM] + [VMEM] * pairs,
+        [VMEM, VMEM, VMEM, HBM, VMEM] + [VMEM] * pairs,
         [pltpu.VMEM((rhs * blocks, BLK), f32), pltpu.SemaphoreType.DMA((quarter // chunk,))],
         flops=4 * rhs * depth * width,
         moved=2 * depth * width + 2 * quarter * coarse_width,
-    )(away, begun, local_factor, coarse_factor, *arrived[::-1])
+        input_output_aliases={4: grp_count},
+    )(away, begun, local_factor, coarse_factor, coarse_part, *arrived[::-1])
     panels = exchange(fine, "grp")
     lower = coarse_depth - 2 * quarter
     size = own * rows
-    spread = call(
+    spread, _ = call(
         functools.partial(coarse_kernel, own, rows, chunk, tile),
-        sds((2 * pairs, size, BLK), f32),
-        [VMEM, VMEM, HBM, VMEM, VMEM],
+        (sds((2 * pairs, size, BLK), f32), coarse_held),
+        [VMEM, HBM, VMEM, VMEM],
         [
             pltpu.VMEM((rows * count, BLK), f32),
-            pltpu.VMEM((lower, coarse_width), coarse_factor.dtype),
-            pltpu.VMEM((rows, 2 * quarter), f32),
+            pltpu.VMEM((rows, coarse_depth), f32),
             pltpu.SemaphoreType.DMA((lower // chunk,)),
         ],
         flops=4 * rows * coarse_depth * coarse_width,
         moved=2 * coarse_depth * coarse_width,
-        limit=24 * MIB,
-    )(coarse_upper, coarse_middle, coarse_factor, member, sums)
+        input_output_aliases={0: 1},
+    )(coarse_part, coarse_factor, member, sums)
     field = sds((pairs, size, BLK), f32)
     kept, crossing = call(
         functools.partial(merge_kernel, own, rows, grp_count, halo),

time: 37.7 us -> 37.2 us (0.987)
  Pallas kernels: 19.2 us -> 18.7 us
    pallas_call x1, Pallas kernels: 3.17 us -> 2.69 us  [on_device(): call(functools.partial(fine_kernel, own, rows, begin, chunk, tile, pairs)...]
where the time goes in v14:
time: 37.2 us; the launch traced here: 37 us
  Pallas kernels  18.7 us (50%)
  starting transfers between devices  13.2 us (35%)
  waiting for transfers between devices  5.07 us (14%)
    ppermute x12, starting transfers between devices, swap(): return lax.ppermute(value, axis, [(i, i ^ distance) for i in range(count)])  13.2 us
    pallas_call x1, Pallas kernels, on_device(): call(functools.partial(coarse_kernel, own, rows, chunk, tile), (sds((2 *...  8.27 us
    ppermute x12, waiting for transfers between devices, swap(): return lax.ppermute(value, axis, [(i, i ^ distance) for i in range(count)])  5.07 us
    pallas_call x1, Pallas kernels, on_device(): call(functools.partial(load_kernel, chunk, tile), (sds((rhs, depth), f32)...  4.94 us
    pallas_call x1, Pallas kernels, on_device(): call(functools.partial(fine_kernel, own, rows, begin, chunk, tile, pairs)...  2.69 us
    pallas_call x1, Pallas kernels, on_device(): call(functools.partial(pack_kernel, own, rows, pad), [sds((begin + halo *...  1.08 us
    pallas_call x1, Pallas kernels, on_device(): call(functools.partial(stage_kernel, own, rows), (sds(residual.shape, f32...  0.93 us
  transfers between devices with their start and end apart: 12, of which 5 were waited for; matrix products, arithmetic and copies ran while one was open for 0% of the time, Pallas kernels for 38%

profile of v14, /device:TPU:0, one launch (start us, length us, event | category | flops | bytes accessed | tf_op | source)
XLA Modules:
  0.0 37.0 jit_solution(17218291628792874561)
XLA Ops:
  0.0 0.5 %collective-permute-start.1 = (f32[8,3072]{1,0:T(8,128)}, f32[8,3072]{1,0:T(8,128)S(1)}, u32[]{:S(2)}, u32[]{:S(2)}) collective-permute-start(f32[8,3072]{1,0:T(8,128)} %residual_hbm.1), channel_id=1, source_target_pairs={{0,1},{1,0},{2,3},{3,2},{4,5},{5,4},{6,7},{7,6},{8,9},{9,8},{10,11... | collective-permute-start | bytes 294920 | tf_op jit(solution)/shard_map/ppermute | solution.py:299
  0.5 0.1 collective-permute-start
  0.5 0.9 %shard_map.55 = (f32[8,3072]{1,0:T(8,128)S(1)}, f32[48,128]{1,0:T(8,128)S(1)}, f32[1,24]{1,0:T(1,128)S(1)}) custom-call(f32[8,3072]{1,0:T(8,128)} %residual_hbm.1, s32[1,24]{1,0:T(1,128)} %bitcast.2), custom_call_target="tpu_custom_call" | custom-call | bytes 196608 | tf_op jit(solution)/shard_map/pallas_call | solution.py:328
  1.5 0.3 collective-permute-done.near_names
  1.7 0.0 collective-permute-done.1.near
  1.7 1.1 %shard_map.56 = (f32[168,128]{1,0:T(8,128)S(1)}, f32[168,128]{1,0:T(8,128)S(1)}, f32[168,128]{1,0:T(8,128)S(1)}, f32[168,128]{1,0:T(8,128)S(1)}, s32[8,128]{1,0:T(8,128)S(1)}, /*index=5*/s32[192,128]{1,0:T(8,128)S(1)}) custom-call(s32[8,8]{1,0:T(8,128)} %margin_hbm.1, f32[8,3072]{1,0:T(8,128)S(1)} %get-tuple-element.31.residual, ...), custom_call_target="tpu_custom_call" | custom-call | tf_op jit(solution)/shard_map/pallas_call | solution.py:340
  2.8 3.8 %collective-permute-start.2 = (f32[168,128]{1,0:T(8,128)S(1)}, f32[168,128]{1,0:T(8,128)S(1)}, u32[]{:S(2)}, u32[]{:S(2)}) collective-permute-start(f32[168,128]{1,0:T(8,128)S(1)} %get-tuple-element.40), channel_id=1, source_target_pairs={{0,6},{1,7},{2,4},{3,5},{4,2},{5,3},{6,0},{7,1},{8,14},{9,15},{10,... | collective-permute-start | bytes 258056 | tf_op jit(solution)/shard_map/ppermute | solution.py:299
  6.6 0.5 %collective-permute-start.3 = (f32[168,128]{1,0:T(8,128)S(1)}, f32[168,128]{1,0:T(8,128)S(1)}, u32[]{:S(2)}, u32[]{:S(2)}) collective-permute-start(f32[168,128]{1,0:T(8,128)S(1)} %get-tuple-element.41), channel_id=1, source_target_pairs={{0,4},{1,5},{2,6},{3,7},{4,0},{5,1},{6,2},{7,3},{8,12},{9,13},{10,... | collective-permute-start | bytes 258056 | tf_op jit(solution)/shard_map/ppermute | solution.py:299
  7.1 0.1 collective-permute-start.4
  7.2 4.9 %shard_map.57 = (f32[8,1024]{1,0:T(8,128)S(1)}, bf16[1,1024,4096]{2,1,0:T(8,128)(2,1)S(1)}, bf16[1024,8192]{1,0:T(8,128)(2,1)S(1)}) custom-call(f32[8,3072]{1,0:T(8,128)S(1)} %get-tuple-element.31.residual, bf16[1,1024,4096]{2,1,0:T(8,128)(2,1)} %fine_hbm.1, bf16[1024,8192]{1,0:T(8,128)(2,1)} %factor_hbm.1, f32[168,128]{1,0:T(8,128)S(1)} %get-tuple-element.36.after.refs_3_), custom_call_target="tpu_custom_call" | custom-call | flops 50331648 | bytes 12582912 | tf_op jit(solution)/shard_map/pallas_call | solution.py:356
  12.2 0.0 collective-permute-done.2.refs_0_
  12.2 0.0 collective-permute-done.3.refs_1_
  12.2 0.0 collective-permute-done.4.refs_2_
  12.2 2.7 %shard_map.58 = (f32[64,128]{1,0:T(8,128)S(1)}, f32[64,128]{1,0:T(8,128)S(1)}, f32[64,128]{1,0:T(8,128)S(1)}, f32[64,128]{1,0:T(8,128)S(1)}, bf16[1024,8192]{1,0...) custom-call(s32[8,128]{1,0:T(8,128)S(1)} %get-tuple-element.35.away, ...), custom_call_target="tpu_custom_call", output_to_operand_aliasing={{4}: (4, {})} | custom-call | flops 134217728 | bytes 12582912 | tf_op jit(solution)/shard_map/pallas_call | solution.py:373
  14.9 2.0 %collective-permute-start.5 = (f32[64,128]{1,0:T(8,128)S(1)}, f32[64,128]{1,0:T(8,128)S(1)}, u32[]{:S(2)}, u32[]{:S(2)}) collective-permute-start(f32[64,128]{1,0:T(8,128)S(1)} %get-tuple-element.48), channel_id=1, source_target_pairs={{0,8},{8,0},{16,24},{24,16},{1,9},{9,1},{17,25},{25,17},{2,10},{10... | collective-permute-start | bytes 98312 | tf_op jit(solution)/shard_map/ppermute | solution.py:299
  16.9 2.6 %collective-permute-start.6 = (f32[64,128]{1,0:T(8,128)S(1)}, f32[64,128]{1,0:T(8,128)S(1)}, u32[]{:S(2)}, u32[]{:S(2)}) collective-permute-start(f32[64,128]{1,0:T(8,128)S(1)} %get-tuple-element.49), channel_id=1, source_target_pairs={{0,16},{8,24},{16,0},{24,8},{1,17},{9,25},{17,1},{25,9},{2,18},{10... | collective-permute-start | bytes 98312 | tf_op jit(solution)/shard_map/ppermute | solution.py:299
  19.5 0.0 collective-permute-start.7
  19.5 8.3 %shard_map.59 = (f32[8,48,128]{2,1,0:T(8,128)S(1)}, bf16[1024,8192]{1,0:T(8,128)(2,1)S(1)}) custom-call(bf16[1024,8192]{1,0:T(8,128)(2,1)S(1)} %get-tuple-element.43.given, bf16[1024,8192]{1,0:T(8,128)(2,1)} %factor_hbm.1, f32[192,64]{1,0:T(8,128)S(1)} %get-tuple-element.44.member, ...), custom_call_target="tpu_custom_call", output_to_operand_aliasing={{1}: (0, {})} | custom-call | flops 67108864 | bytes 16777216 | tf_op jit(solution)/shard_map/pallas_call | solution.py:390
  27.8 0.0 collective-permute-done.5.refs_1_
  27.8 0.0 collective-permute-done.6.refs_2_
  27.8 0.0 collective-permute-done.7.refs_3_
  27.8 0.1 shard_map.60
  28.0 0.1 collective-permute-start.8
  28.0 1.3 %collective-permute-done.8.arrived = f32[4,48,128]{2,1,0:T(8,128)S(1)} collective-permute-done((f32[4,48,128]{2,1,0:T(8,128)S(1)}, f32[4,48,128]{2,1,0:T(8,128)S(1)}, u32[]{:S(2)}, u32[]{:S(2)}) %collective-permute-start.8) | collective-permute-done | bytes 98336 | tf_op jit(solution)/shard_map/ppermute | solution.py:299
  29.3 2.7 %collective-permute-start.9 = (f32[48,128]{1,0:T(8,128)S(1)}, f32[48,128]{1,0:T(8,128)S(1)}, u32[]{:S(2)}, u32[]{:S(2)}) collective-permute-start(f32[48,128]{1,0:T(8,128)S(1)} %get-tuple-element.53), channel_id=1, source_target_pairs={{0,6},{1,7},{2,4},{3,5},{4,2},{5,3},{6,0},{7,1},{8,14},{9,15},{10,... | collective-permute-start | bytes 73736 | tf_op jit(solution)/shard_map/ppermute | solution.py:299
  32.1 0.5 %collective-permute-start.10 = (f32[48,128]{1,0:T(8,128)S(1)}, f32[48,128]{1,0:T(8,128)S(1)}, u32[]{:S(2)}, u32[]{:S(2)}) collective-permute-start(f32[48,128]{1,0:T(8,128)S(1)} %get-tuple-element.54), channel_id=1, source_target_pairs={{0,4},{1,5},{2,6},{3,7},{4,0},{5,1},{6,2},{7,3},{8,12},{9,13},{10,... | collective-permute-start | bytes 73736 | tf_op jit(solution)/shard_map/ppermute | solution.py:299
  32.6 0.3 collective-permute-start.11
  32.9 1.2 %collective-permute-done.9.refs_0_ = f32[48,128]{1,0:T(8,128)S(1)} collective-permute-done((f32[48,128]{1,0:T(8,128)S(1)}, f32[48,128]{1,0:T(8,128)S(1)}, u32[]{:S(2)}, u32[]{:S(2)}) %collective-permute-start.9) | collective-permute-done | bytes 24608 | tf_op jit(solution)/shard_map/ppermute | solution.py:299
  34.1 1.8 %collective-permute-done.10.refs_1_ = f32[48,128]{1,0:T(8,128)S(1)} collective-permute-done((f32[48,128]{1,0:T(8,128)S(1)}, f32[48,128]{1,0:T(8,128)S(1)}, u32[]{:S(2)}, u32[]{:S(2)}) %collective-permute-start.10) | collective-permute-done | bytes 24608 | tf_op jit(solution)/shard_map/ppermute | solution.py:299
  35.9 0.5 %collective-permute-done.11.refs_2_ = f32[48,128]{1,0:T(8,128)S(1)} collective-permute-done((f32[48,128]{1,0:T(8,128)S(1)}, f32[48,128]{1,0:T(8,128)S(1)}, u32[]{:S(2)}, u32[]{:S(2)}) %collective-permute-start.11) | collective-permute-done | bytes 24608 | tf_op jit(solution)/shard_map/ppermute | solution.py:299
  36.4 0.6 %shard_map.62 = f32[2,3072]{1,0:T(2,128)} custom-call(f32[48,128]{1,0:T(8,128)S(1)} %collective-permute-done.9.refs_0_, f32[48,128]{1,0:T(8,128)S(1)} %collective-permute-done.10.refs_1_, f32[48,128]{1,0:T(8,128)S(1)} %collective-permute-done.11.refs_2_, f32[48,128]{1,0:T(8,128)S(1)} %get-tuple-element.56.refs_3_), custom_call_target="tpu_custom_call" | custom-call | tf_op jit(solution)/shard_map/pallas_call | solution.py:412
  (1 shorter events, 0.0 us)
Async XLA Ops:
  0.0 1.7 %collective-permute-start.1 = (f32[8,3072]{1,0:T(8,128)}, f32[8,3072]{1,0:T(8,128)S(1)}, u32[]{:S(2)}, u32[]{:S(2)}) collective-permute-start(f32[8,3072]{1,0:T(8,128)} %residual_hbm.1), channel_id=1, source_target_pairs={{0,1},{1,0},{2,3},{3,2},{4,5},{5,4},{6,7},{7,6},{8,9},{9,8},{10,11... | collective-permute-start | bytes 294920 | tf_op jit(solution)/shard_map/ppermute | solution.py:299
  0.5 1.3 %collective-permute-start = (s32[1,24]{1,0:T(1,128)}, s32[1,24]{1,0:T(1,128)S(1)}, u32[]{:S(2)}, u32[]{:S(2)}) collective-permute-start(s32[1,24]{1,0:T(1,128)} %bitcast.1), channel_id=1, source_target_pairs={{0,1},{1,0},{2,3},{3,2},{4,5},{5,4},{6,7},{7,6},{8,9},{9,8},{10,11... | collective-permute-start | bytes 296 | tf_op jit(solution)/shard_map/ppermute | solution.py:299
  2.8 9.4 %collective-permute-start.2 = (f32[168,128]{1,0:T(8,128)S(1)}, f32[168,128]{1,0:T(8,128)S(1)}, u32[]{:S(2)}, u32[]{:S(2)}) collective-permute-start(f32[168,128]{1,0:T(8,128)S(1)} %get-tuple-element.40), channel_id=1, source_target_pairs={{0,6},{1,7},{2,4},{3,5},{4,2},{5,3},{6,0},{7,1},{8,14},{9,15},{10,... | collective-permute-start | bytes 258056 | tf_op jit(solution)/shard_map/ppermute | solution.py:299
  6.6 5.6 %collective-permute-start.3 = (f32[168,128]{1,0:T(8,128)S(1)}, f32[168,128]{1,0:T(8,128)S(1)}, u32[]{:S(2)}, u32[]{:S(2)}) collective-permute-start(f32[168,128]{1,0:T(8,128)S(1)} %get-tuple-element.41), channel_id=1, source_target_pairs={{0,4},{1,5},{2,6},{3,7},{4,0},{5,1},{6,2},{7,3},{8,12},{9,13},{10,... | collective-permute-start | bytes 258056 | tf_op jit(solution)/shard_map/ppermute | solution.py:299
  7.1 5.1 %collective-permute-start.4 = (f32[168,128]{1,0:T(8,128)S(1)}, f32[168,128]{1,0:T(8,128)S(1)}, u32[]{:S(2)}, u32[]{:S(2)}) collective-permute-start(f32[168,128]{1,0:T(8,128)S(1)} %get-tuple-element.42), channel_id=1, source_target_pairs={{0,2},{1,3},{2,0},{3,1},{4,6},{5,7},{6,4},{7,5},{8,10},{9,11},{10,... | collective-permute-start | bytes 258056 | tf_op jit(solution)/shard_map/ppermute | solution.py:299
  14.9 12.9 %collective-permute-start.5 = (f32[64,128]{1,0:T(8,128)S(1)}, f32[64,128]{1,0:T(8,128)S(1)}, u32[]{:S(2)}, u32[]{:S(2)}) collective-permute-start(f32[64,128]{1,0:T(8,128)S(1)} %get-tuple-element.48), channel_id=1, source_target_pairs={{0,8},{8,0},{16,24},{24,16},{1,9},{9,1},{17,25},{25,17},{2,10},{10... | collective-permute-start | bytes 98312 | tf_op jit(solution)/shard_map/ppermute | solution.py:299
  16.9 10.9 %collective-permute-start.6 = (f32[64,128]{1,0:T(8,128)S(1)}, f32[64,128]{1,0:T(8,128)S(1)}, u32[]{:S(2)}, u32[]{:S(2)}) collective-permute-start(f32[64,128]{1,0:T(8,128)S(1)} %get-tuple-element.49), channel_id=1, source_target_pairs={{0,16},{8,24},{16,0},{24,8},{1,17},{9,25},{17,1},{25,9},{2,18},{10... | collective-permute-start | bytes 98312 | tf_op jit(solution)/shard_map/ppermute | solution.py:299
  19.5 8.3 %collective-permute-start.7 = (f32[64,128]{1,0:T(8,128)S(1)}, f32[64,128]{1,0:T(8,128)S(1)}, u32[]{:S(2)}, u32[]{:S(2)}) collective-permute-start(f32[64,128]{1,0:T(8,128)S(1)} %get-tuple-element.50), channel_id=1, source_target_pairs={{0,24},{8,16},{16,8},{24,0},{1,25},{9,17},{17,9},{25,1},{2,26},{10... | collective-permute-start | bytes 98312 | tf_op jit(solution)/shard_map/ppermute | solution.py:299
  28.0 1.4 %collective-permute-start.8 = (f32[4,48,128]{2,1,0:T(8,128)S(1)}, f32[4,48,128]{2,1,0:T(8,128)S(1)}, u32[]{:S(2)}, u32[]{:S(2)}) collective-permute-start(f32[4,48,128]{2,1,0:T(8,128)S(1)} %get-tuple-element.52), channel_id=1, source_target_pairs={{0,1},{1,0},{2,3},{3,2},{4,5},{5,4},{6,7},{7,6},{8,9},{9,8},{10,11... | collective-permute-start | bytes 294920 | tf_op jit(solution)/shard_map/ppermute | solution.py:299
  29.3 4.8 %collective-permute-start.9 = (f32[48,128]{1,0:T(8,128)S(1)}, f32[48,128]{1,0:T(8,128)S(1)}, u32[]{:S(2)}, u32[]{:S(2)}) collective-permute-start(f32[48,128]{1,0:T(8,128)S(1)} %get-tuple-element.53), channel_id=1, source_target_pairs={{0,6},{1,7},{2,4},{3,5},{4,2},{5,3},{6,0},{7,1},{8,14},{9,15},{10,... | collective-permute-start | bytes 73736 | tf_op jit(solution)/shard_map/ppermute | solution.py:299
  32.1 3.8 %collective-permute-start.10 = (f32[48,128]{1,0:T(8,128)S(1)}, f32[48,128]{1,0:T(8,128)S(1)}, u32[]{:S(2)}, u32[]{:S(2)}) collective-permute-start(f32[48,128]{1,0:T(8,128)S(1)} %get-tuple-element.54), channel_id=1, source_target_pairs={{0,4},{1,5},{2,6},{3,7},{4,0},{5,1},{6,2},{7,3},{8,12},{9,13},{10,... | collective-permute-start | bytes 73736 | tf_op jit(solution)/shard_map/ppermute | solution.py:299
  32.6 3.8 %collective-permute-start.11 = (f32[48,128]{1,0:T(8,128)S(1)}, f32[48,128]{1,0:T(8,128)S(1)}, u32[]{:S(2)}, u32[]{:S(2)}) collective-permute-start(f32[48,128]{1,0:T(8,128)S(1)} %get-tuple-element.55), channel_id=1, source_target_pairs={{0,2},{1,3},{2,0},{3,1},{4,6},{5,7},{6,4},{7,5},{8,10},{9,11},{10,... | collective-permute-start | bytes 73736 | tf_op jit(solution)/shard_map/ppermute | solution.py:299

commit v15 on v14

--- a/solution.py
+++ b/solution.py
@@ -111,9 +111,9 @@
 
 
 def first_product(factor, right, tile):
-    tile = min(tile, factor.shape[0])
+    depth = factor.shape[0]
     parts = [
-        mm(right, factor[n * tile : (n + 1) * tile, :], NT) for n in range(factor.shape[0] // tile)
+        mm(right, factor[at : min(at + tile, depth), :], NT) for at in range(0, depth, tile)
     ]
     return jnp.concatenate(parts, axis=1)
 
@@ -184,8 +184,10 @@
 def fine_kernel(own, rows, begin, chunk, tile, pairs, away, begun, factor, coarse_hbm, given, *refs):
     arrived = refs[:pairs][::-1]
     *outs, coarse, named, sums, table, sems = refs[pairs:]
-    quarter = coarse.shape[0] // 4
-    copies = panel_copies(coarse_hbm, coarse.at[pl.ds(quarter, quarter)], chunk, sems, quarter)
+    first = coarse.shape[0] // 4
+    copies = panel_copies(
+        coarse_hbm, coarse.at[pl.ds(first, sems.shape[0] * chunk)], chunk, sems, first
+    )
     start(copies)
     rhs = begun.shape[0]
     halo = away.shape[0]
@@ -221,7 +223,7 @@
 
 def coarse_kernel(own, rows, chunk, tile, given, factor_hbm, member, sums, out, factor, table, begun, sems):
     depth, width = factor.shape
-    done = depth // 2
+    done = depth - sems.shape[0] * chunk
     held, lower = factor.at[pl.ds(0, done)], factor.at[pl.ds(done, depth - done)]
     copies = panel_copies(factor_hbm, lower, chunk, sems, done)
     start(copies)
@@ -369,6 +371,7 @@
         moved=2 * depth * width + 2 * quarter * coarse_width,
     )(held, local_factor, coarse_factor, arrived[0])
     chunk = quarter // 4
+    middle = 6 * chunk
     count = coarse_width // BLK
     *fine, coarse_part, member, sums = call(
         functools.partial(fine_kernel, own, rows, begin, chunk, tile, pairs),
@@ -379,13 +382,13 @@
             sds((rows * count, BLK), f32),
         ],
         [VMEM, VMEM, VMEM, HBM, VMEM] + [VMEM] * pairs,
-        [pltpu.VMEM((rhs * blocks, BLK), f32), pltpu.SemaphoreType.DMA((quarter // chunk,))],
+        [pltpu.VMEM((rhs * blocks, BLK), f32), pltpu.SemaphoreType.DMA((middle // chunk,))],
         flops=4 * rhs * depth * width,
-        moved=2 * depth * width + 2 * quarter * coarse_width,
+        moved=2 * depth * width + 2 * middle * coarse_width,
         input_output_aliases={4: grp_count},
     )(away, begun, local_factor, coarse_factor, coarse_part, *arrived[::-1])
     panels = exchange(fine, "grp")
-    lower = coarse_depth - 2 * quarter
+    lower = coarse_depth - quarter - middle
     size = own * rows
     spread, _ = call(
         functools.partial(coarse_kernel, own, rows, chunk, tile),

time: 37.2 us -> 38.2 us (1.027)
  Pallas kernels: 18.7 us -> 19.6 us
    pallas_call x1, Pallas kernels: 2.69 us -> 3.82 us  [on_device(): call(functools.partial(fine_kernel, own, rows, begin, chunk, tile, pairs)...]
  transfers between devices with their start and end apart: 12 -> 12, of which waited for: 5 -> 5; matrix products, arithmetic and copies ran while one was open for 0% -> 0% of each run, Pallas kernels for 38% -> 37%
where the time goes in v15:
time: 38.2 us; the launch traced here: 38 us
  Pallas kernels  19.6 us (51%)
  starting transfers between devices  13.2 us (35%)
  waiting for transfers between devices  5.07 us (13%)
    ppermute x12, starting transfers between devices, swap(): return lax.ppermute(value, axis, [(i, i ^ distance) for i in range(count)])  13.2 us
    pallas_call x1, Pallas kernels, on_device(): call(functools.partial(coarse_kernel, own, rows, chunk, tile), (sds((2 *...  8.09 us
    ppermute x12, waiting for transfers between devices, swap(): return lax.ppermute(value, axis, [(i, i ^ distance) for i in range(count)])  5.07 us
    pallas_call x1, Pallas kernels, on_device(): call(functools.partial(load_kernel, chunk, tile), (sds((rhs, depth), f32)...  4.94 us
    pallas_call x1, Pallas kernels, on_device(): call(functools.partial(fine_kernel, own, rows, begin, chunk, tile, pairs)...  3.82 us
    pallas_call x1, Pallas kernels, on_device(): call(functools.partial(pack_kernel, own, rows, pad), [sds((begin + halo *...  1.08 us
    pallas_call x1, Pallas kernels, on_device(): call(functools.partial(stage_kernel, own, rows), (sds(residual.shape, f32...  0.93 us
  transfers between devices with their start and end apart: 12, of which 5 were waited for; matrix products, arithmetic and copies ran while one was open for 0% of the time, Pallas kernels for 37%

profile of v15, /device:TPU:0, one launch (start us, length us, event | category | flops | bytes accessed | tf_op | source)
XLA Modules:
  0.0 38.0 jit_solution(5582562253804300914)
XLA Ops:
  0.0 0.5 %collective-permute-start.1 = (f32[8,3072]{1,0:T(8,128)}, f32[8,3072]{1,0:T(8,128)S(1)}, u32[]{:S(2)}, u32[]{:S(2)}) collective-permute-start(f32[8,3072]{1,0:T(8,128)} %residual_hbm.1), channel_id=1, source_target_pairs={{0,1},{1,0},{2,3},{3,2},{4,5},{5,4},{6,7},{7,6},{8,9},{9,8},{10,11... | collective-permute-start | bytes 294920 | tf_op jit(solution)/shard_map/ppermute | solution.py:301
  0.5 0.1 collective-permute-start
  0.5 0.9 %shard_map.55 = (f32[8,3072]{1,0:T(8,128)S(1)}, f32[48,128]{1,0:T(8,128)S(1)}, f32[1,24]{1,0:T(1,128)S(1)}) custom-call(f32[8,3072]{1,0:T(8,128)} %residual_hbm.1, s32[1,24]{1,0:T(1,128)} %bitcast.2), custom_call_target="tpu_custom_call" | custom-call | bytes 196608 | tf_op jit(solution)/shard_map/pallas_call | solution.py:330
  1.5 0.3 collective-permute-done.near_names
  1.7 0.0 collective-permute-done.1.near
  1.7 1.1 %shard_map.56 = (f32[168,128]{1,0:T(8,128)S(1)}, f32[168,128]{1,0:T(8,128)S(1)}, f32[168,128]{1,0:T(8,128)S(1)}, f32[168,128]{1,0:T(8,128)S(1)}, s32[8,128]{1,0:T(8,128)S(1)}, /*index=5*/s32[192,128]{1,0:T(8,128)S(1)}) custom-call(s32[8,8]{1,0:T(8,128)} %margin_hbm.1, f32[8,3072]{1,0:T(8,128)S(1)} %get-tuple-element.31.residual, ...), custom_call_target="tpu_custom_call" | custom-call | tf_op jit(solution)/shard_map/pallas_call | solution.py:342
  2.8 3.8 %collective-permute-start.2 = (f32[168,128]{1,0:T(8,128)S(1)}, f32[168,128]{1,0:T(8,128)S(1)}, u32[]{:S(2)}, u32[]{:S(2)}) collective-permute-start(f32[168,128]{1,0:T(8,128)S(1)} %get-tuple-element.40), channel_id=1, source_target_pairs={{0,6},{1,7},{2,4},{3,5},{4,2},{5,3},{6,0},{7,1},{8,14},{9,15},{10,... | collective-permute-start | bytes 258056 | tf_op jit(solution)/shard_map/ppermute | solution.py:301
  6.6 0.5 %collective-permute-start.3 = (f32[168,128]{1,0:T(8,128)S(1)}, f32[168,128]{1,0:T(8,128)S(1)}, u32[]{:S(2)}, u32[]{:S(2)}) collective-permute-start(f32[168,128]{1,0:T(8,128)S(1)} %get-tuple-element.41), channel_id=1, source_target_pairs={{0,4},{1,5},{2,6},{3,7},{4,0},{5,1},{6,2},{7,3},{8,12},{9,13},{10,... | collective-permute-start | bytes 258056 | tf_op jit(solution)/shard_map/ppermute | solution.py:301
  7.1 0.1 collective-permute-start.4
  7.2 4.9 %shard_map.57 = (f32[8,1024]{1,0:T(8,128)S(1)}, bf16[1,1024,4096]{2,1,0:T(8,128)(2,1)S(1)}, bf16[1024,8192]{1,0:T(8,128)(2,1)S(1)}) custom-call(f32[8,3072]{1,0:T(8,128)S(1)} %get-tuple-element.31.residual, bf16[1,1024,4096]{2,1,0:T(8,128)(2,1)} %fine_hbm.1, bf16[1024,8192]{1,0:T(8,128)(2,1)} %factor_hbm.1, f32[168,128]{1,0:T(8,128)S(1)} %get-tuple-element.36.after.refs_3_), custom_call_target="tpu_custom_call" | custom-call | flops 50331648 | bytes 12582912 | tf_op jit(solution)/shard_map/pallas_call | solution.py:358
  12.2 0.0 collective-permute-done.2.refs_0_
  12.2 0.0 collective-permute-done.3.refs_1_
  12.2 0.0 collective-permute-done.4.refs_2_
  12.2 3.8 %shard_map.58 = (f32[64,128]{1,0:T(8,128)S(1)}, f32[64,128]{1,0:T(8,128)S(1)}, f32[64,128]{1,0:T(8,128)S(1)}, f32[64,128]{1,0:T(8,128)S(1)}, bf16[1024,8192]{1,0...) custom-call(s32[8,128]{1,0:T(8,128)S(1)} %get-tuple-element.35.away, ...), custom_call_target="tpu_custom_call", output_to_operand_aliasing={{4}: (4, {})} | custom-call | flops 134217728 | bytes 14680064 | tf_op jit(solution)/shard_map/pallas_call | solution.py:376
  16.0 2.0 %collective-permute-start.5 = (f32[64,128]{1,0:T(8,128)S(1)}, f32[64,128]{1,0:T(8,128)S(1)}, u32[]{:S(2)}, u32[]{:S(2)}) collective-permute-start(f32[64,128]{1,0:T(8,128)S(1)} %get-tuple-element.48), channel_id=1, source_target_pairs={{0,8},{8,0},{16,24},{24,16},{1,9},{9,1},{17,25},{25,17},{2,10},{10... | collective-permute-start | bytes 98312 | tf_op jit(solution)/shard_map/ppermute | solution.py:301
  18.1 2.6 %collective-permute-start.6 = (f32[64,128]{1,0:T(8,128)S(1)}, f32[64,128]{1,0:T(8,128)S(1)}, u32[]{:S(2)}, u32[]{:S(2)}) collective-permute-start(f32[64,128]{1,0:T(8,128)S(1)} %get-tuple-element.49), channel_id=1, source_target_pairs={{0,16},{8,24},{16,0},{24,8},{1,17},{9,25},{17,1},{25,9},{2,18},{10... | collective-permute-start | bytes 98312 | tf_op jit(solution)/shard_map/ppermute | solution.py:301
  20.6 0.0 collective-permute-start.7
  20.6 8.1 %shard_map.59 = (f32[8,48,128]{2,1,0:T(8,128)S(1)}, bf16[1024,8192]{1,0:T(8,128)(2,1)S(1)}) custom-call(bf16[1024,8192]{1,0:T(8,128)(2,1)S(1)} %get-tuple-element.43.given, bf16[1024,8192]{1,0:T(8,128)(2,1)} %factor_hbm.1, f32[192,64]{1,0:T(8,128)S(1)} %get-tuple-element.44.member, ...), custom_call_target="tpu_custom_call", output_to_operand_aliasing={{1}: (0, {})} | custom-call | flops 67108864 | bytes 16777216 | tf_op jit(solution)/shard_map/pallas_call | solution.py:393
  28.8 0.0 collective-permute-done.5.refs_1_
  28.8 0.0 collective-permute-done.6.refs_2_
  28.8 0.0 collective-permute-done.7.refs_3_
  28.8 0.1 shard_map.60
  28.9 0.1 collective-permute-start.8
  29.0 1.3 %collective-permute-done.8.arrived = f32[4,48,128]{2,1,0:T(8,128)S(1)} collective-permute-done((f32[4,48,128]{2,1,0:T(8,128)S(1)}, f32[4,48,128]{2,1,0:T(8,128)S(1)}, u32[]{:S(2)}, u32[]{:S(2)}) %collective-permute-start.8) | collective-permute-done | bytes 98336 | tf_op jit(solution)/shard_map/ppermute | solution.py:301
  30.3 2.7 %collective-permute-start.9 = (f32[48,128]{1,0:T(8,128)S(1)}, f32[48,128]{1,0:T(8,128)S(1)}, u32[]{:S(2)}, u32[]{:S(2)}) collective-permute-start(f32[48,128]{1,0:T(8,128)S(1)} %get-tuple-element.53), channel_id=1, source_target_pairs={{0,6},{1,7},{2,4},{3,5},{4,2},{5,3},{6,0},{7,1},{8,14},{9,15},{10,... | collective-permute-start | bytes 73736 | tf_op jit(solution)/shard_map/ppermute | solution.py:301
  33.0 0.5 %collective-permute-start.10 = (f32[48,128]{1,0:T(8,128)S(1)}, f32[48,128]{1,0:T(8,128)S(1)}, u32[]{:S(2)}, u32[]{:S(2)}) collective-permute-start(f32[48,128]{1,0:T(8,128)S(1)} %get-tuple-element.54), channel_id=1, source_target_pairs={{0,4},{1,5},{2,6},{3,7},{4,0},{5,1},{6,2},{7,3},{8,12},{9,13},{10,... | collective-permute-start | bytes 73736 | tf_op jit(solution)/shard_map/ppermute | solution.py:301
  33.5 0.3 collective-permute-start.11
  33.9 1.2 %collective-permute-done.9.refs_0_ = f32[48,128]{1,0:T(8,128)S(1)} collective-permute-done((f32[48,128]{1,0:T(8,128)S(1)}, f32[48,128]{1,0:T(8,128)S(1)}, u32[]{:S(2)}, u32[]{:S(2)}) %collective-permute-start.9) | collective-permute-done | bytes 24608 | tf_op jit(solution)/shard_map/ppermute | solution.py:301
  35.1 1.8 %collective-permute-done.10.refs_1_ = f32[48,128]{1,0:T(8,128)S(1)} collective-permute-done((f32[48,128]{1,0:T(8,128)S(1)}, f32[48,128]{1,0:T(8,128)S(1)}, u32[]{:S(2)}, u32[]{:S(2)}) %collective-permute-start.10) | collective-permute-done | bytes 24608 | tf_op jit(solution)/shard_map/ppermute | solution.py:301
  36.9 0.5 %collective-permute-done.11.refs_2_ = f32[48,128]{1,0:T(8,128)S(1)} collective-permute-done((f32[48,128]{1,0:T(8,128)S(1)}, f32[48,128]{1,0:T(8,128)S(1)}, u32[]{:S(2)}, u32[]{:S(2)}) %collective-permute-start.11) | collective-permute-done | bytes 24608 | tf_op jit(solution)/shard_map/ppermute | solution.py:301
  37.4 0.6 %shard_map.62 = f32[2,3072]{1,0:T(2,128)} custom-call(f32[48,128]{1,0:T(8,128)S(1)} %collective-permute-done.9.refs_0_, f32[48,128]{1,0:T(8,128)S(1)} %collective-permute-done.10.refs_1_, f32[48,128]{1,0:T(8,128)S(1)} %collective-permute-done.11.refs_2_, f32[48,128]{1,0:T(8,128)S(1)} %get-tuple-element.56.refs_3_), custom_call_target="tpu_custom_call" | custom-call | tf_op jit(solution)/shard_map/pallas_call | solution.py:415
  (1 shorter events, 0.0 us)
Async XLA Ops:
  0.0 1.7 %collective-permute-start.1 = (f32[8,3072]{1,0:T(8,128)}, f32[8,3072]{1,0:T(8,128)S(1)}, u32[]{:S(2)}, u32[]{:S(2)}) collective-permute-start(f32[8,3072]{1,0:T(8,128)} %residual_hbm.1), channel_id=1, source_target_pairs={{0,1},{1,0},{2,3},{3,2},{4,5},{5,4},{6,7},{7,6},{8,9},{9,8},{10,11... | collective-permute-start | bytes 294920 | tf_op jit(solution)/shard_map/ppermute | solution.py:301
  0.5 1.3 %collective-permute-start = (s32[1,24]{1,0:T(1,128)}, s32[1,24]{1,0:T(1,128)S(1)}, u32[]{:S(2)}, u32[]{:S(2)}) collective-permute-start(s32[1,24]{1,0:T(1,128)} %bitcast.1), channel_id=1, source_target_pairs={{0,1},{1,0},{2,3},{3,2},{4,5},{5,4},{6,7},{7,6},{8,9},{9,8},{10,11... | collective-permute-start | bytes 296 | tf_op jit(solution)/shard_map/ppermute | solution.py:301
  2.8 9.4 %collective-permute-start.2 = (f32[168,128]{1,0:T(8,128)S(1)}, f32[168,128]{1,0:T(8,128)S(1)}, u32[]{:S(2)}, u32[]{:S(2)}) collective-permute-start(f32[168,128]{1,0:T(8,128)S(1)} %get-tuple-element.40), channel_id=1, source_target_pairs={{0,6},{1,7},{2,4},{3,5},{4,2},{5,3},{6,0},{7,1},{8,14},{9,15},{10,... | collective-permute-start | bytes 258056 | tf_op jit(solution)/shard_map/ppermute | solution.py:301
  6.6 5.6 %collective-permute-start.3 = (f32[168,128]{1,0:T(8,128)S(1)}, f32[168,128]{1,0:T(8,128)S(1)}, u32[]{:S(2)}, u32[]{:S(2)}) collective-permute-start(f32[168,128]{1,0:T(8,128)S(1)} %get-tuple-element.41), channel_id=1, source_target_pairs={{0,4},{1,5},{2,6},{3,7},{4,0},{5,1},{6,2},{7,3},{8,12},{9,13},{10,... | collective-permute-start | bytes 258056 | tf_op jit(solution)/shard_map/ppermute | solution.py:301
  7.1 5.1 %collective-permute-start.4 = (f32[168,128]{1,0:T(8,128)S(1)}, f32[168,128]{1,0:T(8,128)S(1)}, u32[]{:S(2)}, u32[]{:S(2)}) collective-permute-start(f32[168,128]{1,0:T(8,128)S(1)} %get-tuple-element.42), channel_id=1, source_target_pairs={{0,2},{1,3},{2,0},{3,1},{4,6},{5,7},{6,4},{7,5},{8,10},{9,11},{10,... | collective-permute-start | bytes 258056 | tf_op jit(solution)/shard_map/ppermute | solution.py:301
  16.0 12.7 %collective-permute-start.5 = (f32[64,128]{1,0:T(8,128)S(1)}, f32[64,128]{1,0:T(8,128)S(1)}, u32[]{:S(2)}, u32[]{:S(2)}) collective-permute-start(f32[64,128]{1,0:T(8,128)S(1)} %get-tuple-element.48), channel_id=1, source_target_pairs={{0,8},{8,0},{16,24},{24,16},{1,9},{9,1},{17,25},{25,17},{2,10},{10... | collective-permute-start | bytes 98312 | tf_op jit(solution)/shard_map/ppermute | solution.py:301
  18.1 10.7 %collective-permute-start.6 = (f32[64,128]{1,0:T(8,128)S(1)}, f32[64,128]{1,0:T(8,128)S(1)}, u32[]{:S(2)}, u32[]{:S(2)}) collective-permute-start(f32[64,128]{1,0:T(8,128)S(1)} %get-tuple-element.49), channel_id=1, source_target_pairs={{0,16},{8,24},{16,0},{24,8},{1,17},{9,25},{17,1},{25,9},{2,18},{10... | collective-permute-start | bytes 98312 | tf_op jit(solution)/shard_map/ppermute | solution.py:301
  20.6 8.1 %collective-permute-start.7 = (f32[64,128]{1,0:T(8,128)S(1)}, f32[64,128]{1,0:T(8,128)S(1)}, u32[]{:S(2)}, u32[]{:S(2)}) collective-permute-start(f32[64,128]{1,0:T(8,128)S(1)} %get-tuple-element.50), channel_id=1, source_target_pairs={{0,24},{8,16},{16,8},{24,0},{1,25},{9,17},{17,9},{25,1},{2,26},{10... | collective-permute-start | bytes 98312 | tf_op jit(solution)/shard_map/ppermute | solution.py:301
  28.9 1.4 %collective-permute-start.8 = (f32[4,48,128]{2,1,0:T(8,128)S(1)}, f32[4,48,128]{2,1,0:T(8,128)S(1)}, u32[]{:S(2)}, u32[]{:S(2)}) collective-permute-start(f32[4,48,128]{2,1,0:T(8,128)S(1)} %get-tuple-element.52), channel_id=1, source_target_pairs={{0,1},{1,0},{2,3},{3,2},{4,5},{5,4},{6,7},{7,6},{8,9},{9,8},{10,11... | collective-permute-start | bytes 294920 | tf_op jit(solution)/shard_map/ppermute | solution.py:301
  30.3 4.8 %collective-permute-start.9 = (f32[48,128]{1,0:T(8,128)S(1)}, f32[48,128]{1,0:T(8,128)S(1)}, u32[]{:S(2)}, u32[]{:S(2)}) collective-permute-start(f32[48,128]{1,0:T(8,128)S(1)} %get-tuple-element.53), channel_id=1, source_target_pairs={{0,6},{1,7},{2,4},{3,5},{4,2},{5,3},{6,0},{7,1},{8,14},{9,15},{10,... | collective-permute-start | bytes 73736 | tf_op jit(solution)/shard_map/ppermute | solution.py:301
  33.0 3.8 %collective-permute-start.10 = (f32[48,128]{1,0:T(8,128)S(1)}, f32[48,128]{1,0:T(8,128)S(1)}, u32[]{:S(2)}, u32[]{:S(2)}) collective-permute-start(f32[48,128]{1,0:T(8,128)S(1)} %get-tuple-element.54), channel_id=1, source_target_pairs={{0,4},{1,5},{2,6},{3,7},{4,0},{5,1},{6,2},{7,3},{8,12},{9,13},{10,... | collective-permute-start | bytes 73736 | tf_op jit(solution)/shard_map/ppermute | solution.py:301
  33.5 3.8 %collective-permute-start.11 = (f32[48,128]{1,0:T(8,128)S(1)}, f32[48,128]{1,0:T(8,128)S(1)}, u32[]{:S(2)}, u32[]{:S(2)}) collective-permute-start(f32[48,128]{1,0:T(8,128)S(1)} %get-tuple-element.55), channel_id=1, source_target_pairs={{0,2},{1,3},{2,0},{3,1},{4,6},{5,7},{6,4},{7,5},{8,10},{9,11},{10,... | collective-permute-start | bytes 73736 | tf_op jit(solution)/shard_map/ppermute | solution.py:301

commit v16 on v15

--- a/solution.py
+++ b/solution.py
@@ -371,7 +371,7 @@
         moved=2 * depth * width + 2 * quarter * coarse_width,
     )(held, local_factor, coarse_factor, arrived[0])
     chunk = quarter // 4
-    middle = 6 * chunk
+    middle = 2 * chunk
     count = coarse_width // BLK
     *fine, coarse_part, member, sums = call(
         functools.partial(fine_kernel, own, rows, begin, chunk, tile, pairs),

time: 38.2 us -> 38.7 us (1.013)
  Pallas kernels: 19.6 us -> 20.2 us
    pallas_call x1, Pallas kernels: 8.09 us -> 10.4 us  [on_device(): call(functools.partial(coarse_kernel, own, rows, chunk, tile), (sds((2 *...]
    pallas_call x1, Pallas kernels: 3.82 us -> 2.07 us  [on_device(): call(functools.partial(fine_kernel, own, rows, begin, chunk, tile, pairs)...]
  transfers between devices with their start and end apart: 12 -> 12, of which waited for: 5 -> 5; matrix products, arithmetic and copies ran while one was open for 0% -> 0% of each run, Pallas kernels for 37% -> 42%
where the time goes in v16:
time: 38.7 us; the launch traced here: 38.5 us
  Pallas kernels  20.2 us (52%)
  starting transfers between devices  13.2 us (34%)
  waiting for transfers between devices  5.05 us (13%)
    ppermute x12, starting transfers between devices, swap(): return lax.ppermute(value, axis, [(i, i ^ distance) for i in range(count)])  13.2 us
    pallas_call x1, Pallas kernels, on_device(): call(functools.partial(coarse_kernel, own, rows, chunk, tile), (sds((2 *...  10.4 us
    ppermute x12, waiting for transfers between devices, swap(): return lax.ppermute(value, axis, [(i, i ^ distance) for i in range(count)])  5.05 us
    pallas_call x1, Pallas kernels, on_device(): call(functools.partial(load_kernel, chunk, tile), (sds((rhs, depth), f32)...  4.94 us
    pallas_call x1, Pallas kernels, on_device(): call(functools.partial(fine_kernel, own, rows, begin, chunk, tile, pairs)...  2.07 us
    pallas_call x1, Pallas kernels, on_device(): call(functools.partial(pack_kernel, own, rows, pad), [sds((begin + halo *...  1.08 us
    pallas_call x1, Pallas kernels, on_device(): call(functools.partial(stage_kernel, own, rows), (sds(residual.shape, f32...  0.93 us
  transfers between devices with their start and end apart: 12, of which 5 were waited for; matrix products, arithmetic and copies ran while one was open for 0% of the time, Pallas kernels for 42%

profile of v16, /device:TPU:0, one launch (start us, length us, event | category | flops | bytes accessed | tf_op | source)
XLA Modules:
  0.0 38.5 jit_solution(815499542135704242)
XLA Ops:
  0.0 0.5 %collective-permute-start.1 = (f32[8,3072]{1,0:T(8,128)}, f32[8,3072]{1,0:T(8,128)S(1)}, u32[]{:S(2)}, u32[]{:S(2)}) collective-permute-start(f32[8,3072]{1,0:T(8,128)} %residual_hbm.1), channel_id=1, source_target_pairs={{0,1},{1,0},{2,3},{3,2},{4,5},{5,4},{6,7},{7,6},{8,9},{9,8},{10,11... | collective-permute-start | bytes 294920 | tf_op jit(solution)/shard_map/ppermute | solution.py:301
  0.5 0.1 collective-permute-start
  0.5 0.9 %shard_map.55 = (f32[8,3072]{1,0:T(8,128)S(1)}, f32[48,128]{1,0:T(8,128)S(1)}, f32[1,24]{1,0:T(1,128)S(1)}) custom-call(f32[8,3072]{1,0:T(8,128)} %residual_hbm.1, s32[1,24]{1,0:T(1,128)} %bitcast.2), custom_call_target="tpu_custom_call" | custom-call | bytes 196608 | tf_op jit(solution)/shard_map/pallas_call | solution.py:330
  1.5 0.3 collective-permute-done.near_names
  1.7 0.0 collective-permute-done.1.near
  1.7 1.1 %shard_map.56 = (f32[168,128]{1,0:T(8,128)S(1)}, f32[168,128]{1,0:T(8,128)S(1)}, f32[168,128]{1,0:T(8,128)S(1)}, f32[168,128]{1,0:T(8,128)S(1)}, s32[8,128]{1,0:T(8,128)S(1)}, /*index=5*/s32[192,128]{1,0:T(8,128)S(1)}) custom-call(s32[8,8]{1,0:T(8,128)} %margin_hbm.1, f32[8,3072]{1,0:T(8,128)S(1)} %get-tuple-element.31.residual, ...), custom_call_target="tpu_custom_call" | custom-call | tf_op jit(solution)/shard_map/pallas_call | solution.py:342
  2.8 3.8 %collective-permute-start.2 = (f32[168,128]{1,0:T(8,128)S(1)}, f32[168,128]{1,0:T(8,128)S(1)}, u32[]{:S(2)}, u32[]{:S(2)}) collective-permute-start(f32[168,128]{1,0:T(8,128)S(1)} %get-tuple-element.40), channel_id=1, source_target_pairs={{0,6},{1,7},{2,4},{3,5},{4,2},{5,3},{6,0},{7,1},{8,14},{9,15},{10,... | collective-permute-start | bytes 258056 | tf_op jit(solution)/shard_map/ppermute | solution.py:301
  6.6 0.5 %collective-permute-start.3 = (f32[168,128]{1,0:T(8,128)S(1)}, f32[168,128]{1,0:T(8,128)S(1)}, u32[]{:S(2)}, u32[]{:S(2)}) collective-permute-start(f32[168,128]{1,0:T(8,128)S(1)} %get-tuple-element.41), channel_id=1, source_target_pairs={{0,4},{1,5},{2,6},{3,7},{4,0},{5,1},{6,2},{7,3},{8,12},{9,13},{10,... | collective-permute-start | bytes 258056 | tf_op jit(solution)/shard_map/ppermute | solution.py:301
  7.1 0.1 collective-permute-start.4
  7.2 4.9 %shard_map.57 = (f32[8,1024]{1,0:T(8,128)S(1)}, bf16[1,1024,4096]{2,1,0:T(8,128)(2,1)S(1)}, bf16[1024,8192]{1,0:T(8,128)(2,1)S(1)}) custom-call(f32[8,3072]{1,0:T(8,128)S(1)} %get-tuple-element.31.residual, bf16[1,1024,4096]{2,1,0:T(8,128)(2,1)} %fine_hbm.1, bf16[1024,8192]{1,0:T(8,128)(2,1)} %factor_hbm.1, f32[168,128]{1,0:T(8,128)S(1)} %get-tuple-element.36.after.refs_3_), custom_call_target="tpu_custom_call" | custom-call | flops 50331648 | bytes 12582912 | tf_op jit(solution)/shard_map/pallas_call | solution.py:358
  12.2 0.0 collective-permute-done.2.refs_0_
  12.2 0.0 collective-permute-done.3.refs_1_
  12.2 0.0 collective-permute-done.4.refs_2_
  12.2 2.1 %shard_map.58 = (f32[64,128]{1,0:T(8,128)S(1)}, f32[64,128]{1,0:T(8,128)S(1)}, f32[64,128]{1,0:T(8,128)S(1)}, f32[64,128]{1,0:T(8,128)S(1)}, bf16[1024,8192]{1,0...) custom-call(s32[8,128]{1,0:T(8,128)S(1)} %get-tuple-element.35.away, ...), custom_call_target="tpu_custom_call", output_to_operand_aliasing={{4}: (4, {})} | custom-call | flops 134217728 | bytes 10485760 | tf_op jit(solution)/shard_map/pallas_call | solution.py:376
  14.3 2.0 %collective-permute-start.5 = (f32[64,128]{1,0:T(8,128)S(1)}, f32[64,128]{1,0:T(8,128)S(1)}, u32[]{:S(2)}, u32[]{:S(2)}) collective-permute-start(f32[64,128]{1,0:T(8,128)S(1)} %get-tuple-element.48), channel_id=1, source_target_pairs={{0,8},{8,0},{16,24},{24,16},{1,9},{9,1},{17,25},{25,17},{2,10},{10... | collective-permute-start | bytes 98312 | tf_op jit(solution)/shard_map/ppermute | solution.py:301
  16.3 2.6 %collective-permute-start.6 = (f32[64,128]{1,0:T(8,128)S(1)}, f32[64,128]{1,0:T(8,128)S(1)}, u32[]{:S(2)}, u32[]{:S(2)}) collective-permute-start(f32[64,128]{1,0:T(8,128)S(1)} %get-tuple-element.49), channel_id=1, source_target_pairs={{0,16},{8,24},{16,0},{24,8},{1,17},{9,25},{17,1},{25,9},{2,18},{10... | collective-permute-start | bytes 98312 | tf_op jit(solution)/shard_map/ppermute | solution.py:301
  18.9 0.0 collective-permute-start.7
  18.9 10.4 %shard_map.59 = (f32[8,48,128]{2,1,0:T(8,128)S(1)}, bf16[1024,8192]{1,0:T(8,128)(2,1)S(1)}) custom-call(bf16[1024,8192]{1,0:T(8,128)(2,1)S(1)} %get-tuple-element.43.given, bf16[1024,8192]{1,0:T(8,128)(2,1)} %factor_hbm.1, f32[192,64]{1,0:T(8,128)S(1)} %get-tuple-element.44.member, ...), custom_call_target="tpu_custom_call", output_to_operand_aliasing={{1}: (0, {})} | custom-call | flops 67108864 | bytes 16777216 | tf_op jit(solution)/shard_map/pallas_call | solution.py:393
  29.3 0.0 collective-permute-done.5.refs_1_
  29.3 0.0 collective-permute-done.6.refs_2_
  29.3 0.0 collective-permute-done.7.refs_3_
  29.3 0.1 shard_map.60
  29.5 0.1 collective-permute-start.8
  29.5 1.3 %collective-permute-done.8.arrived = f32[4,48,128]{2,1,0:T(8,128)S(1)} collective-permute-done((f32[4,48,128]{2,1,0:T(8,128)S(1)}, f32[4,48,128]{2,1,0:T(8,128)S(1)}, u32[]{:S(2)}, u32[]{:S(2)}) %collective-permute-start.8) | collective-permute-done | bytes 98336 | tf_op jit(solution)/shard_map/ppermute | solution.py:301
  30.8 2.7 %collective-permute-start.9 = (f32[48,128]{1,0:T(8,128)S(1)}, f32[48,128]{1,0:T(8,128)S(1)}, u32[]{:S(2)}, u32[]{:S(2)}) collective-permute-start(f32[48,128]{1,0:T(8,128)S(1)} %get-tuple-element.53), channel_id=1, source_target_pairs={{0,6},{1,7},{2,4},{3,5},{4,2},{5,3},{6,0},{7,1},{8,14},{9,15},{10,... | collective-permute-start | bytes 73736 | tf_op jit(solution)/shard_map/ppermute | solution.py:301
  33.6 0.5 %collective-permute-start.10 = (f32[48,128]{1,0:T(8,128)S(1)}, f32[48,128]{1,0:T(8,128)S(1)}, u32[]{:S(2)}, u32[]{:S(2)}) collective-permute-start(f32[48,128]{1,0:T(8,128)S(1)} %get-tuple-element.54), channel_id=1, source_target_pairs={{0,4},{1,5},{2,6},{3,7},{4,0},{5,1},{6,2},{7,3},{8,12},{9,13},{10,... | collective-permute-start | bytes 73736 | tf_op jit(solution)/shard_map/ppermute | solution.py:301
  34.1 0.3 collective-permute-start.11
  34.4 1.2 %collective-permute-done.9.refs_0_ = f32[48,128]{1,0:T(8,128)S(1)} collective-permute-done((f32[48,128]{1,0:T(8,128)S(1)}, f32[48,128]{1,0:T(8,128)S(1)}, u32[]{:S(2)}, u32[]{:S(2)}) %collective-permute-start.9) | collective-permute-done | bytes 24608 | tf_op jit(solution)/shard_map/ppermute | solution.py:301
  35.6 1.7 %collective-permute-done.10.refs_1_ = f32[48,128]{1,0:T(8,128)S(1)} collective-permute-done((f32[48,128]{1,0:T(8,128)S(1)}, f32[48,128]{1,0:T(8,128)S(1)}, u32[]{:S(2)}, u32[]{:S(2)}) %collective-permute-start.10) | collective-permute-done | bytes 24608 | tf_op jit(solution)/shard_map/ppermute | solution.py:301
  37.4 0.5 %collective-permute-done.11.refs_2_ = f32[48,128]{1,0:T(8,128)S(1)} collective-permute-done((f32[48,128]{1,0:T(8,128)S(1)}, f32[48,128]{1,0:T(8,128)S(1)}, u32[]{:S(2)}, u32[]{:S(2)}) %collective-permute-start.11) | collective-permute-done | bytes 24608 | tf_op jit(solution)/shard_map/ppermute | solution.py:301
  37.9 0.6 %shard_map.62 = f32[2,3072]{1,0:T(2,128)} custom-call(f32[48,128]{1,0:T(8,128)S(1)} %collective-permute-done.9.refs_0_, f32[48,128]{1,0:T(8,128)S(1)} %collective-permute-done.10.refs_1_, f32[48,128]{1,0:T(8,128)S(1)} %collective-permute-done.11.refs_2_, f32[48,128]{1,0:T(8,128)S(1)} %get-tuple-element.56.refs_3_), custom_call_target="tpu_custom_call" | custom-call | tf_op jit(solution)/shard_map/pallas_call | solution.py:415
  (1 shorter events, 0.0 us)
Async XLA Ops:
  0.0 1.7 %collective-permute-start.1 = (f32[8,3072]{1,0:T(8,128)}, f32[8,3072]{1,0:T(8,128)S(1)}, u32[]{:S(2)}, u32[]{:S(2)}) collective-permute-start(f32[8,3072]{1,0:T(8,128)} %residual_hbm.1), channel_id=1, source_target_pairs={{0,1},{1,0},{2,3},{3,2},{4,5},{5,4},{6,7},{7,6},{8,9},{9,8},{10,11... | collective-permute-start | bytes 294920 | tf_op jit(solution)/shard_map/ppermute | solution.py:301
  0.5 1.3 %collective-permute-start = (s32[1,24]{1,0:T(1,128)}, s32[1,24]{1,0:T(1,128)S(1)}, u32[]{:S(2)}, u32[]{:S(2)}) collective-permute-start(s32[1,24]{1,0:T(1,128)} %bitcast.1), channel_id=1, source_target_pairs={{0,1},{1,0},{2,3},{3,2},{4,5},{5,4},{6,7},{7,6},{8,9},{9,8},{10,11... | collective-permute-start | bytes 296 | tf_op jit(solution)/shard_map/ppermute | solution.py:301
  2.8 9.4 %collective-permute-start.2 = (f32[168,128]{1,0:T(8,128)S(1)}, f32[168,128]{1,0:T(8,128)S(1)}, u32[]{:S(2)}, u32[]{:S(2)}) collective-permute-start(f32[168,128]{1,0:T(8,128)S(1)} %get-tuple-element.40), channel_id=1, source_target_pairs={{0,6},{1,7},{2,4},{3,5},{4,2},{5,3},{6,0},{7,1},{8,14},{9,15},{10,... | collective-permute-start | bytes 258056 | tf_op jit(solution)/shard_map/ppermute | solution.py:301
  6.6 5.6 %collective-permute-start.3 = (f32[168,128]{1,0:T(8,128)S(1)}, f32[168,128]{1,0:T(8,128)S(1)}, u32[]{:S(2)}, u32[]{:S(2)}) collective-permute-start(f32[168,128]{1,0:T(8,128)S(1)} %get-tuple-element.41), channel_id=1, source_target_pairs={{0,4},{1,5},{2,6},{3,7},{4,0},{5,1},{6,2},{7,3},{8,12},{9,13},{10,... | collective-permute-start | bytes 258056 | tf_op jit(solution)/shard_map/ppermute | solution.py:301
  7.1 5.1 %collective-permute-start.4 = (f32[168,128]{1,0:T(8,128)S(1)}, f32[168,128]{1,0:T(8,128)S(1)}, u32[]{:S(2)}, u32[]{:S(2)}) collective-permute-start(f32[168,128]{1,0:T(8,128)S(1)} %get-tuple-element.42), channel_id=1, source_target_pairs={{0,2},{1,3},{2,0},{3,1},{4,6},{5,7},{6,4},{7,5},{8,10},{9,11},{10,... | collective-permute-start | bytes 258056 | tf_op jit(solution)/shard_map/ppermute | solution.py:301
  14.3 15.0 %collective-permute-start.5 = (f32[64,128]{1,0:T(8,128)S(1)}, f32[64,128]{1,0:T(8,128)S(1)}, u32[]{:S(2)}, u32[]{:S(2)}) collective-permute-start(f32[64,128]{1,0:T(8,128)S(1)} %get-tuple-element.48), channel_id=1, source_target_pairs={{0,8},{8,0},{16,24},{24,16},{1,9},{9,1},{17,25},{25,17},{2,10},{10... | collective-permute-start | bytes 98312 | tf_op jit(solution)/shard_map/ppermute | solution.py:301
  16.3 13.0 %collective-permute-start.6 = (f32[64,128]{1,0:T(8,128)S(1)}, f32[64,128]{1,0:T(8,128)S(1)}, u32[]{:S(2)}, u32[]{:S(2)}) collective-permute-start(f32[64,128]{1,0:T(8,128)S(1)} %get-tuple-element.49), channel_id=1, source_target_pairs={{0,16},{8,24},{16,0},{24,8},{1,17},{9,25},{17,1},{25,9},{2,18},{10... | collective-permute-start | bytes 98312 | tf_op jit(solution)/shard_map/ppermute | solution.py:301
  18.9 10.4 %collective-permute-start.7 = (f32[64,128]{1,0:T(8,128)S(1)}, f32[64,128]{1,0:T(8,128)S(1)}, u32[]{:S(2)}, u32[]{:S(2)}) collective-permute-start(f32[64,128]{1,0:T(8,128)S(1)} %get-tuple-element.50), channel_id=1, source_target_pairs={{0,24},{8,16},{16,8},{24,0},{1,25},{9,17},{17,9},{25,1},{2,26},{10... | collective-permute-start | bytes 98312 | tf_op jit(solution)/shard_map/ppermute | solution.py:301
  29.5 1.4 %collective-permute-start.8 = (f32[4,48,128]{2,1,0:T(8,128)S(1)}, f32[4,48,128]{2,1,0:T(8,128)S(1)}, u32[]{:S(2)}, u32[]{:S(2)}) collective-permute-start(f32[4,48,128]{2,1,0:T(8,128)S(1)} %get-tuple-element.52), channel_id=1, source_target_pairs={{0,1},{1,0},{2,3},{3,2},{4,5},{5,4},{6,7},{7,6},{8,9},{9,8},{10,11... | collective-permute-start | bytes 294920 | tf_op jit(solution)/shard_map/ppermute | solution.py:301
  30.8 4.8 %collective-permute-start.9 = (f32[48,128]{1,0:T(8,128)S(1)}, f32[48,128]{1,0:T(8,128)S(1)}, u32[]{:S(2)}, u32[]{:S(2)}) collective-permute-start(f32[48,128]{1,0:T(8,128)S(1)} %get-tuple-element.53), channel_id=1, source_target_pairs={{0,6},{1,7},{2,4},{3,5},{4,2},{5,3},{6,0},{7,1},{8,14},{9,15},{10,... | collective-permute-start | bytes 73736 | tf_op jit(solution)/shard_map/ppermute | solution.py:301
  33.6 3.8 %collective-permute-start.10 = (f32[48,128]{1,0:T(8,128)S(1)}, f32[48,128]{1,0:T(8,128)S(1)}, u32[]{:S(2)}, u32[]{:S(2)}) collective-permute-start(f32[48,128]{1,0:T(8,128)S(1)} %get-tuple-element.54), channel_id=1, source_target_pairs={{0,4},{1,5},{2,6},{3,7},{4,0},{5,1},{6,2},{7,3},{8,12},{9,13},{10,... | collective-permute-start | bytes 73736 | tf_op jit(solution)/shard_map/ppermute | solution.py:301
  34.1 3.8 %collective-permute-start.11 = (f32[48,128]{1,0:T(8,128)S(1)}, f32[48,128]{1,0:T(8,128)S(1)}, u32[]{:S(2)}, u32[]{:S(2)}) collective-permute-start(f32[48,128]{1,0:T(8,128)S(1)} %get-tuple-element.55), channel_id=1, source_target_pairs={{0,2},{1,3},{2,0},{3,1},{4,6},{5,7},{6,4},{7,5},{8,10},{9,11},{10,... | collective-permute-start | bytes 73736 | tf_op jit(solution)/shard_map/ppermute | solution.py:301

commit v17 on v14

--- a/solution.py
+++ b/solution.py
@@ -368,7 +368,7 @@
         flops=2 * rhs * depth * own_width,
         moved=2 * depth * width + 2 * quarter * coarse_width,
     )(held, local_factor, coarse_factor, arrived[0])
-    chunk = quarter // 4
+    chunk = max(16, quarter // 8)
     count = coarse_width // BLK
     *fine, coarse_part, member, sums = call(
         functools.partial(fine_kernel, own, rows, begin, chunk, tile, pairs),

time: 37.2 us -> 37.8 us (1.016)
  Pallas kernels: 18.7 us -> 19.2 us
    pallas_call x1, Pallas kernels: 2.69 us -> 3.18 us  [on_device(): call(functools.partial(fine_kernel, own, rows, begin, chunk, tile, pairs)...]
where the time goes in v17:
time: 37.8 us; the launch traced here: 37.6 us
  Pallas kernels  19.2 us (51%)
  starting transfers between devices  13.2 us (35%)
  waiting for transfers between devices  5.07 us (13%)
    ppermute x12, starting transfers between devices, swap(): return lax.ppermute(value, axis, [(i, i ^ distance) for i in range(count)])  13.2 us
    pallas_call x1, Pallas kernels, on_device(): call(functools.partial(coarse_kernel, own, rows, chunk, tile), (sds((2 *...  8.31 us
    ppermute x12, waiting for transfers between devices, swap(): return lax.ppermute(value, axis, [(i, i ^ distance) for i in range(count)])  5.07 us
    pallas_call x1, Pallas kernels, on_device(): call(functools.partial(load_kernel, chunk, tile), (sds((rhs, depth), f32)...  4.94 us
    pallas_call x1, Pallas kernels, on_device(): call(functools.partial(fine_kernel, own, rows, begin, chunk, tile, pairs)...  3.18 us
    pallas_call x1, Pallas kernels, on_device(): call(functools.partial(pack_kernel, own, rows, pad), [sds((begin + halo *...  1.08 us
    pallas_call x1, Pallas kernels, on_device(): call(functools.partial(stage_kernel, own, rows), (sds(residual.shape, f32...  0.93 us
  transfers between devices with their start and end apart: 12, of which 5 were waited for; matrix products, arithmetic and copies ran while one was open for 0% of the time, Pallas kernels for 38%

profile of v17, /device:TPU:0, one launch (start us, length us, event | category | flops | bytes accessed | tf_op | source)
XLA Modules:
  0.0 37.6 jit_solution(4580845925739003937)
XLA Ops:
  0.0 0.5 %collective-permute-start.1 = (f32[8,3072]{1,0:T(8,128)}, f32[8,3072]{1,0:T(8,128)S(1)}, u32[]{:S(2)}, u32[]{:S(2)}) collective-permute-start(f32[8,3072]{1,0:T(8,128)} %residual_hbm.1), channel_id=1, source_target_pairs={{0,1},{1,0},{2,3},{3,2},{4,5},{5,4},{6,7},{7,6},{8,9},{9,8},{10,11... | collective-permute-start | bytes 294920 | tf_op jit(solution)/shard_map/ppermute | solution.py:299
  0.5 0.1 collective-permute-start
  0.5 0.9 %shard_map.55 = (f32[8,3072]{1,0:T(8,128)S(1)}, f32[48,128]{1,0:T(8,128)S(1)}, f32[1,24]{1,0:T(1,128)S(1)}) custom-call(f32[8,3072]{1,0:T(8,128)} %residual_hbm.1, s32[1,24]{1,0:T(1,128)} %bitcast.2), custom_call_target="tpu_custom_call" | custom-call | bytes 196608 | tf_op jit(solution)/shard_map/pallas_call | solution.py:328
  1.5 0.3 collective-permute-done.near_names
  1.7 0.0 collective-permute-done.1.near
  1.7 1.1 %shard_map.56 = (f32[168,128]{1,0:T(8,128)S(1)}, f32[168,128]{1,0:T(8,128)S(1)}, f32[168,128]{1,0:T(8,128)S(1)}, f32[168,128]{1,0:T(8,128)S(1)}, s32[8,128]{1,0:T(8,128)S(1)}, /*index=5*/s32[192,128]{1,0:T(8,128)S(1)}) custom-call(s32[8,8]{1,0:T(8,128)} %margin_hbm.1, f32[8,3072]{1,0:T(8,128)S(1)} %get-tuple-element.31.residual, ...), custom_call_target="tpu_custom_call" | custom-call | tf_op jit(solution)/shard_map/pallas_call | solution.py:340
  2.8 3.8 %collective-permute-start.2 = (f32[168,128]{1,0:T(8,128)S(1)}, f32[168,128]{1,0:T(8,128)S(1)}, u32[]{:S(2)}, u32[]{:S(2)}) collective-permute-start(f32[168,128]{1,0:T(8,128)S(1)} %get-tuple-element.40), channel_id=1, source_target_pairs={{0,6},{1,7},{2,4},{3,5},{4,2},{5,3},{6,0},{7,1},{8,14},{9,15},{10,... | collective-permute-start | bytes 258056 | tf_op jit(solution)/shard_map/ppermute | solution.py:299
  6.6 0.5 %collective-permute-start.3 = (f32[168,128]{1,0:T(8,128)S(1)}, f32[168,128]{1,0:T(8,128)S(1)}, u32[]{:S(2)}, u32[]{:S(2)}) collective-permute-start(f32[168,128]{1,0:T(8,128)S(1)} %get-tuple-element.41), channel_id=1, source_target_pairs={{0,4},{1,5},{2,6},{3,7},{4,0},{5,1},{6,2},{7,3},{8,12},{9,13},{10,... | collective-permute-start | bytes 258056 | tf_op jit(solution)/shard_map/ppermute | solution.py:299
  7.1 0.1 collective-permute-start.4
  7.2 4.9 %shard_map.57 = (f32[8,1024]{1,0:T(8,128)S(1)}, bf16[1,1024,4096]{2,1,0:T(8,128)(2,1)S(1)}, bf16[1024,8192]{1,0:T(8,128)(2,1)S(1)}) custom-call(f32[8,3072]{1,0:T(8,128)S(1)} %get-tuple-element.31.residual, bf16[1,1024,4096]{2,1,0:T(8,128)(2,1)} %fine_hbm.1, bf16[1024,8192]{1,0:T(8,128)(2,1)} %factor_hbm.1, f32[168,128]{1,0:T(8,128)S(1)} %get-tuple-element.36.after.refs_3_), custom_call_target="tpu_custom_call" | custom-call | flops 50331648 | bytes 12582912 | tf_op jit(solution)/shard_map/pallas_call | solution.py:356
  12.2 0.0 collective-permute-done.2.refs_0_
  12.2 0.0 collective-permute-done.3.refs_1_
  12.2 0.0 collective-permute-done.4.refs_2_
  12.2 3.2 %shard_map.58 = (f32[64,128]{1,0:T(8,128)S(1)}, f32[64,128]{1,0:T(8,128)S(1)}, f32[64,128]{1,0:T(8,128)S(1)}, f32[64,128]{1,0:T(8,128)S(1)}, bf16[1024,8192]{1,0...) custom-call(s32[8,128]{1,0:T(8,128)S(1)} %get-tuple-element.35.away, ...), custom_call_target="tpu_custom_call", output_to_operand_aliasing={{4}: (4, {})} | custom-call | flops 134217728 | bytes 12582912 | tf_op jit(solution)/shard_map/pallas_call | solution.py:373
  15.4 2.0 %collective-permute-start.5 = (f32[64,128]{1,0:T(8,128)S(1)}, f32[64,128]{1,0:T(8,128)S(1)}, u32[]{:S(2)}, u32[]{:S(2)}) collective-permute-start(f32[64,128]{1,0:T(8,128)S(1)} %get-tuple-element.48), channel_id=1, source_target_pairs={{0,8},{8,0},{16,24},{24,16},{1,9},{9,1},{17,25},{25,17},{2,10},{10... | collective-permute-start | bytes 98312 | tf_op jit(solution)/shard_map/ppermute | solution.py:299
  17.4 2.6 %collective-permute-start.6 = (f32[64,128]{1,0:T(8,128)S(1)}, f32[64,128]{1,0:T(8,128)S(1)}, u32[]{:S(2)}, u32[]{:S(2)}) collective-permute-start(f32[64,128]{1,0:T(8,128)S(1)} %get-tuple-element.49), channel_id=1, source_target_pairs={{0,16},{8,24},{16,0},{24,8},{1,17},{9,25},{17,1},{25,9},{2,18},{10... | collective-permute-start | bytes 98312 | tf_op jit(solution)/shard_map/ppermute | solution.py:299
  20.0 0.0 collective-permute-start.7
  20.0 8.3 %shard_map.59 = (f32[8,48,128]{2,1,0:T(8,128)S(1)}, bf16[1024,8192]{1,0:T(8,128)(2,1)S(1)}) custom-call(bf16[1024,8192]{1,0:T(8,128)(2,1)S(1)} %get-tuple-element.43.given, bf16[1024,8192]{1,0:T(8,128)(2,1)} %factor_hbm.1, f32[192,64]{1,0:T(8,128)S(1)} %get-tuple-element.44.member, ...), custom_call_target="tpu_custom_call", output_to_operand_aliasing={{1}: (0, {})} | custom-call | flops 67108864 | bytes 16777216 | tf_op jit(solution)/shard_map/pallas_call | solution.py:390
  28.3 0.0 collective-permute-done.5.refs_1_
  28.3 0.0 collective-permute-done.6.refs_2_
  28.3 0.0 collective-permute-done.7.refs_3_
  28.4 0.1 shard_map.60
  28.5 0.1 collective-permute-start.8
  28.6 1.3 %collective-permute-done.8.arrived = f32[4,48,128]{2,1,0:T(8,128)S(1)} collective-permute-done((f32[4,48,128]{2,1,0:T(8,128)S(1)}, f32[4,48,128]{2,1,0:T(8,128)S(1)}, u32[]{:S(2)}, u32[]{:S(2)}) %collective-permute-start.8) | collective-permute-done | bytes 98336 | tf_op jit(solution)/shard_map/ppermute | solution.py:299
  29.9 2.7 %collective-permute-start.9 = (f32[48,128]{1,0:T(8,128)S(1)}, f32[48,128]{1,0:T(8,128)S(1)}, u32[]{:S(2)}, u32[]{:S(2)}) collective-permute-start(f32[48,128]{1,0:T(8,128)S(1)} %get-tuple-element.53), channel_id=1, source_target_pairs={{0,6},{1,7},{2,4},{3,5},{4,2},{5,3},{6,0},{7,1},{8,14},{9,15},{10,... | collective-permute-start | bytes 73736 | tf_op jit(solution)/shard_map/ppermute | solution.py:299
  32.6 0.5 %collective-permute-start.10 = (f32[48,128]{1,0:T(8,128)S(1)}, f32[48,128]{1,0:T(8,128)S(1)}, u32[]{:S(2)}, u32[]{:S(2)}) collective-permute-start(f32[48,128]{1,0:T(8,128)S(1)} %get-tuple-element.54), channel_id=1, source_target_pairs={{0,4},{1,5},{2,6},{3,7},{4,0},{5,1},{6,2},{7,3},{8,12},{9,13},{10,... | collective-permute-start | bytes 73736 | tf_op jit(solution)/shard_map/ppermute | solution.py:299
  33.1 0.3 collective-permute-start.11
  33.4 1.2 %collective-permute-done.9.refs_0_ = f32[48,128]{1,0:T(8,128)S(1)} collective-permute-done((f32[48,128]{1,0:T(8,128)S(1)}, f32[48,128]{1,0:T(8,128)S(1)}, u32[]{:S(2)}, u32[]{:S(2)}) %collective-permute-start.9) | collective-permute-done | bytes 24608 | tf_op jit(solution)/shard_map/ppermute | solution.py:299
  34.7 1.8 %collective-permute-done.10.refs_1_ = f32[48,128]{1,0:T(8,128)S(1)} collective-permute-done((f32[48,128]{1,0:T(8,128)S(1)}, f32[48,128]{1,0:T(8,128)S(1)}, u32[]{:S(2)}, u32[]{:S(2)}) %collective-permute-start.10) | collective-permute-done | bytes 24608 | tf_op jit(solution)/shard_map/ppermute | solution.py:299
  36.4 0.5 %collective-permute-done.11.refs_2_ = f32[48,128]{1,0:T(8,128)S(1)} collective-permute-done((f32[48,128]{1,0:T(8,128)S(1)}, f32[48,128]{1,0:T(8,128)S(1)}, u32[]{:S(2)}, u32[]{:S(2)}) %collective-permute-start.11) | collective-permute-done | bytes 24608 | tf_op jit(solution)/shard_map/ppermute | solution.py:299
  36.9 0.6 %shard_map.62 = f32[2,3072]{1,0:T(2,128)} custom-call(f32[48,128]{1,0:T(8,128)S(1)} %collective-permute-done.9.refs_0_, f32[48,128]{1,0:T(8,128)S(1)} %collective-permute-done.10.refs_1_, f32[48,128]{1,0:T(8,128)S(1)} %collective-permute-done.11.refs_2_, f32[48,128]{1,0:T(8,128)S(1)} %get-tuple-element.56.refs_3_), custom_call_target="tpu_custom_call" | custom-call | tf_op jit(solution)/shard_map/pallas_call | solution.py:412
  (1 shorter events, 0.0 us)
Async XLA Ops:
  0.0 1.7 %collective-permute-start.1 = (f32[8,3072]{1,0:T(8,128)}, f32[8,3072]{1,0:T(8,128)S(1)}, u32[]{:S(2)}, u32[]{:S(2)}) collective-permute-start(f32[8,3072]{1,0:T(8,128)} %residual_hbm.1), channel_id=1, source_target_pairs={{0,1},{1,0},{2,3},{3,2},{4,5},{5,4},{6,7},{7,6},{8,9},{9,8},{10,11... | collective-permute-start | bytes 294920 | tf_op jit(solution)/shard_map/ppermute | solution.py:299
  0.5 1.3 %collective-permute-start = (s32[1,24]{1,0:T(1,128)}, s32[1,24]{1,0:T(1,128)S(1)}, u32[]{:S(2)}, u32[]{:S(2)}) collective-permute-start(s32[1,24]{1,0:T(1,128)} %bitcast.1), channel_id=1, source_target_pairs={{0,1},{1,0},{2,3},{3,2},{4,5},{5,4},{6,7},{7,6},{8,9},{9,8},{10,11... | collective-permute-start | bytes 296 | tf_op jit(solution)/shard_map/ppermute | solution.py:299
  2.8 9.4 %collective-permute-start.2 = (f32[168,128]{1,0:T(8,128)S(1)}, f32[168,128]{1,0:T(8,128)S(1)}, u32[]{:S(2)}, u32[]{:S(2)}) collective-permute-start(f32[168,128]{1,0:T(8,128)S(1)} %get-tuple-element.40), channel_id=1, source_target_pairs={{0,6},{1,7},{2,4},{3,5},{4,2},{5,3},{6,0},{7,1},{8,14},{9,15},{10,... | collective-permute-start | bytes 258056 | tf_op jit(solution)/shard_map/ppermute | solution.py:299
  6.6 5.6 %collective-permute-start.3 = (f32[168,128]{1,0:T(8,128)S(1)}, f32[168,128]{1,0:T(8,128)S(1)}, u32[]{:S(2)}, u32[]{:S(2)}) collective-permute-start(f32[168,128]{1,0:T(8,128)S(1)} %get-tuple-element.41), channel_id=1, source_target_pairs={{0,4},{1,5},{2,6},{3,7},{4,0},{5,1},{6,2},{7,3},{8,12},{9,13},{10,... | collective-permute-start | bytes 258056 | tf_op jit(solution)/shard_map/ppermute | solution.py:299
  7.1 5.1 %collective-permute-start.4 = (f32[168,128]{1,0:T(8,128)S(1)}, f32[168,128]{1,0:T(8,128)S(1)}, u32[]{:S(2)}, u32[]{:S(2)}) collective-permute-start(f32[168,128]{1,0:T(8,128)S(1)} %get-tuple-element.42), channel_id=1, source_target_pairs={{0,2},{1,3},{2,0},{3,1},{4,6},{5,7},{6,4},{7,5},{8,10},{9,11},{10,... | collective-permute-start | bytes 258056 | tf_op jit(solution)/shard_map/ppermute | solution.py:299
  15.4 13.0 %collective-permute-start.5 = (f32[64,128]{1,0:T(8,128)S(1)}, f32[64,128]{1,0:T(8,128)S(1)}, u32[]{:S(2)}, u32[]{:S(2)}) collective-permute-start(f32[64,128]{1,0:T(8,128)S(1)} %get-tuple-element.48), channel_id=1, source_target_pairs={{0,8},{8,0},{16,24},{24,16},{1,9},{9,1},{17,25},{25,17},{2,10},{10... | collective-permute-start | bytes 98312 | tf_op jit(solution)/shard_map/ppermute | solution.py:299
  17.4 10.9 %collective-permute-start.6 = (f32[64,128]{1,0:T(8,128)S(1)}, f32[64,128]{1,0:T(8,128)S(1)}, u32[]{:S(2)}, u32[]{:S(2)}) collective-permute-start(f32[64,128]{1,0:T(8,128)S(1)} %get-tuple-element.49), channel_id=1, source_target_pairs={{0,16},{8,24},{16,0},{24,8},{1,17},{9,25},{17,1},{25,9},{2,18},{10... | collective-permute-start | bytes 98312 | tf_op jit(solution)/shard_map/ppermute | solution.py:299
  20.0 8.3 %collective-permute-start.7 = (f32[64,128]{1,0:T(8,128)S(1)}, f32[64,128]{1,0:T(8,128)S(1)}, u32[]{:S(2)}, u32[]{:S(2)}) collective-permute-start(f32[64,128]{1,0:T(8,128)S(1)} %get-tuple-element.50), channel_id=1, source_target_pairs={{0,24},{8,16},{16,8},{24,0},{1,25},{9,17},{17,9},{25,1},{2,26},{10... | collective-permute-start | bytes 98312 | tf_op jit(solution)/shard_map/ppermute | solution.py:299
  28.5 1.4 %collective-permute-start.8 = (f32[4,48,128]{2,1,0:T(8,128)S(1)}, f32[4,48,128]{2,1,0:T(8,128)S(1)}, u32[]{:S(2)}, u32[]{:S(2)}) collective-permute-start(f32[4,48,128]{2,1,0:T(8,128)S(1)} %get-tuple-element.52), channel_id=1, source_target_pairs={{0,1},{1,0},{2,3},{3,2},{4,5},{5,4},{6,7},{7,6},{8,9},{9,8},{10,11... | collective-permute-start | bytes 294920 | tf_op jit(solution)/shard_map/ppermute | solution.py:299
  29.9 4.8 %collective-permute-start.9 = (f32[48,128]{1,0:T(8,128)S(1)}, f32[48,128]{1,0:T(8,128)S(1)}, u32[]{:S(2)}, u32[]{:S(2)}) collective-permute-start(f32[48,128]{1,0:T(8,128)S(1)} %get-tuple-element.53), channel_id=1, source_target_pairs={{0,6},{1,7},{2,4},{3,5},{4,2},{5,3},{6,0},{7,1},{8,14},{9,15},{10,... | collective-permute-start | bytes 73736 | tf_op jit(solution)/shard_map/ppermute | solution.py:299
  32.6 3.8 %collective-permute-start.10 = (f32[48,128]{1,0:T(8,128)S(1)}, f32[48,128]{1,0:T(8,128)S(1)}, u32[]{:S(2)}, u32[]{:S(2)}) collective-permute-start(f32[48,128]{1,0:T(8,128)S(1)} %get-tuple-element.54), channel_id=1, source_target_pairs={{0,4},{1,5},{2,6},{3,7},{4,0},{5,1},{6,2},{7,3},{8,12},{9,13},{10,... | collective-permute-start | bytes 73736 | tf_op jit(solution)/shard_map/ppermute | solution.py:299
  33.1 3.8 %collective-permute-start.11 = (f32[48,128]{1,0:T(8,128)S(1)}, f32[48,128]{1,0:T(8,128)S(1)}, u32[]{:S(2)}, u32[]{:S(2)}) collective-permute-start(f32[48,128]{1,0:T(8,128)S(1)} %get-tuple-element.55), channel_id=1, source_target_pairs={{0,2},{1,3},{2,0},{3,1},{4,6},{5,7},{6,4},{7,5},{8,10},{9,11},{10,... | collective-permute-start | bytes 73736 | tf_op jit(solution)/shard_map/ppermute | solution.py:299

commit v18 on v14

--- a/solution.py
+++ b/solution.py
@@ -405,7 +405,7 @@
         functools.partial(merge_kernel, own, rows, grp_count, halo),
         [field, field],
         [VMEM] * (2 + grp_count),
-    )(place, spread, *panels)
+    )(place, spread, *panels[::-1])
     back = call(add_kernel, [sds((size, BLK), f32)] * pairs, [VMEM, VMEM])(
         kept, swap(crossing, "sub", 1)
     )

time: 37.2 us -> 37.2 us (level)
  no operation moved by 1% of the time
where the time goes in v18:
time: 37.2 us; the launch traced here: 37 us
  Pallas kernels  18.7 us (50%)
  starting transfers between devices  13.2 us (35%)
  waiting for transfers between devices  4.99 us (13%)
    ppermute x12, starting transfers between devices, swap(): return lax.ppermute(value, axis, [(i, i ^ distance) for i in range(count)])  13.2 us
    pallas_call x1, Pallas kernels, on_device(): call(functools.partial(coarse_kernel, own, rows, chunk, tile), (sds((2 *...  8.27 us
    ppermute x12, waiting for transfers between devices, swap(): return lax.ppermute(value, axis, [(i, i ^ distance) for i in range(count)])  4.99 us
    pallas_call x1, Pallas kernels, on_device(): call(functools.partial(load_kernel, chunk, tile), (sds((rhs, depth), f32)...  4.94 us
    pallas_call x1, Pallas kernels, on_device(): call(functools.partial(fine_kernel, own, rows, begin, chunk, tile, pairs)...  2.69 us
    pallas_call x1, Pallas kernels, on_device(): call(functools.partial(pack_kernel, own, rows, pad), [sds((begin + halo *...  1.08 us
    pallas_call x1, Pallas kernels, on_device(): call(functools.partial(stage_kernel, own, rows), (sds(residual.shape, f32...  0.93 us
  transfers between devices with their start and end apart: 12, of which 5 were waited for; matrix products, arithmetic and copies ran while one was open for 0% of the time, Pallas kernels for 38%

profile of v18, /device:TPU:0, one launch (start us, length us, event | category | flops | bytes accessed | tf_op | source)
XLA Modules:
  0.0 37.0 jit_solution(156426816374693100)
XLA Ops:
  0.0 0.5 %collective-permute-start.1 = (f32[8,3072]{1,0:T(8,128)}, f32[8,3072]{1,0:T(8,128)S(1)}, u32[]{:S(2)}, u32[]{:S(2)}) collective-permute-start(f32[8,3072]{1,0:T(8,128)} %residual_hbm.1), channel_id=1, source_target_pairs={{0,1},{1,0},{2,3},{3,2},{4,5},{5,4},{6,7},{7,6},{8,9},{9,8},{10,11... | collective-permute-start | bytes 294920 | tf_op jit(solution)/shard_map/ppermute | solution.py:299
  0.5 0.1 collective-permute-start
  0.5 0.9 %shard_map.55 = (f32[8,3072]{1,0:T(8,128)S(1)}, f32[48,128]{1,0:T(8,128)S(1)}, f32[1,24]{1,0:T(1,128)S(1)}) custom-call(f32[8,3072]{1,0:T(8,128)} %residual_hbm.1, s32[1,24]{1,0:T(1,128)} %bitcast.2), custom_call_target="tpu_custom_call" | custom-call | bytes 196608 | tf_op jit(solution)/shard_map/pallas_call | solution.py:328
  1.5 0.3 collective-permute-done.near_names
  1.7 0.0 collective-permute-done.1.near
  1.7 1.1 %shard_map.56 = (f32[168,128]{1,0:T(8,128)S(1)}, f32[168,128]{1,0:T(8,128)S(1)}, f32[168,128]{1,0:T(8,128)S(1)}, f32[168,128]{1,0:T(8,128)S(1)}, s32[8,128]{1,0:T(8,128)S(1)}, /*index=5*/s32[192,128]{1,0:T(8,128)S(1)}) custom-call(s32[8,8]{1,0:T(8,128)} %margin_hbm.1, f32[8,3072]{1,0:T(8,128)S(1)} %get-tuple-element.31.residual, ...), custom_call_target="tpu_custom_call" | custom-call | tf_op jit(solution)/shard_map/pallas_call | solution.py:340
  2.8 3.8 %collective-permute-start.2 = (f32[168,128]{1,0:T(8,128)S(1)}, f32[168,128]{1,0:T(8,128)S(1)}, u32[]{:S(2)}, u32[]{:S(2)}) collective-permute-start(f32[168,128]{1,0:T(8,128)S(1)} %get-tuple-element.40), channel_id=1, source_target_pairs={{0,6},{1,7},{2,4},{3,5},{4,2},{5,3},{6,0},{7,1},{8,14},{9,15},{10,... | collective-permute-start | bytes 258056 | tf_op jit(solution)/shard_map/ppermute | solution.py:299
  6.6 0.5 %collective-permute-start.3 = (f32[168,128]{1,0:T(8,128)S(1)}, f32[168,128]{1,0:T(8,128)S(1)}, u32[]{:S(2)}, u32[]{:S(2)}) collective-permute-start(f32[168,128]{1,0:T(8,128)S(1)} %get-tuple-element.41), channel_id=1, source_target_pairs={{0,4},{1,5},{2,6},{3,7},{4,0},{5,1},{6,2},{7,3},{8,12},{9,13},{10,... | collective-permute-start | bytes 258056 | tf_op jit(solution)/shard_map/ppermute | solution.py:299
  7.1 0.1 collective-permute-start.4
  7.2 4.9 %shard_map.57 = (f32[8,1024]{1,0:T(8,128)S(1)}, bf16[1,1024,4096]{2,1,0:T(8,128)(2,1)S(1)}, bf16[1024,8192]{1,0:T(8,128)(2,1)S(1)}) custom-call(f32[8,3072]{1,0:T(8,128)S(1)} %get-tuple-element.31.residual, bf16[1,1024,4096]{2,1,0:T(8,128)(2,1)} %fine_hbm.1, bf16[1024,8192]{1,0:T(8,128)(2,1)} %factor_hbm.1, f32[168,128]{1,0:T(8,128)S(1)} %get-tuple-element.36.after.refs_3_), custom_call_target="tpu_custom_call" | custom-call | flops 50331648 | bytes 12582912 | tf_op jit(solution)/shard_map/pallas_call | solution.py:356
  12.2 0.0 collective-permute-done.2.refs_0_
  12.2 0.0 collective-permute-done.3.refs_1_
  12.2 0.0 collective-permute-done.4.refs_2_
  12.2 2.7 %shard_map.58 = (f32[64,128]{1,0:T(8,128)S(1)}, f32[64,128]{1,0:T(8,128)S(1)}, f32[64,128]{1,0:T(8,128)S(1)}, f32[64,128]{1,0:T(8,128)S(1)}, bf16[1024,8192]{1,0...) custom-call(s32[8,128]{1,0:T(8,128)S(1)} %get-tuple-element.35.away, ...), custom_call_target="tpu_custom_call", output_to_operand_aliasing={{4}: (4, {})} | custom-call | flops 134217728 | bytes 12582912 | tf_op jit(solution)/shard_map/pallas_call | solution.py:373
  14.9 4.1 %collective-permute-start.5 = (f32[64,128]{1,0:T(8,128)S(1)}, f32[64,128]{1,0:T(8,128)S(1)}, u32[]{:S(2)}, u32[]{:S(2)}) collective-permute-start(f32[64,128]{1,0:T(8,128)S(1)} %get-tuple-element.47), channel_id=1, source_target_pairs={{0,24},{8,16},{16,8},{24,0},{1,25},{9,17},{17,9},{25,1},{2,26},{10... | collective-permute-start | bytes 98312 | tf_op jit(solution)/shard_map/ppermute | solution.py:299
  18.9 0.0 collective-permute-start.6
  19.0 0.6 %collective-permute-start.7 = (f32[64,128]{1,0:T(8,128)S(1)}, f32[64,128]{1,0:T(8,128)S(1)}, u32[]{:S(2)}, u32[]{:S(2)}) collective-permute-start(f32[64,128]{1,0:T(8,128)S(1)} %get-tuple-element.49), channel_id=1, source_target_pairs={{0,8},{8,0},{16,24},{24,16},{1,9},{9,1},{17,25},{25,17},{2,10},{10... | collective-permute-start | bytes 98312 | tf_op jit(solution)/shard_map/ppermute | solution.py:299
  19.6 8.3 %shard_map.59 = (f32[8,48,128]{2,1,0:T(8,128)S(1)}, bf16[1024,8192]{1,0:T(8,128)(2,1)S(1)}) custom-call(bf16[1024,8192]{1,0:T(8,128)(2,1)S(1)} %get-tuple-element.43.given, bf16[1024,8192]{1,0:T(8,128)(2,1)} %factor_hbm.1, f32[192,64]{1,0:T(8,128)S(1)} %get-tuple-element.44.member, ...), custom_call_target="tpu_custom_call", output_to_operand_aliasing={{1}: (0, {})} | custom-call | flops 67108864 | bytes 16777216 | tf_op jit(solution)/shard_map/pallas_call | solution.py:390
  27.9 0.0 collective-permute-done.5.refs_0_
  27.9 0.0 collective-permute-done.6.refs_1_
  27.9 0.0 collective-permute-done.7.refs_2_
  27.9 0.1 shard_map.60
  28.0 0.1 collective-permute-start.8
  28.1 1.3 %collective-permute-done.8.arrived = f32[4,48,128]{2,1,0:T(8,128)S(1)} collective-permute-done((f32[4,48,128]{2,1,0:T(8,128)S(1)}, f32[4,48,128]{2,1,0:T(8,128)S(1)}, u32[]{:S(2)}, u32[]{:S(2)}) %collective-permute-start.8) | collective-permute-done | bytes 98336 | tf_op jit(solution)/shard_map/ppermute | solution.py:299
  29.4 2.7 %collective-permute-start.9 = (f32[48,128]{1,0:T(8,128)S(1)}, f32[48,128]{1,0:T(8,128)S(1)}, u32[]{:S(2)}, u32[]{:S(2)}) collective-permute-start(f32[48,128]{1,0:T(8,128)S(1)} %get-tuple-element.53), channel_id=1, source_target_pairs={{0,6},{1,7},{2,4},{3,5},{4,2},{5,3},{6,0},{7,1},{8,14},{9,15},{10,... | collective-permute-start | bytes 73736 | tf_op jit(solution)/shard_map/ppermute | solution.py:299
  32.1 0.5 %collective-permute-start.10 = (f32[48,128]{1,0:T(8,128)S(1)}, f32[48,128]{1,0:T(8,128)S(1)}, u32[]{:S(2)}, u32[]{:S(2)}) collective-permute-start(f32[48,128]{1,0:T(8,128)S(1)} %get-tuple-element.54), channel_id=1, source_target_pairs={{0,4},{1,5},{2,6},{3,7},{4,0},{5,1},{6,2},{7,3},{8,12},{9,13},{10,... | collective-permute-start | bytes 73736 | tf_op jit(solution)/shard_map/ppermute | solution.py:299
  32.6 0.4 %collective-permute-start.11 = (f32[48,128]{1,0:T(8,128)S(1)}, f32[48,128]{1,0:T(8,128)S(1)}, u32[]{:S(2)}, u32[]{:S(2)}) collective-permute-start(f32[48,128]{1,0:T(8,128)S(1)} %get-tuple-element.55), channel_id=1, source_target_pairs={{0,2},{1,3},{2,0},{3,1},{4,6},{5,7},{6,4},{7,5},{8,10},{9,11},{10,... | collective-permute-start | bytes 73736 | tf_op jit(solution)/shard_map/ppermute | solution.py:299
  33.0 1.2 %collective-permute-done.9.refs_0_ = f32[48,128]{1,0:T(8,128)S(1)} collective-permute-done((f32[48,128]{1,0:T(8,128)S(1)}, f32[48,128]{1,0:T(8,128)S(1)}, u32[]{:S(2)}, u32[]{:S(2)}) %collective-permute-start.9) | collective-permute-done | bytes 24608 | tf_op jit(solution)/shard_map/ppermute | solution.py:299
  34.2 1.7 %collective-permute-done.10.refs_1_ = f32[48,128]{1,0:T(8,128)S(1)} collective-permute-done((f32[48,128]{1,0:T(8,128)S(1)}, f32[48,128]{1,0:T(8,128)S(1)}, u32[]{:S(2)}, u32[]{:S(2)}) %collective-permute-start.10) | collective-permute-done | bytes 24608 | tf_op jit(solution)/shard_map/ppermute | solution.py:299
  35.9 0.5 %collective-permute-done.11.refs_2_ = f32[48,128]{1,0:T(8,128)S(1)} collective-permute-done((f32[48,128]{1,0:T(8,128)S(1)}, f32[48,128]{1,0:T(8,128)S(1)}, u32[]{:S(2)}, u32[]{:S(2)}) %collective-permute-start.11) | collective-permute-done | bytes 24608 | tf_op jit(solution)/shard_map/ppermute | solution.py:299
  36.4 0.6 %shard_map.62 = f32[2,3072]{1,0:T(2,128)} custom-call(f32[48,128]{1,0:T(8,128)S(1)} %collective-permute-done.9.refs_0_, f32[48,128]{1,0:T(8,128)S(1)} %collective-permute-done.10.refs_1_, f32[48,128]{1,0:T(8,128)S(1)} %collective-permute-done.11.refs_2_, f32[48,128]{1,0:T(8,128)S(1)} %get-tuple-element.56.refs_3_), custom_call_target="tpu_custom_call" | custom-call | tf_op jit(solution)/shard_map/pallas_call | solution.py:412
  (1 shorter events, 0.0 us)
Async XLA Ops:
  0.0 1.7 %collective-permute-start.1 = (f32[8,3072]{1,0:T(8,128)}, f32[8,3072]{1,0:T(8,128)S(1)}, u32[]{:S(2)}, u32[]{:S(2)}) collective-permute-start(f32[8,3072]{1,0:T(8,128)} %residual_hbm.1), channel_id=1, source_target_pairs={{0,1},{1,0},{2,3},{3,2},{4,5},{5,4},{6,7},{7,6},{8,9},{9,8},{10,11... | collective-permute-start | bytes 294920 | tf_op jit(solution)/shard_map/ppermute | solution.py:299
  0.5 1.3 %collective-permute-start = (s32[1,24]{1,0:T(1,128)}, s32[1,24]{1,0:T(1,128)S(1)}, u32[]{:S(2)}, u32[]{:S(2)}) collective-permute-start(s32[1,24]{1,0:T(1,128)} %bitcast.1), channel_id=1, source_target_pairs={{0,1},{1,0},{2,3},{3,2},{4,5},{5,4},{6,7},{7,6},{8,9},{9,8},{10,11... | collective-permute-start | bytes 296 | tf_op jit(solution)/shard_map/ppermute | solution.py:299
  2.8 9.4 %collective-permute-start.2 = (f32[168,128]{1,0:T(8,128)S(1)}, f32[168,128]{1,0:T(8,128)S(1)}, u32[]{:S(2)}, u32[]{:S(2)}) collective-permute-start(f32[168,128]{1,0:T(8,128)S(1)} %get-tuple-element.40), channel_id=1, source_target_pairs={{0,6},{1,7},{2,4},{3,5},{4,2},{5,3},{6,0},{7,1},{8,14},{9,15},{10,... | collective-permute-start | bytes 258056 | tf_op jit(solution)/shard_map/ppermute | solution.py:299
  6.6 5.6 %collective-permute-start.3 = (f32[168,128]{1,0:T(8,128)S(1)}, f32[168,128]{1,0:T(8,128)S(1)}, u32[]{:S(2)}, u32[]{:S(2)}) collective-permute-start(f32[168,128]{1,0:T(8,128)S(1)} %get-tuple-element.41), channel_id=1, source_target_pairs={{0,4},{1,5},{2,6},{3,7},{4,0},{5,1},{6,2},{7,3},{8,12},{9,13},{10,... | collective-permute-start | bytes 258056 | tf_op jit(solution)/shard_map/ppermute | solution.py:299
  7.1 5.1 %collective-permute-start.4 = (f32[168,128]{1,0:T(8,128)S(1)}, f32[168,128]{1,0:T(8,128)S(1)}, u32[]{:S(2)}, u32[]{:S(2)}) collective-permute-start(f32[168,128]{1,0:T(8,128)S(1)} %get-tuple-element.42), channel_id=1, source_target_pairs={{0,2},{1,3},{2,0},{3,1},{4,6},{5,7},{6,4},{7,5},{8,10},{9,11},{10,... | collective-permute-start | bytes 258056 | tf_op jit(solution)/shard_map/ppermute | solution.py:299
  14.9 13.0 %collective-permute-start.5 = (f32[64,128]{1,0:T(8,128)S(1)}, f32[64,128]{1,0:T(8,128)S(1)}, u32[]{:S(2)}, u32[]{:S(2)}) collective-permute-start(f32[64,128]{1,0:T(8,128)S(1)} %get-tuple-element.47), channel_id=1, source_target_pairs={{0,24},{8,16},{16,8},{24,0},{1,25},{9,17},{17,9},{25,1},{2,26},{10... | collective-permute-start | bytes 98312 | tf_op jit(solution)/shard_map/ppermute | solution.py:299
  18.9 8.9 %collective-permute-start.6 = (f32[64,128]{1,0:T(8,128)S(1)}, f32[64,128]{1,0:T(8,128)S(1)}, u32[]{:S(2)}, u32[]{:S(2)}) collective-permute-start(f32[64,128]{1,0:T(8,128)S(1)} %get-tuple-element.48), channel_id=1, source_target_pairs={{0,16},{8,24},{16,0},{24,8},{1,17},{9,25},{17,1},{25,9},{2,18},{10... | collective-permute-start | bytes 98312 | tf_op jit(solution)/shard_map/ppermute | solution.py:299
  19.0 8.9 %collective-permute-start.7 = (f32[64,128]{1,0:T(8,128)S(1)}, f32[64,128]{1,0:T(8,128)S(1)}, u32[]{:S(2)}, u32[]{:S(2)}) collective-permute-start(f32[64,128]{1,0:T(8,128)S(1)} %get-tuple-element.49), channel_id=1, source_target_pairs={{0,8},{8,0},{16,24},{24,16},{1,9},{9,1},{17,25},{25,17},{2,10},{10... | collective-permute-start | bytes 98312 | tf_op jit(solution)/shard_map/ppermute | solution.py:299
  28.0 1.4 %collective-permute-start.8 = (f32[4,48,128]{2,1,0:T(8,128)S(1)}, f32[4,48,128]{2,1,0:T(8,128)S(1)}, u32[]{:S(2)}, u32[]{:S(2)}) collective-permute-start(f32[4,48,128]{2,1,0:T(8,128)S(1)} %get-tuple-element.52), channel_id=1, source_target_pairs={{0,1},{1,0},{2,3},{3,2},{4,5},{5,4},{6,7},{7,6},{8,9},{9,8},{10,11... | collective-permute-start | bytes 294920 | tf_op jit(solution)/shard_map/ppermute | solution.py:299
  29.4 4.8 %collective-permute-start.9 = (f32[48,128]{1,0:T(8,128)S(1)}, f32[48,128]{1,0:T(8,128)S(1)}, u32[]{:S(2)}, u32[]{:S(2)}) collective-permute-start(f32[48,128]{1,0:T(8,128)S(1)} %get-tuple-element.53), channel_id=1, source_target_pairs={{0,6},{1,7},{2,4},{3,5},{4,2},{5,3},{6,0},{7,1},{8,14},{9,15},{10,... | collective-permute-start | bytes 73736 | tf_op jit(solution)/shard_map/ppermute | solution.py:299
  32.1 3.8 %collective-permute-start.10 = (f32[48,128]{1,0:T(8,128)S(1)}, f32[48,128]{1,0:T(8,128)S(1)}, u32[]{:S(2)}, u32[]{:S(2)}) collective-permute-start(f32[48,128]{1,0:T(8,128)S(1)} %get-tuple-element.54), channel_id=1, source_target_pairs={{0,4},{1,5},{2,6},{3,7},{4,0},{5,1},{6,2},{7,3},{8,12},{9,13},{10,... | collective-permute-start | bytes 73736 | tf_op jit(solution)/shard_map/ppermute | solution.py:299
  32.6 3.8 %collective-permute-start.11 = (f32[48,128]{1,0:T(8,128)S(1)}, f32[48,128]{1,0:T(8,128)S(1)}, u32[]{:S(2)}, u32[]{:S(2)}) collective-permute-start(f32[48,128]{1,0:T(8,128)S(1)} %get-tuple-element.55), channel_id=1, source_target_pairs={{0,2},{1,3},{2,0},{3,1},{4,6},{5,7},{6,4},{7,5},{8,10},{9,11},{10,... | collective-permute-start | bytes 73736 | tf_op jit(solution)/shard_map/ppermute | solution.py:299
